TPU v7x, 128 devices: a whole 4x4x4 slice. The times are simulated.
128 devices in a mesh: lat: 4 (over y_lo, core), lon: 32 (over z, x, y_hi).
Axes of the slice: x: 4, y: 4 (y_hi: 2, y_lo: 2; y = y_hi * 2 + y_lo), z: 4, core: 2. Of those that a mesh axis runs over, the one named last changes fastest.
Arguments:
- query_vectors: bfloat16 [128, 512, 512], P('lat', 'lon'), may hold values from -6 to 6
- key_vectors: bfloat16 [128, 512, 512], P('lat', 'lon'), may hold values from -6 to 6
- value_vectors: bfloat16 [128, 512, 512], P('lat', 'lon'), may hold values from -6 to 6
- output_grads: bfloat16 [128, 512, 512], P('lat', 'lon'), may hold values from -6 to 6
Outputs:
- query_grads: bfloat16 [128, 512, 512], P('lat', 'lon')
- key_grads: bfloat16 [128, 512, 512], P('lat', 'lon')
- value_grads: bfloat16 [128, 512, 512], P('lat', 'lon')
All inputs are finite; a program needn't handle non-finite values.
Results may differ from a plain program's by a relative error of at most 0.0084.
Values may be sent and summed in bfloat16 or wider, within the bound.
No kernel may reach another device: no remote copies, remote signals or barrier semaphores. Data moves between devices by JAX's collectives and lax.ppermute only.
A program may use at most 128 MiB of HBM per device.

v0:
```python
import functools

import jax
import jax.numpy as jnp
from jax import lax
from jax.experimental import pallas as pl
from jax.experimental.pallas import tpu as pltpu
from jax.sharding import PartitionSpec as P

ROWS = 4
CELLS = 64
OWN = ROWS * CELLS
EXT = (ROWS + 2) * CELLS
PAIR = 128
PAIRS = 4
FEAT = 512
SCALE = 64 ** -0.5
LOG2E = 1.4426950408889634
MASKED = -1e30
F32 = jnp.float32
BF16 = jnp.bfloat16
VMEM_LIMIT = 48 * 1024 * 1024


def matmul(a, b, contract):
    return lax.dot_general(a, b, ((contract[:1], contract[1:]), ((), ())), preferred_element_type=F32)


def params():
    return pltpu.CompilerParams(vmem_limit_bytes=VMEM_LIMIT)


def cost(flops, size):
    return pl.CostEstimate(flops=int(flops), bytes_accessed=int(size), transcendentals=0)


def struct(shape, dtype):
    return jax.ShapeDtypeStruct(shape, dtype)


def split_columns(block):
    wide = block.astype(F32)
    return [wide[:, c * 8:(c + 1) * 8].reshape(CELLS, FEAT).astype(BF16) for c in range(2)]


def pack_kernel(q_ref, k_ref, v_ref, g_ref, west_ref, east_ref, kd_ref, vd_ref, north_ref, south_ref):
    step = pl.program_id(0)
    q0, q1 = split_columns(q_ref[...])
    g0, g1 = split_columns(g_ref[...])
    west_ref[0] = q0
    west_ref[1] = g0
    east_ref[0] = q1
    east_ref[1] = g1
    keys = split_columns(k_ref[...])
    values = split_columns(v_ref[...])
    for c in range(2):
        kd_ref[c] = keys[c]
        vd_ref[c] = values[c]

    @pl.when(step == 0)
    def _():
        for c in range(2):
            north_ref[0, c] = keys[c]
            north_ref[1, c] = values[c]

    @pl.when(step == ROWS - 1)
    def _():
        for c in range(2):
            south_ref[0, c] = keys[c]
            south_ref[1, c] = values[c]


def pack(q, k, v, g):
    grid_spec = pl.BlockSpec((8, 16, FEAT), lambda t: (t, 0, 0))
    tile_spec = pl.BlockSpec((2, CELLS, FEAT), lambda t: (0, t, 0))
    edge_spec = pl.BlockSpec((2, 2, CELLS, FEAT), lambda t: (0, 0, 0, 0))
    tiles = struct((2, OWN, FEAT), BF16)
    edge = struct((2, 2, CELLS, FEAT), BF16)
    return pl.pallas_call(
        pack_kernel,
        grid=(ROWS,),
        in_specs=[grid_spec] * 4,
        out_specs=[tile_spec] * 4 + [edge_spec] * 2,
        out_shape=[tiles] * 4 + [edge] * 2,
        compiler_params=params(),
        cost_estimate=cost(0, 5 << 20),
        name="pack",
    )(q, k, v, g)


def head_masks():
    lane = lax.broadcasted_iota(jnp.int32, (1, PAIR), 1)
    first = jnp.where(lane < 64, 1.0, 0.0).astype(F32)
    return first.astype(BF16), (1.0 - first).astype(BF16)


def stacked(parts, masks):
    return jnp.concatenate([part * mask for part in parts for mask in masks], axis=0)


def pole_biases():
    lat = lax.axis_index("lat")
    count = lax.axis_size("lat")
    return (jnp.where(lat == 0, MASKED, 0.0).astype(F32),
            jnp.where(lat == count - 1, MASKED, 0.0).astype(F32))


def fill_keys(ext, own, north, south, which):
    for c in range(2):
        ext[c, 0:CELLS] = north[which, c]
        ext[c, CELLS:CELLS + OWN] = own[c]
        ext[c, CELLS + OWN:EXT] = south[which, c]


def window(ext, columns, t, first=0, last=3):
    parts = [ext[c, (t + first) * CELLS:(t + last) * CELLS] for c in columns]
    return parts[0] if len(parts) == 1 else jnp.concatenate(parts, axis=0)


def score_block(keys, queries, columns, t, biases, first=0, last=3):
    scores = matmul(keys, queries, (1, 1)) * (SCALE * LOG2E)
    if t + first > 0 and t + last < ROWS + 2:
        return scores
    parts = []
    span = (last - first) * CELLS
    for c in range(columns):
        for r in range(first, last):
            base = c * span + (r - first) * CELLS
            part = scores[base:base + CELLS]
            if t + r == 0:
                part = part + biases[0]
            if t + r == ROWS + 1:
                part = part + biases[1]
            parts.append(part)
    return jnp.concatenate(parts, axis=0)


def row_stats(scores, dprobs):
    top = jnp.max(scores, axis=0, keepdims=True)
    weights = jnp.exp2(scores - top)
    total = jnp.sum(weights, axis=0, keepdims=True)
    delta = jnp.sum(weights * dprobs, axis=0, keepdims=True) / total
    return top + jnp.log(total) * LOG2E, delta


def merged(log_a, delta_a, log_b, delta_b):
    top = jnp.maximum(log_a, log_b)
    weight_a = jnp.exp2(log_a - top)
    weight_b = jnp.exp2(log_b - top)
    total = weight_a + weight_b
    return top + jnp.log(total) * LOG2E, (weight_a * delta_a + weight_b * delta_b) / total


def own_heads(lane, x):
    return jnp.where(lane < 64, x[0:CELLS], x[CELLS:2 * CELLS])


def stats_kernel(west, east, kd, vd, north, south, st0, st1, kx, vx):
    masks = head_masks()
    biases = pole_biases()
    fill_keys(kx, kd, north, south, 0)
    fill_keys(vx, vd, north, south, 1)
    for t in range(ROWS):
        at = slice(t * CELLS, (t + 1) * CELLS)
        queries = stacked([west[0, at], east[0, at]], masks)
        grads = stacked([west[1, at], east[1, at]], masks)
        scores = score_block(window(kx, (0, 1), t), queries, 2, t, biases)
        dprobs = matmul(window(vx, (0, 1), t), grads, (1, 1))
        log_total, delta = row_stats(scores, dprobs)
        st0[0, t:t + 1] = log_total[:, :PAIR]
        st1[0, t:t + 1] = log_total[:, PAIR:]
        st0[0, ROWS + t:ROWS + t + 1] = delta[:, :PAIR]
        st1[0, ROWS + t:ROWS + t + 1] = delta[:, PAIR:]


tokens_spec = pl.BlockSpec((2, OWN, PAIR), lambda p: (0, 0, p))
edge_spec = pl.BlockSpec((2, 2, CELLS, PAIR), lambda p: (0, 0, 0, p))
stats_spec = pl.BlockSpec((1, 8, PAIR), lambda p: (p, 0, 0))
stats_shape = struct((PAIRS, 8, PAIR), F32)
key_scratch = [pltpu.VMEM((2, EXT, PAIR), BF16)] * 2


def own_stats(west, east, kd, vd, north, south):
    return pl.pallas_call(
        stats_kernel,
        grid=(PAIRS,),
        in_specs=[tokens_spec] * 4 + [edge_spec] * 2,
        out_specs=[stats_spec] * 2,
        out_shape=[stats_shape] * 2,
        scratch_shapes=key_scratch,
        compiler_params=params(),
        cost_estimate=cost(3e9, 3 << 20),
        name="own_stats",
    )(west, east, kd, vd, north, south)


def halo_kernel(q_west, q_east, kd, vd, north, south, in_west, in_east,
                dq_west, dq_east, out_west, out_east, fin_west, fin_east, kx, vx):
    masks = head_masks()
    biases = pole_biases()
    lane = lax.broadcasted_iota(jnp.int32, (1, PAIR), 1)
    fill_keys(kx, kd, north, south, 0)
    fill_keys(vx, vd, north, south, 1)
    sides = ((q_west, in_west, dq_west, out_west, fin_west), (q_east, in_east, dq_east, out_east, fin_east))
    for c, (q_in, st_in, dq_out, st_out, st_fin) in enumerate(sides):
        for t in range(ROWS):
            at = slice(t * CELLS, (t + 1) * CELLS)
            row, low = slice(t, t + 1), slice(ROWS + t, ROWS + t + 1)
            queries = stacked([q_in[0, at]], masks)
            grads = stacked([q_in[1, at]], masks)
            keys = window(kx, (c,), t)
            scores = score_block(keys, queries, 1, t, biases)
            dprobs = matmul(window(vx, (c,), t), grads, (1, 1))
            log_part, delta_part = row_stats(scores, dprobs)
            log_total, delta = merged(log_part, delta_part, st_in[0, row], st_in[0, low])
            dscores = (jnp.exp2(scores - log_total) * (dprobs - delta)).astype(BF16)
            grad = matmul(dscores, keys, (0, 0)) * SCALE
            dq_out[at] = own_heads(lane, grad).astype(BF16)
            st_out[0, row] = log_part
            st_out[0, low] = delta_part
            st_fin[0, row] = log_total
            st_fin[0, low] = delta


def halo(q_west, q_east, kd, vd, north, south, in_west, in_east):
    grad_spec = pl.BlockSpec((OWN, PAIR), lambda p: (0, p))
    return pl.pallas_call(
        halo_kernel,
        grid=(PAIRS,),
        in_specs=[tokens_spec] * 4 + [edge_spec] * 2 + [stats_spec] * 2,
        out_specs=[grad_spec] * 2 + [stats_spec] * 4,
        out_shape=[struct((OWN, FEAT), BF16)] * 2 + [stats_shape] * 4,
        scratch_shapes=key_scratch,
        compiler_params=params(),
        cost_estimate=cost(3e9, 4 << 20),
        name="halo",
    )(q_west, q_east, kd, vd, north, south, in_west, in_east)


def grads_kernel(west, east, q_west, q_east, kd, vd, north, south, st0, st1, add0, add1, fin_west, fin_east,
                 dq_ref, dk_ref, dv_ref, dnorth, dsouth, kx, vx, dkx, dvx):
    masks = head_masks()
    biases = pole_biases()
    lane = lax.broadcasted_iota(jnp.int32, (1, PAIR), 1)
    fill_keys(kx, kd, north, south, 0)
    fill_keys(vx, vd, north, south, 1)
    dkx[...] = jnp.zeros_like(dkx)
    dvx[...] = jnp.zeros_like(dvx)

    def work(columns, q_parts, g_parts, log_total, delta, t):
        queries = stacked(q_parts, masks)
        grads = stacked(g_parts, masks)
        keys = window(kx, columns, t)
        scores = score_block(keys, queries, len(columns), t, biases)
        dprobs = matmul(window(vx, columns, t), grads, (1, 1))
        probs = jnp.exp2(scores - log_total)
        dscores = (probs * (dprobs - delta)).astype(BF16)
        key_part = matmul(dscores, queries, (1, 0))
        value_part = matmul(probs.astype(BF16), grads, (1, 0))
        for i, c in enumerate(columns):
            here = slice(t * CELLS, (t + 3) * CELLS)
            there = slice(i * 3 * CELLS, (i + 1) * 3 * CELLS)
            dkx[c, here] += key_part[there]
            dvx[c, here] += value_part[there]
        return dscores, keys

    for t in range(ROWS):
        at = slice(t * CELLS, (t + 1) * CELLS)
        row, low = slice(t, t + 1), slice(ROWS + t, ROWS + t + 1)
        log0, delta0 = merged(st0[0, row], st0[0, low], add0[0, row], add0[0, low])
        log1, delta1 = merged(st1[0, row], st1[0, low], add1[0, row], add1[0, low])
        dscores, keys = work((0, 1), [west[0, at], east[0, at]], [west[1, at], east[1, at]],
                             jnp.concatenate([log0, log1], axis=1), jnp.concatenate([delta0, delta1], axis=1), t)
        grad = matmul(dscores, keys, (0, 0)) * SCALE
        dq_ref[0, at] = own_heads(lane, grad[:PAIR])
        dq_ref[1, at] = own_heads(lane, grad[PAIR:])
        work((0,), [q_west[0, at]], [q_west[1, at]], fin_west[0, row], fin_west[0, low], t)
        work((1,), [q_east[0, at]], [q_east[1, at]], fin_east[0, row], fin_east[0, low], t)
    for c in range(2):
        dk_ref[c] = dkx[c, CELLS:CELLS + OWN] * SCALE
        dv_ref[c] = dvx[c, CELLS:CELLS + OWN]
        dnorth[0, c] = (dkx[c, 0:CELLS] * SCALE).astype(BF16)
        dnorth[1, c] = dvx[c, 0:CELLS].astype(BF16)
        dsouth[0, c] = (dkx[c, CELLS + OWN:EXT] * SCALE).astype(BF16)
        dsouth[1, c] = dvx[c, CELLS + OWN:EXT].astype(BF16)


def gradients(*operands):
    return pl.pallas_call(
        grads_kernel,
        grid=(PAIRS,),
        in_specs=[tokens_spec] * 6 + [edge_spec] * 2 + [stats_spec] * 6,
        out_specs=[tokens_spec] * 3 + [edge_spec] * 2,
        out_shape=[struct((2, OWN, FEAT), F32)] * 3 + [struct((2, 2, CELLS, FEAT), BF16)] * 2,
        scratch_shapes=key_scratch + [pltpu.VMEM((2, EXT, PAIR), F32)] * 2,
        compiler_params=params(),
        cost_estimate=cost(8e9, 8 << 20),
        name="gradients",
    )(*operands)


def join_columns(parts):
    return jnp.concatenate([part.reshape(8, 8, FEAT) for part in parts], axis=1).astype(BF16)


def finish_kernel(dq, dk, dv, dq0, dq1, from_north, from_south, q_ref, k_ref, v_ref):
    step = pl.program_id(0)
    first = jnp.where(step == 0, 1.0, 0.0).astype(F32)
    last = jnp.where(step == ROWS - 1, 1.0, 0.0).astype(F32)
    q_ref[...] = join_columns([dq[0] + dq0[...].astype(F32), dq[1] + dq1[...].astype(F32)])
    for which, (own, out) in enumerate(((dk, k_ref), (dv, v_ref))):
        out[...] = join_columns([
            own[c] + from_north[which, c].astype(F32) * first + from_south[which, c].astype(F32) * last
            for c in range(2)
        ])


def finish(*operands):
    grid_spec = pl.BlockSpec((8, 16, FEAT), lambda t: (t, 0, 0))
    tile_spec = pl.BlockSpec((2, CELLS, FEAT), lambda t: (0, t, 0))
    part_spec = pl.BlockSpec((CELLS, FEAT), lambda t: (t, 0))
    edge = pl.BlockSpec((2, 2, CELLS, FEAT), lambda t: (0, 0, 0, 0))
    return pl.pallas_call(
        finish_kernel,
        grid=(ROWS,),
        in_specs=[tile_spec] * 3 + [part_spec] * 2 + [edge] * 2,
        out_specs=[grid_spec] * 3,
        out_shape=[struct((8 * ROWS, 16, FEAT), BF16)] * 3,
        compiler_params=params(),
        cost_estimate=cost(0, 6 << 20),
        name="finish",
    )(*operands)


def shift(x, axis, by, wrap):
    count = lax.axis_size(axis)
    pairs = [(i, (i + by) % count) for i in range(count) if wrap or 0 <= i + by < count]
    return lax.ppermute(x, axis, pairs)


def on_device(query_vectors, key_vectors, value_vectors, output_grads):
    to_east = functools.partial(shift, axis="lon", by=1, wrap=True)
    to_west = functools.partial(shift, axis="lon", by=-1, wrap=True)
    to_south = functools.partial(shift, axis="lat", by=1, wrap=False)
    to_north = functools.partial(shift, axis="lat", by=-1, wrap=False)
    west, east, kd, vd, north_edge, south_edge = pack(query_vectors, key_vectors, value_vectors, output_grads)
    q_west = to_east(east)
    q_east = to_west(west)
    north = to_south(south_edge)
    south = to_north(north_edge)
    st0, st1 = own_stats(west, east, kd, vd, north, south)
    in_west = to_east(st1)
    in_east = to_west(st0)
    dq_west, dq_east, out_west, out_east, fin_west, fin_east = halo(
        q_west, q_east, kd, vd, north, south, in_west, in_east)
    add1 = to_west(out_west)
    add0 = to_east(out_east)
    dq1 = to_west(dq_west)
    dq0 = to_east(dq_east)
    dq, dk, dv, dnorth, dsouth = gradients(
        west, east, q_west, q_east, kd, vd, north, south, st0, st1, add0, add1, fin_west, fin_east)
    from_south = to_north(dnorth)
    from_north = to_south(dsouth)
    return tuple(finish(dq, dk, dv, dq0, dq1, from_north, from_south))


def solution(mesh):
    spec = P("lat", "lon", None)
    return jax.shard_map(on_device, mesh=mesh, in_specs=(spec,) * 4, out_specs=(spec,) * 3, check_vma=False)
```

profile of v0, /device:TPU:1, one launch (start us, length us, event | category | flops | bytes accessed | tf_op | source)
XLA Modules:
  0.0 105.5 jit_solution(9373696901165586593)
XLA Ops:
  0.6 1.0 copy-done.2
  1.7 1.0 copy-done.3
  2.7 1.0 copy-done.4
  3.8 1.0 copy-done.5
  4.8 0.4 pack.1
  5.2 4.6 %collective-permute-start.2 = (bf16[2,2,64,512]{3,2,1,0:T(8,128)(2,1)S(1)}, bf16[2,2,64,512]{3,2,1,0:T(8,128)(2,1)S(1)}, u32[]{:S(2)}, u32[]{:S(2)}) collective-permute-start(bf16[2,2,64,512]{3,2,1,0:T(8,128)(2,1)S(1)} %get-tuple-element.26), channel_id=1, source_target_pairs={{0,32},{32,64},{64,96},{1,33},{33,65},{65,97},{2,34},{34,66},{66,9... | collective-permute-start | bytes 786440 | tf_op jit(solution)/shard_map/ppermute | solution.py:338
  9.8 1.9 %collective-permute-start.3 = (bf16[2,2,64,512]{3,2,1,0:T(8,128)(2,1)S(1)}, bf16[2,2,64,512]{3,2,1,0:T(8,128)(2,1)S(1)}, u32[]{:S(2)}, u32[]{:S(2)}) collective-permute-start(bf16[2,2,64,512]{3,2,1,0:T(8,128)(2,1)S(1)} %get-tuple-element.27), channel_id=1, source_target_pairs={{32,0},{64,32},{96,64},{33,1},{65,33},{97,65},{34,2},{66,34},{98,6... | collective-permute-start | bytes 786440 | tf_op jit(solution)/shard_map/ppermute | solution.py:338
  11.7 8.4 %collective-permute-start.1 = (bf16[2,256,512]{2,1,0:T(8,128)(2,1)S(1)}, bf16[2,256,512]{2,1,0:T(8,128)(2,1)S(1)}, u32[]{:S(2)}, u32[]{:S(2)}) collective-permute-start(bf16[2,256,512]{2,1,0:T(8,128)(2,1)S(1)} %get-tuple-element.22.west), channel_id=1, source_target_pairs={{0,31},{1,0},{2,1},{3,2},{4,3},{5,4},{6,5},{7,6},{8,7},{9,8},{10,9... | collective-permute-start | bytes 1572872 | tf_op jit(solution)/shard_map/ppermute | solution.py:338
  20.1 0.0 collective-permute-start
  20.1 0.0 collective-permute-done.2.north
  20.1 10.6 %collective-permute-done.3.south = bf16[2,2,64,512]{3,2,1,0:T(8,128)(2,1)S(1)} collective-permute-done((bf16[2,2,64,512]{3,2,1,0:T(8,128)(2,1)S(1)}, bf16[2,2,64,512]{3,2,1,0:T(8,128)(2,1)S(1)}, u32[]{:S(2)}, u32[]{:S(2)}) %collective-permute-start.3) | collective-permute-done | bytes 262176 | tf_op jit(solution)/shard_map/ppermute | solution.py:338
  30.7 3.6 %own_stats.1 = (f32[4,8,128]{2,1,0:T(8,128)S(1)}, f32[4,8,128]{2,1,0:T(8,128)S(1)}) custom-call(bf16[2,256,512]{2,1,0:T(8,128)(2,1)S(1)} %get-tuple-element.22.west, bf16[2,256,512]{2,1,0:T(8,128)(2,1)S(1)} %get-tuple-element.23.east, bf16[2,256,512]{2,1,0:T(8,128)(2,1)S(1)} %get-tuple-element.24.kd, bf16[2,256,512]{2,1,0:T(8,128)(2,1)S(1)} %get-tuple-element.25.vd, ...), custom_call_target="tpu_custom_call" | custom-call | flops 3000000000 | bytes 3145728 | tf_op jit(solution)/shard_map/own_stats/pallas_call | solution.py:184
  34.4 9.6 %collective-permute-start.5 = (f32[4,8,128]{2,1,0:T(8,128)S(1)}, f32[4,8,128]{2,1,0:T(8,128)S(1)}, u32[]{:S(2)}, u32[]{:S(2)}) collective-permute-start(f32[4,8,128]{2,1,0:T(8,128)S(1)} %get-tuple-element.28.st0), channel_id=1, source_target_pairs={{0,31},{1,0},{2,1},{3,2},{4,3},{5,4},{6,5},{7,6},{8,7},{9,8},{10,9... | collective-permute-start | bytes 49160 | tf_op jit(solution)/shard_map/ppermute | solution.py:338
  44.0 0.0 collective-permute-start.4
  44.0 0.9 collective-permute-done.5.in_east
  44.9 7.4 %collective-permute-done.4.in_west = f32[4,8,128]{2,1,0:T(8,128)S(1)} collective-permute-done((f32[4,8,128]{2,1,0:T(8,128)S(1)}, f32[4,8,128]{2,1,0:T(8,128)S(1)}, u32[]{:S(2)}, u32[]{:S(2)}) %collective-permute-start.4) | collective-permute-done | bytes 16416 | tf_op jit(solution)/shard_map/ppermute | solution.py:338
  52.3 0.0 collective-permute-done.q_west
  52.3 9.7 %halo.1 = (bf16[256,512]{1,0:T(8,128)(2,1)S(1)}, bf16[256,512]{1,0:T(8,128)(2,1)S(1)}, f32[4,8,128]{2,1,0:T(8,128)S(1)}, f32[4,8,128]{2,1,0:T(8,128)S(1)}, f32[4...) custom-call(bf16[2,256,512]{2,1,0:T(8,128)(2,1)S(1)} %collective-permute-done.q_west, ...), custom_call_target="tpu_custom_call" | custom-call | flops 3000000000 | bytes 4194304 | tf_op jit(solution)/shard_map/halo/pallas_call | solution.py:227
  62.0 0.1 collective-permute-start.6
  62.1 7.2 %collective-permute-start.7 = (f32[4,8,128]{2,1,0:T(8,128)S(1)}, f32[4,8,128]{2,1,0:T(8,128)S(1)}, u32[]{:S(2)}, u32[]{:S(2)}) collective-permute-start(f32[4,8,128]{2,1,0:T(8,128)S(1)} %get-tuple-element.31), channel_id=1, source_target_pairs={{0,31},{1,0},{2,1},{3,2},{4,3},{5,4},{6,5},{7,6},{8,7},{9,8},{10,9... | collective-permute-start | bytes 49160 | tf_op jit(solution)/shard_map/ppermute | solution.py:338
  69.2 0.0 collective-permute-start.8
  69.2 7.2 %collective-permute-start.9 = (bf16[256,512]{1,0:T(8,128)(2,1)S(1)}, bf16[256,512]{1,0:T(8,128)(2,1)S(1)}, u32[]{:S(2)}, u32[]{:S(2)}) collective-permute-start(bf16[256,512]{1,0:T(8,128)(2,1)S(1)} %get-tuple-element.38), channel_id=1, source_target_pairs={{0,31},{1,0},{2,1},{3,2},{4,3},{5,4},{6,5},{7,6},{8,7},{9,8},{10,9... | collective-permute-start | bytes 786440 | tf_op jit(solution)/shard_map/ppermute | solution.py:338
  76.4 0.0 collective-permute-done.6.add0
  76.4 13.6 %gradients.1 = (f32[2,256,512]{2,1,0:T(8,128)S(1)}, f32[2,256,512]{2,1,0:T(8,128)}, f32[2,256,512]{2,1,0:T(8,128)}, bf16[2,2,64,512]{3,2,1,0:T(8,128)(2,1)S(1)}, bf16[2,2,64,512]{3,2,1,0:T(8,128)(2,1)S(1)}) custom-call(bf16[2,256,512]{2,1,0:T(8,128)(2,1)S(1)} %get-tuple-element.22.west, bf16[2,256,512]{2,1,0:T(8,128)(2,1)S(1)} %get-tuple-element.23.east, ...), custom_call_target="tpu_custom_call" | custom-call | flops 8000000000 | bytes 8388608 | tf_op jit(solution)/shard_map/gradients/pallas_call | solution.py:289
  90.0 3.4 %collective-permute-start.10 = (bf16[2,2,64,512]{3,2,1,0:T(8,128)(2,1)S(1)}, bf16[2,2,64,512]{3,2,1,0:T(8,128)(2,1)S(1)}, u32[]{:S(2)}, u32[]{:S(2)}) collective-permute-start(bf16[2,2,64,512]{3,2,1,0:T(8,128)(2,1)S(1)} %get-tuple-element.39), channel_id=1, source_target_pairs={{0,32},{32,64},{64,96},{1,33},{33,65},{65,97},{2,34},{34,66},{66,9... | collective-permute-start | bytes 786440 | tf_op jit(solution)/shard_map/ppermute | solution.py:338
  93.4 1.9 %collective-permute-start.11 = (bf16[2,2,64,512]{3,2,1,0:T(8,128)(2,1)S(1)}, bf16[2,2,64,512]{3,2,1,0:T(8,128)(2,1)S(1)}, u32[]{:S(2)}, u32[]{:S(2)}) collective-permute-start(bf16[2,2,64,512]{3,2,1,0:T(8,128)(2,1)S(1)} %get-tuple-element.40), channel_id=1, source_target_pairs={{32,0},{64,32},{96,64},{33,1},{65,33},{97,65},{34,2},{66,34},{98,6... | collective-permute-start | bytes 786440 | tf_op jit(solution)/shard_map/ppermute | solution.py:338
  95.3 0.0 collective-permute-done.8.dq0
  95.4 1.3 %collective-permute-done.10.from_north = bf16[2,2,64,512]{3,2,1,0:T(8,128)(2,1)S(1)} collective-permute-done((bf16[2,2,64,512]{3,2,1,0:T(8,128)(2,1)S(1)}, bf16[2,2,64,512]{3,2,1,0:T(8,128)(2,1)S(1)}, u32[]{:S(2)}, u32[]{:S(2)}) %collective-permute-start.10) | collective-permute-done | bytes 262176 | tf_op jit(solution)/shard_map/ppermute | solution.py:338
  96.7 4.4 %collective-permute-done.11.from_south = bf16[2,2,64,512]{3,2,1,0:T(8,128)(2,1)S(1)} collective-permute-done((bf16[2,2,64,512]{3,2,1,0:T(8,128)(2,1)S(1)}, bf16[2,2,64,512]{3,2,1,0:T(8,128)(2,1)S(1)}, u32[]{:S(2)}, u32[]{:S(2)}) %collective-permute-start.11) | collective-permute-done | bytes 262176 | tf_op jit(solution)/shard_map/ppermute | solution.py:338
  101.1 1.2 %copy-done = f32[2,256,512]{2,1,0:T(8,128)S(1)} copy-done((f32[2,256,512]{2,1,0:T(8,128)S(1)}, f32[2,256,512]{2,1,0:T(8,128)}, u32[]{:S(2)}) %copy-start) | copy-done | bytes 1048600
  102.3 1.2 %copy-done.1 = f32[2,256,512]{2,1,0:T(8,128)S(1)} copy-done((f32[2,256,512]{2,1,0:T(8,128)S(1)}, f32[2,256,512]{2,1,0:T(8,128)}, u32[]{:S(2)}) %copy-start.1) | copy-done | bytes 1048600
  103.6 2.0 %finish.1 = (bf16[32,16,512]{2,1,0:T(8,128)(2,1)}, bf16[32,16,512]{2,1,0:T(8,128)(2,1)}, bf16[32,16,512]{2,1,0:T(8,128)(2,1)}) custom-call(f32[2,256,512]{2,1,0:T(8,128)S(1)} %get-tuple-element.34.dq, f32[2,256,512]{2,1,0:T(8,128)S(1)} %copy-done, f32[2,256,512]{2,1,0:T(8,128)S(1)} %copy-done.1, bf16[256,512]{1,0:T(8,128)(2,1)S(1)} %collective-permute-done.8.dq0, ...), custom_call_target="tpu_custom_call" | custom-call | bytes 6291456 | tf_op jit(solution)/shard_map/finish/pallas_call | solution.py:323
  (9 shorter events, 0.0 us)
Async XLA Ops:
  0.6 1.0 copy-start.2
  1.7 1.0 copy-start.3
  2.7 1.0 copy-start.4
  3.8 1.0 copy-start.5
  5.2 14.9 %collective-permute-start.2 = (bf16[2,2,64,512]{3,2,1,0:T(8,128)(2,1)S(1)}, bf16[2,2,64,512]{3,2,1,0:T(8,128)(2,1)S(1)}, u32[]{:S(2)}, u32[]{:S(2)}) collective-permute-start(bf16[2,2,64,512]{3,2,1,0:T(8,128)(2,1)S(1)} %get-tuple-element.26), channel_id=1, source_target_pairs={{0,32},{32,64},{64,96},{1,33},{33,65},{65,97},{2,34},{34,66},{66,9... | collective-permute-start | bytes 786440 | tf_op jit(solution)/shard_map/ppermute | solution.py:338
  9.8 20.9 %collective-permute-start.3 = (bf16[2,2,64,512]{3,2,1,0:T(8,128)(2,1)S(1)}, bf16[2,2,64,512]{3,2,1,0:T(8,128)(2,1)S(1)}, u32[]{:S(2)}, u32[]{:S(2)}) collective-permute-start(bf16[2,2,64,512]{3,2,1,0:T(8,128)(2,1)S(1)} %get-tuple-element.27), channel_id=1, source_target_pairs={{32,0},{64,32},{96,64},{33,1},{65,33},{97,65},{34,2},{66,34},{98,6... | collective-permute-start | bytes 786440 | tf_op jit(solution)/shard_map/ppermute | solution.py:338
  11.7 40.6 %collective-permute-start.1 = (bf16[2,256,512]{2,1,0:T(8,128)(2,1)S(1)}, bf16[2,256,512]{2,1,0:T(8,128)(2,1)S(1)}, u32[]{:S(2)}, u32[]{:S(2)}) collective-permute-start(bf16[2,256,512]{2,1,0:T(8,128)(2,1)S(1)} %get-tuple-element.22.west), channel_id=1, source_target_pairs={{0,31},{1,0},{2,1},{3,2},{4,3},{5,4},{6,5},{7,6},{8,7},{9,8},{10,9... | collective-permute-start | bytes 1572872 | tf_op jit(solution)/shard_map/ppermute | solution.py:338
  20.1 32.2 %collective-permute-start = (bf16[2,256,512]{2,1,0:T(8,128)(2,1)S(1)}, bf16[2,256,512]{2,1,0:T(8,128)(2,1)S(1)}, u32[]{:S(2)}, u32[]{:S(2)}) collective-permute-start(bf16[2,256,512]{2,1,0:T(8,128)(2,1)S(1)} %get-tuple-element.23.east), channel_id=1, source_target_pairs={{0,1},{1,2},{2,3},{3,4},{4,5},{5,6},{6,7},{7,8},{8,9},{9,10},{10,1... | collective-permute-start | bytes 1572872 | tf_op jit(solution)/shard_map/ppermute | solution.py:338
  34.4 10.5 %collective-permute-start.5 = (f32[4,8,128]{2,1,0:T(8,128)S(1)}, f32[4,8,128]{2,1,0:T(8,128)S(1)}, u32[]{:S(2)}, u32[]{:S(2)}) collective-permute-start(f32[4,8,128]{2,1,0:T(8,128)S(1)} %get-tuple-element.28.st0), channel_id=1, source_target_pairs={{0,31},{1,0},{2,1},{3,2},{4,3},{5,4},{6,5},{7,6},{8,7},{9,8},{10,9... | collective-permute-start | bytes 49160 | tf_op jit(solution)/shard_map/ppermute | solution.py:338
  44.0 8.3 %collective-permute-start.4 = (f32[4,8,128]{2,1,0:T(8,128)S(1)}, f32[4,8,128]{2,1,0:T(8,128)S(1)}, u32[]{:S(2)}, u32[]{:S(2)}) collective-permute-start(f32[4,8,128]{2,1,0:T(8,128)S(1)} %get-tuple-element.29.st1), channel_id=1, source_target_pairs={{0,1},{1,2},{2,3},{3,4},{4,5},{5,6},{6,7},{7,8},{8,9},{9,10},{10,1... | collective-permute-start | bytes 49160 | tf_op jit(solution)/shard_map/ppermute | solution.py:338
  62.0 14.5 %collective-permute-start.6 = (f32[4,8,128]{2,1,0:T(8,128)S(1)}, f32[4,8,128]{2,1,0:T(8,128)S(1)}, u32[]{:S(2)}, u32[]{:S(2)}) collective-permute-start(f32[4,8,128]{2,1,0:T(8,128)S(1)} %get-tuple-element.30), channel_id=1, source_target_pairs={{0,1},{1,2},{2,3},{3,4},{4,5},{5,6},{6,7},{7,8},{8,9},{9,10},{10,1... | collective-permute-start | bytes 49160 | tf_op jit(solution)/shard_map/ppermute | solution.py:338
  62.1 14.4 %collective-permute-start.7 = (f32[4,8,128]{2,1,0:T(8,128)S(1)}, f32[4,8,128]{2,1,0:T(8,128)S(1)}, u32[]{:S(2)}, u32[]{:S(2)}) collective-permute-start(f32[4,8,128]{2,1,0:T(8,128)S(1)} %get-tuple-element.31), channel_id=1, source_target_pairs={{0,31},{1,0},{2,1},{3,2},{4,3},{5,4},{6,5},{7,6},{8,7},{9,8},{10,9... | collective-permute-start | bytes 49160 | tf_op jit(solution)/shard_map/ppermute | solution.py:338
  69.2 26.1 %collective-permute-start.8 = (bf16[256,512]{1,0:T(8,128)(2,1)S(1)}, bf16[256,512]{1,0:T(8,128)(2,1)S(1)}, u32[]{:S(2)}, u32[]{:S(2)}) collective-permute-start(bf16[256,512]{1,0:T(8,128)(2,1)S(1)} %get-tuple-element.37), channel_id=1, source_target_pairs={{0,1},{1,2},{2,3},{3,4},{4,5},{5,6},{6,7},{7,8},{8,9},{9,10},{10,1... | collective-permute-start | bytes 786440 | tf_op jit(solution)/shard_map/ppermute | solution.py:338
  69.2 26.1 %collective-permute-start.9 = (bf16[256,512]{1,0:T(8,128)(2,1)S(1)}, bf16[256,512]{1,0:T(8,128)(2,1)S(1)}, u32[]{:S(2)}, u32[]{:S(2)}) collective-permute-start(bf16[256,512]{1,0:T(8,128)(2,1)S(1)} %get-tuple-element.38), channel_id=1, source_target_pairs={{0,31},{1,0},{2,1},{3,2},{4,3},{5,4},{6,5},{7,6},{8,7},{9,8},{10,9... | collective-permute-start | bytes 786440 | tf_op jit(solution)/shard_map/ppermute | solution.py:338
  90.0 6.7 %collective-permute-start.10 = (bf16[2,2,64,512]{3,2,1,0:T(8,128)(2,1)S(1)}, bf16[2,2,64,512]{3,2,1,0:T(8,128)(2,1)S(1)}, u32[]{:S(2)}, u32[]{:S(2)}) collective-permute-start(bf16[2,2,64,512]{3,2,1,0:T(8,128)(2,1)S(1)} %get-tuple-element.39), channel_id=1, source_target_pairs={{0,32},{32,64},{64,96},{1,33},{33,65},{65,97},{2,34},{34,66},{66,9... | collective-permute-start | bytes 786440 | tf_op jit(solution)/shard_map/ppermute | solution.py:338
  93.4 7.7 %collective-permute-start.11 = (bf16[2,2,64,512]{3,2,1,0:T(8,128)(2,1)S(1)}, bf16[2,2,64,512]{3,2,1,0:T(8,128)(2,1)S(1)}, u32[]{:S(2)}, u32[]{:S(2)}) collective-permute-start(bf16[2,2,64,512]{3,2,1,0:T(8,128)(2,1)S(1)} %get-tuple-element.40), channel_id=1, source_target_pairs={{32,0},{64,32},{96,64},{33,1},{65,33},{97,65},{34,2},{66,34},{98,6... | collective-permute-start | bytes 786440 | tf_op jit(solution)/shard_map/ppermute | solution.py:338
  101.1 1.2 %copy-start = (f32[2,256,512]{2,1,0:T(8,128)S(1)}, f32[2,256,512]{2,1,0:T(8,128)}, u32[]{:S(2)}) copy-start(f32[2,256,512]{2,1,0:T(8,128)} %get-tuple-element.35.dk) | copy-start | bytes 3145732
  102.3 1.2 %copy-start.1 = (f32[2,256,512]{2,1,0:T(8,128)S(1)}, f32[2,256,512]{2,1,0:T(8,128)}, u32[]{:S(2)}) copy-start(f32[2,256,512]{2,1,0:T(8,128)} %get-tuple-element.36.dv) | copy-start | bytes 3145732
where the time goes:
time: 106 us
  starting transfers between devices  44.2 us (42%)
  Pallas kernels  29.3 us (28%)
  waiting for transfers between devices  24.7 us (23%)
  local copies, waits for them, and re-layouts  6.61 us (6%)
    ppermute x12, starting transfers between devices, shift(): return lax.ppermute(x, axis, pairs)  44.2 us
    ppermute x12, waiting for transfers between devices, shift(): return lax.ppermute(x, axis, pairs)  24.7 us
    pallas_call x1, Pallas kernels, gradients(): pl.pallas_call(grads_kernel, grid=(PAIRS,), in_specs=[tokens_spec] * 6 +...  13.6 us
    pallas_call x1, Pallas kernels, halo(): pl.pallas_call(halo_kernel, grid=(PAIRS,), in_specs=[tokens_spec] * 4 + [...  9.67 us
    unnamed x12, local copies, waits for them, and re-layouts  6.61 us
    pallas_call x1, Pallas kernels, own_stats(): pl.pallas_call(stats_kernel, grid=(PAIRS,), in_specs=[tokens_spec] * 4 +...  3.64 us
  transfers between devices with their start and end apart: 12, of which 5 were waited for; matrix products, arithmetic and copies ran while one was open for 0% of the time, Pallas kernels for 16%

commit v1 on v0

v1 whole, which is shorter than its diff:
```python
import functools

import jax
import jax.numpy as jnp
from jax import lax
from jax.experimental import pallas as pl
from jax.experimental.pallas import tpu as pltpu
from jax.sharding import PartitionSpec as P

ROWS = 4
CELLS = 64
OWN = ROWS * CELLS
PAIR = 128
PAIRS = 4
FEAT = 512
SCALE = 64 ** -0.5
LOG2E = 1.4426950408889634
MASKED = -1e30
F32 = jnp.float32
BF16 = jnp.bfloat16
VMEM_LIMIT = 20 * 1024 * 1024
PACK_LIMIT = 62 * 1024 * 1024


def matmul(a, b, contract):
    return lax.dot_general(a, b, ((contract[:1], contract[1:]), ((), ())), preferred_element_type=F32)


def params(limit=VMEM_LIMIT):
    return pltpu.CompilerParams(vmem_limit_bytes=limit)


def cost(flops, size):
    return pl.CostEstimate(flops=int(flops), bytes_accessed=int(size), transcendentals=0)


def struct(shape, dtype):
    return jax.ShapeDtypeStruct(shape, dtype)


def split_columns(block):
    wide = block.astype(F32)
    return [wide[:, c * 8:(c + 1) * 8].reshape(CELLS, FEAT).astype(BF16) for c in range(2)]


def fetch(refs, buffers, sems):
    copies = [[pltpu.make_async_copy(ref.at[pl.ds(8 * t, 8)], buffers.at[i, t], sems.at[i, t])
               for t in range(ROWS)] for i, ref in enumerate(refs)]
    for t in range(ROWS):
        for copy in copies:
            copy[t].start()
    return copies


def pack_queries_kernel(q_ref, g_ref, west, east, buffers, sems):
    copies = fetch((q_ref, g_ref), buffers, sems)
    for t in range(ROWS):
        for i in range(2):
            copies[i][t].wait()
            first, second = split_columns(buffers[i, t])
            west[i, t * CELLS:(t + 1) * CELLS] = first
            east[i, t * CELLS:(t + 1) * CELLS] = second


def pack_keys_kernel(k_ref, v_ref, kd, vd, north, south, buffers, sems):
    copies = fetch((k_ref, v_ref), buffers, sems)
    for t in range(ROWS):
        for i, out in enumerate((kd, vd)):
            copies[i][t].wait()
            tile = jnp.concatenate(split_columns(buffers[i, t]), axis=0)
            out[t * PAIR:(t + 1) * PAIR] = tile
            if t == 0:
                north[i] = tile
            if t == ROWS - 1:
                south[i] = tile


def pack(kernel, x, y, out_shape, name):
    return pl.pallas_call(
        kernel,
        in_specs=[pl.BlockSpec(memory_space=pltpu.HBM)] * 2,
        out_shape=out_shape,
        scratch_shapes=[pltpu.VMEM((2, ROWS, 8, 16, FEAT), BF16), pltpu.SemaphoreType.DMA((2, ROWS))],
        compiler_params=params(PACK_LIMIT),
        cost_estimate=cost(0, 3 << 20),
        name=name,
    )(x, y)


def head_masks(lanes):
    lane = lax.broadcasted_iota(jnp.int32, (1, lanes), 1)
    return [jnp.where((lane >= 64 * h) & (lane < 64 * (h + 1)), 1.0, 0.0).astype(F32).astype(BF16)
            for h in range(lanes // 64)]


def stacked(parts, masks):
    return jnp.concatenate([part * mask for part in parts for mask in masks], axis=0)


def pole_biases():
    lat = lax.axis_index("lat")
    count = lax.axis_size("lat")
    return (jnp.where(lat == 0, MASKED, 0.0).astype(F32),
            jnp.where(lat == count - 1, MASKED, 0.0).astype(F32))


def key_row(own, north, south, which, row):
    if row == 0:
        return north[which]
    if row == ROWS + 1:
        return south[which]
    return own[(row - 1) * PAIR:row * PAIR]


def window(own, north, south, which, t, column=None):
    rows = [key_row(own, north, south, which, t + i) for i in range(3)]
    if column is not None:
        rows = [row[column * CELLS:(column + 1) * CELLS] for row in rows]
    return jnp.concatenate(rows, axis=0)


def score_block(keys, queries, t, biases):
    scores = matmul(keys, queries, (1, 1)) * (SCALE * LOG2E)
    span = keys.shape[0] // 3
    if t == 0:
        scores = jnp.concatenate([scores[:span] + biases[0], scores[span:]], axis=0)
    if t == ROWS - 1:
        scores = jnp.concatenate([scores[:2 * span], scores[2 * span:] + biases[1]], axis=0)
    return scores


def row_stats(scores, dprobs):
    top = jnp.max(scores, axis=0, keepdims=True)
    weights = jnp.exp2(scores - top)
    total = jnp.sum(weights, axis=0, keepdims=True)
    delta = jnp.sum(weights * dprobs, axis=0, keepdims=True) / total
    return top + jnp.log(total) * LOG2E, delta


def merged(log_a, delta_a, log_b, delta_b):
    top = jnp.maximum(log_a, log_b)
    weight_a = jnp.exp2(log_a - top)
    weight_b = jnp.exp2(log_b - top)
    total = weight_a + weight_b
    return top + jnp.log(total) * LOG2E, (weight_a * delta_a + weight_b * delta_b) / total


def query_part(keys, dscores, lane):
    turned = matmul(keys, dscores, (0, 0)).T * SCALE
    return jnp.where(lane < 64, turned[:CELLS], turned[CELLS:])


EDGE_ROWS = (0, 3)
MID_ROWS = (1, 2)
tokens_spec = pl.BlockSpec((2, OWN, PAIR), lambda p: (0, 0, p))
keys_spec = pl.BlockSpec((ROWS * PAIR, PAIR), lambda p: (0, p))
edge_spec = pl.BlockSpec((2, PAIR, PAIR), lambda p: (0, 0, p))
stats_spec = pl.BlockSpec((1, 8, PAIR), lambda p: (p, 0, 0))
stats_shape = struct((PAIRS, 8, PAIR), F32)
held_spec = pl.BlockSpec((1, 2, 3 * PAIR, 2 * PAIR), lambda p: (p, 0, 0, 0))
held_shape = struct((PAIRS, 2, 3 * PAIR, 2 * PAIR), F32)


def stats_kernel(west, east, kd, vd, north, south, st0, st1, s_edge, d_edge, s_mid, d_mid):
    masks = head_masks(PAIR)
    biases = pole_biases()
    for t in range(ROWS):
        at = slice(t * CELLS, (t + 1) * CELLS)
        queries = stacked([west[0, at], east[0, at]], masks)
        grads = stacked([west[1, at], east[1, at]], masks)
        scores = score_block(window(kd, north, south, 0, t), queries, t, biases)
        dprobs = matmul(window(vd, north, south, 1, t), grads, (1, 1))
        s_out, d_out, place = (s_edge, d_edge, t // 3) if t in EDGE_ROWS else (s_mid, d_mid, t - 1)
        s_out[0, place] = scores
        d_out[0, place] = dprobs
        log_total, delta = row_stats(scores, dprobs)
        st0[0, t:t + 1] = log_total[:, :PAIR]
        st1[0, t:t + 1] = log_total[:, PAIR:]
        st0[0, ROWS + t:ROWS + t + 1] = delta[:, :PAIR]
        st1[0, ROWS + t:ROWS + t + 1] = delta[:, PAIR:]


def own_stats(*operands):
    return pl.pallas_call(
        stats_kernel,
        grid=(PAIRS,),
        in_specs=[tokens_spec] * 2 + [keys_spec] * 2 + [edge_spec] * 2,
        out_specs=[stats_spec] * 2 + [held_spec] * 4,
        out_shape=[stats_shape] * 2 + [held_shape] * 4,
        compiler_params=params(),
        cost_estimate=cost(0, 1 << 10),
        name="own_stats",
    )(*operands)


def halo_kernel(q_west, q_east, kd, vd, north, south, in_west, in_east,
                dq_west, dq_east, out_west, out_east, dkx, dvx):
    masks = head_masks(2 * PAIR)
    biases = pole_biases()
    lane = lax.broadcasted_iota(jnp.int32, (1, PAIR), 1)
    dkx[...] = jnp.zeros_like(dkx)
    dvx[...] = jnp.zeros_like(dvx)
    sides = ((q_west, in_west, dq_west, out_west), (q_east, in_east, dq_east, out_east))
    for t in range(ROWS):
        at = slice(t * CELLS, (t + 1) * CELLS)
        row, low = slice(t, t + 1), slice(ROWS + t, ROWS + t + 1)
        for c, (q_in, st_in, dq_out, st_out) in enumerate(sides):
            queries = stacked([q_in[0, at]], masks)
            grads = stacked([q_in[1, at]], masks)
            keys = window(kd, north, south, 0, t, c)
            scores = score_block(keys, queries, t, biases)
            dprobs = matmul(window(vd, north, south, 1, t, c), grads, (1, 1))
            log_part, delta_part = row_stats(scores, dprobs)
            for j in range(2):
                st_out[j, row] = log_part[:, j * PAIR:(j + 1) * PAIR]
                st_out[j, low] = delta_part[:, j * PAIR:(j + 1) * PAIR]
            log_home = jnp.concatenate([st_in[j, row] for j in range(2)], axis=1)
            delta_home = jnp.concatenate([st_in[j, low] for j in range(2)], axis=1)
            log_total, delta = merged(log_part, delta_part, log_home, delta_home)
            probs = jnp.exp2(scores - log_total)
            dscores = (probs * (dprobs - delta)).astype(BF16)
            for j in range(2):
                lanes = slice(j * PAIR, (j + 1) * PAIR)
                dq_out[at, lanes] = query_part(keys[:, lanes], dscores[:, lanes], lane).astype(BF16)
            key_part = matmul(dscores, queries, (1, 0))
            value_part = matmul(probs.astype(BF16), grads, (1, 0))
            for i in range(3):
                here = slice((t + i) * PAIR + c * CELLS, (t + i) * PAIR + (c + 1) * CELLS)
                dkx[here] += key_part[i * CELLS:(i + 1) * CELLS]
                dvx[here] += value_part[i * CELLS:(i + 1) * CELLS]


def halo(*operands):
    wide = 2 * PAIR
    tokens = pl.BlockSpec((2, OWN, wide), lambda p: (0, 0, p))
    keys = pl.BlockSpec((ROWS * PAIR, wide), lambda p: (0, p))
    edge = pl.BlockSpec((2, PAIR, wide), lambda p: (0, 0, p))
    stats = pl.BlockSpec((2, 8, PAIR), lambda p: (p, 0, 0))
    grads = pl.BlockSpec((OWN, wide), lambda p: (0, p))
    sums = pl.BlockSpec(((ROWS + 2) * PAIR, wide), lambda p: (0, p))
    return pl.pallas_call(
        halo_kernel,
        grid=(2,),
        in_specs=[tokens] * 2 + [keys] * 2 + [edge] * 2 + [stats] * 2,
        out_specs=[grads] * 2 + [stats] * 2 + [sums] * 2,
        out_shape=[struct((OWN, FEAT), BF16)] * 2 + [stats_shape] * 2 + [struct(((ROWS + 2) * PAIR, FEAT), F32)] * 2,
        compiler_params=params(),
        cost_estimate=cost(3e9, 4 << 20),
        name="halo",
    )(*operands)


def own_work(t, place, west, east, kd, north, south, st0, st1, add0, add1, s_in, d_in, masks, lane, dq_ref):
    at = slice(t * CELLS, (t + 1) * CELLS)
    row, low = slice(t, t + 1), slice(ROWS + t, ROWS + t + 1)
    queries = stacked([west[0, at], east[0, at]], masks)
    grads = stacked([west[1, at], east[1, at]], masks)
    log0, delta0 = merged(st0[0, row], st0[0, low], add0[0, row], add0[0, low])
    log1, delta1 = merged(st1[0, row], st1[0, low], add1[0, row], add1[0, low])
    probs = jnp.exp2(s_in[0, place] - jnp.concatenate([log0, log1], axis=1))
    dscores = (probs * (d_in[0, place] - jnp.concatenate([delta0, delta1], axis=1))).astype(BF16)
    keys = window(kd, north, south, 0, t)
    for c in range(2):
        dq_ref[c, at] = query_part(keys, dscores[:, c * PAIR:(c + 1) * PAIR], lane)
    return matmul(dscores, queries, (1, 0)), matmul(probs.astype(BF16), grads, (1, 0))


def edge_kernel(west, east, kd, north, south, st0, st1, add0, add1, s_in, d_in, dkx, dvx,
                dq_ref, dk_ref, dv_ref, dnorth, dsouth):
    masks = head_masks(PAIR)
    lane = lax.broadcasted_iota(jnp.int32, (1, PAIR), 1)
    last = ROWS * PAIR
    parts = [own_work(t, i, west, east, kd, north, south, st0, st1, add0, add1, s_in, d_in, masks, lane, dq_ref)
             for i, t in enumerate(EDGE_ROWS)]
    for which, (sums, out, scale) in enumerate(((dkx, dk_ref, SCALE), (dvx, dv_ref, 1.0))):
        top, bottom = parts[0][which], parts[1][which]
        out[0:2 * PAIR] = sums[PAIR:3 * PAIR] + top[PAIR:]
        out[2 * PAIR:last] = sums[3 * PAIR:PAIR + last] + bottom[:2 * PAIR]
        dnorth[which] = ((sums[0:PAIR] + top[:PAIR]) * scale).astype(BF16)
        dsouth[which] = ((sums[PAIR + last:] + bottom[2 * PAIR:]) * scale).astype(BF16)


def mid_kernel(west, east, kd, north, south, st0, st1, add0, add1, s_in, d_in, dq_in, dk_in, dv_in,
               dq_ref, dk_ref, dv_ref):
    masks = head_masks(PAIR)
    lane = lax.broadcasted_iota(jnp.int32, (1, PAIR), 1)
    parts = [own_work(t, i, west, east, kd, north, south, st0, st1, add0, add1, s_in, d_in, masks, lane, dq_ref)
             for i, t in enumerate(MID_ROWS)]
    for t in EDGE_ROWS:
        at = slice(t * CELLS, (t + 1) * CELLS)
        for c in range(2):
            dq_ref[c, at] = dq_in[c, at]
    for which, (sums, out, scale) in enumerate(((dk_in, dk_ref, SCALE), (dv_in, dv_ref, 1.0))):
        upper, lower = parts[0][which], parts[1][which]
        out[0:PAIR] = (sums[0:PAIR] + upper[:PAIR]) * scale
        out[PAIR:3 * PAIR] = (sums[PAIR:3 * PAIR] + upper[PAIR:] + lower[:2 * PAIR]) * scale
        out[3 * PAIR:] = (sums[3 * PAIR:] + lower[2 * PAIR:]) * scale


OWN_SPECS = [tokens_spec] * 2 + [keys_spec] + [edge_spec] * 2 + [stats_spec] * 4 + [held_spec] * 2
GRAD_SPECS = [tokens_spec] + [keys_spec] * 2
GRAD_SHAPES = [struct((2, OWN, FEAT), F32)] + [struct((ROWS * PAIR, FEAT), F32)] * 2


def edge_gradients(*operands):
    sums = pl.BlockSpec(((ROWS + 2) * PAIR, PAIR), lambda p: (0, p))
    return pl.pallas_call(
        edge_kernel,
        grid=(PAIRS,),
        in_specs=OWN_SPECS + [sums] * 2,
        out_specs=GRAD_SPECS + [edge_spec] * 2,
        out_shape=GRAD_SHAPES + [struct((2, PAIR, FEAT), BF16)] * 2,
        compiler_params=params(),
        cost_estimate=cost(3e9, 8 << 20),
        name="edge_gradients",
    )(*operands)


def mid_gradients(*operands):
    return pl.pallas_call(
        mid_kernel,
        grid=(PAIRS,),
        in_specs=OWN_SPECS + GRAD_SPECS,
        out_specs=GRAD_SPECS,
        out_shape=GRAD_SHAPES,
        compiler_params=params(),
        cost_estimate=cost(3e9, 8 << 20),
        name="mid_gradients",
    )(*operands)


def join_columns(parts):
    return jnp.concatenate([part.reshape(8, 8, FEAT) for part in parts], axis=1).astype(BF16)


def finish_kernel(dq, dk, dv, dq0, dq1, from_north, from_south, q_ref, k_ref, v_ref):
    step = pl.program_id(0)
    first = jnp.where(step == 0, 1.0, 0.0).astype(F32)
    last = jnp.where(step == ROWS - 1, 1.0, 0.0).astype(F32)
    q_ref[...] = join_columns([dq[0] + dq0[...].astype(F32), dq[1] + dq1[...].astype(F32)])
    for which, (own, out) in enumerate(((dk, k_ref), (dv, v_ref))):
        full = own[...] + from_north[which].astype(F32) * first + from_south[which].astype(F32) * last
        out[...] = join_columns([full[:CELLS], full[CELLS:]])


def finish(*operands):
    grid_spec = pl.BlockSpec((8, 16, FEAT), lambda t: (t, 0, 0))
    tile_spec = pl.BlockSpec((2, CELLS, FEAT), lambda t: (0, t, 0))
    row_spec = pl.BlockSpec((PAIR, FEAT), lambda t: (t, 0))
    part_spec = pl.BlockSpec((CELLS, FEAT), lambda t: (t, 0))
    edge = pl.BlockSpec((2, PAIR, FEAT), lambda t: (0, 0, 0))
    return pl.pallas_call(
        finish_kernel,
        grid=(ROWS,),
        in_specs=[tile_spec] + [row_spec] * 2 + [part_spec] * 2 + [edge] * 2,
        out_specs=[grid_spec] * 3,
        out_shape=[struct((8 * ROWS, 16, FEAT), BF16)] * 3,
        compiler_params=params(),
        cost_estimate=cost(0, 6 << 20),
        name="finish",
    )(*operands)


def shift(x, axis, by, wrap):
    count = lax.axis_size(axis)
    pairs = [(i, (i + by) % count) for i in range(count) if wrap or 0 <= i + by < count]
    return lax.ppermute(x, axis, pairs)


def on_device(query_vectors, key_vectors, value_vectors, output_grads):
    to_east = functools.partial(shift, axis="lon", by=1, wrap=True)
    to_west = functools.partial(shift, axis="lon", by=-1, wrap=True)
    to_south = functools.partial(shift, axis="lat", by=1, wrap=False)
    to_north = functools.partial(shift, axis="lat", by=-1, wrap=False)
    tokens = struct((2, OWN, FEAT), BF16)
    tiles = struct((ROWS * PAIR, FEAT), BF16)
    edge = struct((2, PAIR, FEAT), BF16)
    west, east = pack(pack_queries_kernel, query_vectors, output_grads, [tokens] * 2, "pack_queries")
    kd, vd, north_edge, south_edge = pack(pack_keys_kernel, key_vectors, value_vectors,
                                          [tiles] * 2 + [edge] * 2, "pack_keys")
    q_west = to_east(east)
    q_east = to_west(west)
    north = to_south(south_edge)
    south = to_north(north_edge)
    st0, st1, s_edge, d_edge, s_mid, d_mid = own_stats(west, east, kd, vd, north, south)
    in_west = to_east(st1)
    in_east = to_west(st0)
    dq_west, dq_east, out_west, out_east, dkx, dvx = halo(q_west, q_east, kd, vd, north, south, in_west, in_east)
    add1 = to_west(out_west)
    add0 = to_east(out_east)
    dq1 = to_west(dq_west)
    dq0 = to_east(dq_east)
    own = (west, east, kd, north, south, st0, st1, add0, add1)
    dq, dk, dv, dnorth, dsouth = edge_gradients(*own, s_edge, d_edge, dkx, dvx)
    from_south = to_north(dnorth)
    from_north = to_south(dsouth)
    dq, dk, dv = mid_gradients(*own, s_mid, d_mid, dq, dk, dv)
    return tuple(finish(dq, dk, dv, dq0, dq1, from_north, from_south))


def solution(mesh):
    spec = P("lat", "lon", None)
    return jax.shard_map(on_device, mesh=mesh, in_specs=(spec,) * 4, out_specs=(spec,) * 3, check_vma=False)
```

time: 106 us -> 99.3 us (0.937)
  Pallas kernels: 29.3 us -> 25.2 us
  starting transfers between devices: 44.2 us -> 41.3 us
    pallas_call x5 -> x7, Pallas kernels: 29.3 us -> 25.2 us  [the longest x1 7.86 us: halo(): pl.pallas_call(halo_kernel, grid=(2,), in_specs=[tokens] * 2 + [keys] * 2...]
    ppermute x12, starting transfers between devices: 44.2 us -> 41.3 us  [shift(): return lax.ppermute(x, axis, pairs)]
    unnamed x12 -> x16, local copies, waits for them, and re-layouts: 6.61 us -> 6.25 us
  transfers between devices with their start and end apart: 12 -> 12, of which waited for: 5 -> 5; matrix products, arithmetic and copies ran while one was open for 0% -> 0% of each run, Pallas kernels for 16% -> 13%
where the time goes in v1:
time: 99.3 us; the launch traced here: 98.8 us
  starting transfers between devices  41.3 us (42%)
  waiting for transfers between devices  25.3 us (25%)
  Pallas kernels  25.2 us (25%)
  local copies, waits for them, and re-layouts  6.25 us (6%)
    ppermute x12, starting transfers between devices, shift(): return lax.ppermute(x, axis, pairs)  41.3 us
    ppermute x12, waiting for transfers between devices, shift(): return lax.ppermute(x, axis, pairs)  25.3 us
    pallas_call x1, Pallas kernels, halo(): pl.pallas_call(halo_kernel, grid=(2,), in_specs=[tokens] * 2 + [keys] * 2...  7.86 us
    unnamed x16, local copies, waits for them, and re-layouts  6.25 us
    pallas_call x2, Pallas kernels, pack(): pl.pallas_call(kernel, in_specs=[pl.BlockSpec(memory_space=pltpu.HBM)] *...  4.81 us
    pallas_call x1, Pallas kernels, edge_gradients(): pl.pallas_call(edge_kernel, grid=(PAIRS,), in_specs=OWN_SPECS + [sums] *...  3.66 us
    pallas_call x1, Pallas kernels, own_stats(): pl.pallas_call(stats_kernel, grid=(PAIRS,), in_specs=[tokens_spec] * 2 +...  3.61 us
    pallas_call x1, Pallas kernels, mid_gradients(): pl.pallas_call(mid_kernel, grid=(PAIRS,), in_specs=OWN_SPECS + GRAD_SPECS...  3.38 us
  transfers between devices with their start and end apart: 12, of which 5 were waited for; matrix products, arithmetic and copies ran while one was open for 0% of the time, Pallas kernels for 13%

profile of v1, /device:TPU:1, one launch (start us, length us, event | category | flops | bytes accessed | tf_op | source)
XLA Modules:
  0.0 98.8 jit_solution(14250310951944109926)
XLA Ops:
  0.6 2.3 %pack_queries.1 = (bf16[2,256,512]{2,1,0:T(8,128)(2,1)}, bf16[2,256,512]{2,1,0:T(8,128)(2,1)}) custom-call(bf16[32,16,512]{2,1,0:T(8,128)(2,1)} %q_ref.1, bf16[32,16,512]{2,1,0:T(8,128)(2,1)} %g_ref.1), custom_call_target="tpu_custom_call" | custom-call | bytes 3145728 | tf_op jit(solution)/shard_map/pack_queries/pallas_call | solution.py:79
  3.0 9.5 %collective-permute-start.3 = (bf16[2,256,512]{2,1,0:T(8,128)(2,1)}, bf16[2,256,512]{2,1,0:T(8,128)(2,1)S(1)}, u32[]{:S(2)}, u32[]{:S(2)}) collective-permute-start(bf16[2,256,512]{2,1,0:T(8,128)(2,1)} %get-tuple-element.29.west), channel_id=1, source_target_pairs={{0,31},{1,0},{2,1},{3,2},{4,3},{5,4},{6,5},{7,6},{8,7},{9,8},{10,9... | collective-permute-start | bytes 1572872 | tf_op jit(solution)/shard_map/ppermute | solution.py:367
  12.4 0.0 collective-permute-start.2
  12.4 2.5 %pack_keys.1 = (bf16[512,512]{1,0:T(8,128)(2,1)}, bf16[512,512]{1,0:T(8,128)(2,1)}, bf16[2,128,512]{2,1,0:T(8,128)(2,1)}, bf16[2,128,512]{2,1,0:T(8,128)(2,1)}) custom-call(bf16[32,16,512]{2,1,0:T(8,128)(2,1)} %k_ref.1, bf16[32,16,512]{2,1,0:T(8,128)(2,1)} %v_ref.1), custom_call_target="tpu_custom_call" | custom-call | bytes 3145728 | tf_op jit(solution)/shard_map/pack_keys/pallas_call | solution.py:79
  14.9 3.1 %collective-permute-start = (bf16[2,128,512]{2,1,0:T(8,128)(2,1)}, bf16[2,128,512]{2,1,0:T(8,128)(2,1)S(1)}, u32[]{:S(2)}, u32[]{:S(2)}) collective-permute-start(bf16[2,128,512]{2,1,0:T(8,128)(2,1)} %get-tuple-element.32), channel_id=1, source_target_pairs={{0,32},{32,64},{64,96},{1,33},{33,65},{65,97},{2,34},{34,66},{66,9... | collective-permute-start | bytes 786440 | tf_op jit(solution)/shard_map/ppermute | solution.py:367
  18.1 1.9 %collective-permute-start.1 = (bf16[2,128,512]{2,1,0:T(8,128)(2,1)}, bf16[2,128,512]{2,1,0:T(8,128)(2,1)S(1)}, u32[]{:S(2)}, u32[]{:S(2)}) collective-permute-start(bf16[2,128,512]{2,1,0:T(8,128)(2,1)} %get-tuple-element.33), channel_id=1, source_target_pairs={{32,0},{64,32},{96,64},{33,1},{65,33},{97,65},{34,2},{66,34},{98,6... | collective-permute-start | bytes 786440 | tf_op jit(solution)/shard_map/ppermute | solution.py:367
  20.0 13.9 %collective-permute-done.north = bf16[2,128,512]{2,1,0:T(8,128)(2,1)S(1)} collective-permute-done((bf16[2,128,512]{2,1,0:T(8,128)(2,1)}, bf16[2,128,512]{2,1,0:T(8,128)(2,1)S(1)}, u32[]{:S(2)}, u32[]{:S(2)}) %collective-permute-start) | collective-permute-done | bytes 262176 | tf_op jit(solution)/shard_map/ppermute | solution.py:367
  33.9 0.7 collective-permute-done.1.south
  34.7 1.0 %copy-done = bf16[2,256,512]{2,1,0:T(8,128)(2,1)S(1)} copy-done((bf16[2,256,512]{2,1,0:T(8,128)(2,1)S(1)}, bf16[2,256,512]{2,1,0:T(8,128)(2,1)}, u32[]{:S(2)}) %copy-start) | copy-done | bytes 524312
  35.7 1.0 %copy-done.2 = bf16[2,256,512]{2,1,0:T(8,128)(2,1)S(1)} copy-done((bf16[2,256,512]{2,1,0:T(8,128)(2,1)S(1)}, bf16[2,256,512]{2,1,0:T(8,128)(2,1)}, u32[]{:S(2)}) %copy-start.2) | copy-done | bytes 524312
  36.8 1.0 %copy-done.4 = bf16[512,512]{1,0:T(8,128)(2,1)S(1)} copy-done((bf16[512,512]{1,0:T(8,128)(2,1)S(1)}, bf16[512,512]{1,0:T(8,128)(2,1)}, u32[]{:S(2)}) %copy-start.4) | copy-done | bytes 524312
  37.8 1.0 %copy-done.6 = bf16[512,512]{1,0:T(8,128)(2,1)S(1)} copy-done((bf16[512,512]{1,0:T(8,128)(2,1)S(1)}, bf16[512,512]{1,0:T(8,128)(2,1)}, u32[]{:S(2)}) %copy-start.6) | copy-done | bytes 524312
  38.9 3.6 %own_stats.1 = (f32[4,8,128]{2,1,0:T(8,128)S(1)}, f32[4,8,128]{2,1,0:T(8,128)S(1)}, f32[4,2,384,256]{3,2,1,0:T(8,128)S(1)}, f32[4,2,384,256]{3,2,1,0:T(8,128)S(1...) custom-call(bf16[2,256,512]{2,1,0:T(8,128)(2,1)S(1)} %copy-done, bf16[2,256,512]{2,1,0:T(8,128)(2,1)S(1)} %copy-done.2, ...), custom_call_target="tpu_custom_call" | custom-call | bytes 1024 | tf_op jit(solution)/shard_map/own_stats/pallas_call | solution.py:184
  42.5 6.6 %collective-permute-start.5 = (f32[4,8,128]{2,1,0:T(8,128)S(1)}, f32[4,8,128]{2,1,0:T(8,128)S(1)}, u32[]{:S(2)}, u32[]{:S(2)}) collective-permute-start(f32[4,8,128]{2,1,0:T(8,128)S(1)} %get-tuple-element.35.st0), channel_id=1, source_target_pairs={{0,31},{1,0},{2,1},{3,2},{4,3},{5,4},{6,5},{7,6},{8,7},{9,8},{10,9... | collective-permute-start | bytes 49160 | tf_op jit(solution)/shard_map/ppermute | solution.py:367
  49.0 0.0 collective-permute-start.4
  49.0 0.9 collective-permute-done.5.in_east
  49.9 7.4 %collective-permute-done.4.in_west = f32[4,8,128]{2,1,0:T(8,128)S(1)} collective-permute-done((f32[4,8,128]{2,1,0:T(8,128)S(1)}, f32[4,8,128]{2,1,0:T(8,128)S(1)}, u32[]{:S(2)}, u32[]{:S(2)}) %collective-permute-start.4) | collective-permute-done | bytes 16416 | tf_op jit(solution)/shard_map/ppermute | solution.py:367
  57.4 0.0 collective-permute-done.3.q_east
  57.4 0.0 collective-permute-done.2.q_west
  57.4 1.0 %copy-done.5 = bf16[512,512]{1,0:T(8,128)(2,1)S(1)} copy-done((bf16[512,512]{1,0:T(8,128)(2,1)S(1)}, bf16[512,512]{1,0:T(8,128)(2,1)}, u32[]{:S(2)}) %copy-start.5) | copy-done | bytes 524312
  58.4 1.0 %copy-done.7 = bf16[512,512]{1,0:T(8,128)(2,1)S(1)} copy-done((bf16[512,512]{1,0:T(8,128)(2,1)S(1)}, bf16[512,512]{1,0:T(8,128)(2,1)}, u32[]{:S(2)}) %copy-start.7) | copy-done | bytes 524312
  59.5 7.9 %halo.1 = (bf16[256,512]{1,0:T(8,128)(2,1)S(1)}, bf16[256,512]{1,0:T(8,128)(2,1)S(1)}, f32[4,8,128]{2,1,0:T(8,128)S(1)}, f32[4,8,128]{2,1,0:T(8,128)S(1)}, f32[7...) custom-call(bf16[2,256,512]{2,1,0:T(8,128)(2,1)S(1)} %collective-permute-done.2.q_west, ...), custom_call_target="tpu_custom_call" | custom-call | flops 3000000000 | bytes 4194304 | tf_op jit(solution)/shard_map/halo/pallas_call | solution.py:241
  67.3 0.1 collective-permute-start.6
  67.4 7.2 %collective-permute-start.7 = (f32[4,8,128]{2,1,0:T(8,128)S(1)}, f32[4,8,128]{2,1,0:T(8,128)S(1)}, u32[]{:S(2)}, u32[]{:S(2)}) collective-permute-start(f32[4,8,128]{2,1,0:T(8,128)S(1)} %get-tuple-element.38), channel_id=1, source_target_pairs={{0,31},{1,0},{2,1},{3,2},{4,3},{5,4},{6,5},{7,6},{8,7},{9,8},{10,9... | collective-permute-start | bytes 49160 | tf_op jit(solution)/shard_map/ppermute | solution.py:367
  74.6 0.0 collective-permute-start.8
  74.6 7.2 %collective-permute-start.9 = (bf16[256,512]{1,0:T(8,128)(2,1)S(1)}, bf16[256,512]{1,0:T(8,128)(2,1)S(1)}, u32[]{:S(2)}, u32[]{:S(2)}) collective-permute-start(bf16[256,512]{1,0:T(8,128)(2,1)S(1)} %get-tuple-element.52), channel_id=1, source_target_pairs={{0,31},{1,0},{2,1},{3,2},{4,3},{5,4},{6,5},{7,6},{8,7},{9,8},{10,9... | collective-permute-start | bytes 786440 | tf_op jit(solution)/shard_map/ppermute | solution.py:367
  81.8 3.7 %edge_gradients.1 = (f32[2,256,512]{2,1,0:T(8,128)S(1)}, f32[512,512]{1,0:T(8,128)S(1)}, f32[512,512]{1,0:T(8,128)S(1)}, bf16[2,128,512]{2,1,0:T(8,128)(2,1)S(1)}, bf16[2,128,512]{2,1,0:T(8,128)(2,1)S(1)}) custom-call(bf16[2,256,512]{2,1,0:T(8,128)(2,1)S(1)} %copy-done.1, bf16[2,256,512]{2,1,0:T(8,128)(2,1)S(1)} %copy-done.3, ...), custom_call_target="tpu_custom_call" | custom-call | flops 3000000000 | bytes 8388608 | tf_op jit(solution)/shard_map/edge_gradients/pallas_call | solution.py:307
  85.5 3.8 %collective-permute-start.10 = (bf16[2,128,512]{2,1,0:T(8,128)(2,1)S(1)}, bf16[2,128,512]{2,1,0:T(8,128)(2,1)S(1)}, u32[]{:S(2)}, u32[]{:S(2)}) collective-permute-start(bf16[2,128,512]{2,1,0:T(8,128)(2,1)S(1)} %get-tuple-element.53), channel_id=1, source_target_pairs={{0,32},{32,64},{64,96},{1,33},{33,65},{65,97},{2,34},{34,66},{66,9... | collective-permute-start | bytes 786440 | tf_op jit(solution)/shard_map/ppermute | solution.py:367
  89.3 1.9 %collective-permute-start.11 = (bf16[2,128,512]{2,1,0:T(8,128)(2,1)S(1)}, bf16[2,128,512]{2,1,0:T(8,128)(2,1)S(1)}, u32[]{:S(2)}, u32[]{:S(2)}) collective-permute-start(bf16[2,128,512]{2,1,0:T(8,128)(2,1)S(1)} %get-tuple-element.54), channel_id=1, source_target_pairs={{32,0},{64,32},{96,64},{33,1},{65,33},{97,65},{34,2},{66,34},{98,6... | collective-permute-start | bytes 786440 | tf_op jit(solution)/shard_map/ppermute | solution.py:367
  91.2 3.4 %mid_gradients.1 = (f32[2,256,512]{2,1,0:T(8,128)S(1)}, f32[512,512]{1,0:T(8,128)S(1)}, f32[512,512]{1,0:T(8,128)S(1)}) custom-call(bf16[2,256,512]{2,1,0:T(8,128)(2,1)S(1)} %copy-done.1, bf16[2,256,512]{2,1,0:T(8,128)(2,1)S(1)} %copy-done.3, bf16[512,512]{1,0:T(8,128)(2,1)S(1)} %copy-done.5, bf16[2,128,512]{2,1,0:T(8,128)(2,1)S(1)} %collective-permute-done.north, ...), custom_call_target="tpu_custom_call" | custom-call | flops 3000000000 | bytes 8388608 | tf_op jit(solution)/shard_map/mid_gradients/pallas_call | solution.py:320
  94.6 2.3 %collective-permute-done.11.from_south = bf16[2,128,512]{2,1,0:T(8,128)(2,1)S(1)} collective-permute-done((bf16[2,128,512]{2,1,0:T(8,128)(2,1)S(1)}, bf16[2,128,512]{2,1,0:T(8,128)(2,1)S(1)}, u32[]{:S(2)}, u32[]{:S(2)}) %collective-permute-start.11) | collective-permute-done | bytes 262176 | tf_op jit(solution)/shard_map/ppermute | solution.py:367
  97.0 1.9 %finish.1 = (bf16[32,16,512]{2,1,0:T(8,128)(2,1)}, bf16[32,16,512]{2,1,0:T(8,128)(2,1)}, bf16[32,16,512]{2,1,0:T(8,128)(2,1)}) custom-call(f32[2,256,512]{2,1,0:T(8,128)S(1)} %get-tuple-element.48.dq, f32[512,512]{1,0:T(8,128)S(1)} %get-tuple-element.49.dk, f32[512,512]{1,0:T(8,128)S(1)} %get-tuple-element.50.dv, ...), custom_call_target="tpu_custom_call" | custom-call | bytes 6291456 | tf_op jit(solution)/shard_map/finish/pallas_call | solution.py:352
  (15 shorter events, 0.0 us)
Async XLA Ops:
  3.0 54.4 %collective-permute-start.3 = (bf16[2,256,512]{2,1,0:T(8,128)(2,1)}, bf16[2,256,512]{2,1,0:T(8,128)(2,1)S(1)}, u32[]{:S(2)}, u32[]{:S(2)}) collective-permute-start(bf16[2,256,512]{2,1,0:T(8,128)(2,1)} %get-tuple-element.29.west), channel_id=1, source_target_pairs={{0,31},{1,0},{2,1},{3,2},{4,3},{5,4},{6,5},{7,6},{8,7},{9,8},{10,9... | collective-permute-start | bytes 1572872 | tf_op jit(solution)/shard_map/ppermute | solution.py:367
  12.4 44.9 %collective-permute-start.2 = (bf16[2,256,512]{2,1,0:T(8,128)(2,1)}, bf16[2,256,512]{2,1,0:T(8,128)(2,1)S(1)}, u32[]{:S(2)}, u32[]{:S(2)}) collective-permute-start(bf16[2,256,512]{2,1,0:T(8,128)(2,1)} %get-tuple-element.30.east), channel_id=1, source_target_pairs={{0,1},{1,2},{2,3},{3,4},{4,5},{5,6},{6,7},{7,8},{8,9},{9,10},{10,1... | collective-permute-start | bytes 1572872 | tf_op jit(solution)/shard_map/ppermute | solution.py:367
  14.9 19.0 %collective-permute-start = (bf16[2,128,512]{2,1,0:T(8,128)(2,1)}, bf16[2,128,512]{2,1,0:T(8,128)(2,1)S(1)}, u32[]{:S(2)}, u32[]{:S(2)}) collective-permute-start(bf16[2,128,512]{2,1,0:T(8,128)(2,1)} %get-tuple-element.32), channel_id=1, source_target_pairs={{0,32},{32,64},{64,96},{1,33},{33,65},{65,97},{2,34},{34,66},{66,9... | collective-permute-start | bytes 786440 | tf_op jit(solution)/shard_map/ppermute | solution.py:367
  18.1 16.6 %collective-permute-start.1 = (bf16[2,128,512]{2,1,0:T(8,128)(2,1)}, bf16[2,128,512]{2,1,0:T(8,128)(2,1)S(1)}, u32[]{:S(2)}, u32[]{:S(2)}) collective-permute-start(bf16[2,128,512]{2,1,0:T(8,128)(2,1)} %get-tuple-element.33), channel_id=1, source_target_pairs={{32,0},{64,32},{96,64},{33,1},{65,33},{97,65},{34,2},{66,34},{98,6... | collective-permute-start | bytes 786440 | tf_op jit(solution)/shard_map/ppermute | solution.py:367
  34.7 1.0 %copy-start = (bf16[2,256,512]{2,1,0:T(8,128)(2,1)S(1)}, bf16[2,256,512]{2,1,0:T(8,128)(2,1)}, u32[]{:S(2)}) copy-start(bf16[2,256,512]{2,1,0:T(8,128)(2,1)} %get-tuple-element.29.west) | copy-start | bytes 1572868
  35.7 1.0 %copy-start.2 = (bf16[2,256,512]{2,1,0:T(8,128)(2,1)S(1)}, bf16[2,256,512]{2,1,0:T(8,128)(2,1)}, u32[]{:S(2)}) copy-start(bf16[2,256,512]{2,1,0:T(8,128)(2,1)} %get-tuple-element.30.east) | copy-start | bytes 1572868
  36.8 1.0 %copy-start.4 = (bf16[512,512]{1,0:T(8,128)(2,1)S(1)}, bf16[512,512]{1,0:T(8,128)(2,1)}, u32[]{:S(2)}) copy-start(bf16[512,512]{1,0:T(8,128)(2,1)} %get-tuple-element.31.kd) | copy-start | bytes 1572868
  37.8 1.0 %copy-start.6 = (bf16[512,512]{1,0:T(8,128)(2,1)S(1)}, bf16[512,512]{1,0:T(8,128)(2,1)}, u32[]{:S(2)}) copy-start(bf16[512,512]{1,0:T(8,128)(2,1)} %get-tuple-element.34.vd) | copy-start | bytes 1572868
  42.5 7.4 %collective-permute-start.5 = (f32[4,8,128]{2,1,0:T(8,128)S(1)}, f32[4,8,128]{2,1,0:T(8,128)S(1)}, u32[]{:S(2)}, u32[]{:S(2)}) collective-permute-start(f32[4,8,128]{2,1,0:T(8,128)S(1)} %get-tuple-element.35.st0), channel_id=1, source_target_pairs={{0,31},{1,0},{2,1},{3,2},{4,3},{5,4},{6,5},{7,6},{8,7},{9,8},{10,9... | collective-permute-start | bytes 49160 | tf_op jit(solution)/shard_map/ppermute | solution.py:367
  49.0 32.7 %copy-start.1 = (bf16[2,256,512]{2,1,0:T(8,128)(2,1)S(1)}, bf16[2,256,512]{2,1,0:T(8,128)(2,1)}, u32[]{:S(2)}) copy-start(bf16[2,256,512]{2,1,0:T(8,128)(2,1)} %get-tuple-element.29.west) | copy-start | bytes 1572868
  49.0 32.7 %copy-start.3 = (bf16[2,256,512]{2,1,0:T(8,128)(2,1)S(1)}, bf16[2,256,512]{2,1,0:T(8,128)(2,1)}, u32[]{:S(2)}) copy-start(bf16[2,256,512]{2,1,0:T(8,128)(2,1)} %get-tuple-element.30.east) | copy-start | bytes 1572868
  49.0 8.3 %collective-permute-start.4 = (f32[4,8,128]{2,1,0:T(8,128)S(1)}, f32[4,8,128]{2,1,0:T(8,128)S(1)}, u32[]{:S(2)}, u32[]{:S(2)}) collective-permute-start(f32[4,8,128]{2,1,0:T(8,128)S(1)} %get-tuple-element.36.st1), channel_id=1, source_target_pairs={{0,1},{1,2},{2,3},{3,4},{4,5},{5,6},{6,7},{7,8},{8,9},{9,10},{10,1... | collective-permute-start | bytes 49160 | tf_op jit(solution)/shard_map/ppermute | solution.py:367
  57.4 1.0 %copy-start.5 = (bf16[512,512]{1,0:T(8,128)(2,1)S(1)}, bf16[512,512]{1,0:T(8,128)(2,1)}, u32[]{:S(2)}) copy-start(bf16[512,512]{1,0:T(8,128)(2,1)} %get-tuple-element.31.kd) | copy-start | bytes 1572868
  58.4 1.0 %copy-start.7 = (bf16[512,512]{1,0:T(8,128)(2,1)S(1)}, bf16[512,512]{1,0:T(8,128)(2,1)}, u32[]{:S(2)}) copy-start(bf16[512,512]{1,0:T(8,128)(2,1)} %get-tuple-element.34.vd) | copy-start | bytes 1572868
  67.3 14.5 %collective-permute-start.6 = (f32[4,8,128]{2,1,0:T(8,128)S(1)}, f32[4,8,128]{2,1,0:T(8,128)S(1)}, u32[]{:S(2)}, u32[]{:S(2)}) collective-permute-start(f32[4,8,128]{2,1,0:T(8,128)S(1)} %get-tuple-element.37), channel_id=1, source_target_pairs={{0,1},{1,2},{2,3},{3,4},{4,5},{5,6},{6,7},{7,8},{8,9},{9,10},{10,1... | collective-permute-start | bytes 49160 | tf_op jit(solution)/shard_map/ppermute | solution.py:367
  67.4 14.4 %collective-permute-start.7 = (f32[4,8,128]{2,1,0:T(8,128)S(1)}, f32[4,8,128]{2,1,0:T(8,128)S(1)}, u32[]{:S(2)}, u32[]{:S(2)}) collective-permute-start(f32[4,8,128]{2,1,0:T(8,128)S(1)} %get-tuple-element.38), channel_id=1, source_target_pairs={{0,31},{1,0},{2,1},{3,2},{4,3},{5,4},{6,5},{7,6},{8,7},{9,8},{10,9... | collective-permute-start | bytes 49160 | tf_op jit(solution)/shard_map/ppermute | solution.py:367
  74.6 20.0 %collective-permute-start.8 = (bf16[256,512]{1,0:T(8,128)(2,1)S(1)}, bf16[256,512]{1,0:T(8,128)(2,1)S(1)}, u32[]{:S(2)}, u32[]{:S(2)}) collective-permute-start(bf16[256,512]{1,0:T(8,128)(2,1)S(1)} %get-tuple-element.51), channel_id=1, source_target_pairs={{0,1},{1,2},{2,3},{3,4},{4,5},{5,6},{6,7},{7,8},{8,9},{9,10},{10,1... | collective-permute-start | bytes 786440 | tf_op jit(solution)/shard_map/ppermute | solution.py:367
  74.6 20.0 %collective-permute-start.9 = (bf16[256,512]{1,0:T(8,128)(2,1)S(1)}, bf16[256,512]{1,0:T(8,128)(2,1)S(1)}, u32[]{:S(2)}, u32[]{:S(2)}) collective-permute-start(bf16[256,512]{1,0:T(8,128)(2,1)S(1)} %get-tuple-element.52), channel_id=1, source_target_pairs={{0,31},{1,0},{2,1},{3,2},{4,3},{5,4},{6,5},{7,6},{8,7},{9,8},{10,9... | collective-permute-start | bytes 786440 | tf_op jit(solution)/shard_map/ppermute | solution.py:367
  85.5 9.1 %collective-permute-start.10 = (bf16[2,128,512]{2,1,0:T(8,128)(2,1)S(1)}, bf16[2,128,512]{2,1,0:T(8,128)(2,1)S(1)}, u32[]{:S(2)}, u32[]{:S(2)}) collective-permute-start(bf16[2,128,512]{2,1,0:T(8,128)(2,1)S(1)} %get-tuple-element.53), channel_id=1, source_target_pairs={{0,32},{32,64},{64,96},{1,33},{33,65},{65,97},{2,34},{34,66},{66,9... | collective-permute-start | bytes 786440 | tf_op jit(solution)/shard_map/ppermute | solution.py:367
  89.3 7.7 %collective-permute-start.11 = (bf16[2,128,512]{2,1,0:T(8,128)(2,1)S(1)}, bf16[2,128,512]{2,1,0:T(8,128)(2,1)S(1)}, u32[]{:S(2)}, u32[]{:S(2)}) collective-permute-start(bf16[2,128,512]{2,1,0:T(8,128)(2,1)S(1)} %get-tuple-element.54), channel_id=1, source_target_pairs={{32,0},{64,32},{96,64},{33,1},{65,33},{97,65},{34,2},{66,34},{98,6... | collective-permute-start | bytes 786440 | tf_op jit(solution)/shard_map/ppermute | solution.py:367

commit v2 on v1

v2 whole, which is shorter than its diff:
```python
import jax
import jax.numpy as jnp
from jax import lax
from jax.experimental import pallas as pl
from jax.experimental.pallas import tpu as pltpu
from jax.sharding import PartitionSpec as P

ROWS = 4
CELLS = 64
OWN = ROWS * CELLS
PAIR = 128
WIDE = 256
PAIRS = 4
GROUPS = 2
FEAT = 512
SCALE = 64 ** -0.5
LOG2E = 1.4426950408889634
MASKED = -1e30
F32 = jnp.float32
BF16 = jnp.bfloat16
VMEM_LIMIT = 20 * 1024 * 1024
PACK_LIMIT = 62 * 1024 * 1024
EDGE_ROWS = (0, 3)
MID_ROWS = (1, 2)


def matmul(a, b, contract):
    return lax.dot_general(a, b, ((contract[:1], contract[1:]), ((), ())), preferred_element_type=F32)


def params(limit=VMEM_LIMIT):
    return pltpu.CompilerParams(vmem_limit_bytes=limit)


def cost(flops, size):
    return pl.CostEstimate(flops=int(flops), bytes_accessed=int(size), transcendentals=0)


def struct(shape, dtype):
    return jax.ShapeDtypeStruct(shape, dtype)


def grid_row(t):
    return jnp.where(lax.axis_index("lat") % 2 == 0, ROWS - 1 - t, t)


def ordered(first, second):
    swap = lax.axis_index("lon") % 2 == 0
    return jnp.where(swap, second, first), jnp.where(swap, first, second)


def split_columns(block):
    wide = block.astype(F32)
    parts = ordered(*[wide[:, c * 8:(c + 1) * 8].reshape(CELLS, FEAT) for c in range(2)])
    return [part.astype(BF16) for part in parts]


def fetch(refs, buffers, sems):
    copies = [[pltpu.make_async_copy(ref.at[pl.ds(8 * grid_row(t), 8)], buffers.at[i, t], sems.at[i, t])
               for t in range(ROWS)] for i, ref in enumerate(refs)]
    for t in range(ROWS):
        for copy in copies:
            copy[t].start()
    return copies


def pack_queries_kernel(q_ref, g_ref, side_a, side_b, buffers, sems):
    copies = fetch((q_ref, g_ref), buffers, sems)
    for t in range(ROWS):
        for i in range(2):
            copies[i][t].wait()
            first, second = split_columns(buffers[i, t])
            side_a[i, t * CELLS:(t + 1) * CELLS] = first
            side_b[i, t * CELLS:(t + 1) * CELLS] = second


def pack_keys_kernel(k_ref, v_ref, kd, vd, edge_a, edge_b, buffers, sems):
    copies = fetch((k_ref, v_ref), buffers, sems)
    for t in range(ROWS):
        for i, out in enumerate((kd, vd)):
            copies[i][t].wait()
            tile = jnp.concatenate(split_columns(buffers[i, t]), axis=0)
            out[t * PAIR:(t + 1) * PAIR] = tile
            if t == 0:
                edge_a[i] = tile
            if t == ROWS - 1:
                edge_b[i] = tile


def pack(kernel, x, y, out_shape, name, limit):
    return pl.pallas_call(
        kernel,
        in_specs=[pl.BlockSpec(memory_space=pl.ANY)] * 2,
        out_shape=out_shape,
        scratch_shapes=[pltpu.VMEM((2, ROWS, 8, 16, FEAT), BF16), pltpu.SemaphoreType.DMA((2, ROWS))],
        compiler_params=params(limit),
        cost_estimate=cost(0, 3 << 20),
        name=name,
    )(x, y)


def head_masks(lanes):
    lane = lax.broadcasted_iota(jnp.int32, (1, lanes), 1)
    return [jnp.where((lane >= 64 * h) & (lane < 64 * (h + 1)), 1.0, 0.0).astype(F32).astype(BF16)
            for h in range(lanes // 64)]


def stacked(parts, masks):
    return jnp.concatenate([part * mask for part in parts for mask in masks], axis=0)


def key_rows(own, edge_a, edge_b, which, t, lanes=slice(None)):
    rows = []
    for row in range(t, t + 3):
        if row == 0:
            rows.append(edge_a[which, :, lanes])
        elif row == ROWS + 1:
            rows.append(edge_b[which, :, lanes])
        else:
            rows.append(own[(row - 1) * PAIR:row * PAIR, lanes])
    return rows


def window(*where):
    return jnp.concatenate(key_rows(*where), axis=0)


def column_window(column, *where):
    return jnp.concatenate([row[column * CELLS:(column + 1) * CELLS] for row in key_rows(*where)], axis=0)


def score_block(keys, queries, t):
    scores = matmul(keys, queries, (1, 1)) * (SCALE * LOG2E)
    if t == ROWS - 1:
        lat = lax.axis_index("lat")
        outside = (lat == 0) | (lat == lax.axis_size("lat") - 1)
        cut = 2 * (keys.shape[0] // 3)
        bias = jnp.where(outside, MASKED, 0.0).astype(F32)
        scores = jnp.concatenate([scores[:cut], scores[cut:] + bias], axis=0)
    return scores


def row_stats(scores, dprobs):
    top = jnp.max(scores, axis=0, keepdims=True)
    weights = jnp.exp2(scores - top)
    total = jnp.sum(weights, axis=0, keepdims=True)
    delta = jnp.sum(weights * dprobs, axis=0, keepdims=True) / total
    return top + jnp.log(total) * LOG2E, delta


def merged(log_a, delta_a, log_b, delta_b):
    top = jnp.maximum(log_a, log_b)
    weight_a = jnp.exp2(log_a - top)
    weight_b = jnp.exp2(log_b - top)
    total = weight_a + weight_b
    return top + jnp.log(total) * LOG2E, (weight_a * delta_a + weight_b * delta_b) / total


def from_both(mine, theirs, pair, base, t):
    mine_at, theirs_at = base + 2 * t, 8 - base + 2 * t
    return merged(mine[pair, mine_at:mine_at + 1], mine[pair, mine_at + 1:mine_at + 2],
                  theirs[pair, theirs_at:theirs_at + 1], theirs[pair, theirs_at + 1:theirs_at + 2])


def query_part(keys, dscores, lane):
    turned = matmul(keys, dscores, (0, 0)).T * SCALE
    return jnp.where(lane < 64, turned[:CELLS], turned[CELLS:])


def at_tokens(t):
    return slice(t * CELLS, (t + 1) * CELLS)


tokens_spec = pl.BlockSpec((2, OWN, PAIR), lambda p: (0, 0, p))
keys_spec = pl.BlockSpec((ROWS * PAIR, PAIR), lambda p: (0, p))
edge_spec = pl.BlockSpec((2, PAIR, PAIR), lambda p: (0, 0, p))
part_spec = pl.BlockSpec((1, 8, PAIR), lambda p: (p, 0, 0))
held_spec = pl.BlockSpec((1, 2, 3 * PAIR, WIDE), lambda p: (p, 0, 0, 0))
part_shape = struct((PAIRS, 8, PAIR), F32)
held_shape = struct((PAIRS, 2, 3 * PAIR, WIDE), F32)

tokens_wide = pl.BlockSpec((2, OWN, WIDE), lambda g: (0, 0, g))
keys_wide = pl.BlockSpec((ROWS * PAIR, WIDE), lambda g: (0, g))
edge_wide = pl.BlockSpec((2, PAIR, WIDE), lambda g: (0, 0, g))
part_wide = pl.BlockSpec((2, 8, PAIR), lambda g: (g, 0, 0))
stats_wide = pl.BlockSpec((2, 16, PAIR), lambda g: (g, 0, 0))
held_wide = pl.BlockSpec((2, 2, 3 * PAIR, WIDE), lambda g: (g, 0, 0, 0))
halo_wide = pl.BlockSpec((1, 2, 2, 3 * CELLS, WIDE), lambda g: (g, 0, 0, 0, 0))
stats_shape = struct((PAIRS, 16, PAIR), F32)
halo_shape = struct((GROUPS, 2, 2, 3 * CELLS, WIDE), F32)


def own_scores(rows, side_a, side_b, kd, vd, edge_a, edge_b, part, s_out, d_out):
    masks = head_masks(PAIR)
    for place, t in enumerate(rows):
        at = at_tokens(t)
        queries = stacked([side_a[0, at], side_b[0, at]], masks)
        grads = stacked([side_a[1, at], side_b[1, at]], masks)
        scores = score_block(window(kd, edge_a, edge_b, 0, t), queries, t)
        dprobs = matmul(window(vd, edge_a, edge_b, 1, t), grads, (1, 1))
        s_out[0, place] = scores
        d_out[0, place] = dprobs
        for w, values in enumerate(row_stats(scores, dprobs)):
            for c in range(2):
                index = 4 * c + 2 * place + w
                part[0, index:index + 1] = values[:, c * PAIR:(c + 1) * PAIR]


def mid_scores_kernel(side_a, side_b, kd, vd, part, s_out, d_out):
    own_scores(MID_ROWS, side_a, side_b, kd, vd, None, None, part, s_out, d_out)


def edge_scores_kernel(side_a, side_b, kd, vd, edge_a, edge_b, part, s_out, d_out):
    own_scores(EDGE_ROWS, side_a, side_b, kd, vd, edge_a, edge_b, part, s_out, d_out)


def scores_call(kernel, operands, name):
    return pl.pallas_call(
        kernel,
        grid=(PAIRS,),
        in_specs=[tokens_spec] * 2 + [keys_spec] * 2 + [edge_spec] * (len(operands) - 4),
        out_specs=[part_spec] + [held_spec] * 2,
        out_shape=[part_shape] + [held_shape] * 2,
        compiler_params=params(),
        cost_estimate=cost(2e9, 3 << 20),
        name=name,
    )(*operands)


def halo_scores_kernel(q_a, q_b, kd, vd, edge_a, edge_b, part_edge, part_mid,
                       send_a, send_b, s_edge, d_edge, s_mid, d_mid):
    masks = head_masks(WIDE)
    for t in range(ROWS):
        at = at_tokens(t)
        held = (s_edge, d_edge) if t in EDGE_ROWS else (s_mid, d_mid)
        place = t // 3 if t in EDGE_ROWS else t - 1
        part = part_edge if t in EDGE_ROWS else part_mid
        for c, (q_in, send) in enumerate(((q_a, send_a), (q_b, send_b))):
            queries = stacked([q_in[0, at]], masks)
            grads = stacked([q_in[1, at]], masks)
            scores = score_block(column_window(c, kd, edge_a, edge_b, 0, t), queries, t)
            dprobs = matmul(column_window(c, vd, edge_a, edge_b, 1, t), grads, (1, 1))
            held[0][0, place, c] = scores
            held[1][0, place, c] = dprobs
            for w, values in enumerate(row_stats(scores, dprobs)):
                for j in range(2):
                    index = 2 * t + w
                    source = 4 * c + 2 * place + w
                    send[j, index:index + 1] = part[j, source:source + 1]
                    send[j, 8 + index:9 + index] = values[:, j * PAIR:(j + 1) * PAIR]


def halo_scores(*operands):
    return pl.pallas_call(
        halo_scores_kernel,
        grid=(GROUPS,),
        in_specs=[tokens_wide] * 2 + [keys_wide] * 2 + [edge_wide] * 2 + [part_wide] * 2,
        out_specs=[stats_wide] * 2 + [halo_wide] * 4,
        out_shape=[stats_shape] * 2 + [halo_shape] * 4,
        compiler_params=params(),
        cost_estimate=cost(2e9, 3 << 20),
        name="halo_scores",
    )(*operands)


def halo_weights(mine, theirs, s_in, d_in, place, c, t):
    both = [from_both(mine, theirs, j, 8, t) for j in range(2)]
    log_total = jnp.concatenate([one[0] for one in both], axis=1)
    delta = jnp.concatenate([one[1] for one in both], axis=1)
    probs = jnp.exp2(s_in[0, place, c] - log_total)
    return probs.astype(BF16), (probs * (d_in[0, place, c] - delta)).astype(BF16)


def halo_queries_kernel(kd, edge_a, edge_b, send_a, send_b, recv_a, recv_b, s_edge, d_edge, s_mid, d_mid, dq_a, dq_b):
    lane = lax.broadcasted_iota(jnp.int32, (1, PAIR), 1)
    for t in range(ROWS):
        held = (s_edge, d_edge) if t in EDGE_ROWS else (s_mid, d_mid)
        place = t // 3 if t in EDGE_ROWS else t - 1
        for c, (mine, theirs, out) in enumerate(((send_a, recv_a, dq_a), (send_b, recv_b, dq_b))):
            _, dscores = halo_weights(mine, theirs, *held, place, c, t)
            keys = column_window(c, kd, edge_a, edge_b, 0, t)
            for j in range(2):
                lanes = slice(j * PAIR, (j + 1) * PAIR)
                out[at_tokens(t), lanes] = query_part(keys[:, lanes], dscores[:, lanes], lane).astype(BF16)


def halo_queries(*operands):
    grads = pl.BlockSpec((OWN, WIDE), lambda g: (0, g))
    return pl.pallas_call(
        halo_queries_kernel,
        grid=(GROUPS,),
        in_specs=[keys_wide] + [edge_wide] * 2 + [stats_wide] * 4 + [halo_wide] * 4,
        out_specs=[grads] * 2,
        out_shape=[struct((OWN, FEAT), BF16)] * 2,
        compiler_params=params(),
        cost_estimate=cost(2e9, 3 << 20),
        name="halo_queries",
    )(*operands)


def row_gradients(place, t, side_a, side_b, q_a, q_b, kd, edge_a, edge_b, send_a, send_b, recv_a, recv_b,
                  s_own, d_own, s_halo, d_halo, dq_ref):
    at = at_tokens(t)
    masks, wide_masks = head_masks(PAIR), head_masks(WIDE)
    lane = lax.broadcasted_iota(jnp.int32, (1, PAIR), 1)
    key_parts, value_parts = [], []
    for j in range(2):
        lanes = slice(j * PAIR, (j + 1) * PAIR)
        queries = stacked([side_a[0, at, lanes], side_b[0, at, lanes]], masks)
        grads = stacked([side_a[1, at, lanes], side_b[1, at, lanes]], masks)
        both = [from_both(send_a, recv_a, j, 0, t), from_both(send_b, recv_b, j, 0, t)]
        probs = jnp.exp2(s_own[j, place] - jnp.concatenate([one[0] for one in both], axis=1))
        delta = jnp.concatenate([one[1] for one in both], axis=1)
        dscores = (probs * (d_own[j, place] - delta)).astype(BF16)
        keys = window(kd, edge_a, edge_b, 0, t, lanes)
        for c in range(2):
            dq_ref[c, at, lanes] = query_part(keys, dscores[:, c * PAIR:(c + 1) * PAIR], lane)
        key_parts.append(matmul(dscores, queries, (1, 0)))
        value_parts.append(matmul(probs.astype(BF16), grads, (1, 0)))
    sums = [jnp.concatenate(key_parts, axis=1), jnp.concatenate(value_parts, axis=1)]
    halo = []
    for c, (q_in, mine, theirs) in enumerate(((q_a, send_a, recv_a), (q_b, send_b, recv_b))):
        probs, dscores = halo_weights(mine, theirs, s_halo, d_halo, place, c, t)
        halo.append((matmul(dscores, stacked([q_in[0, at]], wide_masks), (1, 0)),
                     matmul(probs, stacked([q_in[1, at]], wide_masks), (1, 0))))
    return [jnp.concatenate([sums[which][(2 * i + c) * CELLS:(2 * i + c + 1) * CELLS]
                             + halo[c][which][i * CELLS:(i + 1) * CELLS] for i in range(3) for c in range(2)], axis=0)
            for which in range(2)]


OPERANDS = 15


def edge_kernel(*refs):
    operands, (_, dq_ref, dk_ref, dv_ref, out_a, out_b) = refs[:OPERANDS], refs[OPERANDS:]
    for place, t in enumerate(EDGE_ROWS):
        parts = row_gradients(place, t, *operands, dq_ref)
        for which, (out, scale) in enumerate(((dk_ref, SCALE), (dv_ref, 1.0))):
            part = parts[which] * scale
            if t == 0:
                out_a[which] = part[:PAIR].astype(BF16)
                out[0:2 * PAIR] = part[PAIR:]
            else:
                out_b[which] = part[2 * PAIR:].astype(BF16)
                out[2 * PAIR:] = part[:2 * PAIR]


def mid_kernel(*refs):
    operands, (dq_in, dk_in, dv_in, dq_ref, dk_ref, dv_ref) = refs[:OPERANDS], refs[OPERANDS:]
    upper, lower = [row_gradients(place, t, *operands, dq_ref) for place, t in enumerate(MID_ROWS)]
    for t in EDGE_ROWS:
        for c in range(2):
            dq_ref[c, at_tokens(t)] = dq_in[c, at_tokens(t)]
    for which, (sums, out, scale) in enumerate(((dk_in, dk_ref, SCALE), (dv_in, dv_ref, 1.0))):
        out[0:PAIR] = sums[0:PAIR] + upper[which][:PAIR] * scale
        out[PAIR:3 * PAIR] = sums[PAIR:3 * PAIR] + (upper[which][PAIR:] + lower[which][:2 * PAIR]) * scale
        out[3 * PAIR:] = sums[3 * PAIR:] + lower[which][2 * PAIR:] * scale


ROW_SPECS = [tokens_wide] * 4 + [keys_wide] + [edge_wide] * 2 + [stats_wide] * 4 + [held_wide] * 2 + [halo_wide] * 2
GRAD_SPECS = [tokens_wide] + [keys_wide] * 2
GRAD_SHAPES = [struct((2, OWN, FEAT), F32)] + [struct((ROWS * PAIR, FEAT), F32)] * 2


def edge_gradients(*operands):
    return pl.pallas_call(
        edge_kernel,
        grid=(GROUPS,),
        in_specs=ROW_SPECS + [pl.BlockSpec(memory_space=pl.ANY)],
        out_specs=GRAD_SPECS + [edge_wide] * 2,
        out_shape=GRAD_SHAPES + [struct((2, PAIR, FEAT), BF16)] * 2,
        compiler_params=params(),
        cost_estimate=cost(3e9, 1 << 10),
        name="edge_gradients",
    )(*operands)


def mid_gradients(*operands):
    return pl.pallas_call(
        mid_kernel,
        grid=(GROUPS,),
        in_specs=ROW_SPECS + GRAD_SPECS,
        out_specs=GRAD_SPECS,
        out_shape=GRAD_SHAPES,
        compiler_params=params(),
        cost_estimate=cost(3e9, 1 << 10),
        name="mid_gradients",
    )(*operands)


def join_columns(side_a, side_b):
    parts = ordered(side_a, side_b)
    return jnp.concatenate([part.reshape(8, 8, FEAT) for part in parts], axis=1).astype(BF16)


def finish_kernel(dq, dk, dv, dq_a, dq_b, from_a, from_b, q_ref, k_ref, v_ref, buffers, sems):
    copies = []
    for t in range(ROWS):
        at = at_tokens(t)
        buffers[0, t] = join_columns(dq[0, at] + dq_a[at].astype(F32), dq[1, at] + dq_b[at].astype(F32))
        for which, own in enumerate((dk, dv)):
            full = own[t * PAIR:(t + 1) * PAIR]
            if t == 0:
                full = full + from_a[which].astype(F32)
            if t == ROWS - 1:
                full = full + from_b[which].astype(F32)
            buffers[1 + which, t] = join_columns(full[:CELLS], full[CELLS:])
        for i, out in enumerate((q_ref, k_ref, v_ref)):
            copies.append(pltpu.make_async_copy(buffers.at[i, t], out.at[pl.ds(8 * grid_row(t), 8)], sems.at[i, t]))
            copies[-1].start()
    for copy in copies:
        copy.wait()


def finish(*operands):
    return pl.pallas_call(
        finish_kernel,
        out_specs=[pl.BlockSpec(memory_space=pl.ANY)] * 3,
        out_shape=[struct((8 * ROWS, 16, FEAT), BF16)] * 3,
        scratch_shapes=[pltpu.VMEM((3, ROWS, 8, 16, FEAT), BF16), pltpu.SemaphoreType.DMA((3, ROWS))],
        compiler_params=params(),
        cost_estimate=cost(0, 6 << 20),
        name="finish",
    )(*operands)


def swap_a(x, axis):
    return lax.ppermute(x, axis, [(i, i ^ 1) for i in range(lax.axis_size(axis))])


def swap_b(x, axis, wrap):
    count = lax.axis_size(axis)
    pairs = []
    for i in range(1, count if wrap else count - 1, 2):
        pairs += [(i, (i + 1) % count), ((i + 1) % count, i)]
    return lax.ppermute(x, axis, pairs)


def over_lon(side_a, side_b):
    return swap_a(side_a, "lon"), swap_b(side_b, "lon", True)


def over_lat(side_a, side_b):
    return swap_a(side_a, "lat"), swap_b(side_b, "lat", False)


def on_device(query_vectors, key_vectors, value_vectors, output_grads):
    tokens = struct((2, OWN, FEAT), BF16)
    tiles = struct((ROWS * PAIR, FEAT), BF16)
    edge = struct((2, PAIR, FEAT), BF16)
    sides = pack(pack_queries_kernel, query_vectors, output_grads, [tokens] * 2, "pack_queries", PACK_LIMIT)
    kd, vd, own_edge_a, own_edge_b = pack(pack_keys_kernel, key_vectors, value_vectors,
                                          [tiles] * 2 + [edge] * 2, "pack_keys", VMEM_LIMIT)
    halos = over_lon(*sides)
    edges = over_lat(own_edge_a, own_edge_b)
    part_mid, *own_mid = scores_call(mid_scores_kernel, (*sides, kd, vd), "mid_scores")
    part_edge, *own_edge = scores_call(edge_scores_kernel, (*sides, kd, vd, *edges), "edge_scores")
    send_a, send_b, *held = halo_scores(*halos, kd, vd, *edges, part_edge, part_mid)
    stats = (send_a, send_b, *over_lon(send_a, send_b))
    halo_dq = halo_queries(kd, *edges, *stats, *held)
    dq_parts = over_lon(*halo_dq)
    shared = (*sides, *halos, kd, *edges, *stats)
    dq, dk, dv, out_a, out_b = edge_gradients(*shared, *own_edge, *held[:2], halo_dq[0])
    key_parts = over_lat(out_a, out_b)
    dq, dk, dv = mid_gradients(*shared, *own_mid, *held[2:], dq, dk, dv)
    return tuple(finish(dq, dk, dv, *dq_parts, *key_parts))


def solution(mesh):
    spec = P("lat", "lon", None)
    return jax.shard_map(on_device, mesh=mesh, in_specs=(spec,) * 4, out_specs=(spec,) * 3, check_vma=False)
```

time: 99.3 us -> 73.3 us (0.74)
  waiting for transfers between devices: 25.3 us -> 10.7 us
  starting transfers between devices: 41.3 us -> 35.7 us
  Pallas kernels: 25.2 us -> 21.6 us
  local copies, waits for them, and re-layouts: 6.25 us -> 4.16 us
    ppermute x12 -> x10, waiting for transfers between devices: 25.3 us -> 10.7 us  [the longest x5 10.7 us: swap_b(): return lax.ppermute(x, axis, pairs)]
    ppermute x12 -> x10, starting transfers between devices: 41.3 us -> 35.7 us  [the longest x5 28.8 us: swap_b(): return lax.ppermute(x, axis, pairs)]
    pallas_call x7 -> x9, Pallas kernels: 25.2 us -> 21.6 us  [the longest x2 4.97 us: scores_call(): pl.pallas_call(kernel, grid=(PAIRS,), in_specs=[tokens_spec] * 2 + [keys_...]
    unnamed x16 -> x10, local copies, waits for them, and re-layouts: 6.25 us -> 4.16 us
  transfers between devices with their start and end apart: 12 -> 10, of which waited for: 5 -> 3; matrix products, arithmetic and copies ran while one was open for 0% -> 0% of each run, Pallas kernels for 13% -> 17%
where the time goes in v2:
time: 73.3 us; the launch traced here: 73 us
  starting transfers between devices  35.7 us (49%)
  Pallas kernels  21.6 us (29%)
  waiting for transfers between devices  10.7 us (15%)
  local copies, waits for them, and re-layouts  4.16 us (6%)
  between operations  0.79 us (1%)
    ppermute x5, starting transfers between devices, swap_b(): return lax.ppermute(x, axis, pairs)  28.8 us
    ppermute x5, waiting for transfers between devices, swap_b(): return lax.ppermute(x, axis, pairs)  10.7 us
    ppermute x5, starting transfers between devices, swap_a(): lax.ppermute(x, axis, [(i, i ^ 1) for i in range(lax.axis_size(axis))])  6.91 us
    pallas_call x2, Pallas kernels, scores_call(): pl.pallas_call(kernel, grid=(PAIRS,), in_specs=[tokens_spec] * 2 + [keys_...  4.97 us
    unnamed x10, local copies, waits for them, and re-layouts  4.16 us
    pallas_call x2, Pallas kernels, pack(): pl.pallas_call(kernel, in_specs=[pl.BlockSpec(memory_space=pl.ANY)] * 2,...  3.97 us
    pallas_call x1, Pallas kernels, halo_queries(): pl.pallas_call(halo_queries_kernel, grid=(GROUPS,), in_specs=[keys_wide]...  3.29 us
    pallas_call x1, Pallas kernels, mid_gradients(): pl.pallas_call(mid_kernel, grid=(GROUPS,), in_specs=ROW_SPECS + GRAD_SPEC...  3.01 us
  transfers between devices with their start and end apart: 10, of which 3 were waited for; matrix products, arithmetic and copies ran while one was open for 0% of the time, Pallas kernels for 17%

profile of v2, /device:TPU:1, one launch (start us, length us, event | category | flops | bytes accessed | tf_op | source)
XLA Modules:
  0.0 73.0 jit_solution(14779510981527132780)
XLA Ops:
  0.6 2.3 %pack_queries.1 = (bf16[2,256,512]{2,1,0:T(8,128)(2,1)}, bf16[2,256,512]{2,1,0:T(8,128)(2,1)}) custom-call(bf16[32,16,512]{2,1,0:T(8,128)(2,1)} %q_ref.1, bf16[32,16,512]{2,1,0:T(8,128)(2,1)} %g_ref.1), custom_call_target="tpu_custom_call" | custom-call | bytes 3145728 | tf_op jit(solution)/shard_map/pack_queries/pallas_call | solution.py:91
  3.0 3.8 %collective-permute-start = (bf16[2,256,512]{2,1,0:T(8,128)(2,1)}, bf16[2,256,512]{2,1,0:T(8,128)(2,1)S(1)}, u32[]{:S(2)}, u32[]{:S(2)}) collective-permute-start(bf16[2,256,512]{2,1,0:T(8,128)(2,1)} %get-tuple-element.31.side_a.refs_0_), channel_id=1, source_target_pairs={{0,1},{1,0},{2,3},{3,2},{4,5},{5,4},{6,7},{7,6},{8,9},{9,8},{10,11... | collective-permute-start | bytes 1572872 | tf_op jit(solution)/shard_map/ppermute | solution.py:428
  6.8 5.8 %collective-permute-start.1 = (bf16[2,256,512]{2,1,0:T(8,128)(2,1)}, bf16[2,256,512]{2,1,0:T(8,128)(2,1)S(1)}, u32[]{:S(2)}, u32[]{:S(2)}) collective-permute-start(bf16[2,256,512]{2,1,0:T(8,128)(2,1)} %get-tuple-element.32.side_b.refs_1_), channel_id=1, source_target_pairs={{1,2},{2,1},{3,4},{4,3},{5,6},{6,5},{7,8},{8,7},{9,10},{10,9},{11,... | collective-permute-start | bytes 1572872 | tf_op jit(solution)/shard_map/ppermute | solution.py:436
  12.6 1.0 %copy-done.3 = bf16[32,16,512]{2,1,0:T(8,128)(2,1)S(1)} copy-done((bf16[32,16,512]{2,1,0:T(8,128)(2,1)S(1)}, bf16[32,16,512]{2,1,0:T(8,128)(2,1)}, u32[]{:S(2)}) %copy-start.3) | copy-done | bytes 524312
  13.6 1.0 %copy-done.4 = bf16[32,16,512]{2,1,0:T(8,128)(2,1)S(1)} copy-done((bf16[32,16,512]{2,1,0:T(8,128)(2,1)S(1)}, bf16[32,16,512]{2,1,0:T(8,128)(2,1)}, u32[]{:S(2)}) %copy-start.4) | copy-done | bytes 524312
  14.7 1.6 %pack_keys.1 = (bf16[512,512]{1,0:T(8,128)(2,1)S(1)}, bf16[512,512]{1,0:T(8,128)(2,1)S(1)}, bf16[2,128,512]{2,1,0:T(8,128)(2,1)S(1)}, bf16[2,128,512]{2,1,0:T(8,128)(2,1)S(1)}) custom-call(bf16[32,16,512]{2,1,0:T(8,128)(2,1)S(1)} %copy-done.3, bf16[32,16,512]{2,1,0:T(8,128)(2,1)S(1)} %copy-done.4), custom_call_target="tpu_custom_call" | custom-call | bytes 3145728 | tf_op jit(solution)/shard_map/pack_keys/pallas_call | solution.py:91
  16.3 1.3 %collective-permute-start.2 = (bf16[2,128,512]{2,1,0:T(8,128)(2,1)S(1)}, bf16[2,128,512]{2,1,0:T(8,128)(2,1)S(1)}, u32[]{:S(2)}, u32[]{:S(2)}) collective-permute-start(bf16[2,128,512]{2,1,0:T(8,128)(2,1)S(1)} %get-tuple-element.34), channel_id=1, source_target_pairs={{0,32},{32,0},{64,96},{96,64},{1,33},{33,1},{65,97},{97,65},{2,34}... | collective-permute-start | bytes 786440 | tf_op jit(solution)/shard_map/ppermute | solution.py:428
  17.6 3.1 %collective-permute-start.3 = (bf16[2,128,512]{2,1,0:T(8,128)(2,1)S(1)}, bf16[2,128,512]{2,1,0:T(8,128)(2,1)S(1)}, u32[]{:S(2)}, u32[]{:S(2)}) collective-permute-start(bf16[2,128,512]{2,1,0:T(8,128)(2,1)S(1)} %get-tuple-element.35), channel_id=1, source_target_pairs={{32,64},{64,32},{33,65},{65,33},{34,66},{66,34},{35,67},{67,35},{3... | collective-permute-start | bytes 786440 | tf_op jit(solution)/shard_map/ppermute | solution.py:436
  20.7 0.0 copy-start
  20.7 1.0 %copy-done = bf16[2,256,512]{2,1,0:T(8,128)(2,1)S(1)} copy-done((bf16[2,256,512]{2,1,0:T(8,128)(2,1)S(1)}, bf16[2,256,512]{2,1,0:T(8,128)(2,1)}, u32[]{:S(2)}) %copy-start) | copy-done | bytes 524312
  21.7 1.0 %copy-done.1 = bf16[2,256,512]{2,1,0:T(8,128)(2,1)S(1)} copy-done((bf16[2,256,512]{2,1,0:T(8,128)(2,1)S(1)}, bf16[2,256,512]{2,1,0:T(8,128)(2,1)}, u32[]{:S(2)}) %copy-start.1) | copy-done | bytes 524312
  22.8 2.4 %mid_scores.1 = (f32[4,8,128]{2,1,0:T(8,128)S(1)}, f32[4,2,384,256]{3,2,1,0:T(8,128)S(1)}, f32[4,2,384,256]{3,2,1,0:T(8,128)S(1)}) custom-call(bf16[2,256,512]{2,1,0:T(8,128)(2,1)S(1)} %copy-done, bf16[2,256,512]{2,1,0:T(8,128)(2,1)S(1)} %copy-done.1, bf16[512,512]{1,0:T(8,128)(2,1)S(1)} %get-tuple-element.33.kd.refs_4_, ...), custom_call_target="tpu_custom_call" | custom-call | flops 2000000000 | bytes 3145728 | tf_op jit(solution)/shard_map/mid_scores/pallas_call | solution.py:218
  25.2 0.0 collective-permute-done.2.edge_a.refs_5_
  25.2 8.4 %collective-permute-done.3.edge_b.refs_6_ = bf16[2,128,512]{2,1,0:T(8,128)(2,1)S(1)} collective-permute-done((bf16[2,128,512]{2,1,0:T(8,128)(2,1)S(1)}, bf16[2,128,512]{2,1,0:T(8,128)(2,1)S(1)}, u32[]{:S(2)}, u32[]{:S(2)}) %collective-permute-start.3) | collective-permute-done | bytes 262176 | tf_op jit(solution)/shard_map/ppermute | solution.py:436
  33.6 2.5 %edge_scores.1 = (f32[4,8,128]{2,1,0:T(8,128)S(1)}, f32[4,2,384,256]{3,2,1,0:T(8,128)S(1)}, f32[4,2,384,256]{3,2,1,0:T(8,128)S(1)}) custom-call(bf16[2,256,512]{2,1,0:T(8,128)(2,1)S(1)} %copy-done, bf16[2,256,512]{2,1,0:T(8,128)(2,1)S(1)} %copy-done.1, bf16[512,512]{1,0:T(8,128)(2,1)S(1)} %get-tuple-element.33.kd.refs_4_, ...), custom_call_target="tpu_custom_call" | custom-call | flops 2000000000 | bytes 3145728 | tf_op jit(solution)/shard_map/edge_scores/pallas_call | solution.py:218
  36.2 0.0 collective-permute-done.q_a.refs_2_
  36.2 0.0 collective-permute-done.1.q_b.refs_3_
  36.2 2.2 %halo_scores.1 = (f32[4,16,128]{2,1,0:T(8,128)S(1)}, f32[4,16,128]{2,1,0:T(8,128)S(1)}, f32[2,2,2,192,256]{4,3,2,1,0:T(8,128)S(1)}, f32[2,2,2,192,256]{4,3,2,1,0...) custom-call(bf16[2,256,512]{2,1,0:T(8,128)(2,1)S(1)} %collective-permute-done.q_a.refs_2_, ...), custom_call_target="tpu_custom_call" | custom-call | flops 2000000000 | bytes 3145728 | tf_op jit(solution)/shard_map/halo_scores/pallas_call | solution.py:254
  38.4 1.6 %collective-permute-start.4 = (f32[4,16,128]{2,1,0:T(8,128)S(1)}, f32[4,16,128]{2,1,0:T(8,128)S(1)}, u32[]{:S(2)}, u32[]{:S(2)}) collective-permute-start(f32[4,16,128]{2,1,0:T(8,128)S(1)} %get-tuple-element.39.send_a.refs_7_), channel_id=1, source_target_pairs={{0,1},{1,0},{2,3},{3,2},{4,5},{5,4},{6,7},{7,6},{8,9},{9,8},{10,11... | collective-permute-start | bytes 98312 | tf_op jit(solution)/shard_map/ppermute | solution.py:428
  40.0 7.1 %collective-permute-start.5 = (f32[4,16,128]{2,1,0:T(8,128)S(1)}, f32[4,16,128]{2,1,0:T(8,128)S(1)}, u32[]{:S(2)}, u32[]{:S(2)}) collective-permute-start(f32[4,16,128]{2,1,0:T(8,128)S(1)} %get-tuple-element.40.send_b.refs_8_), channel_id=1, source_target_pairs={{1,2},{2,1},{3,4},{4,3},{5,6},{6,5},{7,8},{8,7},{9,10},{10,9},{11,... | collective-permute-start | bytes 98312 | tf_op jit(solution)/shard_map/ppermute | solution.py:436
  47.1 1.4 %collective-permute-done.5.recv_b.refs_10_ = f32[4,16,128]{2,1,0:T(8,128)S(1)} collective-permute-done((f32[4,16,128]{2,1,0:T(8,128)S(1)}, f32[4,16,128]{2,1,0:T(8,128)S(1)}, u32[]{:S(2)}, u32[]{:S(2)}) %collective-permute-start.5) | collective-permute-done | bytes 32800 | tf_op jit(solution)/shard_map/ppermute | solution.py:436
  48.5 3.3 %halo_queries.1 = (bf16[256,512]{1,0:T(8,128)(2,1)S(1)}, bf16[256,512]{1,0:T(8,128)(2,1)S(1)}) custom-call(bf16[512,512]{1,0:T(8,128)(2,1)S(1)} %get-tuple-element.33.kd.refs_4_, bf16[2,128,512]{2,1,0:T(8,128)(2,1)S(1)} %collective-permute-done.2.edge_a.refs_5_, bf16[2,128,512]{2,1,0:T(8,128)(2,1)S(1)} %collective-permute-done.3.edge_b.refs_6_, ...), custom_call_target="tpu_custom_call" | custom-call | flops 2000000000 | bytes 3145728 | tf_op jit(solution)/shard_map/halo_queries/pallas_call | solution.py:289
  51.8 0.1 collective-permute-start.6
  51.9 2.9 %edge_gradients.1 = (f32[2,256,512]{2,1,0:T(8,128)S(1)}, f32[512,512]{1,0:T(8,128)S(1)}, f32[512,512]{1,0:T(8,128)S(1)}, bf16[2,128,512]{2,1,0:T(8,128)(2,1)S(1)}, bf16[2,128,512]{2,1,0:T(8,128)(2,1)S(1)}) custom-call(bf16[2,256,512]{2,1,0:T(8,128)(2,1)S(1)} %copy-done, bf16[2,256,512]{2,1,0:T(8,128)(2,1)S(1)} %copy-done.2, ...), custom_call_target="tpu_custom_call" | custom-call | flops 3000000000 | bytes 1024 | tf_op jit(solution)/shard_map/edge_gradients/pallas_call | solution.py:366
  54.8 0.1 collective-permute-start.8
  54.9 4.6 %collective-permute-start.9 = (bf16[2,128,512]{2,1,0:T(8,128)(2,1)S(1)}, bf16[2,128,512]{2,1,0:T(8,128)(2,1)S(1)}, u32[]{:S(2)}, u32[]{:S(2)}) collective-permute-start(bf16[2,128,512]{2,1,0:T(8,128)(2,1)S(1)} %get-tuple-element.58), channel_id=1, source_target_pairs={{32,64},{64,32},{33,65},{65,33},{34,66},{66,34},{35,67},{67,35},{3... | collective-permute-start | bytes 786440 | tf_op jit(solution)/shard_map/ppermute | solution.py:436
  59.5 8.3 %collective-permute-start.7 = (bf16[256,512]{1,0:T(8,128)(2,1)S(1)}, bf16[256,512]{1,0:T(8,128)(2,1)S(1)}, u32[]{:S(2)}, u32[]{:S(2)}) collective-permute-start(bf16[256,512]{1,0:T(8,128)(2,1)S(1)} %get-tuple-element.56), channel_id=1, source_target_pairs={{1,2},{2,1},{3,4},{4,3},{5,6},{6,5},{7,8},{8,7},{9,10},{10,9},{11,... | collective-permute-start | bytes 786440 | tf_op jit(solution)/shard_map/ppermute | solution.py:436
  67.8 3.0 %mid_gradients.1 = (f32[2,256,512]{2,1,0:T(8,128)S(1)}, f32[512,512]{1,0:T(8,128)S(1)}, f32[512,512]{1,0:T(8,128)S(1)}) custom-call(bf16[2,256,512]{2,1,0:T(8,128)(2,1)S(1)} %copy-done, bf16[2,256,512]{2,1,0:T(8,128)(2,1)S(1)} %copy-done.2, bf16[2,256,512]{2,1,0:T(8,128)(2,1)S(1)} %collective-permute-done.q_a.refs_2_, ...), custom_call_target="tpu_custom_call" | custom-call | flops 3000000000 | bytes 1024 | tf_op jit(solution)/shard_map/mid_gradients/pallas_call | solution.py:379
  70.8 0.0 collective-permute-done.9.from_b
  70.8 0.8 %collective-permute-done.7.dq_b = bf16[256,512]{1,0:T(8,128)(2,1)S(1)} collective-permute-done((bf16[256,512]{1,0:T(8,128)(2,1)S(1)}, bf16[256,512]{1,0:T(8,128)(2,1)S(1)}, u32[]{:S(2)}, u32[]{:S(2)}) %collective-permute-start.7) | collective-permute-done | bytes 262176 | tf_op jit(solution)/shard_map/ppermute | solution.py:436
  71.6 0.0 collective-permute-done.6.dq_a
  71.6 1.3 %finish.1 = (bf16[32,16,512]{2,1,0:T(8,128)(2,1)}, bf16[32,16,512]{2,1,0:T(8,128)(2,1)}, bf16[32,16,512]{2,1,0:T(8,128)(2,1)}) custom-call(f32[2,256,512]{2,1,0:T(8,128)S(1)} %get-tuple-element.53.dq, f32[512,512]{1,0:T(8,128)S(1)} %get-tuple-element.54.dk, f32[512,512]{1,0:T(8,128)S(1)} %get-tuple-element.55.dv, ...), custom_call_target="tpu_custom_call" | custom-call | bytes 6291456 | tf_op jit(solution)/shard_map/finish/pallas_call | solution.py:416
  (7 shorter events, 0.0 us)
Async XLA Ops:
  3.0 33.2 %collective-permute-start = (bf16[2,256,512]{2,1,0:T(8,128)(2,1)}, bf16[2,256,512]{2,1,0:T(8,128)(2,1)S(1)}, u32[]{:S(2)}, u32[]{:S(2)}) collective-permute-start(bf16[2,256,512]{2,1,0:T(8,128)(2,1)} %get-tuple-element.31.side_a.refs_0_), channel_id=1, source_target_pairs={{0,1},{1,0},{2,3},{3,2},{4,5},{5,4},{6,7},{7,6},{8,9},{9,8},{10,11... | collective-permute-start | bytes 1572872 | tf_op jit(solution)/shard_map/ppermute | solution.py:428
  6.8 29.4 %collective-permute-start.1 = (bf16[2,256,512]{2,1,0:T(8,128)(2,1)}, bf16[2,256,512]{2,1,0:T(8,128)(2,1)S(1)}, u32[]{:S(2)}, u32[]{:S(2)}) collective-permute-start(bf16[2,256,512]{2,1,0:T(8,128)(2,1)} %get-tuple-element.32.side_b.refs_1_), channel_id=1, source_target_pairs={{1,2},{2,1},{3,4},{4,3},{5,6},{6,5},{7,8},{8,7},{9,10},{10,9},{11,... | collective-permute-start | bytes 1572872 | tf_op jit(solution)/shard_map/ppermute | solution.py:436
  12.6 1.0 %copy-start.3 = (bf16[32,16,512]{2,1,0:T(8,128)(2,1)S(1)}, bf16[32,16,512]{2,1,0:T(8,128)(2,1)}, u32[]{:S(2)}) copy-start(bf16[32,16,512]{2,1,0:T(8,128)(2,1)} %k_ref.1) | copy-start | bytes 1572868
  13.6 1.0 %copy-start.4 = (bf16[32,16,512]{2,1,0:T(8,128)(2,1)S(1)}, bf16[32,16,512]{2,1,0:T(8,128)(2,1)}, u32[]{:S(2)}) copy-start(bf16[32,16,512]{2,1,0:T(8,128)(2,1)} %v_ref.1) | copy-start | bytes 1572868
  16.3 8.9 %collective-permute-start.2 = (bf16[2,128,512]{2,1,0:T(8,128)(2,1)S(1)}, bf16[2,128,512]{2,1,0:T(8,128)(2,1)S(1)}, u32[]{:S(2)}, u32[]{:S(2)}) collective-permute-start(bf16[2,128,512]{2,1,0:T(8,128)(2,1)S(1)} %get-tuple-element.34), channel_id=1, source_target_pairs={{0,32},{32,0},{64,96},{96,64},{1,33},{33,1},{65,97},{97,65},{2,34}... | collective-permute-start | bytes 786440 | tf_op jit(solution)/shard_map/ppermute | solution.py:428
  17.6 16.1 %collective-permute-start.3 = (bf16[2,128,512]{2,1,0:T(8,128)(2,1)S(1)}, bf16[2,128,512]{2,1,0:T(8,128)(2,1)S(1)}, u32[]{:S(2)}, u32[]{:S(2)}) collective-permute-start(bf16[2,128,512]{2,1,0:T(8,128)(2,1)S(1)} %get-tuple-element.35), channel_id=1, source_target_pairs={{32,64},{64,32},{33,65},{65,33},{34,66},{66,34},{35,67},{67,35},{3... | collective-permute-start | bytes 786440 | tf_op jit(solution)/shard_map/ppermute | solution.py:436
  20.7 1.0 %copy-start = (bf16[2,256,512]{2,1,0:T(8,128)(2,1)S(1)}, bf16[2,256,512]{2,1,0:T(8,128)(2,1)}, u32[]{:S(2)}) copy-start(bf16[2,256,512]{2,1,0:T(8,128)(2,1)} %get-tuple-element.31.side_a.refs_0_) | copy-start | bytes 1572868
  21.7 1.0 %copy-start.1 = (bf16[2,256,512]{2,1,0:T(8,128)(2,1)S(1)}, bf16[2,256,512]{2,1,0:T(8,128)(2,1)}, u32[]{:S(2)}) copy-start(bf16[2,256,512]{2,1,0:T(8,128)(2,1)} %get-tuple-element.32.side_b.refs_1_) | copy-start | bytes 1572868
  38.4 8.7 %collective-permute-start.4 = (f32[4,16,128]{2,1,0:T(8,128)S(1)}, f32[4,16,128]{2,1,0:T(8,128)S(1)}, u32[]{:S(2)}, u32[]{:S(2)}) collective-permute-start(f32[4,16,128]{2,1,0:T(8,128)S(1)} %get-tuple-element.39.send_a.refs_7_), channel_id=1, source_target_pairs={{0,1},{1,0},{2,3},{3,2},{4,5},{5,4},{6,7},{7,6},{8,9},{9,8},{10,11... | collective-permute-start | bytes 98312 | tf_op jit(solution)/shard_map/ppermute | solution.py:428
  40.0 8.5 %collective-permute-start.5 = (f32[4,16,128]{2,1,0:T(8,128)S(1)}, f32[4,16,128]{2,1,0:T(8,128)S(1)}, u32[]{:S(2)}, u32[]{:S(2)}) collective-permute-start(f32[4,16,128]{2,1,0:T(8,128)S(1)} %get-tuple-element.40.send_b.refs_8_), channel_id=1, source_target_pairs={{1,2},{2,1},{3,4},{4,3},{5,6},{6,5},{7,8},{8,7},{9,10},{10,9},{11,... | collective-permute-start | bytes 98312 | tf_op jit(solution)/shard_map/ppermute | solution.py:436
  48.5 3.4 %copy-start.2 = (bf16[2,256,512]{2,1,0:T(8,128)(2,1)S(1)}, bf16[2,256,512]{2,1,0:T(8,128)(2,1)}, u32[]{:S(2)}) copy-start(bf16[2,256,512]{2,1,0:T(8,128)(2,1)} %get-tuple-element.32.side_b.refs_1_) | copy-start | bytes 1572868
  51.8 19.8 %collective-permute-start.6 = (bf16[256,512]{1,0:T(8,128)(2,1)S(1)}, bf16[256,512]{1,0:T(8,128)(2,1)S(1)}, u32[]{:S(2)}, u32[]{:S(2)}) collective-permute-start(bf16[256,512]{1,0:T(8,128)(2,1)S(1)} %get-tuple-element.49.refs_15_), channel_id=1, source_target_pairs={{0,1},{1,0},{2,3},{3,2},{4,5},{5,4},{6,7},{7,6},{8,9},{9,8},{10,11... | collective-permute-start | bytes 786440 | tf_op jit(solution)/shard_map/ppermute | solution.py:428
  54.8 16.0 %collective-permute-start.8 = (bf16[2,128,512]{2,1,0:T(8,128)(2,1)S(1)}, bf16[2,128,512]{2,1,0:T(8,128)(2,1)S(1)}, u32[]{:S(2)}, u32[]{:S(2)}) collective-permute-start(bf16[2,128,512]{2,1,0:T(8,128)(2,1)S(1)} %get-tuple-element.57), channel_id=1, source_target_pairs={{0,32},{32,0},{64,96},{96,64},{1,33},{33,1},{65,97},{97,65},{2,34}... | collective-permute-start | bytes 786440 | tf_op jit(solution)/shard_map/ppermute | solution.py:428
  54.9 15.9 %collective-permute-start.9 = (bf16[2,128,512]{2,1,0:T(8,128)(2,1)S(1)}, bf16[2,128,512]{2,1,0:T(8,128)(2,1)S(1)}, u32[]{:S(2)}, u32[]{:S(2)}) collective-permute-start(bf16[2,128,512]{2,1,0:T(8,128)(2,1)S(1)} %get-tuple-element.58), channel_id=1, source_target_pairs={{32,64},{64,32},{33,65},{65,33},{34,66},{66,34},{35,67},{67,35},{3... | collective-permute-start | bytes 786440 | tf_op jit(solution)/shard_map/ppermute | solution.py:436
  59.5 12.1 %collective-permute-start.7 = (bf16[256,512]{1,0:T(8,128)(2,1)S(1)}, bf16[256,512]{1,0:T(8,128)(2,1)S(1)}, u32[]{:S(2)}, u32[]{:S(2)}) collective-permute-start(bf16[256,512]{1,0:T(8,128)(2,1)S(1)} %get-tuple-element.56), channel_id=1, source_target_pairs={{1,2},{2,1},{3,4},{4,3},{5,6},{6,5},{7,8},{8,7},{9,10},{10,9},{11,... | collective-permute-start | bytes 786440 | tf_op jit(solution)/shard_map/ppermute | solution.py:436

commit v3 on v2

v3 whole, which is shorter than its diff:
```python
import functools

import jax
import jax.numpy as jnp
from jax import lax
from jax.experimental import pallas as pl
from jax.experimental.pallas import tpu as pltpu
from jax.sharding import PartitionSpec as P

ROWS = 4
CELLS = 64
CHUNK = 2 * CELLS
PAIR = 128
WIDE = 256
PAIRS = 4
GROUPS = 2
FEAT = 512
SCALE = 64 ** -0.5
LOG2E = 1.4426950408889634
MASKED = -1e30
F32 = jnp.float32
BF16 = jnp.bfloat16
VMEM_LIMIT = 20 * 1024 * 1024
PACK_LIMIT = 62 * 1024 * 1024
EDGE_ROWS = (0, 3)
MID_ROWS = (1, 2)


def matmul(a, b, contract):
    return lax.dot_general(a, b, ((contract[:1], contract[1:]), ((), ())), preferred_element_type=F32)


def params(limit=VMEM_LIMIT):
    return pltpu.CompilerParams(vmem_limit_bytes=limit)


def cost(flops, size):
    return pl.CostEstimate(flops=int(flops), bytes_accessed=int(size), transcendentals=0)


def struct(shape, dtype):
    return jax.ShapeDtypeStruct(shape, dtype)


def grid_row(t):
    return jnp.where(lax.axis_index("lat") % 2 == 0, ROWS - 1 - t, t)


def ordered(first, second):
    swap = lax.axis_index("lon") % 2 == 0
    return jnp.where(swap, second, first), jnp.where(swap, first, second)


def split_columns(block):
    wide = block.astype(F32)
    parts = ordered(*[wide[:, c * 8:(c + 1) * 8].reshape(CELLS, FEAT) for c in range(2)])
    return [part.astype(BF16) for part in parts]


def fetch(refs, rows, buffers, sems):
    copies = [[pltpu.make_async_copy(ref.at[pl.ds(8 * grid_row(t), 8)], buffers.at[i, place], sems.at[i, place])
               for place, t in enumerate(rows)] for i, ref in enumerate(refs)]
    for place in range(len(rows)):
        for copy in copies:
            copy[place].start()
    return copies


def pack_queries_kernel(rows, q_ref, g_ref, *refs):
    side_a, side_b, buffers, sems = refs[-4:]
    copies = fetch((q_ref, g_ref), rows, buffers, sems)
    for place in range(2):
        for i in range(2):
            copies[i][place].wait()
            side_a[i, at_tokens(place)], side_b[i, at_tokens(place)] = split_columns(buffers[i, place])


def pack_keys_kernel(rows, k_ref, v_ref, _, kd, vd, edge_a, edge_b, buffers, sems):
    copies = fetch((k_ref, v_ref), rows, buffers, sems)
    for t in rows:
        for i, out in enumerate((kd, vd)):
            copies[i][t].wait()
            tile = jnp.concatenate(split_columns(buffers[i, t]), axis=0)
            out[t * PAIR:(t + 1) * PAIR] = tile
            if t == 0:
                edge_a[i] = tile
            if t == ROWS - 1:
                edge_b[i] = tile


def pack(kernel, rows, operands, out_shape, name, limit):
    return pl.pallas_call(
        functools.partial(kernel, rows),
        in_specs=[pl.BlockSpec(memory_space=pl.ANY)] * len(operands),
        out_shape=out_shape,
        scratch_shapes=[pltpu.VMEM((2, len(rows), 8, 16, FEAT), BF16), pltpu.SemaphoreType.DMA((2, len(rows)))],
        compiler_params=params(limit),
        cost_estimate=cost(0, 0),
        name=name,
    )(*operands)


def head_masks(lanes):
    lane = lax.broadcasted_iota(jnp.int32, (1, lanes), 1)
    return [jnp.where((lane >= 64 * h) & (lane < 64 * (h + 1)), 1.0, 0.0).astype(F32).astype(BF16)
            for h in range(lanes // 64)]


def stacked(parts, masks):
    return jnp.concatenate([part * mask for part in parts for mask in masks], axis=0)


def key_rows(own, edges, which, t, lanes=slice(None)):
    rows = []
    for row in range(t, t + 3):
        if row == 0:
            rows.append(edges[0][which, :, lanes])
        elif row == ROWS + 1:
            rows.append(edges[1][which, :, lanes])
        else:
            rows.append(own[(row - 1) * PAIR:row * PAIR, lanes])
    return rows


def window(*where):
    return jnp.concatenate(key_rows(*where), axis=0)


def column_window(column, *where):
    return jnp.concatenate([row[column * CELLS:(column + 1) * CELLS] for row in key_rows(*where)], axis=0)


def score_block(keys, queries, t):
    scores = matmul(keys, queries, (1, 1)) * (SCALE * LOG2E)
    if t == ROWS - 1:
        lat = lax.axis_index("lat")
        outside = (lat == 0) | (lat == lax.axis_size("lat") - 1)
        cut = 2 * (keys.shape[0] // 3)
        bias = jnp.where(outside, MASKED, 0.0).astype(F32)
        scores = jnp.concatenate([scores[:cut], scores[cut:] + bias], axis=0)
    return scores


def row_stats(scores, dprobs):
    top = jnp.max(scores, axis=0, keepdims=True)
    weights = jnp.exp2(scores - top)
    total = jnp.sum(weights, axis=0, keepdims=True)
    delta = jnp.sum(weights * dprobs, axis=0, keepdims=True) / total
    return top + jnp.log(total) * LOG2E, delta


def merged(log_a, delta_a, log_b, delta_b):
    top = jnp.maximum(log_a, log_b)
    weight_a = jnp.exp2(log_a - top)
    weight_b = jnp.exp2(log_b - top)
    total = weight_a + weight_b
    return top + jnp.log(total) * LOG2E, (weight_a * delta_a + weight_b * delta_b) / total


def both_parts(mine, theirs, pair, base):
    other = 4 - base
    return merged(mine[pair, base:base + 2], mine[pair, base + 2:base + 4],
                  theirs[pair, other:other + 2], theirs[pair, other + 2:other + 4])


def turned_window(own_turned, edges_turned, t, j):
    at = slice(j * PAIR, (j + 1) * PAIR)
    rows = []
    for row in range(t, t + 3):
        if row in (0, ROWS + 1):
            rows.append(edges_turned[row // (ROWS + 1), at])
        else:
            rows.append(own_turned[at, (row - 1) * PAIR:row * PAIR])
    return jnp.concatenate(rows, axis=1)


def query_parts(keys_turned, dscores, lane):
    turned = matmul(keys_turned, dscores, (1, 0)) * SCALE
    parts = [turned[:, c * PAIR:(c + 1) * PAIR].T for c in range(2)]
    return [jnp.where(lane < 64, part[:CELLS], part[CELLS:]) for part in parts]


def at_tokens(place):
    return slice(place * CELLS, (place + 1) * CELLS)


def pair_lanes(j):
    return slice(j * PAIR, (j + 1) * PAIR)


tokens_spec = pl.BlockSpec((2, CHUNK, PAIR), lambda p: (0, 0, p))
keys_spec = pl.BlockSpec((ROWS * PAIR, PAIR), lambda p: (0, p))
edge_spec = pl.BlockSpec((2, PAIR, PAIR), lambda p: (0, 0, p))
stats_spec = pl.BlockSpec((1, 8, PAIR), lambda p: (p, 0, 0))
held_spec = pl.BlockSpec((1, 2, 3 * PAIR, WIDE), lambda p: (p, 0, 0, 0))
stats_shape = struct((PAIRS, 8, PAIR), F32)
held_shape = struct((PAIRS, 2, 3 * PAIR, WIDE), F32)

tokens_wide = pl.BlockSpec((2, CHUNK, WIDE), lambda g: (0, 0, g))
part_wide = pl.BlockSpec((CHUNK, WIDE), lambda g: (0, g))
keys_wide = pl.BlockSpec((ROWS * PAIR, WIDE), lambda g: (0, g))
edge_wide = pl.BlockSpec((2, PAIR, WIDE), lambda g: (0, 0, g))
turned_wide = pl.BlockSpec((WIDE, ROWS * PAIR), lambda g: (g, 0))
edge_turned_wide = pl.BlockSpec((2, WIDE, PAIR), lambda g: (0, g, 0))
stats_wide = pl.BlockSpec((2, 8, PAIR), lambda g: (g, 0, 0))
held_wide = pl.BlockSpec((2, 2, 3 * PAIR, WIDE), lambda g: (g, 0, 0, 0))
halo_wide = pl.BlockSpec((1, 2, 2, 3 * CELLS, WIDE), lambda g: (g, 0, 0, 0, 0))
halo_shape = struct((GROUPS, 2, 2, 3 * CELLS, WIDE), F32)
any_spec = pl.BlockSpec(memory_space=pl.ANY)


def own_scores(rows, side_a, side_b, kd, vd, edges, part, s_out, d_out):
    masks = head_masks(PAIR)
    for place, t in enumerate(rows):
        at = at_tokens(place)
        queries = stacked([side_a[0, at], side_b[0, at]], masks)
        grads = stacked([side_a[1, at], side_b[1, at]], masks)
        scores = score_block(window(kd, edges, 0, t), queries, t)
        dprobs = matmul(window(vd, edges, 1, t), grads, (1, 1))
        s_out[0, place] = scores
        d_out[0, place] = dprobs
        for w, values in enumerate(row_stats(scores, dprobs)):
            for c in range(2):
                index = 4 * c + 2 * w + place
                part[0, index:index + 1] = values[:, pair_lanes(c)]


def mid_scores_kernel(side_a, side_b, kd, vd, part, s_out, d_out, turned):
    own_scores(MID_ROWS, side_a, side_b, kd, vd, None, part, s_out, d_out)
    turned[...] = kd[...].T


def edge_scores_kernel(side_a, side_b, kd, vd, edge_a, edge_b, part, s_out, d_out, turned):
    own_scores(EDGE_ROWS, side_a, side_b, kd, vd, (edge_a, edge_b), part, s_out, d_out)
    turned[0] = edge_a[0].T
    turned[1] = edge_b[0].T


def scores_call(kernel, operands, turned_spec, turned_shape, name):
    return pl.pallas_call(
        kernel,
        grid=(PAIRS,),
        in_specs=[tokens_spec] * 2 + [keys_spec] * 2 + [edge_spec] * (len(operands) - 4),
        out_specs=[stats_spec] + [held_spec] * 2 + [turned_spec],
        out_shape=[stats_shape] + [held_shape] * 2 + [struct(turned_shape, BF16)],
        compiler_params=params(),
        cost_estimate=cost(0, 0),
        name=name,
    )(*operands)


def mid_scores(*operands):
    spec = pl.BlockSpec((PAIR, ROWS * PAIR), lambda p: (p, 0))
    return scores_call(mid_scores_kernel, operands, spec, (FEAT, ROWS * PAIR), "mid_scores")


def edge_scores(*operands):
    spec = pl.BlockSpec((2, PAIR, PAIR), lambda p: (0, p, 0))
    return scores_call(edge_scores_kernel, operands, spec, (2, FEAT, PAIR), "edge_scores")


def halo_scores_kernel(rows, *refs):
    q_a, q_b, kd, vd, part, _, *edges = refs[:-4]
    send_a, send_b, s_out, d_out = refs[-4:]
    masks = head_masks(WIDE)
    for c, (q_in, send) in enumerate(((q_a, send_a), (q_b, send_b))):
        for j in range(2):
            send[j, 0:4] = part[j, 4 * c:4 * c + 4]
        for place, t in enumerate(rows):
            at = at_tokens(place)
            queries = stacked([q_in[0, at]], masks)
            grads = stacked([q_in[1, at]], masks)
            scores = score_block(column_window(c, kd, edges, 0, t), queries, t)
            dprobs = matmul(column_window(c, vd, edges, 1, t), grads, (1, 1))
            s_out[0, place, c] = scores
            d_out[0, place, c] = dprobs
            for w, values in enumerate(row_stats(scores, dprobs)):
                index = 4 + 2 * w + place
                for j in range(2):
                    send[j, index:index + 1] = values[:, pair_lanes(j)]


def halo_scores(rows, halos, kd, vd, part, edges, before, name):
    return pl.pallas_call(
        functools.partial(halo_scores_kernel, rows),
        grid=(GROUPS,),
        in_specs=[tokens_wide] * 2 + [keys_wide] * 2 + [stats_wide, any_spec] + [edge_wide] * len(edges),
        out_specs=[stats_wide] * 2 + [halo_wide] * 2,
        out_shape=[stats_shape] * 2 + [halo_shape] * 2,
        compiler_params=params(),
        cost_estimate=cost(0, 0),
        name=name,
    )(*halos, kd, vd, part, before, *edges)


def halo_weights(mine, theirs, s_in, d_in, c):
    both = [both_parts(mine, theirs, j, 4) for j in range(2)]
    log_total = jnp.concatenate([one[0] for one in both], axis=1)
    delta = jnp.concatenate([one[1] for one in both], axis=1)
    weights = []
    for place in range(2):
        probs = jnp.exp2(s_in[0, place, c] - log_total[place:place + 1])
        dscores = probs * (d_in[0, place, c] - delta[place:place + 1])
        weights.append((probs.astype(BF16), dscores.astype(BF16)))
    return weights


def halo_queries_kernel(rows, *refs):
    send_a, send_b, recv_a, recv_b, s_in, d_in, own_turned, *edges_turned = refs[:-2]
    outs = refs[-2:]
    lane = lax.broadcasted_iota(jnp.int32, (1, PAIR), 1)
    weights = [halo_weights(mine, theirs, s_in, d_in, c)
               for c, (mine, theirs) in enumerate(((send_a, recv_a), (send_b, recv_b)))]
    none = jnp.zeros((CELLS, PAIR), BF16)
    for place, t in enumerate(rows):
        for j in range(2):
            pieces = []
            for i in range(3):
                part_a, part_b = [weights[c][place][1][at_tokens(i), pair_lanes(j)] for c in range(2)]
                pieces += [jnp.concatenate([part_a, none], axis=1), jnp.concatenate([none, part_b], axis=1)]
            keys_turned = turned_window(own_turned, edges_turned[0] if edges_turned else None, t, j)
            for out, part in zip(outs, query_parts(keys_turned, jnp.concatenate(pieces, axis=0), lane)):
                out[at_tokens(place), pair_lanes(j)] = part.astype(BF16)


def halo_queries(rows, stats, held, turned, name):
    return pl.pallas_call(
        functools.partial(halo_queries_kernel, rows),
        grid=(GROUPS,),
        in_specs=[stats_wide] * 4 + [halo_wide] * 2 + [turned_wide] + [edge_turned_wide] * (len(turned) - 1),
        out_specs=[part_wide] * 2,
        out_shape=[struct((CHUNK, FEAT), BF16)] * 2,
        compiler_params=params(),
        cost_estimate=cost(0, 0),
        name=name,
    )(*stats, *held, *turned)


def row_gradients(rows, side_a, side_b, q_a, q_b, send_a, send_b, recv_a, recv_b, s_own, d_own, s_halo, d_halo,
                  own_turned, edges_turned, dq_ref):
    masks, wide_masks = head_masks(PAIR), head_masks(WIDE)
    lane = lax.broadcasted_iota(jnp.int32, (1, PAIR), 1)
    sides = ((q_a, send_a, recv_a), (q_b, send_b, recv_b))
    halo = [halo_weights(mine, theirs, s_halo, d_halo, c) for c, (_, mine, theirs) in enumerate(sides)]
    merged_rows = []
    for j in range(2):
        both = [both_parts(mine, theirs, j, 0) for _, mine, theirs in sides]
        merged_rows.append([jnp.concatenate([one[w] for one in both], axis=1) for w in range(2)])
    results = []
    for place, t in enumerate(rows):
        at, row = at_tokens(place), slice(place, place + 1)
        sums = [[], []]
        for j in range(2):
            lanes = pair_lanes(j)
            queries = stacked([side_a[0, at, lanes], side_b[0, at, lanes]], masks)
            grads = stacked([side_a[1, at, lanes], side_b[1, at, lanes]], masks)
            log_total, delta = merged_rows[j]
            probs = jnp.exp2(s_own[j, place] - log_total[row])
            dscores = (probs * (d_own[j, place] - delta[row])).astype(BF16)
            for c, part in enumerate(query_parts(turned_window(own_turned, edges_turned, t, j), dscores, lane)):
                dq_ref[c, at, lanes] = part
            sums[0].append(matmul(dscores, queries, (1, 0)))
            sums[1].append(matmul(probs.astype(BF16), grads, (1, 0)))
        sums = [jnp.concatenate(parts, axis=1) for parts in sums]
        edge_parts = []
        for c in range(2):
            probs, dscores = halo[c][place]
            edge_parts.append((matmul(dscores, stacked([sides[c][0][0, at]], wide_masks), (1, 0)),
                               matmul(probs, stacked([sides[c][0][1, at]], wide_masks), (1, 0))))
        results.append([jnp.concatenate([sums[w][at_tokens(2 * i + c)] + edge_parts[c][w][at_tokens(i)]
                                         for i in range(3) for c in range(2)], axis=0) for w in range(2)])
    return results


def edge_kernel(*refs):
    operands, (_, dq_ref, dk_ref, dv_ref, out_a, out_b) = refs[:14], refs[14:]
    upper, lower = row_gradients(EDGE_ROWS, *operands, dq_ref)
    for which, (out, scale) in enumerate(((dk_ref, SCALE), (dv_ref, 1.0))):
        top, bottom = upper[which] * scale, lower[which] * scale
        out_a[which] = top[:PAIR].astype(BF16)
        out[0:2 * PAIR] = top[PAIR:]
        out_b[which] = bottom[2 * PAIR:].astype(BF16)
        out[2 * PAIR:] = bottom[:2 * PAIR]


def mid_kernel(*refs):
    operands, (_, dk_in, dv_in, dq_ref, dk_ref, dv_ref) = refs[:13], refs[13:]
    upper, lower = row_gradients(MID_ROWS, *operands, None, dq_ref)
    for which, (sums, out, scale) in enumerate(((dk_in, dk_ref, SCALE), (dv_in, dv_ref, 1.0))):
        out[0:PAIR] = sums[0:PAIR] + upper[which][:PAIR] * scale
        out[PAIR:3 * PAIR] = sums[PAIR:3 * PAIR] + (upper[which][PAIR:] + lower[which][:2 * PAIR]) * scale
        out[3 * PAIR:] = sums[3 * PAIR:] + lower[which][2 * PAIR:] * scale


ROW_SPECS = [tokens_wide] * 4 + [stats_wide] * 4 + [held_wide] * 2 + [halo_wide] * 2 + [turned_wide]
GRAD_SPECS = [tokens_wide] + [keys_wide] * 2
GRAD_SHAPES = [struct((2, CHUNK, FEAT), F32)] + [struct((ROWS * PAIR, FEAT), F32)] * 2


def edge_gradients(*operands):
    return pl.pallas_call(
        edge_kernel,
        grid=(GROUPS,),
        in_specs=ROW_SPECS + [edge_turned_wide, any_spec],
        out_specs=GRAD_SPECS + [edge_wide] * 2,
        out_shape=GRAD_SHAPES + [struct((2, PAIR, FEAT), BF16)] * 2,
        compiler_params=params(),
        cost_estimate=cost(0, 0),
        name="edge_gradients",
    )(*operands)


def mid_gradients(*operands):
    return pl.pallas_call(
        mid_kernel,
        grid=(GROUPS,),
        in_specs=ROW_SPECS + [any_spec] + [keys_wide] * 2,
        out_specs=GRAD_SPECS,
        out_shape=GRAD_SHAPES,
        compiler_params=params(),
        cost_estimate=cost(0, 0),
        name="mid_gradients",
    )(*operands)


def join_columns(side_a, side_b):
    parts = ordered(side_a, side_b)
    return jnp.concatenate([part.reshape(8, 8, FEAT) for part in parts], axis=1).astype(BF16)


def finish_kernel(dq_edge, dq_mid, dk, dv, edge_dq_a, edge_dq_b, mid_dq_a, mid_dq_b, from_a, from_b,
                  q_ref, k_ref, v_ref, buffers, sems):
    copies = []

    def send(i, t, value):
        buffers[i, t] = value
        out = (q_ref, k_ref, v_ref)[i]
        copies.append(pltpu.make_async_copy(buffers.at[i, t], out.at[pl.ds(8 * grid_row(t), 8)], sems.at[i, t]))
        copies[-1].start()

    for t in range(ROWS):
        for which, own in enumerate((dk, dv)):
            full = own[t * PAIR:(t + 1) * PAIR]
            if t == 0:
                full = full + from_a[which].astype(F32)
            if t == ROWS - 1:
                full = full + from_b[which].astype(F32)
            send(1 + which, t, join_columns(full[:CELLS], full[CELLS:]))
    for rows, dq, side_a, side_b in ((EDGE_ROWS, dq_edge, edge_dq_a, edge_dq_b), (MID_ROWS, dq_mid, mid_dq_a, mid_dq_b)):
        for place, t in enumerate(rows):
            at = at_tokens(place)
            send(0, t, join_columns(dq[0, at] + side_a[at].astype(F32), dq[1, at] + side_b[at].astype(F32)))
    for copy in copies:
        copy.wait()


def finish(*operands):
    return pl.pallas_call(
        finish_kernel,
        out_specs=[any_spec] * 3,
        out_shape=[struct((8 * ROWS, 16, FEAT), BF16)] * 3,
        scratch_shapes=[pltpu.VMEM((3, ROWS, 8, 16, FEAT), BF16), pltpu.SemaphoreType.DMA((3, ROWS))],
        compiler_params=params(),
        cost_estimate=cost(0, 0),
        name="finish",
    )(*operands)


def swap_a(x, axis):
    return lax.ppermute(x, axis, [(i, i ^ 1) for i in range(lax.axis_size(axis))])


def swap_b(x, axis, wrap):
    count = lax.axis_size(axis)
    pairs = []
    for i in range(1, count if wrap else count - 1, 2):
        pairs += [(i, (i + 1) % count), ((i + 1) % count, i)]
    return lax.ppermute(x, axis, pairs)


def over_lon(side_a, side_b):
    from_b = swap_b(side_b, "lon", True)
    return swap_a(side_a, "lon"), from_b


def over_lat(side_a, side_b):
    from_b = swap_b(side_b, "lat", False)
    return swap_a(side_a, "lat"), from_b


def on_device(query_vectors, key_vectors, value_vectors, output_grads):
    tokens = struct((2, CHUNK, FEAT), BF16)
    tiles = struct((ROWS * PAIR, FEAT), BF16)
    edge = struct((2, PAIR, FEAT), BF16)
    sides = pack(pack_queries_kernel, EDGE_ROWS, (query_vectors, output_grads), [tokens] * 2, "pack_edge", PACK_LIMIT)
    kd, vd, own_edge_a, own_edge_b = pack(pack_keys_kernel, range(ROWS), (key_vectors, value_vectors, sides[0]),
                                          [tiles] * 2 + [edge] * 2, "pack_keys", VMEM_LIMIT)
    mid_sides = pack(pack_queries_kernel, MID_ROWS, (query_vectors, output_grads, own_edge_a),
                     [tokens] * 2, "pack_mid", VMEM_LIMIT)
    halos = over_lon(*sides)
    edges = over_lat(own_edge_a, own_edge_b)
    mid_halos = over_lon(*mid_sides)

    mid_part, *mid_own, turned = mid_scores(*mid_sides, kd, vd)
    part, *own, edges_turned = edge_scores(*sides, kd, vd, *edges)
    send_a, send_b, *held = halo_scores(EDGE_ROWS, halos, kd, vd, part, edges, mid_part, "edge_halo_scores")
    stats = (send_a, send_b, *over_lon(send_a, send_b))
    halo_dq = halo_queries(EDGE_ROWS, stats, held, (turned, edges_turned), "edge_halo_queries")
    dq_parts = over_lon(*halo_dq)
    dq, dk, dv, out_a, out_b = edge_gradients(*sides, *halos, *stats, *own, *held, turned, edges_turned, halo_dq[0])
    key_parts = over_lat(out_a, out_b)

    send_a, send_b, *held = halo_scores(MID_ROWS, mid_halos, kd, vd, mid_part, (), out_a, "mid_halo_scores")
    stats = (send_a, send_b, *over_lon(send_a, send_b))
    halo_dq = halo_queries(MID_ROWS, stats, held, (turned,), "mid_halo_queries")
    mid_dq_parts = over_lon(*halo_dq)
    mid_dq, dk, dv = mid_gradients(*mid_sides, *mid_halos, *stats, *mid_own, *held, turned, halo_dq[0], dk, dv)
    return tuple(finish(dq, mid_dq, dk, dv, *dq_parts, *mid_dq_parts, *key_parts))


def solution(mesh):
    spec = P("lat", "lon", None)
    return jax.shard_map(on_device, mesh=mesh, in_specs=(spec,) * 4, out_specs=(spec,) * 3, check_vma=False)
```

time: 73.3 us -> 83.2 us (1.14)
  starting transfers between devices: 35.7 us -> 50.9 us
  waiting for transfers between devices: 10.7 us -> 5.15 us
    ppermute x5 -> x8, starting transfers between devices: 28.8 us -> 40.7 us  [swap_b(): return lax.ppermute(x, axis, pairs)]
    ppermute x5 -> x8, waiting for transfers between devices: 10.7 us -> 2.15 us  [swap_b(): return lax.ppermute(x, axis, pairs)]
    ppermute x5 -> x8, starting transfers between devices: 6.91 us -> 10.2 us  [swap_a(): lax.ppermute(x, axis, [(i, i ^ 1) for i in range(lax.axis_size(axis))])]
    ppermute x5 -> x8, waiting for transfers between devices: 0.01 us -> 3 us  [swap_a(): lax.ppermute(x, axis, [(i, i ^ 1) for i in range(lax.axis_size(axis))])]
    pallas_call x7 -> x10, Pallas kernels: 16.7 us -> 15.9 us  [the longest x3 4.36 us: pack(): pl.pallas_call(functools.partial(kernel, rows), in_specs=[pl.BlockSpec(me...]
  transfers between devices with their start and end apart: 10 -> 16, of which waited for: 3 -> 3; matrix products, arithmetic and copies ran while one was open for 0% -> 0% of each run, Pallas kernels for 17% -> 20%
where the time goes in v3:
time: 83.2 us; the launch traced here: 82.8 us
  starting transfers between devices  50.9 us (61%)
  Pallas kernels  21.6 us (26%)
  waiting for transfers between devices  5.15 us (6%)
  local copies, waits for them, and re-layouts  4.21 us (5%)
  between operations  0.86 us (1%)
    ppermute x8, starting transfers between devices, swap_b(): return lax.ppermute(x, axis, pairs)  40.7 us
    ppermute x8, starting transfers between devices, swap_a(): lax.ppermute(x, axis, [(i, i ^ 1) for i in range(lax.axis_size(axis))])  10.2 us
    pallas_call x2, Pallas kernels, scores_call(): pl.pallas_call(kernel, grid=(PAIRS,), in_specs=[tokens_spec] * 2 + [keys_...  5.71 us
    pallas_call x3, Pallas kernels, pack(): pl.pallas_call(functools.partial(kernel, rows), in_specs=[pl.BlockSpec(me...  4.36 us
    unnamed x10, local copies, waits for them, and re-layouts  4.21 us
    pallas_call x1, Pallas kernels, edge_gradients(): pl.pallas_call(edge_kernel, grid=(GROUPS,), in_specs=ROW_SPECS + [edge_tu...  3.23 us
    ppermute x8, waiting for transfers between devices, swap_a(): lax.ppermute(x, axis, [(i, i ^ 1) for i in range(lax.axis_size(axis))])  3 us
    pallas_call x2, Pallas kernels, halo_scores(): pl.pallas_call(functools.partial(halo_scores_kernel, rows), grid=(GROUPS,...  2.73 us
  transfers between devices with their start and end apart: 16, of which 3 were waited for; matrix products, arithmetic and copies ran while one was open for 0% of the time, Pallas kernels for 20%

profile of v3, /device:TPU:1, one launch (start us, length us, event | category | flops | bytes accessed | tf_op | source)
XLA Modules:
  0.0 82.8 jit_solution(9575806627324554026)
XLA Ops:
  0.6 1.9 %pack_edge.1 = (bf16[2,128,512]{2,1,0:T(8,128)(2,1)}, bf16[2,128,512]{2,1,0:T(8,128)(2,1)}) custom-call(bf16[32,16,512]{2,1,0:T(8,128)(2,1)} %q_ref.3, bf16[32,16,512]{2,1,0:T(8,128)(2,1)} %g_ref.3), custom_call_target="tpu_custom_call" | custom-call | tf_op jit(solution)/shard_map/pack_edge/pallas_call | solution.py:92
  2.6 1.1 %copy-done.3 = bf16[32,16,512]{2,1,0:T(8,128)(2,1)S(1)} copy-done((bf16[32,16,512]{2,1,0:T(8,128)(2,1)S(1)}, bf16[32,16,512]{2,1,0:T(8,128)(2,1)}, u32[]{:S(2)}) %copy-start.3) | copy-done | bytes 524312
  3.7 1.0 %copy-done.4 = bf16[32,16,512]{2,1,0:T(8,128)(2,1)S(1)} copy-done((bf16[32,16,512]{2,1,0:T(8,128)(2,1)S(1)}, bf16[32,16,512]{2,1,0:T(8,128)(2,1)}, u32[]{:S(2)}) %copy-start.4) | copy-done | bytes 524312
  4.7 1.6 %pack_keys.1 = (bf16[512,512]{1,0:T(8,128)(2,1)S(1)}, bf16[512,512]{1,0:T(8,128)(2,1)S(1)}, bf16[2,128,512]{2,1,0:T(8,128)(2,1)S(1)}, bf16[2,128,512]{2,1,0:T(8,128)(2,1)S(1)}) custom-call(bf16[32,16,512]{2,1,0:T(8,128)(2,1)S(1)} %copy-done.3, bf16[32,16,512]{2,1,0:T(8,128)(2,1)S(1)} %copy-done.4, bf16[2,128,512]{2,1,0:T(8,128)(2,1)} %get-tuple-element.39._.side_a.refs_0_), custom_call_target="tpu_custom_call" | custom-call | tf_op jit(solution)/shard_map/pack_keys/pallas_call | solution.py:92
  6.4 1.5 %collective-permute-start.2 = (bf16[2,128,512]{2,1,0:T(8,128)(2,1)S(1)}, bf16[2,128,512]{2,1,0:T(8,128)(2,1)S(1)}, u32[]{:S(2)}, u32[]{:S(2)}) collective-permute-start(bf16[2,128,512]{2,1,0:T(8,128)(2,1)S(1)} %get-tuple-element.43.refs_0_), channel_id=1, source_target_pairs={{0,32},{32,0},{64,96},{96,64},{1,33},{33,1},{65,97},{97,65},{2,34}... | collective-permute-start | bytes 786440 | tf_op jit(solution)/shard_map/ppermute | solution.py:470
  7.9 3.2 %collective-permute-start.3 = (bf16[2,128,512]{2,1,0:T(8,128)(2,1)S(1)}, bf16[2,128,512]{2,1,0:T(8,128)(2,1)S(1)}, u32[]{:S(2)}, u32[]{:S(2)}) collective-permute-start(bf16[2,128,512]{2,1,0:T(8,128)(2,1)S(1)} %get-tuple-element.44), channel_id=1, source_target_pairs={{32,64},{64,32},{33,65},{65,33},{34,66},{66,34},{35,67},{67,35},{3... | collective-permute-start | bytes 786440 | tf_op jit(solution)/shard_map/ppermute | solution.py:478
  11.1 2.7 %collective-permute-start = (bf16[2,128,512]{2,1,0:T(8,128)(2,1)}, bf16[2,128,512]{2,1,0:T(8,128)(2,1)S(1)}, u32[]{:S(2)}, u32[]{:S(2)}) collective-permute-start(bf16[2,128,512]{2,1,0:T(8,128)(2,1)} %get-tuple-element.39._.side_a.refs_0_), channel_id=1, source_target_pairs={{0,1},{1,0},{2,3},{3,2},{4,5},{5,4},{6,7},{7,6},{8,9},{9,8},{10,11... | collective-permute-start | bytes 786440 | tf_op jit(solution)/shard_map/ppermute | solution.py:470
  13.8 6.0 %collective-permute-start.1 = (bf16[2,128,512]{2,1,0:T(8,128)(2,1)}, bf16[2,128,512]{2,1,0:T(8,128)(2,1)S(1)}, u32[]{:S(2)}, u32[]{:S(2)}) collective-permute-start(bf16[2,128,512]{2,1,0:T(8,128)(2,1)} %get-tuple-element.40.side_b.refs_1_), channel_id=1, source_target_pairs={{1,2},{2,1},{3,4},{4,3},{5,6},{6,5},{7,8},{8,7},{9,10},{10,9},{11,... | collective-permute-start | bytes 786440 | tf_op jit(solution)/shard_map/ppermute | solution.py:478
  19.8 1.0 %copy-done = bf16[32,16,512]{2,1,0:T(8,128)(2,1)S(1)} copy-done((bf16[32,16,512]{2,1,0:T(8,128)(2,1)S(1)}, bf16[32,16,512]{2,1,0:T(8,128)(2,1)}, u32[]{:S(2)}) %copy-start) | copy-done | bytes 524312
  20.8 1.0 %copy-done.1 = bf16[32,16,512]{2,1,0:T(8,128)(2,1)S(1)} copy-done((bf16[32,16,512]{2,1,0:T(8,128)(2,1)S(1)}, bf16[32,16,512]{2,1,0:T(8,128)(2,1)}, u32[]{:S(2)}) %copy-start.1) | copy-done | bytes 524312
  21.9 0.8 pack_mid.1
  22.8 3.2 %collective-permute-start.7 = (bf16[2,128,512]{2,1,0:T(8,128)(2,1)S(1)}, bf16[2,128,512]{2,1,0:T(8,128)(2,1)S(1)}, u32[]{:S(2)}, u32[]{:S(2)}) collective-permute-start(bf16[2,128,512]{2,1,0:T(8,128)(2,1)S(1)} %get-tuple-element.47.side_b.refs_1_), channel_id=1, source_target_pairs={{1,2},{2,1},{3,4},{4,3},{5,6},{6,5},{7,8},{8,7},{9,10},{10,9},{11,... | collective-permute-start | bytes 786440 | tf_op jit(solution)/shard_map/ppermute | solution.py:478
  26.0 2.4 %mid_scores.1 = (f32[4,8,128]{2,1,0:T(8,128)S(1)}, f32[4,2,384,256]{3,2,1,0:T(8,128)S(1)}, f32[4,2,384,256]{3,2,1,0:T(8,128)S(1)}, bf16[512,512]{1,0:T(8,128)(2,1)S(1)}) custom-call(bf16[2,128,512]{2,1,0:T(8,128)(2,1)S(1)} %get-tuple-element.46.side_a.refs_0_, bf16[2,128,512]{2,1,0:T(8,128)(2,1)S(1)} %get-tuple-element.47.side_b.refs_1_, ...), custom_call_target="tpu_custom_call" | custom-call | tf_op jit(solution)/shard_map/mid_scores/pallas_call | solution.py:240
  28.4 3.3 %edge_scores.1 = (f32[4,8,128]{2,1,0:T(8,128)S(1)}, f32[4,2,384,256]{3,2,1,0:T(8,128)S(1)}, f32[4,2,384,256]{3,2,1,0:T(8,128)S(1)}, bf16[2,512,128]{2,1,0:T(8,128)(2,1)S(1)}) custom-call(bf16[2,128,512]{2,1,0:T(8,128)(2,1)} %get-tuple-element.39._.side_a.refs_0_, bf16[2,128,512]{2,1,0:T(8,128)(2,1)S(1)} %copy-done.2, ...), custom_call_target="tpu_custom_call" | custom-call | tf_op jit(solution)/shard_map/edge_scores/pallas_call | solution.py:240
  31.7 3.0 %collective-permute-done.refs_0_.refs_2_ = bf16[2,128,512]{2,1,0:T(8,128)(2,1)S(1)} collective-permute-done((bf16[2,128,512]{2,1,0:T(8,128)(2,1)}, bf16[2,128,512]{2,1,0:T(8,128)(2,1)S(1)}, u32[]{:S(2)}, u32[]{:S(2)}) %collective-permute-start) | collective-permute-done | bytes 262176 | tf_op jit(solution)/shard_map/ppermute | solution.py:470
  34.7 1.4 %edge_halo_scores.1 = (f32[4,8,128]{2,1,0:T(8,128)S(1)}, f32[4,8,128]{2,1,0:T(8,128)S(1)}, f32[2,2,2,192,256]{4,3,2,1,0:T(8,128)S(1)}, f32[2,2,2,192,256]{4,3,2,1,0:T(8,128)S(1)}) custom-call(bf16[2,128,512]{2,1,0:T(8,128)(2,1)S(1)} %collective-permute-done.refs_0_.refs_2_, bf16[2,128,512]{2,1,0:T(8,128)(2,1)S(1)} %collective-permute-done.1.refs_1_.refs_3_, ...), custom_call_target="tpu_custom_call" | custom-call | tf_op jit(solution)/shard_map/edge_halo_scores/pallas_call | solution.py:284
  36.1 1.8 %collective-permute-start.4 = (f32[4,8,128]{2,1,0:T(8,128)S(1)}, f32[4,8,128]{2,1,0:T(8,128)S(1)}, u32[]{:S(2)}, u32[]{:S(2)}) collective-permute-start(f32[4,8,128]{2,1,0:T(8,128)S(1)} %get-tuple-element.49.refs_0_.refs_4_), channel_id=1, source_target_pairs={{0,1},{1,0},{2,3},{3,2},{4,5},{5,4},{6,7},{7,6},{8,9},{9,8},{10,11... | collective-permute-start | bytes 49160 | tf_op jit(solution)/shard_map/ppermute | solution.py:470
  37.9 8.0 %collective-permute-start.5 = (f32[4,8,128]{2,1,0:T(8,128)S(1)}, f32[4,8,128]{2,1,0:T(8,128)S(1)}, u32[]{:S(2)}, u32[]{:S(2)}) collective-permute-start(f32[4,8,128]{2,1,0:T(8,128)S(1)} %get-tuple-element.50.refs_1_.refs_5_), channel_id=1, source_target_pairs={{1,2},{2,1},{3,4},{4,3},{5,6},{6,5},{7,8},{8,7},{9,10},{10,9},{11,... | collective-permute-start | bytes 49160 | tf_op jit(solution)/shard_map/ppermute | solution.py:478
  45.9 1.1 %collective-permute-done.5.refs_3_.refs_7_ = f32[4,8,128]{2,1,0:T(8,128)S(1)} collective-permute-done((f32[4,8,128]{2,1,0:T(8,128)S(1)}, f32[4,8,128]{2,1,0:T(8,128)S(1)}, u32[]{:S(2)}, u32[]{:S(2)}) %collective-permute-start.5) | collective-permute-done | bytes 16416 | tf_op jit(solution)/shard_map/ppermute | solution.py:478
  47.0 0.9 %edge_halo_queries.1 = (bf16[128,512]{1,0:T(8,128)(2,1)S(1)}, bf16[128,512]{1,0:T(8,128)(2,1)S(1)}) custom-call(f32[4,8,128]{2,1,0:T(8,128)S(1)} %get-tuple-element.49.refs_0_.refs_4_, f32[4,8,128]{2,1,0:T(8,128)S(1)} %get-tuple-element.50.refs_1_.refs_5_, f32[4,8,128]{2,1,0:T(8,128)S(1)} %collective-permute-done.4.refs_2_.refs_6_, ...), custom_call_target="tpu_custom_call" | custom-call | tf_op jit(solution)/shard_map/edge_halo_queries/pallas_call | solution.py:327
  48.1 3.2 %edge_gradients.1 = (f32[2,128,512]{2,1,0:T(8,128)S(1)}, f32[512,512]{1,0:T(8,128)S(1)}, f32[512,512]{1,0:T(8,128)S(1)}, bf16[2,128,512]{2,1,0:T(8,128)(2,1)S(1)}, bf16[2,128,512]{2,1,0:T(8,128)(2,1)S(1)}) custom-call(bf16[2,128,512]{2,1,0:T(8,128)(2,1)} %get-tuple-element.39._.side_a.refs_0_, bf16[2,128,512]{2,1,0:T(8,128)(2,1)S(1)} %copy-done.2, ...), custom_call_target="tpu_custom_call" | custom-call | tf_op jit(solution)/shard_map/edge_gradients/pallas_call | solution.py:401
  51.3 0.1 collective-permute-start.14
  51.4 4.6 %collective-permute-start.15 = (bf16[2,128,512]{2,1,0:T(8,128)(2,1)S(1)}, bf16[2,128,512]{2,1,0:T(8,128)(2,1)S(1)}, u32[]{:S(2)}, u32[]{:S(2)}) collective-permute-start(bf16[2,128,512]{2,1,0:T(8,128)(2,1)S(1)} %get-tuple-element.74), channel_id=1, source_target_pairs={{32,64},{64,32},{33,65},{65,33},{34,66},{66,34},{35,67},{67,35},{3... | collective-permute-start | bytes 786440 | tf_op jit(solution)/shard_map/ppermute | solution.py:478
  56.1 1.3 %mid_halo_scores.1 = (f32[4,8,128]{2,1,0:T(8,128)S(1)}, f32[4,8,128]{2,1,0:T(8,128)S(1)}, f32[2,2,2,192,256]{4,3,2,1,0:T(8,128)S(1)}, f32[2,2,2,192,256]{4,3,2,1,0:T(8,128)S(1)}) custom-call(bf16[2,128,512]{2,1,0:T(8,128)(2,1)S(1)} %collective-permute-done.6.refs_0_.refs_2_, bf16[2,128,512]{2,1,0:T(8,128)(2,1)S(1)} %collective-permute-done.7.refs_1_.refs_3_, ...), custom_call_target="tpu_custom_call" | custom-call | tf_op jit(solution)/shard_map/mid_halo_scores/pallas_call | solution.py:284
  57.4 3.9 %collective-permute-start.8 = (f32[4,8,128]{2,1,0:T(8,128)S(1)}, f32[4,8,128]{2,1,0:T(8,128)S(1)}, u32[]{:S(2)}, u32[]{:S(2)}) collective-permute-start(f32[4,8,128]{2,1,0:T(8,128)S(1)} %get-tuple-element.60.refs_0_.refs_4_), channel_id=1, source_target_pairs={{0,1},{1,0},{2,3},{3,2},{4,5},{5,4},{6,7},{7,6},{8,9},{9,8},{10,11... | collective-permute-start | bytes 49160 | tf_op jit(solution)/shard_map/ppermute | solution.py:470
  61.3 6.9 %collective-permute-start.9 = (f32[4,8,128]{2,1,0:T(8,128)S(1)}, f32[4,8,128]{2,1,0:T(8,128)S(1)}, u32[]{:S(2)}, u32[]{:S(2)}) collective-permute-start(f32[4,8,128]{2,1,0:T(8,128)S(1)} %get-tuple-element.61.refs_1_.refs_5_), channel_id=1, source_target_pairs={{1,2},{2,1},{3,4},{4,3},{5,6},{6,5},{7,8},{8,7},{9,10},{10,9},{11,... | collective-permute-start | bytes 49160 | tf_op jit(solution)/shard_map/ppermute | solution.py:478
  68.2 2.6 %collective-permute-start.11 = (bf16[128,512]{1,0:T(8,128)(2,1)S(1)}, bf16[128,512]{1,0:T(8,128)(2,1)S(1)}, u32[]{:S(2)}, u32[]{:S(2)}) collective-permute-start(bf16[128,512]{1,0:T(8,128)(2,1)S(1)} %get-tuple-element.72), channel_id=1, source_target_pairs={{1,2},{2,1},{3,4},{4,3},{5,6},{6,5},{7,8},{8,7},{9,10},{10,9},{11,... | collective-permute-start | bytes 393224 | tf_op jit(solution)/shard_map/ppermute | solution.py:478
  70.8 0.9 %mid_halo_queries.1 = (bf16[128,512]{1,0:T(8,128)(2,1)S(1)}, bf16[128,512]{1,0:T(8,128)(2,1)S(1)}) custom-call(f32[4,8,128]{2,1,0:T(8,128)S(1)} %get-tuple-element.60.refs_0_.refs_4_, f32[4,8,128]{2,1,0:T(8,128)S(1)} %get-tuple-element.61.refs_1_.refs_5_, f32[4,8,128]{2,1,0:T(8,128)S(1)} %collective-permute-done.8.refs_2_.refs_6_, ...), custom_call_target="tpu_custom_call" | custom-call | tf_op jit(solution)/shard_map/mid_halo_queries/pallas_call | solution.py:327
  71.8 6.2 %collective-permute-start.13 = (bf16[128,512]{1,0:T(8,128)(2,1)S(1)}, bf16[128,512]{1,0:T(8,128)(2,1)S(1)}, u32[]{:S(2)}, u32[]{:S(2)}) collective-permute-start(bf16[128,512]{1,0:T(8,128)(2,1)S(1)} %get-tuple-element.73), channel_id=1, source_target_pairs={{1,2},{2,1},{3,4},{4,3},{5,6},{6,5},{7,8},{8,7},{9,10},{10,9},{11,... | collective-permute-start | bytes 393224 | tf_op jit(solution)/shard_map/ppermute | solution.py:478
  78.0 2.5 %mid_gradients.1 = (f32[2,128,512]{2,1,0:T(8,128)S(1)}, f32[512,512]{1,0:T(8,128)S(1)}, f32[512,512]{1,0:T(8,128)S(1)}) custom-call(bf16[2,128,512]{2,1,0:T(8,128)(2,1)S(1)} %get-tuple-element.46.side_a.refs_0_, bf16[2,128,512]{2,1,0:T(8,128)(2,1)S(1)} %get-tuple-element.47.side_b.refs_1_, bf16[2,128,512]{2,1,0:T(8,128)(2,1)S(1)} %collective-permute-done.6.refs_0_.refs_2_, ...), custom_call_target="tpu_custom_call" | custom-call | tf_op jit(solution)/shard_map/mid_gradients/pallas_call | solution.py:414
  80.5 1.0 %collective-permute-done.13.mid_dq_b = bf16[128,512]{1,0:T(8,128)(2,1)S(1)} collective-permute-done((bf16[128,512]{1,0:T(8,128)(2,1)S(1)}, bf16[128,512]{1,0:T(8,128)(2,1)S(1)}, u32[]{:S(2)}, u32[]{:S(2)}) %collective-permute-start.13) | collective-permute-done | bytes 131104 | tf_op jit(solution)/shard_map/ppermute | solution.py:478
  81.5 1.3 %finish.1 = (bf16[32,16,512]{2,1,0:T(8,128)(2,1)}, bf16[32,16,512]{2,1,0:T(8,128)(2,1)}, bf16[32,16,512]{2,1,0:T(8,128)(2,1)}) custom-call(f32[2,128,512]{2,1,0:T(8,128)S(1)} %get-tuple-element.58.dq_edge, f32[2,128,512]{2,1,0:T(8,128)S(1)} %get-tuple-element.69.dq_mid, f32[512,512]{1,0:T(8,128)S(1)} %get-tuple-element.70.dk, ...), custom_call_target="tpu_custom_call" | custom-call | tf_op jit(solution)/shard_map/finish/pallas_call | solution.py:458
  (22 shorter events, 0.3 us)
Async XLA Ops:
  2.6 25.8 %copy-start.2 = (bf16[2,128,512]{2,1,0:T(8,128)(2,1)S(1)}, bf16[2,128,512]{2,1,0:T(8,128)(2,1)}, u32[]{:S(2)}) copy-start(bf16[2,128,512]{2,1,0:T(8,128)(2,1)} %get-tuple-element.40.side_b.refs_1_) | copy-start | bytes 786436
  2.6 1.1 %copy-start.3 = (bf16[32,16,512]{2,1,0:T(8,128)(2,1)S(1)}, bf16[32,16,512]{2,1,0:T(8,128)(2,1)}, u32[]{:S(2)}) copy-start(bf16[32,16,512]{2,1,0:T(8,128)(2,1)} %k_ref.1) | copy-start | bytes 1572868
  3.7 1.0 %copy-start.4 = (bf16[32,16,512]{2,1,0:T(8,128)(2,1)S(1)}, bf16[32,16,512]{2,1,0:T(8,128)(2,1)}, u32[]{:S(2)}) copy-start(bf16[32,16,512]{2,1,0:T(8,128)(2,1)} %v_ref.1) | copy-start | bytes 1572868
  6.4 16.4 %collective-permute-start.2 = (bf16[2,128,512]{2,1,0:T(8,128)(2,1)S(1)}, bf16[2,128,512]{2,1,0:T(8,128)(2,1)S(1)}, u32[]{:S(2)}, u32[]{:S(2)}) collective-permute-start(bf16[2,128,512]{2,1,0:T(8,128)(2,1)S(1)} %get-tuple-element.43.refs_0_), channel_id=1, source_target_pairs={{0,32},{32,0},{64,96},{96,64},{1,33},{33,1},{65,97},{97,65},{2,34}... | collective-permute-start | bytes 786440 | tf_op jit(solution)/shard_map/ppermute | solution.py:470
  7.9 20.5 %collective-permute-start.3 = (bf16[2,128,512]{2,1,0:T(8,128)(2,1)S(1)}, bf16[2,128,512]{2,1,0:T(8,128)(2,1)S(1)}, u32[]{:S(2)}, u32[]{:S(2)}) collective-permute-start(bf16[2,128,512]{2,1,0:T(8,128)(2,1)S(1)} %get-tuple-element.44), channel_id=1, source_target_pairs={{32,64},{64,32},{33,65},{65,33},{34,66},{66,34},{35,67},{67,35},{3... | collective-permute-start | bytes 786440 | tf_op jit(solution)/shard_map/ppermute | solution.py:478
  11.1 23.6 %collective-permute-start = (bf16[2,128,512]{2,1,0:T(8,128)(2,1)}, bf16[2,128,512]{2,1,0:T(8,128)(2,1)S(1)}, u32[]{:S(2)}, u32[]{:S(2)}) collective-permute-start(bf16[2,128,512]{2,1,0:T(8,128)(2,1)} %get-tuple-element.39._.side_a.refs_0_), channel_id=1, source_target_pairs={{0,1},{1,0},{2,3},{3,2},{4,5},{5,4},{6,7},{7,6},{8,9},{9,8},{10,11... | collective-permute-start | bytes 786440 | tf_op jit(solution)/shard_map/ppermute | solution.py:470
  13.8 21.0 %collective-permute-start.1 = (bf16[2,128,512]{2,1,0:T(8,128)(2,1)}, bf16[2,128,512]{2,1,0:T(8,128)(2,1)S(1)}, u32[]{:S(2)}, u32[]{:S(2)}) collective-permute-start(bf16[2,128,512]{2,1,0:T(8,128)(2,1)} %get-tuple-element.40.side_b.refs_1_), channel_id=1, source_target_pairs={{1,2},{2,1},{3,4},{4,3},{5,6},{6,5},{7,8},{8,7},{9,10},{10,9},{11,... | collective-permute-start | bytes 786440 | tf_op jit(solution)/shard_map/ppermute | solution.py:478
  19.8 1.0 %copy-start = (bf16[32,16,512]{2,1,0:T(8,128)(2,1)S(1)}, bf16[32,16,512]{2,1,0:T(8,128)(2,1)}, u32[]{:S(2)}) copy-start(bf16[32,16,512]{2,1,0:T(8,128)(2,1)} %q_ref.3) | copy-start | bytes 1572868
  20.8 1.0 %copy-start.1 = (bf16[32,16,512]{2,1,0:T(8,128)(2,1)S(1)}, bf16[32,16,512]{2,1,0:T(8,128)(2,1)}, u32[]{:S(2)}) copy-start(bf16[32,16,512]{2,1,0:T(8,128)(2,1)} %g_ref.3) | copy-start | bytes 1572868
  22.7 33.4 %collective-permute-start.6 = (bf16[2,128,512]{2,1,0:T(8,128)(2,1)S(1)}, bf16[2,128,512]{2,1,0:T(8,128)(2,1)S(1)}, u32[]{:S(2)}, u32[]{:S(2)}) collective-permute-start(bf16[2,128,512]{2,1,0:T(8,128)(2,1)S(1)} %get-tuple-element.46.side_a.refs_0_), channel_id=1, source_target_pairs={{0,1},{1,0},{2,3},{3,2},{4,5},{5,4},{6,7},{7,6},{8,9},{9,8},{10,11... | collective-permute-start | bytes 786440 | tf_op jit(solution)/shard_map/ppermute | solution.py:470
  22.8 33.3 %collective-permute-start.7 = (bf16[2,128,512]{2,1,0:T(8,128)(2,1)S(1)}, bf16[2,128,512]{2,1,0:T(8,128)(2,1)S(1)}, u32[]{:S(2)}, u32[]{:S(2)}) collective-permute-start(bf16[2,128,512]{2,1,0:T(8,128)(2,1)S(1)} %get-tuple-element.47.side_b.refs_1_), channel_id=1, source_target_pairs={{1,2},{2,1},{3,4},{4,3},{5,6},{6,5},{7,8},{8,7},{9,10},{10,9},{11,... | collective-permute-start | bytes 786440 | tf_op jit(solution)/shard_map/ppermute | solution.py:478
  36.1 9.8 %collective-permute-start.4 = (f32[4,8,128]{2,1,0:T(8,128)S(1)}, f32[4,8,128]{2,1,0:T(8,128)S(1)}, u32[]{:S(2)}, u32[]{:S(2)}) collective-permute-start(f32[4,8,128]{2,1,0:T(8,128)S(1)} %get-tuple-element.49.refs_0_.refs_4_), channel_id=1, source_target_pairs={{0,1},{1,0},{2,3},{3,2},{4,5},{5,4},{6,7},{7,6},{8,9},{9,8},{10,11... | collective-permute-start | bytes 49160 | tf_op jit(solution)/shard_map/ppermute | solution.py:470
  37.9 9.1 %collective-permute-start.5 = (f32[4,8,128]{2,1,0:T(8,128)S(1)}, f32[4,8,128]{2,1,0:T(8,128)S(1)}, u32[]{:S(2)}, u32[]{:S(2)}) collective-permute-start(f32[4,8,128]{2,1,0:T(8,128)S(1)} %get-tuple-element.50.refs_1_.refs_5_), channel_id=1, source_target_pairs={{1,2},{2,1},{3,4},{4,3},{5,6},{6,5},{7,8},{8,7},{9,10},{10,9},{11,... | collective-permute-start | bytes 49160 | tf_op jit(solution)/shard_map/ppermute | solution.py:478
  48.0 23.8 %collective-permute-start.10 = (bf16[128,512]{1,0:T(8,128)(2,1)S(1)}, bf16[128,512]{1,0:T(8,128)(2,1)S(1)}, u32[]{:S(2)}, u32[]{:S(2)}) collective-permute-start(bf16[128,512]{1,0:T(8,128)(2,1)S(1)} %get-tuple-element.57.refs_14_), channel_id=1, source_target_pairs={{0,1},{1,0},{2,3},{3,2},{4,5},{5,4},{6,7},{7,6},{8,9},{9,8},{10,11... | collective-permute-start | bytes 393224 | tf_op jit(solution)/shard_map/ppermute | solution.py:470
  51.3 30.2 %collective-permute-start.14 = (bf16[2,128,512]{2,1,0:T(8,128)(2,1)S(1)}, bf16[2,128,512]{2,1,0:T(8,128)(2,1)S(1)}, u32[]{:S(2)}, u32[]{:S(2)}) collective-permute-start(bf16[2,128,512]{2,1,0:T(8,128)(2,1)S(1)} %get-tuple-element.59.refs_5_), channel_id=1, source_target_pairs={{0,32},{32,0},{64,96},{96,64},{1,33},{33,1},{65,97},{97,65},{2,34}... | collective-permute-start | bytes 786440 | tf_op jit(solution)/shard_map/ppermute | solution.py:470
  51.4 30.1 %collective-permute-start.15 = (bf16[2,128,512]{2,1,0:T(8,128)(2,1)S(1)}, bf16[2,128,512]{2,1,0:T(8,128)(2,1)S(1)}, u32[]{:S(2)}, u32[]{:S(2)}) collective-permute-start(bf16[2,128,512]{2,1,0:T(8,128)(2,1)S(1)} %get-tuple-element.74), channel_id=1, source_target_pairs={{32,64},{64,32},{33,65},{65,33},{34,66},{66,34},{35,67},{67,35},{3... | collective-permute-start | bytes 786440 | tf_op jit(solution)/shard_map/ppermute | solution.py:478
  57.4 10.8 %collective-permute-start.8 = (f32[4,8,128]{2,1,0:T(8,128)S(1)}, f32[4,8,128]{2,1,0:T(8,128)S(1)}, u32[]{:S(2)}, u32[]{:S(2)}) collective-permute-start(f32[4,8,128]{2,1,0:T(8,128)S(1)} %get-tuple-element.60.refs_0_.refs_4_), channel_id=1, source_target_pairs={{0,1},{1,0},{2,3},{3,2},{4,5},{5,4},{6,7},{7,6},{8,9},{9,8},{10,11... | collective-permute-start | bytes 49160 | tf_op jit(solution)/shard_map/ppermute | solution.py:470
  61.3 9.5 %collective-permute-start.9 = (f32[4,8,128]{2,1,0:T(8,128)S(1)}, f32[4,8,128]{2,1,0:T(8,128)S(1)}, u32[]{:S(2)}, u32[]{:S(2)}) collective-permute-start(f32[4,8,128]{2,1,0:T(8,128)S(1)} %get-tuple-element.61.refs_1_.refs_5_), channel_id=1, source_target_pairs={{1,2},{2,1},{3,4},{4,3},{5,6},{6,5},{7,8},{8,7},{9,10},{10,9},{11,... | collective-permute-start | bytes 49160 | tf_op jit(solution)/shard_map/ppermute | solution.py:478
  68.2 12.3 %collective-permute-start.11 = (bf16[128,512]{1,0:T(8,128)(2,1)S(1)}, bf16[128,512]{1,0:T(8,128)(2,1)S(1)}, u32[]{:S(2)}, u32[]{:S(2)}) collective-permute-start(bf16[128,512]{1,0:T(8,128)(2,1)S(1)} %get-tuple-element.72), channel_id=1, source_target_pairs={{1,2},{2,1},{3,4},{4,3},{5,6},{6,5},{7,8},{8,7},{9,10},{10,9},{11,... | collective-permute-start | bytes 393224 | tf_op jit(solution)/shard_map/ppermute | solution.py:478
  71.7 8.8 %collective-permute-start.12 = (bf16[128,512]{1,0:T(8,128)(2,1)S(1)}, bf16[128,512]{1,0:T(8,128)(2,1)S(1)}, u32[]{:S(2)}, u32[]{:S(2)}) collective-permute-start(bf16[128,512]{1,0:T(8,128)(2,1)S(1)} %get-tuple-element.66.refs_13_), channel_id=1, source_target_pairs={{0,1},{1,0},{2,3},{3,2},{4,5},{5,4},{6,7},{7,6},{8,9},{9,8},{10,11... | collective-permute-start | bytes 393224 | tf_op jit(solution)/shard_map/ppermute | solution.py:470
  71.8 9.7 %collective-permute-start.13 = (bf16[128,512]{1,0:T(8,128)(2,1)S(1)}, bf16[128,512]{1,0:T(8,128)(2,1)S(1)}, u32[]{:S(2)}, u32[]{:S(2)}) collective-permute-start(bf16[128,512]{1,0:T(8,128)(2,1)S(1)} %get-tuple-element.73), channel_id=1, source_target_pairs={{1,2},{2,1},{3,4},{4,3},{5,6},{6,5},{7,8},{8,7},{9,10},{10,9},{11,... | collective-permute-start | bytes 393224 | tf_op jit(solution)/shard_map/ppermute | solution.py:478

commit v4 on v3

--- a/solution.py
+++ b/solution.py
@@ -24,6 +24,8 @@
 PACK_LIMIT = 62 * 1024 * 1024
 EDGE_ROWS = (0, 3)
 MID_ROWS = (1, 2)
+ORDER = EDGE_ROWS + MID_ROWS
+EDGE, MID = 0, 1
 
 
 def matmul(a, b, contract):
@@ -47,7 +49,7 @@
 
 
 def ordered(first, second):
-    swap = lax.axis_index("lon") % 2 == 0
+    swap = lax.axis_index("lon") % 2 == 1
     return jnp.where(swap, second, first), jnp.where(swap, first, second)
 
 
@@ -66,18 +68,40 @@
     return copies
 
 
-def pack_queries_kernel(rows, q_ref, g_ref, *refs):
-    side_a, side_b, buffers, sems = refs[-4:]
-    copies = fetch((q_ref, g_ref), rows, buffers, sems)
-    for place in range(2):
+def pack_queries_kernel(q_ref, g_ref, side_0, side_1, buffers, sems, packed, out_sems):
+    copies = fetch((q_ref, g_ref), ORDER, buffers, sems)
+    sends = []
+    for place in range(ROWS):
         for i in range(2):
             copies[i][place].wait()
-            side_a[i, at_tokens(place)], side_b[i, at_tokens(place)] = split_columns(buffers[i, place])
-
-
-def pack_keys_kernel(rows, k_ref, v_ref, _, kd, vd, edge_a, edge_b, buffers, sems):
-    copies = fetch((k_ref, v_ref), rows, buffers, sems)
-    for t in rows:
+            for side, (value, out) in enumerate(zip(split_columns(buffers[i, place]), (side_0, side_1))):
+                packed[side, i, place] = value
+                sends.append(pltpu.make_async_copy(packed.at[side, i, place],
+                                                   out.at[i, pl.ds(place * CELLS, CELLS)], out_sems.at[side, i, place]))
+                sends[-1].start()
+    for send in sends:
+        send.wait()
+
+
+def pack_queries(*operands):
+    return pl.pallas_call(
+        pack_queries_kernel,
+        in_specs=[pl.BlockSpec(memory_space=pl.ANY)] * 2,
+        out_specs=[pl.BlockSpec(memory_space=pl.ANY)] * 2,
+        out_shape=[struct((2, ROWS * CELLS, FEAT), BF16)] * 2,
+        scratch_shapes=[
+            pltpu.VMEM((2, ROWS, 8, 16, FEAT), BF16), pltpu.SemaphoreType.DMA((2, ROWS)),
+            pltpu.VMEM((2, 2, ROWS, CELLS, FEAT), BF16), pltpu.SemaphoreType.DMA((2, 2, ROWS)),
+        ],
+        compiler_params=params(PACK_LIMIT),
+        cost_estimate=cost(0, 3 << 20),
+        name="pack_queries",
+    )(*operands)
+
+
+def pack_keys_kernel(k_ref, v_ref, kd, vd, edge_a, edge_b, buffers, sems):
+    copies = fetch((k_ref, v_ref), range(ROWS), buffers, sems)
+    for t in range(ROWS):
         for i, out in enumerate((kd, vd)):
             copies[i][t].wait()
             tile = jnp.concatenate(split_columns(buffers[i, t]), axis=0)
@@ -88,15 +112,15 @@
                 edge_b[i] = tile
 
 
-def pack(kernel, rows, operands, out_shape, name, limit):
-    return pl.pallas_call(
-        functools.partial(kernel, rows),
-        in_specs=[pl.BlockSpec(memory_space=pl.ANY)] * len(operands),
-        out_shape=out_shape,
-        scratch_shapes=[pltpu.VMEM((2, len(rows), 8, 16, FEAT), BF16), pltpu.SemaphoreType.DMA((2, len(rows)))],
-        compiler_params=params(limit),
-        cost_estimate=cost(0, 0),
-        name=name,
+def pack_keys(*operands):
+    return pl.pallas_call(
+        pack_keys_kernel,
+        in_specs=[pl.BlockSpec(memory_space=pl.ANY)] * 2,
+        out_shape=[struct((ROWS * PAIR, FEAT), BF16)] * 2 + [struct((2, PAIR, FEAT), BF16)] * 2,
+        scratch_shapes=[pltpu.VMEM((2, ROWS, 8, 16, FEAT), BF16), pltpu.SemaphoreType.DMA((2, ROWS))],
+        compiler_params=params(),
+        cost_estimate=cost(0, 3 << 20),
+        name="pack_keys",
     )(*operands)
 
 
@@ -188,21 +212,35 @@
     return slice(j * PAIR, (j + 1) * PAIR)
 
 
-tokens_spec = pl.BlockSpec((2, CHUNK, PAIR), lambda p: (0, 0, p))
+def tokens_spec(group):
+    return pl.BlockSpec((2, CHUNK, PAIR), lambda p: (0, group, p))
+
+
 keys_spec = pl.BlockSpec((ROWS * PAIR, PAIR), lambda p: (0, p))
 edge_spec = pl.BlockSpec((2, PAIR, PAIR), lambda p: (0, 0, p))
-stats_spec = pl.BlockSpec((1, 8, PAIR), lambda p: (p, 0, 0))
+part_spec = pl.BlockSpec((1, 8, PAIR), lambda p: (p, 0, 0))
 held_spec = pl.BlockSpec((1, 2, 3 * PAIR, WIDE), lambda p: (p, 0, 0, 0))
-stats_shape = struct((PAIRS, 8, PAIR), F32)
+part_shape = struct((PAIRS, 8, PAIR), F32)
+stats_shape = struct((PAIRS, 16, PAIR), F32)
 held_shape = struct((PAIRS, 2, 3 * PAIR, WIDE), F32)
 
-tokens_wide = pl.BlockSpec((2, CHUNK, WIDE), lambda g: (0, 0, g))
-part_wide = pl.BlockSpec((CHUNK, WIDE), lambda g: (0, g))
+
+def tokens_wide(group):
+    return pl.BlockSpec((2, CHUNK, WIDE), lambda g: (0, group, g))
+
+
+def stats_wide(group):
+    return pl.BlockSpec((2, 8, PAIR), lambda g: (g, group, 0))
+
+
+all_tokens = pl.BlockSpec((2, 2 * CHUNK, WIDE), lambda g: (0, 0, g))
+all_stats = pl.BlockSpec((2, 16, PAIR), lambda g: (g, 0, 0))
+all_parts = pl.BlockSpec((2 * CHUNK, WIDE), lambda g: (0, g))
+sums_wide = pl.BlockSpec((2, CHUNK, WIDE), lambda g: (0, 0, g))
 keys_wide = pl.BlockSpec((ROWS * PAIR, WIDE), lambda g: (0, g))
 edge_wide = pl.BlockSpec((2, PAIR, WIDE), lambda g: (0, 0, g))
 turned_wide = pl.BlockSpec((WIDE, ROWS * PAIR), lambda g: (g, 0))
 edge_turned_wide = pl.BlockSpec((2, WIDE, PAIR), lambda g: (0, g, 0))
-stats_wide = pl.BlockSpec((2, 8, PAIR), lambda g: (g, 0, 0))
 held_wide = pl.BlockSpec((2, 2, 3 * PAIR, WIDE), lambda g: (g, 0, 0, 0))
 halo_wide = pl.BlockSpec((1, 2, 2, 3 * CELLS, WIDE), lambda g: (g, 0, 0, 0, 0))
 halo_shape = struct((GROUPS, 2, 2, 3 * CELLS, WIDE), F32)
@@ -225,72 +263,94 @@
                 part[0, index:index + 1] = values[:, pair_lanes(c)]
 
 
-def mid_scores_kernel(side_a, side_b, kd, vd, part, s_out, d_out, turned):
-    own_scores(MID_ROWS, side_a, side_b, kd, vd, None, part, s_out, d_out)
+def mid_scores_kernel(side_0, side_1, kd, vd, part, s_out, d_out, turned):
+    own_scores(MID_ROWS, side_0, side_1, kd, vd, None, part, s_out, d_out)
     turned[...] = kd[...].T
 
 
-def edge_scores_kernel(side_a, side_b, kd, vd, edge_a, edge_b, part, s_out, d_out, turned):
-    own_scores(EDGE_ROWS, side_a, side_b, kd, vd, (edge_a, edge_b), part, s_out, d_out)
+def edge_scores_kernel(side_0, side_1, kd, vd, edge_a, edge_b, part, s_out, d_out):
+    own_scores(EDGE_ROWS, side_0, side_1, kd, vd, (edge_a, edge_b), part, s_out, d_out)
+
+
+def mid_scores(*operands):
+    return pl.pallas_call(
+        mid_scores_kernel,
+        grid=(PAIRS,),
+        in_specs=[tokens_spec(MID)] * 2 + [keys_spec] * 2,
+        out_specs=[part_spec] + [held_spec] * 2 + [pl.BlockSpec((PAIR, ROWS * PAIR), lambda p: (p, 0))],
+        out_shape=[part_shape] + [held_shape] * 2 + [struct((FEAT, ROWS * PAIR), BF16)],
+        compiler_params=params(),
+        cost_estimate=cost(2e9, 1 << 10),
+        name="mid_scores",
+    )(*operands)
+
+
+def edge_scores(*operands):
+    return pl.pallas_call(
+        edge_scores_kernel,
+        grid=(PAIRS,),
+        in_specs=[tokens_spec(EDGE)] * 2 + [keys_spec] * 2 + [edge_spec] * 2,
+        out_specs=[part_spec] + [held_spec] * 2,
+        out_shape=[part_shape] + [held_shape] * 2,
+        compiler_params=params(),
+        cost_estimate=cost(2e9, 1 << 10),
+        name="edge_scores",
+    )(*operands)
+
+
+def turn_edges_kernel(edge_a, edge_b, turned):
     turned[0] = edge_a[0].T
     turned[1] = edge_b[0].T
 
 
-def scores_call(kernel, operands, turned_spec, turned_shape, name):
-    return pl.pallas_call(
-        kernel,
+def turn_edges(*operands):
+    return pl.pallas_call(
+        turn_edges_kernel,
         grid=(PAIRS,),
-        in_specs=[tokens_spec] * 2 + [keys_spec] * 2 + [edge_spec] * (len(operands) - 4),
-        out_specs=[stats_spec] + [held_spec] * 2 + [turned_spec],
-        out_shape=[stats_shape] + [held_shape] * 2 + [struct(turned_shape, BF16)],
-        compiler_params=params(),
-        cost_estimate=cost(0, 0),
-        name=name,
-    )(*operands)
-
-
-def mid_scores(*operands):
-    spec = pl.BlockSpec((PAIR, ROWS * PAIR), lambda p: (p, 0))
-    return scores_call(mid_scores_kernel, operands, spec, (FEAT, ROWS * PAIR), "mid_scores")
-
-
-def edge_scores(*operands):
-    spec = pl.BlockSpec((2, PAIR, PAIR), lambda p: (0, p, 0))
-    return scores_call(edge_scores_kernel, operands, spec, (2, FEAT, PAIR), "edge_scores")
-
-
-def halo_scores_kernel(rows, *refs):
-    q_a, q_b, kd, vd, part, _, *edges = refs[:-4]
-    send_a, send_b, s_out, d_out = refs[-4:]
+        in_specs=[edge_spec] * 2,
+        out_specs=pl.BlockSpec((2, PAIR, PAIR), lambda p: (0, p, 0)),
+        out_shape=struct((2, FEAT, PAIR), BF16),
+        compiler_params=params(),
+        cost_estimate=cost(1e9, 1 << 10),
+        name="turn_edges",
+    )(*operands)
+
+
+def halo_scores_kernel(q_0, q_1, kd, vd, edge_a, edge_b, edge_part, mid_part,
+                       send_0, send_1, s_edge, d_edge, s_mid, d_mid):
     masks = head_masks(WIDE)
-    for c, (q_in, send) in enumerate(((q_a, send_a), (q_b, send_b))):
-        for j in range(2):
-            send[j, 0:4] = part[j, 4 * c:4 * c + 4]
-        for place, t in enumerate(rows):
-            at = at_tokens(place)
-            queries = stacked([q_in[0, at]], masks)
-            grads = stacked([q_in[1, at]], masks)
-            scores = score_block(column_window(c, kd, edges, 0, t), queries, t)
-            dprobs = matmul(column_window(c, vd, edges, 1, t), grads, (1, 1))
-            s_out[0, place, c] = scores
-            d_out[0, place, c] = dprobs
-            for w, values in enumerate(row_stats(scores, dprobs)):
-                index = 4 + 2 * w + place
-                for j in range(2):
-                    send[j, index:index + 1] = values[:, pair_lanes(j)]
-
-
-def halo_scores(rows, halos, kd, vd, part, edges, before, name):
-    return pl.pallas_call(
-        functools.partial(halo_scores_kernel, rows),
+    groups = ((EDGE_ROWS, edge_part, s_edge, d_edge), (MID_ROWS, mid_part, s_mid, d_mid))
+    for group, (rows, part, s_out, d_out) in enumerate(groups):
+        base = 8 * group
+        for c, (q_in, send) in enumerate(((q_0, send_0), (q_1, send_1))):
+            for j in range(2):
+                send[j, base:base + 4] = part[j, 4 * c:4 * c + 4]
+            for place, t in enumerate(rows):
+                at = at_tokens(2 * group + place)
+                queries = stacked([q_in[0, at]], masks)
+                grads = stacked([q_in[1, at]], masks)
+                scores = score_block(column_window(c, kd, (edge_a, edge_b), 0, t), queries, t)
+                dprobs = matmul(column_window(c, vd, (edge_a, edge_b), 1, t), grads, (1, 1))
+                s_out[0, place, c] = scores
+                d_out[0, place, c] = dprobs
+                for w, values in enumerate(row_stats(scores, dprobs)):
+                    index = base + 4 + 2 * w + place
+                    for j in range(2):
+                        send[j, index:index + 1] = values[:, pair_lanes(j)]
+
+
+def halo_scores(*operands):
+    part = pl.BlockSpec((2, 8, PAIR), lambda g: (g, 0, 0))
+    return pl.pallas_call(
+        halo_scores_kernel,
         grid=(GROUPS,),
-        in_specs=[tokens_wide] * 2 + [keys_wide] * 2 + [stats_wide, any_spec] + [edge_wide] * len(edges),
-        out_specs=[stats_wide] * 2 + [halo_wide] * 2,
-        out_shape=[stats_shape] * 2 + [halo_shape] * 2,
-        compiler_params=params(),
-        cost_estimate=cost(0, 0),
-        name=name,
-    )(*halos, kd, vd, part, before, *edges)
+        in_specs=[all_tokens] * 2 + [keys_wide] * 2 + [edge_wide] * 2 + [part] * 2,
+        out_specs=[all_stats] * 2 + [halo_wide] * 4,
+        out_shape=[stats_shape] * 2 + [halo_shape] * 4,
+        compiler_params=params(),
+        cost_estimate=cost(2e9, 1 << 10),
+        name="halo_scores",
+    )(*operands)
 
 
 def halo_weights(mine, theirs, s_in, d_in, c):
@@ -305,35 +365,37 @@
     return weights
 
 
-def halo_queries_kernel(rows, *refs):
-    send_a, send_b, recv_a, recv_b, s_in, d_in, own_turned, *edges_turned = refs[:-2]
-    outs = refs[-2:]
+def halo_queries_kernel(send_0, send_1, recv_0, recv_1, s_edge, d_edge, s_mid, d_mid, own_turned, edges_turned,
+                        out_0, out_1):
     lane = lax.broadcasted_iota(jnp.int32, (1, PAIR), 1)
-    weights = [halo_weights(mine, theirs, s_in, d_in, c)
-               for c, (mine, theirs) in enumerate(((send_a, recv_a), (send_b, recv_b)))]
     none = jnp.zeros((CELLS, PAIR), BF16)
-    for place, t in enumerate(rows):
-        for j in range(2):
-            pieces = []
-            for i in range(3):
-                part_a, part_b = [weights[c][place][1][at_tokens(i), pair_lanes(j)] for c in range(2)]
-                pieces += [jnp.concatenate([part_a, none], axis=1), jnp.concatenate([none, part_b], axis=1)]
-            keys_turned = turned_window(own_turned, edges_turned[0] if edges_turned else None, t, j)
-            for out, part in zip(outs, query_parts(keys_turned, jnp.concatenate(pieces, axis=0), lane)):
-                out[at_tokens(place), pair_lanes(j)] = part.astype(BF16)
-
-
-def halo_queries(rows, stats, held, turned, name):
-    return pl.pallas_call(
-        functools.partial(halo_queries_kernel, rows),
+    groups = ((EDGE_ROWS, s_edge, d_edge), (MID_ROWS, s_mid, d_mid))
+    for group, (rows, s_in, d_in) in enumerate(groups):
+        stats = [ref.at[:, pl.ds(8 * group, 8)] for ref in (send_0, send_1, recv_0, recv_1)]
+        weights = [halo_weights(stats[c], stats[2 + c], s_in, d_in, c) for c in range(2)]
+        for place, t in enumerate(rows):
+            for j in range(2):
+                pieces = []
+                for i in range(3):
+                    parts = [weights[c][place][1][at_tokens(i), pair_lanes(j)] for c in range(2)]
+                    pieces += [jnp.concatenate([parts[0], none], axis=1), jnp.concatenate([none, parts[1]], axis=1)]
+                keys_turned = turned_window(own_turned, edges_turned, t, j)
+                grads = query_parts(keys_turned, jnp.concatenate(pieces, axis=0), lane)
+                for out, grad in zip((out_0, out_1), grads):
+                    out[at_tokens(2 * group + place), pair_lanes(j)] = grad.astype(BF16)
+
+
+def halo_queries(*operands):
+    return pl.pallas_call(
+        halo_queries_kernel,
         grid=(GROUPS,),
-        in_specs=[stats_wide] * 4 + [halo_wide] * 2 + [turned_wide] + [edge_turned_wide] * (len(turned) - 1),
-        out_specs=[part_wide] * 2,
-        out_shape=[struct((CHUNK, FEAT), BF16)] * 2,
-        compiler_params=params(),
-        cost_estimate=cost(0, 0),
-        name=name,
-    )(*stats, *held, *turned)
+        in_specs=[all_stats] * 4 + [halo_wide] * 4 + [turned_wide, edge_turned_wide],
+        out_specs=[all_parts] * 2,
+        out_shape=[struct((2 * CHUNK, FEAT), BF16)] * 2,
+        compiler_params=params(),
+        cost_estimate=cost(2e9, 1 << 10),
+        name="halo_queries",
+    )(*operands)
 
 
 def row_gradients(rows, side_a, side_b, q_a, q_b, send_a, send_b, recv_a, recv_b, s_own, d_own, s_halo, d_halo,
@@ -392,8 +454,11 @@
         out[3 * PAIR:] = sums[3 * PAIR:] + lower[which][2 * PAIR:] * scale
 
 
-ROW_SPECS = [tokens_wide] * 4 + [stats_wide] * 4 + [held_wide] * 2 + [halo_wide] * 2 + [turned_wide]
-GRAD_SPECS = [tokens_wide] + [keys_wide] * 2
+def row_specs(group):
+    return ([tokens_wide(group)] * 4 + [stats_wide(group)] * 4 + [held_wide] * 2 + [halo_wide] * 2 + [turned_wide])
+
+
+GRAD_SPECS = [sums_wide] + [keys_wide] * 2
 GRAD_SHAPES = [struct((2, CHUNK, FEAT), F32)] + [struct((ROWS * PAIR, FEAT), F32)] * 2
 
 
@@ -401,11 +466,11 @@
     return pl.pallas_call(
         edge_kernel,
         grid=(GROUPS,),
-        in_specs=ROW_SPECS + [edge_turned_wide, any_spec],
+        in_specs=row_specs(EDGE) + [edge_turned_wide, any_spec],
         out_specs=GRAD_SPECS + [edge_wide] * 2,
         out_shape=GRAD_SHAPES + [struct((2, PAIR, FEAT), BF16)] * 2,
         compiler_params=params(),
-        cost_estimate=cost(0, 0),
+        cost_estimate=cost(3e9, 1 << 10),
         name="edge_gradients",
     )(*operands)
 
@@ -414,11 +479,11 @@
     return pl.pallas_call(
         mid_kernel,
         grid=(GROUPS,),
-        in_specs=ROW_SPECS + [any_spec] + [keys_wide] * 2,
+        in_specs=row_specs(MID) + [any_spec] + [keys_wide] * 2,
         out_specs=GRAD_SPECS,
         out_shape=GRAD_SHAPES,
         compiler_params=params(),
-        cost_estimate=cost(0, 0),
+        cost_estimate=cost(3e9, 1 << 10),
         name="mid_gradients",
     )(*operands)
 
@@ -428,7 +493,7 @@
     return jnp.concatenate([part.reshape(8, 8, FEAT) for part in parts], axis=1).astype(BF16)
 
 
-def finish_kernel(dq_edge, dq_mid, dk, dv, edge_dq_a, edge_dq_b, mid_dq_a, mid_dq_b, from_a, from_b,
+def finish_kernel(dq_edge, dq_mid, dk, dv, dq_0, dq_1, from_a, from_b,
                   q_ref, k_ref, v_ref, buffers, sems):
     copies = []
 
@@ -446,10 +511,10 @@
             if t == ROWS - 1:
                 full = full + from_b[which].astype(F32)
             send(1 + which, t, join_columns(full[:CELLS], full[CELLS:]))
-    for rows, dq, side_a, side_b in ((EDGE_ROWS, dq_edge, edge_dq_a, edge_dq_b), (MID_ROWS, dq_mid, mid_dq_a, mid_dq_b)):
-        for place, t in enumerate(rows):
-            at = at_tokens(place)
-            send(0, t, join_columns(dq[0, at] + side_a[at].astype(F32), dq[1, at] + side_b[at].astype(F32)))
+    for place, t in enumerate(ORDER):
+        dq = (dq_edge, dq_mid)[place // 2]
+        at, there = at_tokens(place % 2), at_tokens(place)
+        send(0, t, join_columns(dq[0, at] + dq_0[there].astype(F32), dq[1, at] + dq_1[there].astype(F32)))
     for copy in copies:
         copy.wait()
 
@@ -461,7 +526,7 @@
         out_shape=[struct((8 * ROWS, 16, FEAT), BF16)] * 3,
         scratch_shapes=[pltpu.VMEM((3, ROWS, 8, 16, FEAT), BF16), pltpu.SemaphoreType.DMA((3, ROWS))],
         compiler_params=params(),
-        cost_estimate=cost(0, 0),
+        cost_estimate=cost(0, 1 << 10),
         name="finish",
     )(*operands)
 
@@ -478,44 +543,31 @@
     return lax.ppermute(x, axis, pairs)
 
 
-def over_lon(side_a, side_b):
-    from_b = swap_b(side_b, "lon", True)
-    return swap_a(side_a, "lon"), from_b
+def over_lon(side_0, side_1):
+    return swap_b(side_0, "lon", True), swap_a(side_1, "lon")
 
 
 def over_lat(side_a, side_b):
-    from_b = swap_b(side_b, "lat", False)
-    return swap_a(side_a, "lat"), from_b
+    return swap_a(side_a, "lat"), swap_b(side_b, "lat", False)
 
 
 def on_device(query_vectors, key_vectors, value_vectors, output_grads):
-    tokens = struct((2, CHUNK, FEAT), BF16)
-    tiles = struct((ROWS * PAIR, FEAT), BF16)
-    edge = struct((2, PAIR, FEAT), BF16)
-    sides = pack(pack_queries_kernel, EDGE_ROWS, (query_vectors, output_grads), [tokens] * 2, "pack_edge", PACK_LIMIT)
-    kd, vd, own_edge_a, own_edge_b = pack(pack_keys_kernel, range(ROWS), (key_vectors, value_vectors, sides[0]),
-                                          [tiles] * 2 + [edge] * 2, "pack_keys", VMEM_LIMIT)
-    mid_sides = pack(pack_queries_kernel, MID_ROWS, (query_vectors, output_grads, own_edge_a),
-                     [tokens] * 2, "pack_mid", VMEM_LIMIT)
+    sides = pack_queries(query_vectors, output_grads)
+    kd, vd, own_edge_a, own_edge_b = pack_keys(key_vectors, value_vectors)
     halos = over_lon(*sides)
     edges = over_lat(own_edge_a, own_edge_b)
-    mid_halos = over_lon(*mid_sides)
-
-    mid_part, *mid_own, turned = mid_scores(*mid_sides, kd, vd)
-    part, *own, edges_turned = edge_scores(*sides, kd, vd, *edges)
-    send_a, send_b, *held = halo_scores(EDGE_ROWS, halos, kd, vd, part, edges, mid_part, "edge_halo_scores")
-    stats = (send_a, send_b, *over_lon(send_a, send_b))
-    halo_dq = halo_queries(EDGE_ROWS, stats, held, (turned, edges_turned), "edge_halo_queries")
+    mid_part, *mid_own, turned = mid_scores(*sides, kd, vd)
+    edge_part, *edge_own = edge_scores(*sides, kd, vd, *edges)
+    *sends, s_edge, d_edge, s_mid, d_mid = halo_scores(*halos, kd, vd, *edges, edge_part, mid_part)
+    stats = (*sends, *over_lon(*sends))
+    edges_turned = turn_edges(*edges)
+    halo_dq = halo_queries(*stats, s_edge, d_edge, s_mid, d_mid, turned, edges_turned)
     dq_parts = over_lon(*halo_dq)
-    dq, dk, dv, out_a, out_b = edge_gradients(*sides, *halos, *stats, *own, *held, turned, edges_turned, halo_dq[0])
+    shared = (*sides, *halos, *stats)
+    dq_edge, dk, dv, out_a, out_b = edge_gradients(*shared, *edge_own, s_edge, d_edge, turned, edges_turned, halo_dq[0])
     key_parts = over_lat(out_a, out_b)
-
-    send_a, send_b, *held = halo_scores(MID_ROWS, mid_halos, kd, vd, mid_part, (), out_a, "mid_halo_scores")
-    stats = (send_a, send_b, *over_lon(send_a, send_b))
-    halo_dq = halo_queries(MID_ROWS, stats, held, (turned,), "mid_halo_queries")
-    mid_dq_parts = over_lon(*halo_dq)
-    mid_dq, dk, dv = mid_gradients(*mid_sides, *mid_halos, *stats, *mid_own, *held, turned, halo_dq[0], dk, dv)
-    return tuple(finish(dq, mid_dq, dk, dv, *dq_parts, *mid_dq_parts, *key_parts))
+    dq_mid, dk, dv = mid_gradients(*shared, *mid_own, s_mid, d_mid, turned, halo_dq[0], dk, dv)
+    return tuple(finish(dq_edge, dq_mid, dk, dv, *dq_parts, *key_parts))
 
 
 def solution(mesh):

time: 83.2 us -> 72.8 us (0.87)
  starting transfers between devices: 50.9 us -> 27.6 us
  waiting for transfers between devices: 5.15 us -> 21.1 us
  Pallas kernels: 21.6 us -> 18.8 us
    ppermute x8 -> x5, starting transfers between devices: 40.7 us -> 26.2 us  [swap_b(): return lax.ppermute(x, axis, pairs)]
    ppermute x8 -> x5, waiting for transfers between devices: 2.15 us -> 14.4 us  [swap_b(): return lax.ppermute(x, axis, pairs)]
    ppermute x8 -> x5, starting transfers between devices: 10.2 us -> 1.43 us  [swap_a(): lax.ppermute(x, axis, [(i, i ^ 1) for i in range(lax.axis_size(axis))])]
    ppermute x8 -> x5, waiting for transfers between devices: 3 us -> 6.74 us  [swap_a(): lax.ppermute(x, axis, [(i, i ^ 1) for i in range(lax.axis_size(axis))])]
    pallas_call x11 -> x9, Pallas kernels: 20.4 us -> 17.5 us  [the longest x1 2.55 us: mid_gradients(): pl.pallas_call(mid_kernel, grid=(GROUPS,), in_specs=row_specs(MID) + [any...]
    unnamed x10 -> x12, local copies, waits for them, and re-layouts: 4.21 us -> 4.17 us
  transfers between devices with their start and end apart: 16 -> 10, of which waited for: 3 -> 5; matrix products, arithmetic and copies ran while one was open for 0% -> 0% of each run, Pallas kernels for 20% -> 16%
where the time goes in v4:
time: 72.8 us; the launch traced here: 72.5 us
  starting transfers between devices  27.6 us (38%)
  waiting for transfers between devices  21.1 us (29%)
  Pallas kernels  18.8 us (26%)
  local copies, waits for them, and re-layouts  4.17 us (6%)
  between operations  0.78 us (1%)
    ppermute x5, starting transfers between devices, swap_b(): return lax.ppermute(x, axis, pairs)  26.2 us
    ppermute x5, waiting for transfers between devices, swap_b(): return lax.ppermute(x, axis, pairs)  14.4 us
    ppermute x5, waiting for transfers between devices, swap_a(): lax.ppermute(x, axis, [(i, i ^ 1) for i in range(lax.axis_size(axis))])  6.74 us
    unnamed x12, local copies, waits for them, and re-layouts  4.17 us
    pallas_call x1, Pallas kernels, mid_gradients(): pl.pallas_call(mid_kernel, grid=(GROUPS,), in_specs=row_specs(MID) + [any...  2.55 us
    pallas_call x1, Pallas kernels, edge_gradients(): pl.pallas_call(edge_kernel, grid=(GROUPS,), in_specs=row_specs(EDGE) + [e...  2.47 us
    pallas_call x1, Pallas kernels, edge_scores(): pl.pallas_call(edge_scores_kernel, grid=(PAIRS,), in_specs=[tokens_spec(E...  2.43 us
    pallas_call x1, Pallas kernels, mid_scores(): pl.pallas_call(mid_scores_kernel, grid=(PAIRS,), in_specs=[tokens_spec(MI...  2.37 us
  transfers between devices with their start and end apart: 10, of which 5 were waited for; matrix products, arithmetic and copies ran while one was open for 0% of the time, Pallas kernels for 16%

profile of v4, /device:TPU:1, one launch (start us, length us, event | category | flops | bytes accessed | tf_op | source)
XLA Modules:
  0.0 72.5 jit_solution(8606341919167920856)
XLA Ops:
  0.6 2.2 %pack_queries.1 = (bf16[2,256,512]{2,1,0:T(8,128)(2,1)}, bf16[2,256,512]{2,1,0:T(8,128)(2,1)}) custom-call(bf16[32,16,512]{2,1,0:T(8,128)(2,1)} %q_ref.1, bf16[32,16,512]{2,1,0:T(8,128)(2,1)} %g_ref.1), custom_call_target="tpu_custom_call" | custom-call | bytes 3145728 | tf_op jit(solution)/shard_map/pack_queries/pallas_call | solution.py:87
  2.8 9.5 %collective-permute-start = (bf16[2,256,512]{2,1,0:T(8,128)(2,1)}, bf16[2,256,512]{2,1,0:T(8,128)(2,1)S(1)}, u32[]{:S(2)}, u32[]{:S(2)}) collective-permute-start(bf16[2,256,512]{2,1,0:T(8,128)(2,1)} %get-tuple-element.32.side_0.refs_0_), channel_id=1, source_target_pairs={{1,2},{2,1},{3,4},{4,3},{5,6},{6,5},{7,8},{8,7},{9,10},{10,9},{11,... | collective-permute-start | bytes 1572872 | tf_op jit(solution)/shard_map/ppermute | solution.py:543
  12.3 0.0 collective-permute-start.1
  12.3 1.0 %copy-done.4 = bf16[32,16,512]{2,1,0:T(8,128)(2,1)S(1)} copy-done((bf16[32,16,512]{2,1,0:T(8,128)(2,1)S(1)}, bf16[32,16,512]{2,1,0:T(8,128)(2,1)}, u32[]{:S(2)}) %copy-start.4) | copy-done | bytes 524312
  13.4 1.0 %copy-done.5 = bf16[32,16,512]{2,1,0:T(8,128)(2,1)S(1)} copy-done((bf16[32,16,512]{2,1,0:T(8,128)(2,1)S(1)}, bf16[32,16,512]{2,1,0:T(8,128)(2,1)}, u32[]{:S(2)}) %copy-start.5) | copy-done | bytes 524312
  14.4 1.6 %pack_keys.1 = (bf16[512,512]{1,0:T(8,128)(2,1)S(1)}, bf16[512,512]{1,0:T(8,128)(2,1)S(1)}, bf16[2,128,512]{2,1,0:T(8,128)(2,1)S(1)}, bf16[2,128,512]{2,1,0:T(8,128)(2,1)S(1)}) custom-call(bf16[32,16,512]{2,1,0:T(8,128)(2,1)S(1)} %copy-done.4, bf16[32,16,512]{2,1,0:T(8,128)(2,1)S(1)} %copy-done.5), custom_call_target="tpu_custom_call" | custom-call | bytes 3145728 | tf_op jit(solution)/shard_map/pack_keys/pallas_call | solution.py:116
  16.0 1.0 %collective-permute-start.2 = (bf16[2,128,512]{2,1,0:T(8,128)(2,1)S(1)}, bf16[2,128,512]{2,1,0:T(8,128)(2,1)S(1)}, u32[]{:S(2)}, u32[]{:S(2)}) collective-permute-start(bf16[2,128,512]{2,1,0:T(8,128)(2,1)S(1)} %get-tuple-element.36), channel_id=1, source_target_pairs={{0,32},{32,0},{64,96},{96,64},{1,33},{33,1},{65,97},{97,65},{2,34}... | collective-permute-start | bytes 786440 | tf_op jit(solution)/shard_map/ppermute | solution.py:535
  17.1 2.2 %collective-permute-start.3 = (bf16[2,128,512]{2,1,0:T(8,128)(2,1)S(1)}, bf16[2,128,512]{2,1,0:T(8,128)(2,1)S(1)}, u32[]{:S(2)}, u32[]{:S(2)}) collective-permute-start(bf16[2,128,512]{2,1,0:T(8,128)(2,1)S(1)} %get-tuple-element.37), channel_id=1, source_target_pairs={{32,64},{64,32},{33,65},{65,33},{34,66},{66,34},{35,67},{67,35},{3... | collective-permute-start | bytes 786440 | tf_op jit(solution)/shard_map/ppermute | solution.py:543
  19.3 0.0 copy-start
  19.3 1.0 %copy-done = bf16[2,256,512]{2,1,0:T(8,128)(2,1)S(1)} copy-done((bf16[2,256,512]{2,1,0:T(8,128)(2,1)S(1)}, bf16[2,256,512]{2,1,0:T(8,128)(2,1)}, u32[]{:S(2)}) %copy-start) | copy-done | bytes 524312
  20.3 1.0 %copy-done.2 = bf16[2,256,512]{2,1,0:T(8,128)(2,1)S(1)} copy-done((bf16[2,256,512]{2,1,0:T(8,128)(2,1)S(1)}, bf16[2,256,512]{2,1,0:T(8,128)(2,1)}, u32[]{:S(2)}) %copy-start.2) | copy-done | bytes 524312
  21.4 2.4 %mid_scores.1 = (f32[4,8,128]{2,1,0:T(8,128)S(1)}, f32[4,2,384,256]{3,2,1,0:T(8,128)S(1)}, f32[4,2,384,256]{3,2,1,0:T(8,128)S(1)}, bf16[512,512]{1,0:T(8,128)(2,1)S(1)}) custom-call(bf16[2,256,512]{2,1,0:T(8,128)(2,1)S(1)} %copy-done, bf16[2,256,512]{2,1,0:T(8,128)(2,1)S(1)} %copy-done.2, bf16[512,512]{1,0:T(8,128)(2,1)S(1)} %get-tuple-element.34.kd, ...), custom_call_target="tpu_custom_call" | custom-call | flops 2000000000 | bytes 1024 | tf_op jit(solution)/shard_map/mid_scores/pallas_call | solution.py:276
  23.8 10.6 %collective-permute-done.3.edge_b = bf16[2,128,512]{2,1,0:T(8,128)(2,1)S(1)} collective-permute-done((bf16[2,128,512]{2,1,0:T(8,128)(2,1)S(1)}, bf16[2,128,512]{2,1,0:T(8,128)(2,1)S(1)}, u32[]{:S(2)}, u32[]{:S(2)}) %collective-permute-start.3) | collective-permute-done | bytes 262176 | tf_op jit(solution)/shard_map/ppermute | solution.py:543
  34.4 2.4 %edge_scores.1 = (f32[4,8,128]{2,1,0:T(8,128)S(1)}, f32[4,2,384,256]{3,2,1,0:T(8,128)S(1)}, f32[4,2,384,256]{3,2,1,0:T(8,128)S(1)}) custom-call(bf16[2,256,512]{2,1,0:T(8,128)(2,1)S(1)} %copy-done, bf16[2,256,512]{2,1,0:T(8,128)(2,1)S(1)} %copy-done.2, bf16[512,512]{1,0:T(8,128)(2,1)S(1)} %get-tuple-element.34.kd, ...), custom_call_target="tpu_custom_call" | custom-call | flops 2000000000 | bytes 1024 | tf_op jit(solution)/shard_map/edge_scores/pallas_call | solution.py:289
  36.8 0.0 collective-permute-done.q_0.refs_2_
  36.8 0.0 collective-permute-done.1.q_1.refs_3_
  36.8 2.2 %halo_scores.1 = (f32[4,16,128]{2,1,0:T(8,128)S(1)}, f32[4,16,128]{2,1,0:T(8,128)S(1)}, f32[2,2,2,192,256]{4,3,2,1,0:T(8,128)S(1)}, f32[2,2,2,192,256]{4,3,2,1,0...) custom-call(bf16[2,256,512]{2,1,0:T(8,128)(2,1)S(1)} %collective-permute-done.q_0.refs_2_, ...), custom_call_target="tpu_custom_call" | custom-call | flops 2000000000 | bytes 1024 | tf_op jit(solution)/shard_map/halo_scores/pallas_call | solution.py:344
  39.0 7.3 %collective-permute-start.4 = (f32[4,16,128]{2,1,0:T(8,128)S(1)}, f32[4,16,128]{2,1,0:T(8,128)S(1)}, u32[]{:S(2)}, u32[]{:S(2)}) collective-permute-start(f32[4,16,128]{2,1,0:T(8,128)S(1)} %get-tuple-element.40.send_0.refs_4_), channel_id=1, source_target_pairs={{1,2},{2,1},{3,4},{4,3},{5,6},{6,5},{7,8},{8,7},{9,10},{10,9},{11,... | collective-permute-start | bytes 98312 | tf_op jit(solution)/shard_map/ppermute | solution.py:543
  46.3 0.5 turn_edges.1.edges_turned.refs_13_
  46.8 0.8 %collective-permute-done.4.recv_0.refs_6_ = f32[4,16,128]{2,1,0:T(8,128)S(1)} collective-permute-done((f32[4,16,128]{2,1,0:T(8,128)S(1)}, f32[4,16,128]{2,1,0:T(8,128)S(1)}, u32[]{:S(2)}, u32[]{:S(2)}) %collective-permute-start.4) | collective-permute-done | bytes 32800 | tf_op jit(solution)/shard_map/ppermute | solution.py:543
  47.7 3.0 %collective-permute-done.5.recv_1.refs_7_ = f32[4,16,128]{2,1,0:T(8,128)S(1)} collective-permute-done((f32[4,16,128]{2,1,0:T(8,128)S(1)}, f32[4,16,128]{2,1,0:T(8,128)S(1)}, u32[]{:S(2)}, u32[]{:S(2)}) %collective-permute-start.5) | collective-permute-done | bytes 32800 | tf_op jit(solution)/shard_map/ppermute | solution.py:535
  50.6 1.2 %halo_queries.1 = (bf16[256,512]{1,0:T(8,128)(2,1)S(1)}, bf16[256,512]{1,0:T(8,128)(2,1)S(1)}) custom-call(f32[4,16,128]{2,1,0:T(8,128)S(1)} %get-tuple-element.40.send_0.refs_4_, f32[4,16,128]{2,1,0:T(8,128)S(1)} %get-tuple-element.41.send_1.refs_5_, f32[4,16,128]{2,1,0:T(8,128)S(1)} %collective-permute-done.4.recv_0.refs_6_, ...), custom_call_target="tpu_custom_call" | custom-call | flops 2000000000 | bytes 1024 | tf_op jit(solution)/shard_map/halo_queries/pallas_call | solution.py:389
  51.9 4.3 %collective-permute-start.6 = (bf16[256,512]{1,0:T(8,128)(2,1)S(1)}, bf16[256,512]{1,0:T(8,128)(2,1)S(1)}, u32[]{:S(2)}, u32[]{:S(2)}) collective-permute-start(bf16[256,512]{1,0:T(8,128)(2,1)S(1)} %get-tuple-element.49.refs_14_.refs_13_), channel_id=1, source_target_pairs={{1,2},{2,1},{3,4},{4,3},{5,6},{6,5},{7,8},{8,7},{9,10},{10,9},{11,... | collective-permute-start | bytes 786440 | tf_op jit(solution)/shard_map/ppermute | solution.py:543
  56.2 2.5 %edge_gradients.1 = (f32[2,128,512]{2,1,0:T(8,128)S(1)}, f32[512,512]{1,0:T(8,128)S(1)}, f32[512,512]{1,0:T(8,128)S(1)}, bf16[2,128,512]{2,1,0:T(8,128)(2,1)S(1)}, bf16[2,128,512]{2,1,0:T(8,128)(2,1)S(1)}) custom-call(bf16[2,256,512]{2,1,0:T(8,128)(2,1)S(1)} %copy-done.1, bf16[2,256,512]{2,1,0:T(8,128)(2,1)S(1)} %copy-done.3, ...), custom_call_target="tpu_custom_call" | custom-call | flops 3000000000 | bytes 1024 | tf_op jit(solution)/shard_map/edge_gradients/pallas_call | solution.py:466
  58.7 0.1 collective-permute-start.8
  58.8 2.9 %collective-permute-start.9 = (bf16[2,128,512]{2,1,0:T(8,128)(2,1)S(1)}, bf16[2,128,512]{2,1,0:T(8,128)(2,1)S(1)}, u32[]{:S(2)}, u32[]{:S(2)}) collective-permute-start(bf16[2,128,512]{2,1,0:T(8,128)(2,1)S(1)} %get-tuple-element.60), channel_id=1, source_target_pairs={{32,64},{64,32},{33,65},{65,33},{34,66},{66,34},{35,67},{67,35},{3... | collective-permute-start | bytes 786440 | tf_op jit(solution)/shard_map/ppermute | solution.py:543
  61.6 0.3 collective-permute-start.7
  61.9 2.5 %mid_gradients.1 = (f32[2,128,512]{2,1,0:T(8,128)S(1)}, f32[512,512]{1,0:T(8,128)S(1)}, f32[512,512]{1,0:T(8,128)S(1)}) custom-call(bf16[2,256,512]{2,1,0:T(8,128)(2,1)S(1)} %copy-done.1, bf16[2,256,512]{2,1,0:T(8,128)(2,1)S(1)} %copy-done.3, bf16[2,256,512]{2,1,0:T(8,128)(2,1)S(1)} %collective-permute-done.q_0.refs_2_, ...), custom_call_target="tpu_custom_call" | custom-call | flops 3000000000 | bytes 1024 | tf_op jit(solution)/shard_map/mid_gradients/pallas_call | solution.py:479
  64.5 0.0 collective-permute-done.8.from_a
  64.5 2.9 %collective-permute-done.9.from_b = bf16[2,128,512]{2,1,0:T(8,128)(2,1)S(1)} collective-permute-done((bf16[2,128,512]{2,1,0:T(8,128)(2,1)S(1)}, bf16[2,128,512]{2,1,0:T(8,128)(2,1)S(1)}, u32[]{:S(2)}, u32[]{:S(2)}) %collective-permute-start.9) | collective-permute-done | bytes 262176 | tf_op jit(solution)/shard_map/ppermute | solution.py:543
  67.4 3.8 %collective-permute-done.7.dq_1 = bf16[256,512]{1,0:T(8,128)(2,1)S(1)} collective-permute-done((bf16[256,512]{1,0:T(8,128)(2,1)S(1)}, bf16[256,512]{1,0:T(8,128)(2,1)S(1)}, u32[]{:S(2)}, u32[]{:S(2)}) %collective-permute-start.7) | collective-permute-done | bytes 262176 | tf_op jit(solution)/shard_map/ppermute | solution.py:535
  71.2 1.3 %finish.1 = (bf16[32,16,512]{2,1,0:T(8,128)(2,1)}, bf16[32,16,512]{2,1,0:T(8,128)(2,1)}, bf16[32,16,512]{2,1,0:T(8,128)(2,1)}) custom-call(f32[2,128,512]{2,1,0:T(8,128)S(1)} %get-tuple-element.50.dq_edge, f32[2,128,512]{2,1,0:T(8,128)S(1)} %get-tuple-element.55.dq_mid, f32[512,512]{1,0:T(8,128)S(1)} %get-tuple-element.56.dk, ...), custom_call_target="tpu_custom_call" | custom-call | bytes 1024 | tf_op jit(solution)/shard_map/finish/pallas_call | solution.py:523
  (10 shorter events, 0.0 us)
Async XLA Ops:
  2.8 34.0 %collective-permute-start = (bf16[2,256,512]{2,1,0:T(8,128)(2,1)}, bf16[2,256,512]{2,1,0:T(8,128)(2,1)S(1)}, u32[]{:S(2)}, u32[]{:S(2)}) collective-permute-start(bf16[2,256,512]{2,1,0:T(8,128)(2,1)} %get-tuple-element.32.side_0.refs_0_), channel_id=1, source_target_pairs={{1,2},{2,1},{3,4},{4,3},{5,6},{6,5},{7,8},{8,7},{9,10},{10,9},{11,... | collective-permute-start | bytes 1572872 | tf_op jit(solution)/shard_map/ppermute | solution.py:543
  12.3 24.5 %collective-permute-start.1 = (bf16[2,256,512]{2,1,0:T(8,128)(2,1)}, bf16[2,256,512]{2,1,0:T(8,128)(2,1)S(1)}, u32[]{:S(2)}, u32[]{:S(2)}) collective-permute-start(bf16[2,256,512]{2,1,0:T(8,128)(2,1)} %get-tuple-element.33.side_1.refs_1_), channel_id=1, source_target_pairs={{0,1},{1,0},{2,3},{3,2},{4,5},{5,4},{6,7},{7,6},{8,9},{9,8},{10,11... | collective-permute-start | bytes 1572872 | tf_op jit(solution)/shard_map/ppermute | solution.py:535
  12.3 1.0 %copy-start.4 = (bf16[32,16,512]{2,1,0:T(8,128)(2,1)S(1)}, bf16[32,16,512]{2,1,0:T(8,128)(2,1)}, u32[]{:S(2)}) copy-start(bf16[32,16,512]{2,1,0:T(8,128)(2,1)} %k_ref.1) | copy-start | bytes 1572868
  13.4 1.0 %copy-start.5 = (bf16[32,16,512]{2,1,0:T(8,128)(2,1)S(1)}, bf16[32,16,512]{2,1,0:T(8,128)(2,1)}, u32[]{:S(2)}) copy-start(bf16[32,16,512]{2,1,0:T(8,128)(2,1)} %v_ref.1) | copy-start | bytes 1572868
  16.0 7.7 %collective-permute-start.2 = (bf16[2,128,512]{2,1,0:T(8,128)(2,1)S(1)}, bf16[2,128,512]{2,1,0:T(8,128)(2,1)S(1)}, u32[]{:S(2)}, u32[]{:S(2)}) collective-permute-start(bf16[2,128,512]{2,1,0:T(8,128)(2,1)S(1)} %get-tuple-element.36), channel_id=1, source_target_pairs={{0,32},{32,0},{64,96},{96,64},{1,33},{33,1},{65,97},{97,65},{2,34}... | collective-permute-start | bytes 786440 | tf_op jit(solution)/shard_map/ppermute | solution.py:535
  17.1 17.3 %collective-permute-start.3 = (bf16[2,128,512]{2,1,0:T(8,128)(2,1)S(1)}, bf16[2,128,512]{2,1,0:T(8,128)(2,1)S(1)}, u32[]{:S(2)}, u32[]{:S(2)}) collective-permute-start(bf16[2,128,512]{2,1,0:T(8,128)(2,1)S(1)} %get-tuple-element.37), channel_id=1, source_target_pairs={{32,64},{64,32},{33,65},{65,33},{34,66},{66,34},{35,67},{67,35},{3... | collective-permute-start | bytes 786440 | tf_op jit(solution)/shard_map/ppermute | solution.py:543
  19.3 1.0 %copy-start = (bf16[2,256,512]{2,1,0:T(8,128)(2,1)S(1)}, bf16[2,256,512]{2,1,0:T(8,128)(2,1)}, u32[]{:S(2)}) copy-start(bf16[2,256,512]{2,1,0:T(8,128)(2,1)} %get-tuple-element.32.side_0.refs_0_) | copy-start | bytes 1572868
  20.3 1.0 %copy-start.2 = (bf16[2,256,512]{2,1,0:T(8,128)(2,1)S(1)}, bf16[2,256,512]{2,1,0:T(8,128)(2,1)}, u32[]{:S(2)}) copy-start(bf16[2,256,512]{2,1,0:T(8,128)(2,1)} %get-tuple-element.33.side_1.refs_1_) | copy-start | bytes 1572868
  39.0 8.6 %collective-permute-start.4 = (f32[4,16,128]{2,1,0:T(8,128)S(1)}, f32[4,16,128]{2,1,0:T(8,128)S(1)}, u32[]{:S(2)}, u32[]{:S(2)}) collective-permute-start(f32[4,16,128]{2,1,0:T(8,128)S(1)} %get-tuple-element.40.send_0.refs_4_), channel_id=1, source_target_pairs={{1,2},{2,1},{3,4},{4,3},{5,6},{6,5},{7,8},{8,7},{9,10},{10,9},{11,... | collective-permute-start | bytes 98312 | tf_op jit(solution)/shard_map/ppermute | solution.py:543
  46.3 4.3 %collective-permute-start.5 = (f32[4,16,128]{2,1,0:T(8,128)S(1)}, f32[4,16,128]{2,1,0:T(8,128)S(1)}, u32[]{:S(2)}, u32[]{:S(2)}) collective-permute-start(f32[4,16,128]{2,1,0:T(8,128)S(1)} %get-tuple-element.41.send_1.refs_5_), channel_id=1, source_target_pairs={{0,1},{1,0},{2,3},{3,2},{4,5},{5,4},{6,7},{7,6},{8,9},{9,8},{10,11... | collective-permute-start | bytes 98312 | tf_op jit(solution)/shard_map/ppermute | solution.py:535
  50.6 5.6 %copy-start.1 = (bf16[2,256,512]{2,1,0:T(8,128)(2,1)S(1)}, bf16[2,256,512]{2,1,0:T(8,128)(2,1)}, u32[]{:S(2)}) copy-start(bf16[2,256,512]{2,1,0:T(8,128)(2,1)} %get-tuple-element.32.side_0.refs_0_) | copy-start | bytes 1572868
  50.6 5.6 %copy-start.3 = (bf16[2,256,512]{2,1,0:T(8,128)(2,1)S(1)}, bf16[2,256,512]{2,1,0:T(8,128)(2,1)}, u32[]{:S(2)}) copy-start(bf16[2,256,512]{2,1,0:T(8,128)(2,1)} %get-tuple-element.33.side_1.refs_1_) | copy-start | bytes 1572868
  51.9 19.3 %collective-permute-start.6 = (bf16[256,512]{1,0:T(8,128)(2,1)S(1)}, bf16[256,512]{1,0:T(8,128)(2,1)S(1)}, u32[]{:S(2)}, u32[]{:S(2)}) collective-permute-start(bf16[256,512]{1,0:T(8,128)(2,1)S(1)} %get-tuple-element.49.refs_14_.refs_13_), channel_id=1, source_target_pairs={{1,2},{2,1},{3,4},{4,3},{5,6},{6,5},{7,8},{8,7},{9,10},{10,9},{11,... | collective-permute-start | bytes 786440 | tf_op jit(solution)/shard_map/ppermute | solution.py:543
  58.7 5.8 %collective-permute-start.8 = (bf16[2,128,512]{2,1,0:T(8,128)(2,1)S(1)}, bf16[2,128,512]{2,1,0:T(8,128)(2,1)S(1)}, u32[]{:S(2)}, u32[]{:S(2)}) collective-permute-start(bf16[2,128,512]{2,1,0:T(8,128)(2,1)S(1)} %get-tuple-element.59), channel_id=1, source_target_pairs={{0,32},{32,0},{64,96},{96,64},{1,33},{33,1},{65,97},{97,65},{2,34}... | collective-permute-start | bytes 786440 | tf_op jit(solution)/shard_map/ppermute | solution.py:535
  58.8 8.7 %collective-permute-start.9 = (bf16[2,128,512]{2,1,0:T(8,128)(2,1)S(1)}, bf16[2,128,512]{2,1,0:T(8,128)(2,1)S(1)}, u32[]{:S(2)}, u32[]{:S(2)}) collective-permute-start(bf16[2,128,512]{2,1,0:T(8,128)(2,1)S(1)} %get-tuple-element.60), channel_id=1, source_target_pairs={{32,64},{64,32},{33,65},{65,33},{34,66},{66,34},{35,67},{67,35},{3... | collective-permute-start | bytes 786440 | tf_op jit(solution)/shard_map/ppermute | solution.py:543
  61.6 9.6 %collective-permute-start.7 = (bf16[256,512]{1,0:T(8,128)(2,1)S(1)}, bf16[256,512]{1,0:T(8,128)(2,1)S(1)}, u32[]{:S(2)}, u32[]{:S(2)}) collective-permute-start(bf16[256,512]{1,0:T(8,128)(2,1)S(1)} %get-tuple-element.58), channel_id=1, source_target_pairs={{0,1},{1,0},{2,3},{3,2},{4,5},{5,4},{6,7},{7,6},{8,9},{9,8},{10,11... | collective-permute-start | bytes 786440 | tf_op jit(solution)/shard_map/ppermute | solution.py:535

commit v5 on v4

--- a/solution.py
+++ b/solution.py
@@ -435,7 +435,7 @@
 
 
 def edge_kernel(*refs):
-    operands, (_, dq_ref, dk_ref, dv_ref, out_a, out_b) = refs[:14], refs[14:]
+    operands, (_, _, dq_ref, dk_ref, dv_ref, out_a, out_b) = refs[:14], refs[14:]
     upper, lower = row_gradients(EDGE_ROWS, *operands, dq_ref)
     for which, (out, scale) in enumerate(((dk_ref, SCALE), (dv_ref, 1.0))):
         top, bottom = upper[which] * scale, lower[which] * scale
@@ -446,7 +446,7 @@
 
 
 def mid_kernel(*refs):
-    operands, (_, dk_in, dv_in, dq_ref, dk_ref, dv_ref) = refs[:13], refs[13:]
+    operands, (dk_in, dv_in, dq_ref, dk_ref, dv_ref) = refs[:13], refs[13:]
     upper, lower = row_gradients(MID_ROWS, *operands, None, dq_ref)
     for which, (sums, out, scale) in enumerate(((dk_in, dk_ref, SCALE), (dv_in, dv_ref, 1.0))):
         out[0:PAIR] = sums[0:PAIR] + upper[which][:PAIR] * scale
@@ -466,7 +466,7 @@
     return pl.pallas_call(
         edge_kernel,
         grid=(GROUPS,),
-        in_specs=row_specs(EDGE) + [edge_turned_wide, any_spec],
+        in_specs=row_specs(EDGE) + [edge_turned_wide, any_spec, any_spec],
         out_specs=GRAD_SPECS + [edge_wide] * 2,
         out_shape=GRAD_SHAPES + [struct((2, PAIR, FEAT), BF16)] * 2,
         compiler_params=params(),
@@ -479,7 +479,7 @@
     return pl.pallas_call(
         mid_kernel,
         grid=(GROUPS,),
-        in_specs=row_specs(MID) + [any_spec] + [keys_wide] * 2,
+        in_specs=row_specs(MID) + [keys_wide] * 2,
         out_specs=GRAD_SPECS,
         out_shape=GRAD_SHAPES,
         compiler_params=params(),
@@ -564,9 +564,9 @@
     halo_dq = halo_queries(*stats, s_edge, d_edge, s_mid, d_mid, turned, edges_turned)
     dq_parts = over_lon(*halo_dq)
     shared = (*sides, *halos, *stats)
-    dq_edge, dk, dv, out_a, out_b = edge_gradients(*shared, *edge_own, s_edge, d_edge, turned, edges_turned, halo_dq[0])
+    dq_edge, dk, dv, out_a, out_b = edge_gradients(*shared, *edge_own, s_edge, d_edge, turned, edges_turned, *halo_dq)
     key_parts = over_lat(out_a, out_b)
-    dq_mid, dk, dv = mid_gradients(*shared, *mid_own, s_mid, d_mid, turned, halo_dq[0], dk, dv)
+    dq_mid, dk, dv = mid_gradients(*shared, *mid_own, s_mid, d_mid, turned, dk, dv)
     return tuple(finish(dq_edge, dq_mid, dk, dv, *dq_parts, *key_parts))
 
 

time: 72.8 us -> 68.7 us (0.944)
  waiting for transfers between devices: 21.1 us -> 17.1 us
    ppermute x5, waiting for transfers between devices: 6.74 us -> 3.21 us  [swap_a(): lax.ppermute(x, axis, [(i, i ^ 1) for i in range(lax.axis_size(axis))])]
  transfers between devices with their start and end apart: 10 -> 10, of which waited for: 5 -> 5; matrix products, arithmetic and copies ran while one was open for 0% -> 0% of each run, Pallas kernels for 16% -> 18%
where the time goes in v5:
time: 68.7 us; the launch traced here: 68.3 us
  starting transfers between devices  27.4 us (40%)
  Pallas kernels  18.8 us (27%)
  waiting for transfers between devices  17.1 us (25%)
  local copies, waits for them, and re-layouts  4.17 us (6%)
  between operations  0.78 us (1%)
    ppermute x5, starting transfers between devices, swap_b(): return lax.ppermute(x, axis, pairs)  26.2 us
    ppermute x5, waiting for transfers between devices, swap_b(): return lax.ppermute(x, axis, pairs)  13.9 us
    unnamed x12, local copies, waits for them, and re-layouts  4.17 us
    ppermute x5, waiting for transfers between devices, swap_a(): lax.ppermute(x, axis, [(i, i ^ 1) for i in range(lax.axis_size(axis))])  3.21 us
    pallas_call x1, Pallas kernels, mid_gradients(): pl.pallas_call(mid_kernel, grid=(GROUPS,), in_specs=row_specs(MID) + [key...  2.57 us
    pallas_call x1, Pallas kernels, edge_gradients(): pl.pallas_call(edge_kernel, grid=(GROUPS,), in_specs=row_specs(EDGE) + [e...  2.5 us
    pallas_call x1, Pallas kernels, edge_scores(): pl.pallas_call(edge_scores_kernel, grid=(PAIRS,), in_specs=[tokens_spec(E...  2.43 us
    pallas_call x1, Pallas kernels, mid_scores(): pl.pallas_call(mid_scores_kernel, grid=(PAIRS,), in_specs=[tokens_spec(MI...  2.37 us
  transfers between devices with their start and end apart: 10, of which 5 were waited for; matrix products, arithmetic and copies ran while one was open for 0% of the time, Pallas kernels for 18%

profile of v5, /device:TPU:1, one launch (start us, length us, event | category | flops | bytes accessed | tf_op | source)
XLA Modules:
  0.0 68.3 jit_solution(15164681705638978207)
XLA Ops:
  0.6 2.2 %pack_queries.1 = (bf16[2,256,512]{2,1,0:T(8,128)(2,1)}, bf16[2,256,512]{2,1,0:T(8,128)(2,1)}) custom-call(bf16[32,16,512]{2,1,0:T(8,128)(2,1)} %q_ref.1, bf16[32,16,512]{2,1,0:T(8,128)(2,1)} %g_ref.1), custom_call_target="tpu_custom_call" | custom-call | bytes 3145728 | tf_op jit(solution)/shard_map/pack_queries/pallas_call | solution.py:87
  2.8 9.5 %collective-permute-start = (bf16[2,256,512]{2,1,0:T(8,128)(2,1)}, bf16[2,256,512]{2,1,0:T(8,128)(2,1)S(1)}, u32[]{:S(2)}, u32[]{:S(2)}) collective-permute-start(bf16[2,256,512]{2,1,0:T(8,128)(2,1)} %get-tuple-element.32.side_0.refs_0_), channel_id=1, source_target_pairs={{1,2},{2,1},{3,4},{4,3},{5,6},{6,5},{7,8},{8,7},{9,10},{10,9},{11,... | collective-permute-start | bytes 1572872 | tf_op jit(solution)/shard_map/ppermute | solution.py:543
  12.3 0.0 collective-permute-start.1
  12.3 1.0 %copy-done.4 = bf16[32,16,512]{2,1,0:T(8,128)(2,1)S(1)} copy-done((bf16[32,16,512]{2,1,0:T(8,128)(2,1)S(1)}, bf16[32,16,512]{2,1,0:T(8,128)(2,1)}, u32[]{:S(2)}) %copy-start.4) | copy-done | bytes 524312
  13.4 1.0 %copy-done.5 = bf16[32,16,512]{2,1,0:T(8,128)(2,1)S(1)} copy-done((bf16[32,16,512]{2,1,0:T(8,128)(2,1)S(1)}, bf16[32,16,512]{2,1,0:T(8,128)(2,1)}, u32[]{:S(2)}) %copy-start.5) | copy-done | bytes 524312
  14.4 1.6 %pack_keys.1 = (bf16[512,512]{1,0:T(8,128)(2,1)S(1)}, bf16[512,512]{1,0:T(8,128)(2,1)S(1)}, bf16[2,128,512]{2,1,0:T(8,128)(2,1)S(1)}, bf16[2,128,512]{2,1,0:T(8,128)(2,1)S(1)}) custom-call(bf16[32,16,512]{2,1,0:T(8,128)(2,1)S(1)} %copy-done.4, bf16[32,16,512]{2,1,0:T(8,128)(2,1)S(1)} %copy-done.5), custom_call_target="tpu_custom_call" | custom-call | bytes 3145728 | tf_op jit(solution)/shard_map/pack_keys/pallas_call | solution.py:116
  16.0 1.0 %collective-permute-start.2 = (bf16[2,128,512]{2,1,0:T(8,128)(2,1)S(1)}, bf16[2,128,512]{2,1,0:T(8,128)(2,1)S(1)}, u32[]{:S(2)}, u32[]{:S(2)}) collective-permute-start(bf16[2,128,512]{2,1,0:T(8,128)(2,1)S(1)} %get-tuple-element.36), channel_id=1, source_target_pairs={{0,32},{32,0},{64,96},{96,64},{1,33},{33,1},{65,97},{97,65},{2,34}... | collective-permute-start | bytes 786440 | tf_op jit(solution)/shard_map/ppermute | solution.py:535
  17.1 2.2 %collective-permute-start.3 = (bf16[2,128,512]{2,1,0:T(8,128)(2,1)S(1)}, bf16[2,128,512]{2,1,0:T(8,128)(2,1)S(1)}, u32[]{:S(2)}, u32[]{:S(2)}) collective-permute-start(bf16[2,128,512]{2,1,0:T(8,128)(2,1)S(1)} %get-tuple-element.37), channel_id=1, source_target_pairs={{32,64},{64,32},{33,65},{65,33},{34,66},{66,34},{35,67},{67,35},{3... | collective-permute-start | bytes 786440 | tf_op jit(solution)/shard_map/ppermute | solution.py:543
  19.3 0.0 copy-start
  19.3 1.0 %copy-done = bf16[2,256,512]{2,1,0:T(8,128)(2,1)S(1)} copy-done((bf16[2,256,512]{2,1,0:T(8,128)(2,1)S(1)}, bf16[2,256,512]{2,1,0:T(8,128)(2,1)}, u32[]{:S(2)}) %copy-start) | copy-done | bytes 524312
  20.3 1.0 %copy-done.2 = bf16[2,256,512]{2,1,0:T(8,128)(2,1)S(1)} copy-done((bf16[2,256,512]{2,1,0:T(8,128)(2,1)S(1)}, bf16[2,256,512]{2,1,0:T(8,128)(2,1)}, u32[]{:S(2)}) %copy-start.2) | copy-done | bytes 524312
  21.4 2.4 %mid_scores.1 = (f32[4,8,128]{2,1,0:T(8,128)S(1)}, f32[4,2,384,256]{3,2,1,0:T(8,128)S(1)}, f32[4,2,384,256]{3,2,1,0:T(8,128)S(1)}, bf16[512,512]{1,0:T(8,128)(2,1)S(1)}) custom-call(bf16[2,256,512]{2,1,0:T(8,128)(2,1)S(1)} %copy-done, bf16[2,256,512]{2,1,0:T(8,128)(2,1)S(1)} %copy-done.2, bf16[512,512]{1,0:T(8,128)(2,1)S(1)} %get-tuple-element.34.kd, ...), custom_call_target="tpu_custom_call" | custom-call | flops 2000000000 | bytes 1024 | tf_op jit(solution)/shard_map/mid_scores/pallas_call | solution.py:276
  23.7 0.0 collective-permute-done.2.edge_a
  23.8 10.6 %collective-permute-done.3.edge_b = bf16[2,128,512]{2,1,0:T(8,128)(2,1)S(1)} collective-permute-done((bf16[2,128,512]{2,1,0:T(8,128)(2,1)S(1)}, bf16[2,128,512]{2,1,0:T(8,128)(2,1)S(1)}, u32[]{:S(2)}, u32[]{:S(2)}) %collective-permute-start.3) | collective-permute-done | bytes 262176 | tf_op jit(solution)/shard_map/ppermute | solution.py:543
  34.4 2.4 %edge_scores.1 = (f32[4,8,128]{2,1,0:T(8,128)S(1)}, f32[4,2,384,256]{3,2,1,0:T(8,128)S(1)}, f32[4,2,384,256]{3,2,1,0:T(8,128)S(1)}) custom-call(bf16[2,256,512]{2,1,0:T(8,128)(2,1)S(1)} %copy-done, bf16[2,256,512]{2,1,0:T(8,128)(2,1)S(1)} %copy-done.2, bf16[512,512]{1,0:T(8,128)(2,1)S(1)} %get-tuple-element.34.kd, ...), custom_call_target="tpu_custom_call" | custom-call | flops 2000000000 | bytes 1024 | tf_op jit(solution)/shard_map/edge_scores/pallas_call | solution.py:289
  36.8 0.0 collective-permute-done.q_0.refs_2_
  36.8 0.0 collective-permute-done.1.q_1.refs_3_
  36.8 2.2 %halo_scores.1 = (f32[4,16,128]{2,1,0:T(8,128)S(1)}, f32[4,16,128]{2,1,0:T(8,128)S(1)}, f32[2,2,2,192,256]{4,3,2,1,0:T(8,128)S(1)}, f32[2,2,2,192,256]{4,3,2,1,0...) custom-call(bf16[2,256,512]{2,1,0:T(8,128)(2,1)S(1)} %collective-permute-done.q_0.refs_2_, ...), custom_call_target="tpu_custom_call" | custom-call | flops 2000000000 | bytes 1024 | tf_op jit(solution)/shard_map/halo_scores/pallas_call | solution.py:344
  39.0 7.3 %collective-permute-start.4 = (f32[4,16,128]{2,1,0:T(8,128)S(1)}, f32[4,16,128]{2,1,0:T(8,128)S(1)}, u32[]{:S(2)}, u32[]{:S(2)}) collective-permute-start(f32[4,16,128]{2,1,0:T(8,128)S(1)} %get-tuple-element.40.send_0.refs_4_), channel_id=1, source_target_pairs={{1,2},{2,1},{3,4},{4,3},{5,6},{6,5},{7,8},{8,7},{9,10},{10,9},{11,... | collective-permute-start | bytes 98312 | tf_op jit(solution)/shard_map/ppermute | solution.py:543
  46.3 0.5 turn_edges.1.edges_turned.refs_13_
  46.8 0.8 %collective-permute-done.4.recv_0.refs_6_ = f32[4,16,128]{2,1,0:T(8,128)S(1)} collective-permute-done((f32[4,16,128]{2,1,0:T(8,128)S(1)}, f32[4,16,128]{2,1,0:T(8,128)S(1)}, u32[]{:S(2)}, u32[]{:S(2)}) %collective-permute-start.4) | collective-permute-done | bytes 32800 | tf_op jit(solution)/shard_map/ppermute | solution.py:543
  47.7 3.0 %collective-permute-done.5.recv_1.refs_7_ = f32[4,16,128]{2,1,0:T(8,128)S(1)} collective-permute-done((f32[4,16,128]{2,1,0:T(8,128)S(1)}, f32[4,16,128]{2,1,0:T(8,128)S(1)}, u32[]{:S(2)}, u32[]{:S(2)}) %collective-permute-start.5) | collective-permute-done | bytes 32800 | tf_op jit(solution)/shard_map/ppermute | solution.py:535
  50.6 1.2 %halo_queries.1 = (bf16[256,512]{1,0:T(8,128)(2,1)S(1)}, bf16[256,512]{1,0:T(8,128)(2,1)S(1)}) custom-call(f32[4,16,128]{2,1,0:T(8,128)S(1)} %get-tuple-element.40.send_0.refs_4_, f32[4,16,128]{2,1,0:T(8,128)S(1)} %get-tuple-element.41.send_1.refs_5_, f32[4,16,128]{2,1,0:T(8,128)S(1)} %collective-permute-done.4.recv_0.refs_6_, ...), custom_call_target="tpu_custom_call" | custom-call | flops 2000000000 | bytes 1024 | tf_op jit(solution)/shard_map/halo_queries/pallas_call | solution.py:389
  51.9 4.3 %collective-permute-start.6 = (bf16[256,512]{1,0:T(8,128)(2,1)S(1)}, bf16[256,512]{1,0:T(8,128)(2,1)S(1)}, u32[]{:S(2)}, u32[]{:S(2)}) collective-permute-start(bf16[256,512]{1,0:T(8,128)(2,1)S(1)} %get-tuple-element.49.refs_14_), channel_id=1, source_target_pairs={{1,2},{2,1},{3,4},{4,3},{5,6},{6,5},{7,8},{8,7},{9,10},{10,9},{11,... | collective-permute-start | bytes 786440 | tf_op jit(solution)/shard_map/ppermute | solution.py:543
  56.2 0.0 collective-permute-start.7
  56.2 2.5 %edge_gradients.1 = (f32[2,128,512]{2,1,0:T(8,128)S(1)}, f32[512,512]{1,0:T(8,128)S(1)}, f32[512,512]{1,0:T(8,128)S(1)}, bf16[2,128,512]{2,1,0:T(8,128)(2,1)S(1)}, bf16[2,128,512]{2,1,0:T(8,128)(2,1)S(1)}) custom-call(bf16[2,256,512]{2,1,0:T(8,128)(2,1)S(1)} %copy-done.1, bf16[2,256,512]{2,1,0:T(8,128)(2,1)S(1)} %copy-done.3, ...), custom_call_target="tpu_custom_call" | custom-call | flops 3000000000 | bytes 1024 | tf_op jit(solution)/shard_map/edge_gradients/pallas_call | solution.py:466
  58.7 0.1 collective-permute-start.8
  58.8 2.9 %collective-permute-start.9 = (bf16[2,128,512]{2,1,0:T(8,128)(2,1)S(1)}, bf16[2,128,512]{2,1,0:T(8,128)(2,1)S(1)}, u32[]{:S(2)}, u32[]{:S(2)}) collective-permute-start(bf16[2,128,512]{2,1,0:T(8,128)(2,1)S(1)} %get-tuple-element.60), channel_id=1, source_target_pairs={{32,64},{64,32},{33,65},{65,33},{34,66},{66,34},{35,67},{67,35},{3... | collective-permute-start | bytes 786440 | tf_op jit(solution)/shard_map/ppermute | solution.py:543
  61.7 2.6 %mid_gradients.1 = (f32[2,128,512]{2,1,0:T(8,128)S(1)}, f32[512,512]{1,0:T(8,128)S(1)}, f32[512,512]{1,0:T(8,128)S(1)}) custom-call(bf16[2,256,512]{2,1,0:T(8,128)(2,1)S(1)} %copy-done.1, bf16[2,256,512]{2,1,0:T(8,128)(2,1)S(1)} %copy-done.3, bf16[2,256,512]{2,1,0:T(8,128)(2,1)S(1)} %collective-permute-done.q_0.refs_2_, ...), custom_call_target="tpu_custom_call" | custom-call | flops 3000000000 | bytes 1024 | tf_op jit(solution)/shard_map/mid_gradients/pallas_call | solution.py:479
  64.3 2.5 %collective-permute-done.9.from_b = bf16[2,128,512]{2,1,0:T(8,128)(2,1)S(1)} collective-permute-done((bf16[2,128,512]{2,1,0:T(8,128)(2,1)S(1)}, bf16[2,128,512]{2,1,0:T(8,128)(2,1)S(1)}, u32[]{:S(2)}, u32[]{:S(2)}) %collective-permute-start.9) | collective-permute-done | bytes 262176 | tf_op jit(solution)/shard_map/ppermute | solution.py:543
  66.8 0.2 collective-permute-done.7.dq_1
  67.0 1.3 %finish.1 = (bf16[32,16,512]{2,1,0:T(8,128)(2,1)}, bf16[32,16,512]{2,1,0:T(8,128)(2,1)}, bf16[32,16,512]{2,1,0:T(8,128)(2,1)}) custom-call(f32[2,128,512]{2,1,0:T(8,128)S(1)} %get-tuple-element.51.dq_edge, f32[2,128,512]{2,1,0:T(8,128)S(1)} %get-tuple-element.56.dq_mid, f32[512,512]{1,0:T(8,128)S(1)} %get-tuple-element.57.dk, ...), custom_call_target="tpu_custom_call" | custom-call | bytes 1024 | tf_op jit(solution)/shard_map/finish/pallas_call | solution.py:523
  (10 shorter events, 0.0 us)
Async XLA Ops:
  2.8 34.0 %collective-permute-start = (bf16[2,256,512]{2,1,0:T(8,128)(2,1)}, bf16[2,256,512]{2,1,0:T(8,128)(2,1)S(1)}, u32[]{:S(2)}, u32[]{:S(2)}) collective-permute-start(bf16[2,256,512]{2,1,0:T(8,128)(2,1)} %get-tuple-element.32.side_0.refs_0_), channel_id=1, source_target_pairs={{1,2},{2,1},{3,4},{4,3},{5,6},{6,5},{7,8},{8,7},{9,10},{10,9},{11,... | collective-permute-start | bytes 1572872 | tf_op jit(solution)/shard_map/ppermute | solution.py:543
  12.3 24.5 %collective-permute-start.1 = (bf16[2,256,512]{2,1,0:T(8,128)(2,1)}, bf16[2,256,512]{2,1,0:T(8,128)(2,1)S(1)}, u32[]{:S(2)}, u32[]{:S(2)}) collective-permute-start(bf16[2,256,512]{2,1,0:T(8,128)(2,1)} %get-tuple-element.33.side_1.refs_1_), channel_id=1, source_target_pairs={{0,1},{1,0},{2,3},{3,2},{4,5},{5,4},{6,7},{7,6},{8,9},{9,8},{10,11... | collective-permute-start | bytes 1572872 | tf_op jit(solution)/shard_map/ppermute | solution.py:535
  12.3 1.0 %copy-start.4 = (bf16[32,16,512]{2,1,0:T(8,128)(2,1)S(1)}, bf16[32,16,512]{2,1,0:T(8,128)(2,1)}, u32[]{:S(2)}) copy-start(bf16[32,16,512]{2,1,0:T(8,128)(2,1)} %k_ref.1) | copy-start | bytes 1572868
  13.4 1.0 %copy-start.5 = (bf16[32,16,512]{2,1,0:T(8,128)(2,1)S(1)}, bf16[32,16,512]{2,1,0:T(8,128)(2,1)}, u32[]{:S(2)}) copy-start(bf16[32,16,512]{2,1,0:T(8,128)(2,1)} %v_ref.1) | copy-start | bytes 1572868
  16.0 7.7 %collective-permute-start.2 = (bf16[2,128,512]{2,1,0:T(8,128)(2,1)S(1)}, bf16[2,128,512]{2,1,0:T(8,128)(2,1)S(1)}, u32[]{:S(2)}, u32[]{:S(2)}) collective-permute-start(bf16[2,128,512]{2,1,0:T(8,128)(2,1)S(1)} %get-tuple-element.36), channel_id=1, source_target_pairs={{0,32},{32,0},{64,96},{96,64},{1,33},{33,1},{65,97},{97,65},{2,34}... | collective-permute-start | bytes 786440 | tf_op jit(solution)/shard_map/ppermute | solution.py:535
  17.1 17.3 %collective-permute-start.3 = (bf16[2,128,512]{2,1,0:T(8,128)(2,1)S(1)}, bf16[2,128,512]{2,1,0:T(8,128)(2,1)S(1)}, u32[]{:S(2)}, u32[]{:S(2)}) collective-permute-start(bf16[2,128,512]{2,1,0:T(8,128)(2,1)S(1)} %get-tuple-element.37), channel_id=1, source_target_pairs={{32,64},{64,32},{33,65},{65,33},{34,66},{66,34},{35,67},{67,35},{3... | collective-permute-start | bytes 786440 | tf_op jit(solution)/shard_map/ppermute | solution.py:543
  19.3 1.0 %copy-start = (bf16[2,256,512]{2,1,0:T(8,128)(2,1)S(1)}, bf16[2,256,512]{2,1,0:T(8,128)(2,1)}, u32[]{:S(2)}) copy-start(bf16[2,256,512]{2,1,0:T(8,128)(2,1)} %get-tuple-element.32.side_0.refs_0_) | copy-start | bytes 1572868
  20.3 1.0 %copy-start.2 = (bf16[2,256,512]{2,1,0:T(8,128)(2,1)S(1)}, bf16[2,256,512]{2,1,0:T(8,128)(2,1)}, u32[]{:S(2)}) copy-start(bf16[2,256,512]{2,1,0:T(8,128)(2,1)} %get-tuple-element.33.side_1.refs_1_) | copy-start | bytes 1572868
  39.0 8.6 %collective-permute-start.4 = (f32[4,16,128]{2,1,0:T(8,128)S(1)}, f32[4,16,128]{2,1,0:T(8,128)S(1)}, u32[]{:S(2)}, u32[]{:S(2)}) collective-permute-start(f32[4,16,128]{2,1,0:T(8,128)S(1)} %get-tuple-element.40.send_0.refs_4_), channel_id=1, source_target_pairs={{1,2},{2,1},{3,4},{4,3},{5,6},{6,5},{7,8},{8,7},{9,10},{10,9},{11,... | collective-permute-start | bytes 98312 | tf_op jit(solution)/shard_map/ppermute | solution.py:543
  46.3 4.3 %collective-permute-start.5 = (f32[4,16,128]{2,1,0:T(8,128)S(1)}, f32[4,16,128]{2,1,0:T(8,128)S(1)}, u32[]{:S(2)}, u32[]{:S(2)}) collective-permute-start(f32[4,16,128]{2,1,0:T(8,128)S(1)} %get-tuple-element.41.send_1.refs_5_), channel_id=1, source_target_pairs={{0,1},{1,0},{2,3},{3,2},{4,5},{5,4},{6,7},{7,6},{8,9},{9,8},{10,11... | collective-permute-start | bytes 98312 | tf_op jit(solution)/shard_map/ppermute | solution.py:535
  50.6 5.6 %copy-start.1 = (bf16[2,256,512]{2,1,0:T(8,128)(2,1)S(1)}, bf16[2,256,512]{2,1,0:T(8,128)(2,1)}, u32[]{:S(2)}) copy-start(bf16[2,256,512]{2,1,0:T(8,128)(2,1)} %get-tuple-element.32.side_0.refs_0_) | copy-start | bytes 1572868
  50.6 5.6 %copy-start.3 = (bf16[2,256,512]{2,1,0:T(8,128)(2,1)S(1)}, bf16[2,256,512]{2,1,0:T(8,128)(2,1)}, u32[]{:S(2)}) copy-start(bf16[2,256,512]{2,1,0:T(8,128)(2,1)} %get-tuple-element.33.side_1.refs_1_) | copy-start | bytes 1572868
  51.9 14.9 %collective-permute-start.6 = (bf16[256,512]{1,0:T(8,128)(2,1)S(1)}, bf16[256,512]{1,0:T(8,128)(2,1)S(1)}, u32[]{:S(2)}, u32[]{:S(2)}) collective-permute-start(bf16[256,512]{1,0:T(8,128)(2,1)S(1)} %get-tuple-element.49.refs_14_), channel_id=1, source_target_pairs={{1,2},{2,1},{3,4},{4,3},{5,6},{6,5},{7,8},{8,7},{9,10},{10,9},{11,... | collective-permute-start | bytes 786440 | tf_op jit(solution)/shard_map/ppermute | solution.py:543
  56.2 10.8 %collective-permute-start.7 = (bf16[256,512]{1,0:T(8,128)(2,1)S(1)}, bf16[256,512]{1,0:T(8,128)(2,1)S(1)}, u32[]{:S(2)}, u32[]{:S(2)}) collective-permute-start(bf16[256,512]{1,0:T(8,128)(2,1)S(1)} %get-tuple-element.50.refs_15_), channel_id=1, source_target_pairs={{0,1},{1,0},{2,3},{3,2},{4,5},{5,4},{6,7},{7,6},{8,9},{9,8},{10,11... | collective-permute-start | bytes 786440 | tf_op jit(solution)/shard_map/ppermute | solution.py:535
  58.7 5.6 %collective-permute-start.8 = (bf16[2,128,512]{2,1,0:T(8,128)(2,1)S(1)}, bf16[2,128,512]{2,1,0:T(8,128)(2,1)S(1)}, u32[]{:S(2)}, u32[]{:S(2)}) collective-permute-start(bf16[2,128,512]{2,1,0:T(8,128)(2,1)S(1)} %get-tuple-element.59), channel_id=1, source_target_pairs={{0,32},{32,0},{64,96},{96,64},{1,33},{33,1},{65,97},{97,65},{2,34}... | collective-permute-start | bytes 786440 | tf_op jit(solution)/shard_map/ppermute | solution.py:535
  58.8 8.0 %collective-permute-start.9 = (bf16[2,128,512]{2,1,0:T(8,128)(2,1)S(1)}, bf16[2,128,512]{2,1,0:T(8,128)(2,1)S(1)}, u32[]{:S(2)}, u32[]{:S(2)}) collective-permute-start(bf16[2,128,512]{2,1,0:T(8,128)(2,1)S(1)} %get-tuple-element.60), channel_id=1, source_target_pairs={{32,64},{64,32},{33,65},{65,33},{34,66},{66,34},{35,67},{67,35},{3... | collective-permute-start | bytes 786440 | tf_op jit(solution)/shard_map/ppermute | solution.py:543

commit v6 on v5

--- a/solution.py
+++ b/solution.py
@@ -22,6 +22,7 @@
 BF16 = jnp.bfloat16
 VMEM_LIMIT = 20 * 1024 * 1024
 PACK_LIMIT = 62 * 1024 * 1024
+any_spec = pl.BlockSpec(memory_space=pl.ANY)
 EDGE_ROWS = (0, 3)
 MID_ROWS = (1, 2)
 ORDER = EDGE_ROWS + MID_ROWS
@@ -68,8 +69,18 @@
     return copies
 
 
-def pack_queries_kernel(q_ref, g_ref, side_0, side_1, buffers, sems, packed, out_sems):
+def key_tile(buffer):
+    return jnp.concatenate(split_columns(buffer), axis=0)
+
+
+def pack_queries_kernel(q_ref, g_ref, k_ref, v_ref, side_0, side_1, edge_a, edge_b,
+                        buffers, sems, key_buffers, key_sems, packed, out_sems):
+    key_copies = fetch((k_ref, v_ref), (ROWS - 1, 0), key_buffers, key_sems)
     copies = fetch((q_ref, g_ref), ORDER, buffers, sems)
+    for i in range(2):
+        for place, edge in enumerate((edge_b, edge_a)):
+            key_copies[i][place].wait()
+            edge[i] = key_tile(key_buffers[i, place])
     sends = []
     for place in range(ROWS):
         for i in range(2):
@@ -86,11 +97,12 @@
 def pack_queries(*operands):
     return pl.pallas_call(
         pack_queries_kernel,
-        in_specs=[pl.BlockSpec(memory_space=pl.ANY)] * 2,
-        out_specs=[pl.BlockSpec(memory_space=pl.ANY)] * 2,
-        out_shape=[struct((2, ROWS * CELLS, FEAT), BF16)] * 2,
+        in_specs=[any_spec] * 4,
+        out_specs=[any_spec] * 2 + [pl.BlockSpec(memory_space=pltpu.VMEM)] * 2,
+        out_shape=[struct((2, ROWS * CELLS, FEAT), BF16)] * 2 + [struct((2, PAIR, FEAT), BF16)] * 2,
         scratch_shapes=[
             pltpu.VMEM((2, ROWS, 8, 16, FEAT), BF16), pltpu.SemaphoreType.DMA((2, ROWS)),
+            pltpu.VMEM((2, 2, 8, 16, FEAT), BF16), pltpu.SemaphoreType.DMA((2, 2)),
             pltpu.VMEM((2, 2, ROWS, CELLS, FEAT), BF16), pltpu.SemaphoreType.DMA((2, 2, ROWS)),
         ],
         compiler_params=params(PACK_LIMIT),
@@ -99,24 +111,19 @@
     )(*operands)
 
 
-def pack_keys_kernel(k_ref, v_ref, kd, vd, edge_a, edge_b, buffers, sems):
+def pack_keys_kernel(k_ref, v_ref, kd, vd, buffers, sems):
     copies = fetch((k_ref, v_ref), range(ROWS), buffers, sems)
     for t in range(ROWS):
         for i, out in enumerate((kd, vd)):
             copies[i][t].wait()
-            tile = jnp.concatenate(split_columns(buffers[i, t]), axis=0)
-            out[t * PAIR:(t + 1) * PAIR] = tile
-            if t == 0:
-                edge_a[i] = tile
-            if t == ROWS - 1:
-                edge_b[i] = tile
+            out[t * PAIR:(t + 1) * PAIR] = key_tile(buffers[i, t])
 
 
 def pack_keys(*operands):
     return pl.pallas_call(
         pack_keys_kernel,
-        in_specs=[pl.BlockSpec(memory_space=pl.ANY)] * 2,
-        out_shape=[struct((ROWS * PAIR, FEAT), BF16)] * 2 + [struct((2, PAIR, FEAT), BF16)] * 2,
+        in_specs=[any_spec] * 2,
+        out_shape=[struct((ROWS * PAIR, FEAT), BF16)] * 2,
         scratch_shapes=[pltpu.VMEM((2, ROWS, 8, 16, FEAT), BF16), pltpu.SemaphoreType.DMA((2, ROWS))],
         compiler_params=params(),
         cost_estimate=cost(0, 3 << 20),
@@ -182,9 +189,8 @@
 
 
 def both_parts(mine, theirs, pair, base):
-    other = 4 - base
     return merged(mine[pair, base:base + 2], mine[pair, base + 2:base + 4],
-                  theirs[pair, other:other + 2], theirs[pair, other + 2:other + 4])
+                  theirs[pair, base:base + 2], theirs[pair, base + 2:base + 4])
 
 
 def turned_window(own_turned, edges_turned, t, j):
@@ -218,10 +224,9 @@
 
 keys_spec = pl.BlockSpec((ROWS * PAIR, PAIR), lambda p: (0, p))
 edge_spec = pl.BlockSpec((2, PAIR, PAIR), lambda p: (0, 0, p))
-part_spec = pl.BlockSpec((1, 8, PAIR), lambda p: (p, 0, 0))
+stats_spec = pl.BlockSpec((1, 8, PAIR), lambda p: (p, 0, 0))
 held_spec = pl.BlockSpec((1, 2, 3 * PAIR, WIDE), lambda p: (p, 0, 0, 0))
-part_shape = struct((PAIRS, 8, PAIR), F32)
-stats_shape = struct((PAIRS, 16, PAIR), F32)
+stats_shape = struct((PAIRS, 8, PAIR), F32)
 held_shape = struct((PAIRS, 2, 3 * PAIR, WIDE), F32)
 
 
@@ -229,12 +234,8 @@
     return pl.BlockSpec((2, CHUNK, WIDE), lambda g: (0, group, g))
 
 
-def stats_wide(group):
-    return pl.BlockSpec((2, 8, PAIR), lambda g: (g, group, 0))
-
-
 all_tokens = pl.BlockSpec((2, 2 * CHUNK, WIDE), lambda g: (0, 0, g))
-all_stats = pl.BlockSpec((2, 16, PAIR), lambda g: (g, 0, 0))
+stats_wide = pl.BlockSpec((2, 8, PAIR), lambda g: (g, 0, 0))
 all_parts = pl.BlockSpec((2 * CHUNK, WIDE), lambda g: (0, g))
 sums_wide = pl.BlockSpec((2, CHUNK, WIDE), lambda g: (0, 0, g))
 keys_wide = pl.BlockSpec((ROWS * PAIR, WIDE), lambda g: (0, g))
@@ -243,33 +244,36 @@
 edge_turned_wide = pl.BlockSpec((2, WIDE, PAIR), lambda g: (0, g, 0))
 held_wide = pl.BlockSpec((2, 2, 3 * PAIR, WIDE), lambda g: (g, 0, 0, 0))
 halo_wide = pl.BlockSpec((1, 2, 2, 3 * CELLS, WIDE), lambda g: (g, 0, 0, 0, 0))
-halo_shape = struct((GROUPS, 2, 2, 3 * CELLS, WIDE), F32)
-any_spec = pl.BlockSpec(memory_space=pl.ANY)
-
-
-def own_scores(rows, side_a, side_b, kd, vd, edges, part, s_out, d_out):
+halo_shape = struct((GROUPS, 2, 2, 3 * CELLS, WIDE), BF16)
+
+
+def own_scores(rows, base, side_0, side_1, kd, vd, edges, parts, s_out, d_out):
     masks = head_masks(PAIR)
     for place, t in enumerate(rows):
         at = at_tokens(place)
-        queries = stacked([side_a[0, at], side_b[0, at]], masks)
-        grads = stacked([side_a[1, at], side_b[1, at]], masks)
+        queries = stacked([side_0[0, at], side_1[0, at]], masks)
+        grads = stacked([side_0[1, at], side_1[1, at]], masks)
         scores = score_block(window(kd, edges, 0, t), queries, t)
         dprobs = matmul(window(vd, edges, 1, t), grads, (1, 1))
         s_out[0, place] = scores
         d_out[0, place] = dprobs
         for w, values in enumerate(row_stats(scores, dprobs)):
             for c in range(2):
-                index = 4 * c + 2 * w + place
-                part[0, index:index + 1] = values[:, pair_lanes(c)]
-
-
-def mid_scores_kernel(side_0, side_1, kd, vd, part, s_out, d_out, turned):
-    own_scores(MID_ROWS, side_0, side_1, kd, vd, None, part, s_out, d_out)
+                index = base + 2 * w + place
+                parts[c][0, index:index + 1] = values[:, pair_lanes(c)]
+
+
+def mid_scores_kernel(side_0, side_1, kd, vd, part_0, part_1, s_out, d_out, turned):
+    for part in (part_0, part_1):
+        part[0, 0:4] = jnp.zeros((4, PAIR), F32)
+    own_scores(MID_ROWS, 4, side_0, side_1, kd, vd, None, (part_0, part_1), s_out, d_out)
     turned[...] = kd[...].T
 
 
-def edge_scores_kernel(side_0, side_1, kd, vd, edge_a, edge_b, part, s_out, d_out):
-    own_scores(EDGE_ROWS, side_0, side_1, kd, vd, (edge_a, edge_b), part, s_out, d_out)
+def edge_scores_kernel(side_0, side_1, kd, vd, edge_a, edge_b, mid_0, mid_1, part_0, part_1, s_out, d_out):
+    for part, mid in ((part_0, mid_0), (part_1, mid_1)):
+        part[0, 4:8] = mid[0, 4:8]
+    own_scores(EDGE_ROWS, 0, side_0, side_1, kd, vd, (edge_a, edge_b), (part_0, part_1), s_out, d_out)
 
 
 def mid_scores(*operands):
@@ -277,8 +281,8 @@
         mid_scores_kernel,
         grid=(PAIRS,),
         in_specs=[tokens_spec(MID)] * 2 + [keys_spec] * 2,
-        out_specs=[part_spec] + [held_spec] * 2 + [pl.BlockSpec((PAIR, ROWS * PAIR), lambda p: (p, 0))],
-        out_shape=[part_shape] + [held_shape] * 2 + [struct((FEAT, ROWS * PAIR), BF16)],
+        out_specs=[stats_spec] * 2 + [held_spec] * 2 + [pl.BlockSpec((PAIR, ROWS * PAIR), lambda p: (p, 0))],
+        out_shape=[stats_shape] * 2 + [held_shape] * 2 + [struct((FEAT, ROWS * PAIR), BF16)],
         compiler_params=params(),
         cost_estimate=cost(2e9, 1 << 10),
         name="mid_scores",
@@ -289,9 +293,9 @@
     return pl.pallas_call(
         edge_scores_kernel,
         grid=(PAIRS,),
-        in_specs=[tokens_spec(EDGE)] * 2 + [keys_spec] * 2 + [edge_spec] * 2,
-        out_specs=[part_spec] + [held_spec] * 2,
-        out_shape=[part_shape] + [held_shape] * 2,
+        in_specs=[tokens_spec(EDGE)] * 2 + [keys_spec] * 2 + [edge_spec] * 2 + [stats_spec] * 2,
+        out_specs=[stats_spec] * 2 + [held_spec] * 2,
+        out_shape=[stats_shape] * 2 + [held_shape] * 2,
         compiler_params=params(),
         cost_estimate=cost(2e9, 1 << 10),
         name="edge_scores",
@@ -316,68 +320,44 @@
     )(*operands)
 
 
-def halo_scores_kernel(q_0, q_1, kd, vd, edge_a, edge_b, edge_part, mid_part,
-                       send_0, send_1, s_edge, d_edge, s_mid, d_mid):
+def halo_kernel(q_0, q_1, kd, vd, edge_a, edge_b, own_0, own_1, own_turned, edges_turned,
+                part_0, part_1, out_0, out_1, p_edge, ds_edge, p_mid, ds_mid, s_held, d_held):
     masks = head_masks(WIDE)
-    groups = ((EDGE_ROWS, edge_part, s_edge, d_edge), (MID_ROWS, mid_part, s_mid, d_mid))
-    for group, (rows, part, s_out, d_out) in enumerate(groups):
-        base = 8 * group
-        for c, (q_in, send) in enumerate(((q_0, send_0), (q_1, send_1))):
-            for j in range(2):
-                send[j, base:base + 4] = part[j, 4 * c:4 * c + 4]
-            for place, t in enumerate(rows):
-                at = at_tokens(2 * group + place)
+    lane = lax.broadcasted_iota(jnp.int32, (1, PAIR), 1)
+    none = jnp.zeros((CELLS, PAIR), BF16)
+    sides = ((q_0, own_0, part_0), (q_1, own_1, part_1))
+    groups = ((EDGE_ROWS, p_edge, ds_edge), (MID_ROWS, p_mid, ds_mid))
+    for group, (rows, _, _) in enumerate(groups):
+        for place, t in enumerate(rows):
+            at = at_tokens(2 * group + place)
+            for c, (q_in, _, part) in enumerate(sides):
                 queries = stacked([q_in[0, at]], masks)
                 grads = stacked([q_in[1, at]], masks)
                 scores = score_block(column_window(c, kd, (edge_a, edge_b), 0, t), queries, t)
                 dprobs = matmul(column_window(c, vd, (edge_a, edge_b), 1, t), grads, (1, 1))
-                s_out[0, place, c] = scores
-                d_out[0, place, c] = dprobs
+                s_held[group, place, c] = scores
+                d_held[group, place, c] = dprobs
                 for w, values in enumerate(row_stats(scores, dprobs)):
-                    index = base + 4 + 2 * w + place
+                    index = 4 * group + 2 * w + place
                     for j in range(2):
-                        send[j, index:index + 1] = values[:, pair_lanes(j)]
-
-
-def halo_scores(*operands):
-    part = pl.BlockSpec((2, 8, PAIR), lambda g: (g, 0, 0))
-    return pl.pallas_call(
-        halo_scores_kernel,
-        grid=(GROUPS,),
-        in_specs=[all_tokens] * 2 + [keys_wide] * 2 + [edge_wide] * 2 + [part] * 2,
-        out_specs=[all_stats] * 2 + [halo_wide] * 4,
-        out_shape=[stats_shape] * 2 + [halo_shape] * 4,
-        compiler_params=params(),
-        cost_estimate=cost(2e9, 1 << 10),
-        name="halo_scores",
-    )(*operands)
-
-
-def halo_weights(mine, theirs, s_in, d_in, c):
-    both = [both_parts(mine, theirs, j, 4) for j in range(2)]
-    log_total = jnp.concatenate([one[0] for one in both], axis=1)
-    delta = jnp.concatenate([one[1] for one in both], axis=1)
-    weights = []
-    for place in range(2):
-        probs = jnp.exp2(s_in[0, place, c] - log_total[place:place + 1])
-        dscores = probs * (d_in[0, place, c] - delta[place:place + 1])
-        weights.append((probs.astype(BF16), dscores.astype(BF16)))
-    return weights
-
-
-def halo_queries_kernel(send_0, send_1, recv_0, recv_1, s_edge, d_edge, s_mid, d_mid, own_turned, edges_turned,
-                        out_0, out_1):
-    lane = lax.broadcasted_iota(jnp.int32, (1, PAIR), 1)
-    none = jnp.zeros((CELLS, PAIR), BF16)
-    groups = ((EDGE_ROWS, s_edge, d_edge), (MID_ROWS, s_mid, d_mid))
-    for group, (rows, s_in, d_in) in enumerate(groups):
-        stats = [ref.at[:, pl.ds(8 * group, 8)] for ref in (send_0, send_1, recv_0, recv_1)]
-        weights = [halo_weights(stats[c], stats[2 + c], s_in, d_in, c) for c in range(2)]
+                        part[j, index:index + 1] = values[:, pair_lanes(j)]
+    for group, (rows, p_out, ds_out) in enumerate(groups):
+        rows_merged = []
+        for _, own, part in sides:
+            both = [both_parts(part, own, j, 4 * group) for j in range(2)]
+            rows_merged.append([jnp.concatenate([one[w] for one in both], axis=1) for w in range(2)])
         for place, t in enumerate(rows):
+            low = []
+            for c in range(2):
+                log_total, delta = rows_merged[c]
+                probs = jnp.exp2(s_held[group, place, c] - log_total[place:place + 1])
+                low.append((probs * (d_held[group, place, c] - delta[place:place + 1])).astype(BF16))
+                p_out[0, place, c] = probs.astype(BF16)
+                ds_out[0, place, c] = low[c]
             for j in range(2):
                 pieces = []
                 for i in range(3):
-                    parts = [weights[c][place][1][at_tokens(i), pair_lanes(j)] for c in range(2)]
+                    parts = [low[c][at_tokens(i), pair_lanes(j)] for c in range(2)]
                     pieces += [jnp.concatenate([parts[0], none], axis=1), jnp.concatenate([none, parts[1]], axis=1)]
                 keys_turned = turned_window(own_turned, edges_turned, t, j)
                 grads = query_parts(keys_turned, jnp.concatenate(pieces, axis=0), lane)
@@ -385,28 +365,27 @@
                     out[at_tokens(2 * group + place), pair_lanes(j)] = grad.astype(BF16)
 
 
-def halo_queries(*operands):
-    return pl.pallas_call(
-        halo_queries_kernel,
+def halo(*operands):
+    return pl.pallas_call(
+        halo_kernel,
         grid=(GROUPS,),
-        in_specs=[all_stats] * 4 + [halo_wide] * 4 + [turned_wide, edge_turned_wide],
-        out_specs=[all_parts] * 2,
-        out_shape=[struct((2 * CHUNK, FEAT), BF16)] * 2,
+        in_specs=[all_tokens] * 2 + [keys_wide] * 2 + [edge_wide] * 2 + [stats_wide] * 2 + [turned_wide, edge_turned_wide],
+        out_specs=[stats_wide] * 2 + [all_parts] * 2 + [halo_wide] * 4,
+        out_shape=[stats_shape] * 2 + [struct((2 * CHUNK, FEAT), BF16)] * 2 + [halo_shape] * 4,
+        scratch_shapes=[pltpu.VMEM((2, 2, 2, 3 * CELLS, WIDE), F32)] * 2,
         compiler_params=params(),
         cost_estimate=cost(2e9, 1 << 10),
-        name="halo_queries",
-    )(*operands)
-
-
-def row_gradients(rows, side_a, side_b, q_a, q_b, send_a, send_b, recv_a, recv_b, s_own, d_own, s_halo, d_halo,
+        name="halo",
+    )(*operands)
+
+
+def row_gradients(rows, base, side_0, side_1, q_0, q_1, own_0, own_1, recv_0, recv_1, s_own, d_own, p_halo, ds_halo,
                   own_turned, edges_turned, dq_ref):
     masks, wide_masks = head_masks(PAIR), head_masks(WIDE)
     lane = lax.broadcasted_iota(jnp.int32, (1, PAIR), 1)
-    sides = ((q_a, send_a, recv_a), (q_b, send_b, recv_b))
-    halo = [halo_weights(mine, theirs, s_halo, d_halo, c) for c, (_, mine, theirs) in enumerate(sides)]
     merged_rows = []
     for j in range(2):
-        both = [both_parts(mine, theirs, j, 0) for _, mine, theirs in sides]
+        both = [both_parts(own_0, recv_0, j, base), both_parts(own_1, recv_1, j, base)]
         merged_rows.append([jnp.concatenate([one[w] for one in both], axis=1) for w in range(2)])
     results = []
     for place, t in enumerate(rows):
@@ -414,8 +393,8 @@
         sums = [[], []]
         for j in range(2):
             lanes = pair_lanes(j)
-            queries = stacked([side_a[0, at, lanes], side_b[0, at, lanes]], masks)
-            grads = stacked([side_a[1, at, lanes], side_b[1, at, lanes]], masks)
+            queries = stacked([side_0[0, at, lanes], side_1[0, at, lanes]], masks)
+            grads = stacked([side_0[1, at, lanes], side_1[1, at, lanes]], masks)
             log_total, delta = merged_rows[j]
             probs = jnp.exp2(s_own[j, place] - log_total[row])
             dscores = (probs * (d_own[j, place] - delta[row])).astype(BF16)
@@ -425,10 +404,9 @@
             sums[1].append(matmul(probs.astype(BF16), grads, (1, 0)))
         sums = [jnp.concatenate(parts, axis=1) for parts in sums]
         edge_parts = []
-        for c in range(2):
-            probs, dscores = halo[c][place]
-            edge_parts.append((matmul(dscores, stacked([sides[c][0][0, at]], wide_masks), (1, 0)),
-                               matmul(probs, stacked([sides[c][0][1, at]], wide_masks), (1, 0))))
+        for c, q_in in enumerate((q_0, q_1)):
+            edge_parts.append((matmul(ds_halo[0, place, c], stacked([q_in[0, at]], wide_masks), (1, 0)),
+                               matmul(p_halo[0, place, c], stacked([q_in[1, at]], wide_masks), (1, 0))))
         results.append([jnp.concatenate([sums[w][at_tokens(2 * i + c)] + edge_parts[c][w][at_tokens(i)]
                                          for i in range(3) for c in range(2)], axis=0) for w in range(2)])
     return results
@@ -436,7 +414,7 @@
 
 def edge_kernel(*refs):
     operands, (_, _, dq_ref, dk_ref, dv_ref, out_a, out_b) = refs[:14], refs[14:]
-    upper, lower = row_gradients(EDGE_ROWS, *operands, dq_ref)
+    upper, lower = row_gradients(EDGE_ROWS, 0, *operands, dq_ref)
     for which, (out, scale) in enumerate(((dk_ref, SCALE), (dv_ref, 1.0))):
         top, bottom = upper[which] * scale, lower[which] * scale
         out_a[which] = top[:PAIR].astype(BF16)
@@ -447,7 +425,7 @@
 
 def mid_kernel(*refs):
     operands, (dk_in, dv_in, dq_ref, dk_ref, dv_ref) = refs[:13], refs[13:]
-    upper, lower = row_gradients(MID_ROWS, *operands, None, dq_ref)
+    upper, lower = row_gradients(MID_ROWS, 4, *operands, None, dq_ref)
     for which, (sums, out, scale) in enumerate(((dk_in, dk_ref, SCALE), (dv_in, dv_ref, 1.0))):
         out[0:PAIR] = sums[0:PAIR] + upper[which][:PAIR] * scale
         out[PAIR:3 * PAIR] = sums[PAIR:3 * PAIR] + (upper[which][PAIR:] + lower[which][:2 * PAIR]) * scale
@@ -455,7 +433,7 @@
 
 
 def row_specs(group):
-    return ([tokens_wide(group)] * 4 + [stats_wide(group)] * 4 + [held_wide] * 2 + [halo_wide] * 2 + [turned_wide])
+    return ([tokens_wide(group)] * 4 + [stats_wide] * 4 + [held_wide] * 2 + [halo_wide] * 2 + [turned_wide])
 
 
 GRAD_SPECS = [sums_wide] + [keys_wide] * 2
@@ -547,26 +525,23 @@
     return swap_b(side_0, "lon", True), swap_a(side_1, "lon")
 
 
-def over_lat(side_a, side_b):
-    return swap_a(side_a, "lat"), swap_b(side_b, "lat", False)
-
-
 def on_device(query_vectors, key_vectors, value_vectors, output_grads):
-    sides = pack_queries(query_vectors, output_grads)
-    kd, vd, own_edge_a, own_edge_b = pack_keys(key_vectors, value_vectors)
+    *sides, own_edge_a, own_edge_b = pack_queries(query_vectors, output_grads, key_vectors, value_vectors)
+    kd, vd = pack_keys(key_vectors, value_vectors)
+    edge_b = swap_b(own_edge_b, "lat", False)
     halos = over_lon(*sides)
-    edges = over_lat(own_edge_a, own_edge_b)
-    mid_part, *mid_own, turned = mid_scores(*sides, kd, vd)
-    edge_part, *edge_own = edge_scores(*sides, kd, vd, *edges)
-    *sends, s_edge, d_edge, s_mid, d_mid = halo_scores(*halos, kd, vd, *edges, edge_part, mid_part)
-    stats = (*sends, *over_lon(*sends))
+    edges = (swap_a(own_edge_a, "lat"), edge_b)
+    mid_0, mid_1, *mid_own, turned = mid_scores(*sides, kd, vd)
+    own_0, own_1, *edge_own = edge_scores(*sides, kd, vd, *edges, mid_0, mid_1)
     edges_turned = turn_edges(*edges)
-    halo_dq = halo_queries(*stats, s_edge, d_edge, s_mid, d_mid, turned, edges_turned)
+    part_0, part_1, *rest = halo(*halos, kd, vd, *edges, *over_lon(own_0, own_1), turned, edges_turned)
+    halo_dq, edge_weights, mid_weights = rest[:2], rest[2:4], rest[4:]
+    stats = (own_0, own_1, *over_lon(part_0, part_1))
     dq_parts = over_lon(*halo_dq)
     shared = (*sides, *halos, *stats)
-    dq_edge, dk, dv, out_a, out_b = edge_gradients(*shared, *edge_own, s_edge, d_edge, turned, edges_turned, *halo_dq)
-    key_parts = over_lat(out_a, out_b)
-    dq_mid, dk, dv = mid_gradients(*shared, *mid_own, s_mid, d_mid, turned, dk, dv)
+    dq_edge, dk, dv, out_a, out_b = edge_gradients(*shared, *edge_own, *edge_weights, turned, edges_turned, *halo_dq)
+    key_parts = (swap_a(out_a, "lat"), swap_b(out_b, "lat", False))
+    dq_mid, dk, dv = mid_gradients(*shared, *mid_own, *mid_weights, turned, dk, dv)
     return tuple(finish(dq_edge, dq_mid, dk, dv, *dq_parts, *key_parts))
 
 

time: 68.7 us -> 70.3 us (1.023)
  starting transfers between devices: 27.4 us -> 33.2 us
  waiting for transfers between devices: 17.1 us -> 11.7 us
  Pallas kernels: 18.8 us -> 20.2 us
    ppermute x5 -> x6, waiting for transfers between devices: 13.9 us -> 5.41 us  [swap_b(): return lax.ppermute(x, axis, pairs)]
    ppermute x5 -> x6, starting transfers between devices: 26.2 us -> 31.4 us  [swap_b(): return lax.ppermute(x, axis, pairs)]
    ppermute x5 -> x6, waiting for transfers between devices: 3.21 us -> 6.26 us  [swap_a(): lax.ppermute(x, axis, [(i, i ^ 1) for i in range(lax.axis_size(axis))])]
    pallas_call x4 -> x3, Pallas kernels: 7.23 us -> 8.79 us  [the longest x1 3.76 us: halo(): pl.pallas_call(halo_kernel, grid=(GROUPS,), in_specs=[all_tokens] * 2 + [...]
    ppermute x5 -> x6, starting transfers between devices: 1.13 us -> 1.8 us  [swap_a(): lax.ppermute(x, axis, [(i, i ^ 1) for i in range(lax.axis_size(axis))])]
  transfers between devices with their start and end apart: 10 -> 12, of which waited for: 5 -> 6; matrix products, arithmetic and copies ran while one was open for 0% -> 0% of each run, Pallas kernels for 18% -> 17%
where the time goes in v6:
time: 70.3 us; the launch traced here: 70 us
  starting transfers between devices  33.2 us (47%)
  Pallas kernels  20.2 us (29%)
  waiting for transfers between devices  11.7 us (17%)
  local copies, waits for them, and re-layouts  4.17 us (6%)
  between operations  0.77 us (1%)
    ppermute x6, starting transfers between devices, swap_b(): return lax.ppermute(x, axis, pairs)  31.4 us
    ppermute x6, waiting for transfers between devices, swap_a(): lax.ppermute(x, axis, [(i, i ^ 1) for i in range(lax.axis_size(axis))])  6.26 us
    ppermute x6, waiting for transfers between devices, swap_b(): return lax.ppermute(x, axis, pairs)  5.41 us
    unnamed x12, local copies, waits for them, and re-layouts  4.17 us
    pallas_call x1, Pallas kernels, halo(): pl.pallas_call(halo_kernel, grid=(GROUPS,), in_specs=[all_tokens] * 2 + [...  3.76 us
    pallas_call x1, Pallas kernels, pack_queries(): pl.pallas_call(pack_queries_kernel, in_specs=[any_spec] * 4, out_specs=[a...  3.42 us
    pallas_call x1, Pallas kernels, mid_gradients(): pl.pallas_call(mid_kernel, grid=(GROUPS,), in_specs=row_specs(MID) + [key...  2.47 us
    pallas_call x1, Pallas kernels, edge_scores(): pl.pallas_call(edge_scores_kernel, grid=(PAIRS,), in_specs=[tokens_spec(E...  2.44 us
  transfers between devices with their start and end apart: 12, of which 6 were waited for; matrix products, arithmetic and copies ran while one was open for 0% of the time, Pallas kernels for 17%

profile of v6, /device:TPU:1, one launch (start us, length us, event | category | flops | bytes accessed | tf_op | source)
XLA Modules:
  0.0 70.0 jit_solution(6528735180526429080)
XLA Ops:
  0.6 3.4 %pack_queries.1 = (bf16[2,256,512]{2,1,0:T(8,128)(2,1)}, bf16[2,256,512]{2,1,0:T(8,128)(2,1)}, bf16[2,128,512]{2,1,0:T(8,128)(2,1)}, bf16[2,128,512]{2,1,0:T(8,128)(2,1)}) custom-call(bf16[32,16,512]{2,1,0:T(8,128)(2,1)} %q_ref.1, bf16[32,16,512]{2,1,0:T(8,128)(2,1)} %g_ref.1, bf16[32,16,512]{2,1,0:T(8,128)(2,1)} %k_ref.3, bf16[32,16,512]{2,1,0:T(8,128)(2,1)} %v_ref.3), custom_call_target="tpu_custom_call" | custom-call | bytes 3145728 | tf_op jit(solution)/shard_map/pack_queries/pallas_call | solution.py:98
  4.1 1.5 %collective-permute-start.2 = (bf16[2,128,512]{2,1,0:T(8,128)(2,1)}, bf16[2,128,512]{2,1,0:T(8,128)(2,1)S(1)}, u32[]{:S(2)}, u32[]{:S(2)}) collective-permute-start(bf16[2,128,512]{2,1,0:T(8,128)(2,1)} %get-tuple-element.38), channel_id=1, source_target_pairs={{0,32},{32,0},{64,96},{96,64},{1,33},{33,1},{65,97},{97,65},{2,34}... | collective-permute-start | bytes 786440 | tf_op jit(solution)/shard_map/ppermute | solution.py:513
  5.6 3.2 %collective-permute-start.3 = (bf16[2,128,512]{2,1,0:T(8,128)(2,1)}, bf16[2,128,512]{2,1,0:T(8,128)(2,1)S(1)}, u32[]{:S(2)}, u32[]{:S(2)}) collective-permute-start(bf16[2,128,512]{2,1,0:T(8,128)(2,1)} %get-tuple-element.39), channel_id=1, source_target_pairs={{32,64},{64,32},{33,65},{65,33},{34,66},{66,34},{35,67},{67,35},{3... | collective-permute-start | bytes 786440 | tf_op jit(solution)/shard_map/ppermute | solution.py:521
  8.8 8.4 %collective-permute-start = (bf16[2,256,512]{2,1,0:T(8,128)(2,1)}, bf16[2,256,512]{2,1,0:T(8,128)(2,1)S(1)}, u32[]{:S(2)}, u32[]{:S(2)}) collective-permute-start(bf16[2,256,512]{2,1,0:T(8,128)(2,1)} %get-tuple-element.34.side_0.refs_0_), channel_id=1, source_target_pairs={{1,2},{2,1},{3,4},{4,3},{5,6},{6,5},{7,8},{8,7},{9,10},{10,9},{11,... | collective-permute-start | bytes 1572872 | tf_op jit(solution)/shard_map/ppermute | solution.py:521
  17.1 1.0 %copy-done.4 = bf16[32,16,512]{2,1,0:T(8,128)(2,1)S(1)} copy-done((bf16[32,16,512]{2,1,0:T(8,128)(2,1)S(1)}, bf16[32,16,512]{2,1,0:T(8,128)(2,1)}, u32[]{:S(2)}) %copy-start.4) | copy-done | bytes 524312
  18.2 1.0 %copy-done.5 = bf16[32,16,512]{2,1,0:T(8,128)(2,1)S(1)} copy-done((bf16[32,16,512]{2,1,0:T(8,128)(2,1)S(1)}, bf16[32,16,512]{2,1,0:T(8,128)(2,1)}, u32[]{:S(2)}) %copy-start.5) | copy-done | bytes 524312
  19.2 1.6 %pack_keys.1 = (bf16[512,512]{1,0:T(8,128)(2,1)S(1)}, bf16[512,512]{1,0:T(8,128)(2,1)S(1)}) custom-call(bf16[32,16,512]{2,1,0:T(8,128)(2,1)S(1)} %copy-done.4, bf16[32,16,512]{2,1,0:T(8,128)(2,1)S(1)} %copy-done.5), custom_call_target="tpu_custom_call" | custom-call | bytes 3145728 | tf_op jit(solution)/shard_map/pack_keys/pallas_call | solution.py:123
  20.8 0.0 copy-start
  20.8 1.0 %copy-done = bf16[2,256,512]{2,1,0:T(8,128)(2,1)S(1)} copy-done((bf16[2,256,512]{2,1,0:T(8,128)(2,1)S(1)}, bf16[2,256,512]{2,1,0:T(8,128)(2,1)}, u32[]{:S(2)}) %copy-start) | copy-done | bytes 524312
  21.9 1.0 %copy-done.2 = bf16[2,256,512]{2,1,0:T(8,128)(2,1)S(1)} copy-done((bf16[2,256,512]{2,1,0:T(8,128)(2,1)S(1)}, bf16[2,256,512]{2,1,0:T(8,128)(2,1)}, u32[]{:S(2)}) %copy-start.2) | copy-done | bytes 524312
  22.9 2.4 %mid_scores.1 = (f32[4,8,128]{2,1,0:T(8,128)S(1)}, f32[4,8,128]{2,1,0:T(8,128)S(1)}, f32[4,2,384,256]{3,2,1,0:T(8,128)S(1)}, f32[4,2,384,256]{3,2,1,0:T(8,128)S(1)}, bf16[512,512]{1,0:T(8,128)(2,1)S(1)}) custom-call(bf16[2,256,512]{2,1,0:T(8,128)(2,1)S(1)} %copy-done, bf16[2,256,512]{2,1,0:T(8,128)(2,1)S(1)} %copy-done.2, ...), custom_call_target="tpu_custom_call" | custom-call | flops 2000000000 | bytes 1024 | tf_op jit(solution)/shard_map/mid_scores/pallas_call | solution.py:280
  25.3 1.2 %collective-permute-done.3.edge_b = bf16[2,128,512]{2,1,0:T(8,128)(2,1)S(1)} collective-permute-done((bf16[2,128,512]{2,1,0:T(8,128)(2,1)}, bf16[2,128,512]{2,1,0:T(8,128)(2,1)S(1)}, u32[]{:S(2)}, u32[]{:S(2)}) %collective-permute-start.3) | collective-permute-done | bytes 262176 | tf_op jit(solution)/shard_map/ppermute | solution.py:521
  26.5 2.4 %edge_scores.1 = (f32[4,8,128]{2,1,0:T(8,128)S(1)}, f32[4,8,128]{2,1,0:T(8,128)S(1)}, f32[4,2,384,256]{3,2,1,0:T(8,128)S(1)}, f32[4,2,384,256]{3,2,1,0:T(8,128)S(1)}) custom-call(bf16[2,256,512]{2,1,0:T(8,128)(2,1)S(1)} %copy-done, bf16[2,256,512]{2,1,0:T(8,128)(2,1)S(1)} %copy-done.2, bf16[512,512]{1,0:T(8,128)(2,1)S(1)} %get-tuple-element.36.kd, ...), custom_call_target="tpu_custom_call" | custom-call | flops 2000000000 | bytes 1024 | tf_op jit(solution)/shard_map/edge_scores/pallas_call | solution.py:293
  28.9 9.8 %collective-permute-start.4 = (f32[4,8,128]{2,1,0:T(8,128)S(1)}, f32[4,8,128]{2,1,0:T(8,128)S(1)}, u32[]{:S(2)}, u32[]{:S(2)}) collective-permute-start(f32[4,8,128]{2,1,0:T(8,128)S(1)} %get-tuple-element.42.refs_4_), channel_id=1, source_target_pairs={{1,2},{2,1},{3,4},{4,3},{5,6},{6,5},{7,8},{8,7},{9,10},{10,9},{11,... | collective-permute-start | bytes 49160 | tf_op jit(solution)/shard_map/ppermute | solution.py:521
  38.7 0.5 turn_edges.1.edges_turned.refs_13_
  39.2 0.7 %collective-permute-done.4.own_0 = f32[4,8,128]{2,1,0:T(8,128)S(1)} collective-permute-done((f32[4,8,128]{2,1,0:T(8,128)S(1)}, f32[4,8,128]{2,1,0:T(8,128)S(1)}, u32[]{:S(2)}, u32[]{:S(2)}) %collective-permute-start.4) | collective-permute-done | bytes 16416 | tf_op jit(solution)/shard_map/ppermute | solution.py:521
  40.0 2.9 %collective-permute-done.5.own_1 = f32[4,8,128]{2,1,0:T(8,128)S(1)} collective-permute-done((f32[4,8,128]{2,1,0:T(8,128)S(1)}, f32[4,8,128]{2,1,0:T(8,128)S(1)}, u32[]{:S(2)}, u32[]{:S(2)}) %collective-permute-start.5) | collective-permute-done | bytes 16416 | tf_op jit(solution)/shard_map/ppermute | solution.py:513
  42.8 0.0 collective-permute-done.q_0.refs_2_
  42.8 0.0 collective-permute-done.1.q_1.refs_3_
  42.8 0.0 copy-start.3
  42.9 3.8 %halo.1 = (f32[4,8,128]{2,1,0:T(8,128)S(1)}, f32[4,8,128]{2,1,0:T(8,128)S(1)}, bf16[256,512]{1,0:T(8,128)(2,1)S(1)}, bf16[256,512]{1,0:T(8,128)(2,1)S(1)}, bf16[...) custom-call(bf16[2,256,512]{2,1,0:T(8,128)(2,1)S(1)} %collective-per, ...), custom_call_target="tpu_custom_call" | custom-call | flops 2000000000 | bytes 1024 | tf_op jit(solution)/shard_map/halo/pallas_call | solution.py:369
  46.6 4.3 %collective-permute-start.6 = (f32[4,8,128]{2,1,0:T(8,128)S(1)}, f32[4,8,128]{2,1,0:T(8,128)S(1)}, u32[]{:S(2)}, u32[]{:S(2)}) collective-permute-start(f32[4,8,128]{2,1,0:T(8,128)S(1)} %get-tuple-element.45), channel_id=1, source_target_pairs={{1,2},{2,1},{3,4},{4,3},{5,6},{6,5},{7,8},{8,7},{9,10},{10,9},{11,... | collective-permute-start | bytes 49160 | tf_op jit(solution)/shard_map/ppermute | solution.py:521
  50.9 3.0 %collective-permute-start.8 = (bf16[256,512]{1,0:T(8,128)(2,1)S(1)}, bf16[256,512]{1,0:T(8,128)(2,1)S(1)}, u32[]{:S(2)}, u32[]{:S(2)}) collective-permute-start(bf16[256,512]{1,0:T(8,128)(2,1)S(1)} %get-tuple-element.51.refs_14_), channel_id=1, source_target_pairs={{1,2},{2,1},{3,4},{4,3},{5,6},{6,5},{7,8},{8,7},{9,10},{10,9},{11,... | collective-permute-start | bytes 786440 | tf_op jit(solution)/shard_map/ppermute | solution.py:521
  53.9 0.0 collective-permute-start.9
  53.9 1.1 %collective-permute-done.6.refs_6_ = f32[4,8,128]{2,1,0:T(8,128)S(1)} collective-permute-done((f32[4,8,128]{2,1,0:T(8,128)S(1)}, f32[4,8,128]{2,1,0:T(8,128)S(1)}, u32[]{:S(2)}, u32[]{:S(2)}) %collective-permute-start.6) | collective-permute-done | bytes 16416 | tf_op jit(solution)/shard_map/ppermute | solution.py:521
  55.0 3.4 %collective-permute-done.7.refs_7_ = f32[4,8,128]{2,1,0:T(8,128)S(1)} collective-permute-done((f32[4,8,128]{2,1,0:T(8,128)S(1)}, f32[4,8,128]{2,1,0:T(8,128)S(1)}, u32[]{:S(2)}, u32[]{:S(2)}) %collective-permute-start.7) | collective-permute-done | bytes 16416 | tf_op jit(solution)/shard_map/ppermute | solution.py:513
  58.4 2.3 %edge_gradients.1 = (f32[2,128,512]{2,1,0:T(8,128)S(1)}, f32[512,512]{1,0:T(8,128)S(1)}, f32[512,512]{1,0:T(8,128)S(1)}, bf16[2,128,512]{2,1,0:T(8,128)(2,1)S(1)}, bf16[2,128,512]{2,1,0:T(8,128)(2,1)S(1)}) custom-call(bf16[2,256,512]{2,1,0:T(8,128)(2,1)S(1)} %copy-done.1, bf16[2,256,512]{2,1,0:T(8,128)(2,1)S(1)} %copy-done.3, ...), custom_call_target="tpu_custom_call" | custom-call | flops 3000000000 | bytes 1024 | tf_op jit(solution)/shard_map/edge_gradients/pallas_call | solution.py:444
  60.8 0.3 collective-permute-start.10
  61.0 2.8 %collective-permute-start.11 = (bf16[2,128,512]{2,1,0:T(8,128)(2,1)S(1)}, bf16[2,128,512]{2,1,0:T(8,128)(2,1)S(1)}, u32[]{:S(2)}, u32[]{:S(2)}) collective-permute-start(bf16[2,128,512]{2,1,0:T(8,128)(2,1)S(1)} %get-tuple-element.64), channel_id=1, source_target_pairs={{32,64},{64,32},{33,65},{65,33},{34,66},{66,34},{35,67},{67,35},{3... | collective-permute-start | bytes 786440 | tf_op jit(solution)/shard_map/ppermute | solution.py:521
  63.8 2.5 %mid_gradients.1 = (f32[2,128,512]{2,1,0:T(8,128)S(1)}, f32[512,512]{1,0:T(8,128)S(1)}, f32[512,512]{1,0:T(8,128)S(1)}) custom-call(bf16[2,256,512]{2,1,0:T(8,128)(2,1)S(1)} %copy-done.1, bf16[2,256,512]{2,1,0:T(8,128)(2,1)S(1)} %copy-done.3, bf16[2,256,512]{2,1,0:T(8,128)(2,1)S(1)} %collective-permute-done.q_0.refs_2_, ...), custom_call_target="tpu_custom_call" | custom-call | flops 3000000000 | bytes 1024 | tf_op jit(solution)/shard_map/mid_gradients/pallas_call | solution.py:457
  66.3 2.4 %collective-permute-done.11.from_b = bf16[2,128,512]{2,1,0:T(8,128)(2,1)S(1)} collective-permute-done((bf16[2,128,512]{2,1,0:T(8,128)(2,1)S(1)}, bf16[2,128,512]{2,1,0:T(8,128)(2,1)S(1)}, u32[]{:S(2)}, u32[]{:S(2)}) %collective-permute-start.11) | collective-permute-done | bytes 262176 | tf_op jit(solution)/shard_map/ppermute | solution.py:521
  68.7 1.3 %finish.1 = (bf16[32,16,512]{2,1,0:T(8,128)(2,1)}, bf16[32,16,512]{2,1,0:T(8,128)(2,1)}, bf16[32,16,512]{2,1,0:T(8,128)(2,1)}) custom-call(f32[2,128,512]{2,1,0:T(8,128)S(1)} %get-tuple-element.53.dq_edge, f32[2,128,512]{2,1,0:T(8,128)S(1)} %get-tuple-element.60.dq_mid, f32[512,512]{1,0:T(8,128)S(1)} %get-tuple-element.61.dk, ...), custom_call_target="tpu_custom_call" | custom-call | bytes 1024 | tf_op jit(solution)/shard_map/finish/pallas_call | solution.py:501
  (13 shorter events, 0.0 us)
Async XLA Ops:
  4.1 21.2 %collective-permute-start.2 = (bf16[2,128,512]{2,1,0:T(8,128)(2,1)}, bf16[2,128,512]{2,1,0:T(8,128)(2,1)S(1)}, u32[]{:S(2)}, u32[]{:S(2)}) collective-permute-start(bf16[2,128,512]{2,1,0:T(8,128)(2,1)} %get-tuple-element.38), channel_id=1, source_target_pairs={{0,32},{32,0},{64,96},{96,64},{1,33},{33,1},{65,97},{97,65},{2,34}... | collective-permute-start | bytes 786440 | tf_op jit(solution)/shard_map/ppermute | solution.py:513
  5.6 20.9 %collective-permute-start.3 = (bf16[2,128,512]{2,1,0:T(8,128)(2,1)}, bf16[2,128,512]{2,1,0:T(8,128)(2,1)S(1)}, u32[]{:S(2)}, u32[]{:S(2)}) collective-permute-start(bf16[2,128,512]{2,1,0:T(8,128)(2,1)} %get-tuple-element.39), channel_id=1, source_target_pairs={{32,64},{64,32},{33,65},{65,33},{34,66},{66,34},{35,67},{67,35},{3... | collective-permute-start | bytes 786440 | tf_op jit(solution)/shard_map/ppermute | solution.py:521
  8.8 34.1 %collective-permute-start = (bf16[2,256,512]{2,1,0:T(8,128)(2,1)}, bf16[2,256,512]{2,1,0:T(8,128)(2,1)S(1)}, u32[]{:S(2)}, u32[]{:S(2)}) collective-permute-start(bf16[2,256,512]{2,1,0:T(8,128)(2,1)} %get-tuple-element.34.side_0.refs_0_), channel_id=1, source_target_pairs={{1,2},{2,1},{3,4},{4,3},{5,6},{6,5},{7,8},{8,7},{9,10},{10,9},{11,... | collective-permute-start | bytes 1572872 | tf_op jit(solution)/shard_map/ppermute | solution.py:521
  17.1 25.7 %collective-permute-start.1 = (bf16[2,256,512]{2,1,0:T(8,128)(2,1)}, bf16[2,256,512]{2,1,0:T(8,128)(2,1)S(1)}, u32[]{:S(2)}, u32[]{:S(2)}) collective-permute-start(bf16[2,256,512]{2,1,0:T(8,128)(2,1)} %get-tuple-element.35.side_1.refs_1_), channel_id=1, source_target_pairs={{0,1},{1,0},{2,3},{3,2},{4,5},{5,4},{6,7},{7,6},{8,9},{9,8},{10,11... | collective-permute-start | bytes 1572872 | tf_op jit(solution)/shard_map/ppermute | solution.py:513
  17.1 1.0 %copy-start.4 = (bf16[32,16,512]{2,1,0:T(8,128)(2,1)S(1)}, bf16[32,16,512]{2,1,0:T(8,128)(2,1)}, u32[]{:S(2)}) copy-start(bf16[32,16,512]{2,1,0:T(8,128)(2,1)} %k_ref.3) | copy-start | bytes 1572868
  18.2 1.0 %copy-start.5 = (bf16[32,16,512]{2,1,0:T(8,128)(2,1)S(1)}, bf16[32,16,512]{2,1,0:T(8,128)(2,1)}, u32[]{:S(2)}) copy-start(bf16[32,16,512]{2,1,0:T(8,128)(2,1)} %v_ref.3) | copy-start | bytes 1572868
  20.8 1.0 %copy-start = (bf16[2,256,512]{2,1,0:T(8,128)(2,1)S(1)}, bf16[2,256,512]{2,1,0:T(8,128)(2,1)}, u32[]{:S(2)}) copy-start(bf16[2,256,512]{2,1,0:T(8,128)(2,1)} %get-tuple-element.34.side_0.refs_0_) | copy-start | bytes 1572868
  21.9 1.0 %copy-start.2 = (bf16[2,256,512]{2,1,0:T(8,128)(2,1)S(1)}, bf16[2,256,512]{2,1,0:T(8,128)(2,1)}, u32[]{:S(2)}) copy-start(bf16[2,256,512]{2,1,0:T(8,128)(2,1)} %get-tuple-element.35.side_1.refs_1_) | copy-start | bytes 1572868
  28.9 11.0 %collective-permute-start.4 = (f32[4,8,128]{2,1,0:T(8,128)S(1)}, f32[4,8,128]{2,1,0:T(8,128)S(1)}, u32[]{:S(2)}, u32[]{:S(2)}) collective-permute-start(f32[4,8,128]{2,1,0:T(8,128)S(1)} %get-tuple-element.42.refs_4_), channel_id=1, source_target_pairs={{1,2},{2,1},{3,4},{4,3},{5,6},{6,5},{7,8},{8,7},{9,10},{10,9},{11,... | collective-permute-start | bytes 49160 | tf_op jit(solution)/shard_map/ppermute | solution.py:521
  38.7 4.1 %collective-permute-start.5 = (f32[4,8,128]{2,1,0:T(8,128)S(1)}, f32[4,8,128]{2,1,0:T(8,128)S(1)}, u32[]{:S(2)}, u32[]{:S(2)}) collective-permute-start(f32[4,8,128]{2,1,0:T(8,128)S(1)} %get-tuple-element.43.refs_5_), channel_id=1, source_target_pairs={{0,1},{1,0},{2,3},{3,2},{4,5},{5,4},{6,7},{7,6},{8,9},{9,8},{10,11... | collective-permute-start | bytes 49160 | tf_op jit(solution)/shard_map/ppermute | solution.py:513
  42.8 15.6 %copy-start.1 = (bf16[2,256,512]{2,1,0:T(8,128)(2,1)S(1)}, bf16[2,256,512]{2,1,0:T(8,128)(2,1)}, u32[]{:S(2)}) copy-start(bf16[2,256,512]{2,1,0:T(8,128)(2,1)} %get-tuple-element.34.side_0.refs_0_) | copy-start | bytes 1572868
  42.8 15.6 %copy-start.3 = (bf16[2,256,512]{2,1,0:T(8,128)(2,1)S(1)}, bf16[2,256,512]{2,1,0:T(8,128)(2,1)}, u32[]{:S(2)}) copy-start(bf16[2,256,512]{2,1,0:T(8,128)(2,1)} %get-tuple-element.35.side_1.refs_1_) | copy-start | bytes 1572868
  46.6 8.4 %collective-permute-start.6 = (f32[4,8,128]{2,1,0:T(8,128)S(1)}, f32[4,8,128]{2,1,0:T(8,128)S(1)}, u32[]{:S(2)}, u32[]{:S(2)}) collective-permute-start(f32[4,8,128]{2,1,0:T(8,128)S(1)} %get-tuple-element.45), channel_id=1, source_target_pairs={{1,2},{2,1},{3,4},{4,3},{5,6},{6,5},{7,8},{8,7},{9,10},{10,9},{11,... | collective-permute-start | bytes 49160 | tf_op jit(solution)/shard_map/ppermute | solution.py:521
  50.9 7.5 %collective-permute-start.7 = (f32[4,8,128]{2,1,0:T(8,128)S(1)}, f32[4,8,128]{2,1,0:T(8,128)S(1)}, u32[]{:S(2)}, u32[]{:S(2)}) collective-permute-start(f32[4,8,128]{2,1,0:T(8,128)S(1)} %get-tuple-element.46), channel_id=1, source_target_pairs={{0,1},{1,0},{2,3},{3,2},{4,5},{5,4},{6,7},{7,6},{8,9},{9,8},{10,11... | collective-permute-start | bytes 49160 | tf_op jit(solution)/shard_map/ppermute | solution.py:513
  50.9 15.4 %collective-permute-start.8 = (bf16[256,512]{1,0:T(8,128)(2,1)S(1)}, bf16[256,512]{1,0:T(8,128)(2,1)S(1)}, u32[]{:S(2)}, u32[]{:S(2)}) collective-permute-start(bf16[256,512]{1,0:T(8,128)(2,1)S(1)} %get-tuple-element.51.refs_14_), channel_id=1, source_target_pairs={{1,2},{2,1},{3,4},{4,3},{5,6},{6,5},{7,8},{8,7},{9,10},{10,9},{11,... | collective-permute-start | bytes 786440 | tf_op jit(solution)/shard_map/ppermute | solution.py:521
  53.9 12.4 %collective-permute-start.9 = (bf16[256,512]{1,0:T(8,128)(2,1)S(1)}, bf16[256,512]{1,0:T(8,128)(2,1)S(1)}, u32[]{:S(2)}, u32[]{:S(2)}) collective-permute-start(bf16[256,512]{1,0:T(8,128)(2,1)S(1)} %get-tuple-element.52.refs_15_), channel_id=1, source_target_pairs={{0,1},{1,0},{2,3},{3,2},{4,5},{5,4},{6,7},{7,6},{8,9},{9,8},{10,11... | collective-permute-start | bytes 786440 | tf_op jit(solution)/shard_map/ppermute | solution.py:513
  60.8 5.6 %collective-permute-start.10 = (bf16[2,128,512]{2,1,0:T(8,128)(2,1)S(1)}, bf16[2,128,512]{2,1,0:T(8,128)(2,1)S(1)}, u32[]{:S(2)}, u32[]{:S(2)}) collective-permute-start(bf16[2,128,512]{2,1,0:T(8,128)(2,1)S(1)} %get-tuple-element.63), channel_id=1, source_target_pairs={{0,32},{32,0},{64,96},{96,64},{1,33},{33,1},{65,97},{97,65},{2,34}... | collective-permute-start | bytes 786440 | tf_op jit(solution)/shard_map/ppermute | solution.py:513
  61.0 7.7 %collective-permute-start.11 = (bf16[2,128,512]{2,1,0:T(8,128)(2,1)S(1)}, bf16[2,128,512]{2,1,0:T(8,128)(2,1)S(1)}, u32[]{:S(2)}, u32[]{:S(2)}) collective-permute-start(bf16[2,128,512]{2,1,0:T(8,128)(2,1)S(1)} %get-tuple-element.64), channel_id=1, source_target_pairs={{32,64},{64,32},{33,65},{65,33},{34,66},{66,34},{35,67},{67,35},{3... | collective-permute-start | bytes 786440 | tf_op jit(solution)/shard_map/ppermute | solution.py:521

commit v7 on v5

--- a/solution.py
+++ b/solution.py
@@ -22,6 +22,7 @@
 BF16 = jnp.bfloat16
 VMEM_LIMIT = 20 * 1024 * 1024
 PACK_LIMIT = 62 * 1024 * 1024
+any_spec = pl.BlockSpec(memory_space=pl.ANY)
 EDGE_ROWS = (0, 3)
 MID_ROWS = (1, 2)
 ORDER = EDGE_ROWS + MID_ROWS
@@ -49,7 +50,7 @@
 
 
 def ordered(first, second):
-    swap = lax.axis_index("lon") % 2 == 1
+    swap = lax.axis_index("lon") % 2 == 0
     return jnp.where(swap, second, first), jnp.where(swap, first, second)
 
 
@@ -68,30 +69,46 @@
     return copies
 
 
-def pack_queries_kernel(q_ref, g_ref, side_0, side_1, buffers, sems, packed, out_sems):
+def key_tile(buffer):
+    return jnp.concatenate(split_columns(buffer), axis=0)
+
+
+def pack_queries_kernel(q_ref, g_ref, k_ref, v_ref, side_0, side_1, edge_a, edge_b, buffers, sems, key_buffers, key_sems,
+                        packed, out_sems, packed_keys, key_out_sems):
+    key_copies = fetch((k_ref, v_ref), EDGE_ROWS, key_buffers, key_sems)
     copies = fetch((q_ref, g_ref), ORDER, buffers, sems)
     sends = []
+
+    def send(source, out, sem):
+        sends.append(pltpu.make_async_copy(source, out, sem))
+        sends[-1].start()
+
+    for place, edge in enumerate((edge_a, edge_b)):
+        for i in range(2):
+            key_copies[i][place].wait()
+            packed_keys[place, i] = key_tile(key_buffers[i, place])
+            send(packed_keys.at[place, i], edge.at[i], key_out_sems.at[place, i])
     for place in range(ROWS):
         for i in range(2):
             copies[i][place].wait()
             for side, (value, out) in enumerate(zip(split_columns(buffers[i, place]), (side_0, side_1))):
                 packed[side, i, place] = value
-                sends.append(pltpu.make_async_copy(packed.at[side, i, place],
-                                                   out.at[i, pl.ds(place * CELLS, CELLS)], out_sems.at[side, i, place]))
-                sends[-1].start()
-    for send in sends:
-        send.wait()
+                send(packed.at[side, i, place], out.at[i, pl.ds(place * CELLS, CELLS)], out_sems.at[side, i, place])
+    for copy in sends:
+        copy.wait()
 
 
 def pack_queries(*operands):
     return pl.pallas_call(
         pack_queries_kernel,
-        in_specs=[pl.BlockSpec(memory_space=pl.ANY)] * 2,
-        out_specs=[pl.BlockSpec(memory_space=pl.ANY)] * 2,
-        out_shape=[struct((2, ROWS * CELLS, FEAT), BF16)] * 2,
+        in_specs=[any_spec] * 4,
+        out_specs=[any_spec] * 4,
+        out_shape=[struct((2, ROWS * CELLS, FEAT), BF16)] * 2 + [struct((2, PAIR, FEAT), BF16)] * 2,
         scratch_shapes=[
             pltpu.VMEM((2, ROWS, 8, 16, FEAT), BF16), pltpu.SemaphoreType.DMA((2, ROWS)),
+            pltpu.VMEM((2, 2, 8, 16, FEAT), BF16), pltpu.SemaphoreType.DMA((2, 2)),
             pltpu.VMEM((2, 2, ROWS, CELLS, FEAT), BF16), pltpu.SemaphoreType.DMA((2, 2, ROWS)),
+            pltpu.VMEM((2, 2, PAIR, FEAT), BF16), pltpu.SemaphoreType.DMA((2, 2)),
         ],
         compiler_params=params(PACK_LIMIT),
         cost_estimate=cost(0, 3 << 20),
@@ -99,24 +116,19 @@
     )(*operands)
 
 
-def pack_keys_kernel(k_ref, v_ref, kd, vd, edge_a, edge_b, buffers, sems):
+def pack_keys_kernel(k_ref, v_ref, kd, vd, buffers, sems):
     copies = fetch((k_ref, v_ref), range(ROWS), buffers, sems)
     for t in range(ROWS):
         for i, out in enumerate((kd, vd)):
             copies[i][t].wait()
-            tile = jnp.concatenate(split_columns(buffers[i, t]), axis=0)
-            out[t * PAIR:(t + 1) * PAIR] = tile
-            if t == 0:
-                edge_a[i] = tile
-            if t == ROWS - 1:
-                edge_b[i] = tile
+            out[t * PAIR:(t + 1) * PAIR] = key_tile(buffers[i, t])
 
 
 def pack_keys(*operands):
     return pl.pallas_call(
         pack_keys_kernel,
-        in_specs=[pl.BlockSpec(memory_space=pl.ANY)] * 2,
-        out_shape=[struct((ROWS * PAIR, FEAT), BF16)] * 2 + [struct((2, PAIR, FEAT), BF16)] * 2,
+        in_specs=[any_spec] * 2,
+        out_shape=[struct((ROWS * PAIR, FEAT), BF16)] * 2,
         scratch_shapes=[pltpu.VMEM((2, ROWS, 8, 16, FEAT), BF16), pltpu.SemaphoreType.DMA((2, ROWS))],
         compiler_params=params(),
         cost_estimate=cost(0, 3 << 20),
@@ -242,9 +254,9 @@
 turned_wide = pl.BlockSpec((WIDE, ROWS * PAIR), lambda g: (g, 0))
 edge_turned_wide = pl.BlockSpec((2, WIDE, PAIR), lambda g: (0, g, 0))
 held_wide = pl.BlockSpec((2, 2, 3 * PAIR, WIDE), lambda g: (g, 0, 0, 0))
-halo_wide = pl.BlockSpec((1, 2, 2, 3 * CELLS, WIDE), lambda g: (g, 0, 0, 0, 0))
-halo_shape = struct((GROUPS, 2, 2, 3 * CELLS, WIDE), F32)
-any_spec = pl.BlockSpec(memory_space=pl.ANY)
+halo_wide = pl.BlockSpec((1, 2, 3 * CELLS, WIDE), lambda g: (g, 0, 0, 0))
+halo_shape = struct((GROUPS, 2, 3 * CELLS, WIDE), F32)
+weight_shape = struct((GROUPS, 2, 3 * CELLS, WIDE), BF16)
 
 
 def own_scores(rows, side_a, side_b, kd, vd, edges, part, s_out, d_out):
@@ -316,97 +328,85 @@
     )(*operands)
 
 
-def halo_scores_kernel(q_0, q_1, kd, vd, edge_a, edge_b, edge_part, mid_part,
-                       send_0, send_1, s_edge, d_edge, s_mid, d_mid):
+def halo_scores_kernel(c, q_in, kd, vd, edge_a, edge_b, edge_part, mid_part, send, s_edge, d_edge, s_mid, d_mid):
     masks = head_masks(WIDE)
     groups = ((EDGE_ROWS, edge_part, s_edge, d_edge), (MID_ROWS, mid_part, s_mid, d_mid))
     for group, (rows, part, s_out, d_out) in enumerate(groups):
         base = 8 * group
-        for c, (q_in, send) in enumerate(((q_0, send_0), (q_1, send_1))):
-            for j in range(2):
-                send[j, base:base + 4] = part[j, 4 * c:4 * c + 4]
-            for place, t in enumerate(rows):
-                at = at_tokens(2 * group + place)
-                queries = stacked([q_in[0, at]], masks)
-                grads = stacked([q_in[1, at]], masks)
-                scores = score_block(column_window(c, kd, (edge_a, edge_b), 0, t), queries, t)
-                dprobs = matmul(column_window(c, vd, (edge_a, edge_b), 1, t), grads, (1, 1))
-                s_out[0, place, c] = scores
-                d_out[0, place, c] = dprobs
-                for w, values in enumerate(row_stats(scores, dprobs)):
-                    index = base + 4 + 2 * w + place
-                    for j in range(2):
-                        send[j, index:index + 1] = values[:, pair_lanes(j)]
-
-
-def halo_scores(*operands):
+        for j in range(2):
+            send[j, base:base + 4] = part[j, 4 * c:4 * c + 4]
+        for place, t in enumerate(rows):
+            at = at_tokens(2 * group + place)
+            queries = stacked([q_in[0, at]], masks)
+            grads = stacked([q_in[1, at]], masks)
+            scores = score_block(column_window(c, kd, (edge_a, edge_b), 0, t), queries, t)
+            dprobs = matmul(column_window(c, vd, (edge_a, edge_b), 1, t), grads, (1, 1))
+            s_out[0, place] = scores
+            d_out[0, place] = dprobs
+            for w, values in enumerate(row_stats(scores, dprobs)):
+                index = base + 4 + 2 * w + place
+                for j in range(2):
+                    send[j, index:index + 1] = values[:, pair_lanes(j)]
+
+
+def halo_scores(c, *operands):
     part = pl.BlockSpec((2, 8, PAIR), lambda g: (g, 0, 0))
     return pl.pallas_call(
-        halo_scores_kernel,
+        functools.partial(halo_scores_kernel, c),
         grid=(GROUPS,),
-        in_specs=[all_tokens] * 2 + [keys_wide] * 2 + [edge_wide] * 2 + [part] * 2,
-        out_specs=[all_stats] * 2 + [halo_wide] * 4,
-        out_shape=[stats_shape] * 2 + [halo_shape] * 4,
+        in_specs=[all_tokens] + [keys_wide] * 2 + [edge_wide] * 2 + [part] * 2,
+        out_specs=[all_stats] + [halo_wide] * 4,
+        out_shape=[stats_shape] + [halo_shape] * 4,
         compiler_params=params(),
         cost_estimate=cost(2e9, 1 << 10),
-        name="halo_scores",
-    )(*operands)
-
-
-def halo_weights(mine, theirs, s_in, d_in, c):
-    both = [both_parts(mine, theirs, j, 4) for j in range(2)]
-    log_total = jnp.concatenate([one[0] for one in both], axis=1)
-    delta = jnp.concatenate([one[1] for one in both], axis=1)
-    weights = []
-    for place in range(2):
-        probs = jnp.exp2(s_in[0, place, c] - log_total[place:place + 1])
-        dscores = probs * (d_in[0, place, c] - delta[place:place + 1])
-        weights.append((probs.astype(BF16), dscores.astype(BF16)))
-    return weights
-
-
-def halo_queries_kernel(send_0, send_1, recv_0, recv_1, s_edge, d_edge, s_mid, d_mid, own_turned, edges_turned,
-                        out_0, out_1):
+        name="halo_scores_" + "ab"[c],
+    )(*operands)
+
+
+def halo_queries_kernel(c, send, recv, s_edge, d_edge, s_mid, d_mid, own_turned, edges_turned,
+                        out, p_edge, ds_edge, p_mid, ds_mid):
     lane = lax.broadcasted_iota(jnp.int32, (1, PAIR), 1)
     none = jnp.zeros((CELLS, PAIR), BF16)
-    groups = ((EDGE_ROWS, s_edge, d_edge), (MID_ROWS, s_mid, d_mid))
-    for group, (rows, s_in, d_in) in enumerate(groups):
-        stats = [ref.at[:, pl.ds(8 * group, 8)] for ref in (send_0, send_1, recv_0, recv_1)]
-        weights = [halo_weights(stats[c], stats[2 + c], s_in, d_in, c) for c in range(2)]
+    groups = ((EDGE_ROWS, s_edge, d_edge, p_edge, ds_edge), (MID_ROWS, s_mid, d_mid, p_mid, ds_mid))
+    for group, (rows, s_in, d_in, p_out, ds_out) in enumerate(groups):
+        mine, theirs = [ref.at[:, pl.ds(8 * group, 8)] for ref in (send, recv)]
+        both = [both_parts(mine, theirs, j, 4) for j in range(2)]
+        log_total, delta = [jnp.concatenate([one[w] for one in both], axis=1) for w in range(2)]
         for place, t in enumerate(rows):
+            probs = jnp.exp2(s_in[0, place] - log_total[place:place + 1])
+            dscores = (probs * (d_in[0, place] - delta[place:place + 1])).astype(BF16)
+            p_out[0, place] = probs.astype(BF16)
+            ds_out[0, place] = dscores
             for j in range(2):
                 pieces = []
                 for i in range(3):
-                    parts = [weights[c][place][1][at_tokens(i), pair_lanes(j)] for c in range(2)]
-                    pieces += [jnp.concatenate([parts[0], none], axis=1), jnp.concatenate([none, parts[1]], axis=1)]
-                keys_turned = turned_window(own_turned, edges_turned, t, j)
-                grads = query_parts(keys_turned, jnp.concatenate(pieces, axis=0), lane)
-                for out, grad in zip((out_0, out_1), grads):
-                    out[at_tokens(2 * group + place), pair_lanes(j)] = grad.astype(BF16)
-
-
-def halo_queries(*operands):
-    return pl.pallas_call(
-        halo_queries_kernel,
+                    part = dscores[at_tokens(i), pair_lanes(j)]
+                    pieces += [none, part] if c else [part, none]
+                turned = matmul(turned_window(own_turned, edges_turned, t, j), jnp.concatenate(pieces, axis=0), (1, 0))
+                grad = turned.T * SCALE
+                out[at_tokens(2 * group + place), pair_lanes(j)] = jnp.where(lane < 64, grad[:CELLS], grad[CELLS:]).astype(BF16)
+
+
+def halo_queries(c, *operands):
+    return pl.pallas_call(
+        functools.partial(halo_queries_kernel, c),
         grid=(GROUPS,),
-        in_specs=[all_stats] * 4 + [halo_wide] * 4 + [turned_wide, edge_turned_wide],
-        out_specs=[all_parts] * 2,
-        out_shape=[struct((2 * CHUNK, FEAT), BF16)] * 2,
+        in_specs=[all_stats] * 2 + [halo_wide] * 4 + [turned_wide, edge_turned_wide],
+        out_specs=[all_parts] + [halo_wide] * 4,
+        out_shape=[struct((2 * CHUNK, FEAT), BF16)] + [weight_shape] * 4,
         compiler_params=params(),
         cost_estimate=cost(2e9, 1 << 10),
-        name="halo_queries",
-    )(*operands)
-
-
-def row_gradients(rows, side_a, side_b, q_a, q_b, send_a, send_b, recv_a, recv_b, s_own, d_own, s_halo, d_halo,
+        name="halo_queries_" + "ab"[c],
+    )(*operands)
+
+
+def row_gradients(rows, side_0, side_1, q_0, q_1, send_0, send_1, recv_0, recv_1, s_own, d_own, p_0, ds_0, p_1, ds_1,
                   own_turned, edges_turned, dq_ref):
     masks, wide_masks = head_masks(PAIR), head_masks(WIDE)
     lane = lax.broadcasted_iota(jnp.int32, (1, PAIR), 1)
-    sides = ((q_a, send_a, recv_a), (q_b, send_b, recv_b))
-    halo = [halo_weights(mine, theirs, s_halo, d_halo, c) for c, (_, mine, theirs) in enumerate(sides)]
     merged_rows = []
     for j in range(2):
-        both = [both_parts(mine, theirs, j, 0) for _, mine, theirs in sides]
+        both = [both_parts(send_0, recv_0, j, 0), both_parts(send_1, recv_1, j, 0)]
         merged_rows.append([jnp.concatenate([one[w] for one in both], axis=1) for w in range(2)])
     results = []
     for place, t in enumerate(rows):
@@ -414,8 +414,8 @@
         sums = [[], []]
         for j in range(2):
             lanes = pair_lanes(j)
-            queries = stacked([side_a[0, at, lanes], side_b[0, at, lanes]], masks)
-            grads = stacked([side_a[1, at, lanes], side_b[1, at, lanes]], masks)
+            queries = stacked([side_0[0, at, lanes], side_1[0, at, lanes]], masks)
+            grads = stacked([side_0[1, at, lanes], side_1[1, at, lanes]], masks)
             log_total, delta = merged_rows[j]
             probs = jnp.exp2(s_own[j, place] - log_total[row])
             dscores = (probs * (d_own[j, place] - delta[row])).astype(BF16)
@@ -425,17 +425,16 @@
             sums[1].append(matmul(probs.astype(BF16), grads, (1, 0)))
         sums = [jnp.concatenate(parts, axis=1) for parts in sums]
         edge_parts = []
-        for c in range(2):
-            probs, dscores = halo[c][place]
-            edge_parts.append((matmul(dscores, stacked([sides[c][0][0, at]], wide_masks), (1, 0)),
-                               matmul(probs, stacked([sides[c][0][1, at]], wide_masks), (1, 0))))
+        for q_in, p_halo, ds_halo in ((q_0, p_0, ds_0), (q_1, p_1, ds_1)):
+            edge_parts.append((matmul(ds_halo[0, place], stacked([q_in[0, at]], wide_masks), (1, 0)),
+                               matmul(p_halo[0, place], stacked([q_in[1, at]], wide_masks), (1, 0))))
         results.append([jnp.concatenate([sums[w][at_tokens(2 * i + c)] + edge_parts[c][w][at_tokens(i)]
                                          for i in range(3) for c in range(2)], axis=0) for w in range(2)])
     return results
 
 
 def edge_kernel(*refs):
-    operands, (_, _, dq_ref, dk_ref, dv_ref, out_a, out_b) = refs[:14], refs[14:]
+    operands, (_, _, dq_ref, dk_ref, dv_ref, out_a, out_b) = refs[:16], refs[16:]
     upper, lower = row_gradients(EDGE_ROWS, *operands, dq_ref)
     for which, (out, scale) in enumerate(((dk_ref, SCALE), (dv_ref, 1.0))):
         top, bottom = upper[which] * scale, lower[which] * scale
@@ -446,7 +445,7 @@
 
 
 def mid_kernel(*refs):
-    operands, (dk_in, dv_in, dq_ref, dk_ref, dv_ref) = refs[:13], refs[13:]
+    operands, (dk_in, dv_in, dq_ref, dk_ref, dv_ref) = refs[:15], refs[15:]
     upper, lower = row_gradients(MID_ROWS, *operands, None, dq_ref)
     for which, (sums, out, scale) in enumerate(((dk_in, dk_ref, SCALE), (dv_in, dv_ref, 1.0))):
         out[0:PAIR] = sums[0:PAIR] + upper[which][:PAIR] * scale
@@ -455,7 +454,7 @@
 
 
 def row_specs(group):
-    return ([tokens_wide(group)] * 4 + [stats_wide(group)] * 4 + [held_wide] * 2 + [halo_wide] * 2 + [turned_wide])
+    return ([tokens_wide(group)] * 4 + [stats_wide(group)] * 4 + [held_wide] * 2 + [halo_wide] * 4 + [turned_wide])
 
 
 GRAD_SPECS = [sums_wide] + [keys_wide] * 2
@@ -543,30 +542,34 @@
     return lax.ppermute(x, axis, pairs)
 
 
-def over_lon(side_0, side_1):
-    return swap_b(side_0, "lon", True), swap_a(side_1, "lon")
-
-
-def over_lat(side_a, side_b):
-    return swap_a(side_a, "lat"), swap_b(side_b, "lat", False)
+def swap_lon(c, x):
+    return swap_b(x, "lon", True) if c else swap_a(x, "lon")
 
 
 def on_device(query_vectors, key_vectors, value_vectors, output_grads):
-    sides = pack_queries(query_vectors, output_grads)
-    kd, vd, own_edge_a, own_edge_b = pack_keys(key_vectors, value_vectors)
-    halos = over_lon(*sides)
-    edges = over_lat(own_edge_a, own_edge_b)
+    *sides, own_edge_a, own_edge_b = pack_queries(query_vectors, output_grads, key_vectors, value_vectors)
+    kd, vd = pack_keys(key_vectors, value_vectors)
+    edge_b = swap_b(own_edge_b, "lat", False)
+    halos = [swap_lon(c, side) for c, side in enumerate(sides)]
+    edges = (swap_a(own_edge_a, "lat"), edge_b)
     mid_part, *mid_own, turned = mid_scores(*sides, kd, vd)
     edge_part, *edge_own = edge_scores(*sides, kd, vd, *edges)
-    *sends, s_edge, d_edge, s_mid, d_mid = halo_scores(*halos, kd, vd, *edges, edge_part, mid_part)
-    stats = (*sends, *over_lon(*sends))
     edges_turned = turn_edges(*edges)
-    halo_dq = halo_queries(*stats, s_edge, d_edge, s_mid, d_mid, turned, edges_turned)
-    dq_parts = over_lon(*halo_dq)
-    shared = (*sides, *halos, *stats)
-    dq_edge, dk, dv, out_a, out_b = edge_gradients(*shared, *edge_own, s_edge, d_edge, turned, edges_turned, *halo_dq)
-    key_parts = over_lat(out_a, out_b)
-    dq_mid, dk, dv = mid_gradients(*shared, *mid_own, s_mid, d_mid, turned, dk, dv)
+    sends, recvs, halo_dq, dq_parts, weights = [], [], [], [], []
+    for c in range(2):
+        send, *held = halo_scores(c, halos[c], kd, vd, *edges, edge_part, mid_part)
+        recv = swap_lon(c, send)
+        grad, *weight = halo_queries(c, send, recv, *held, turned, edges_turned)
+        sends.append(send)
+        recvs.append(recv)
+        halo_dq.append(grad)
+        dq_parts.append(swap_lon(c, grad))
+        weights.append(weight)
+    shared = (*sides, *halos, *sends, *recvs)
+    dq_edge, dk, dv, out_a, out_b = edge_gradients(*shared, *edge_own, *weights[0][:2], *weights[1][:2], turned, edges_turned,
+                                                   *halo_dq)
+    key_parts = (swap_a(out_a, "lat"), swap_b(out_b, "lat", False))
+    dq_mid, dk, dv = mid_gradients(*shared, *mid_own, *weights[0][2:], *weights[1][2:], turned, dk, dv)
     return tuple(finish(dq_edge, dq_mid, dk, dv, *dq_parts, *key_parts))
 
 

time: 68.7 us -> 62.8 us (0.914)
  waiting for transfers between devices: 17.1 us -> 3.6 us
  starting transfers between devices: 27.4 us -> 33.1 us
  Pallas kernels: 18.8 us -> 20.8 us
    ppermute x5, waiting for transfers between devices: 13.9 us -> 3.59 us  [swap_b(): return lax.ppermute(x, axis, pairs)]
    ppermute x5, starting transfers between devices: 26.2 us -> 31.3 us  [swap_b(): return lax.ppermute(x, axis, pairs)]
    ppermute x5, waiting for transfers between devices: 3.21 us -> 0.01 us  [swap_a(): lax.ppermute(x, axis, [(i, i ^ 1) for i in range(lax.axis_size(axis))])]
    pallas_call x4 -> x6, Pallas kernels: 7.23 us -> 9.23 us  [the longest x2 2.76 us: halo_scores(): pl.pallas_call(functools.partial(halo_scores_kernel, c), grid=(GROUPS,),...]
  transfers between devices with their start and end apart: 10 -> 10, of which waited for: 5 -> 2; matrix products, arithmetic and copies ran while one was open for 0% -> 0% of each run, Pallas kernels for 18% -> 27%
where the time goes in v7:
time: 62.8 us; the launch traced here: 62.4 us
  starting transfers between devices  33.1 us (53%)
  Pallas kernels  20.8 us (33%)
  local copies, waits for them, and re-layouts  4.17 us (7%)
  waiting for transfers between devices  3.6 us (6%)
  between operations  0.84 us (1%)
    ppermute x5, starting transfers between devices, swap_b(): return lax.ppermute(x, axis, pairs)  31.3 us
    unnamed x12, local copies, waits for them, and re-layouts  4.17 us
    ppermute x5, waiting for transfers between devices, swap_b(): return lax.ppermute(x, axis, pairs)  3.59 us
    pallas_call x2, Pallas kernels, halo_scores(): pl.pallas_call(functools.partial(halo_scores_kernel, c), grid=(GROUPS,),...  2.76 us
    pallas_call x1, Pallas kernels, pack_queries(): pl.pallas_call(pack_queries_kernel, in_specs=[any_spec] * 4, out_specs=[a...  2.67 us
    pallas_call x1, Pallas kernels, mid_gradients(): pl.pallas_call(mid_kernel, grid=(GROUPS,), in_specs=row_specs(MID) + [key...  2.52 us
    pallas_call x1, Pallas kernels, edge_scores(): pl.pallas_call(edge_scores_kernel, grid=(PAIRS,), in_specs=[tokens_spec(E...  2.45 us
    pallas_call x1, Pallas kernels, edge_gradients(): pl.pallas_call(edge_kernel, grid=(GROUPS,), in_specs=row_specs(EDGE) + [e...  2.43 us
  transfers between devices with their start and end apart: 10, of which 2 were waited for; matrix products, arithmetic and copies ran while one was open for 0% of the time, Pallas kernels for 27%

profile of v7, /device:TPU:1, one launch (start us, length us, event | category | flops | bytes accessed | tf_op | source)
XLA Modules:
  0.0 62.4 jit_solution(4867925451359377964)
XLA Ops:
  0.6 2.7 %pack_queries.1 = (bf16[2,256,512]{2,1,0:T(8,128)(2,1)}, bf16[2,256,512]{2,1,0:T(8,128)(2,1)}, bf16[2,128,512]{2,1,0:T(8,128)(2,1)}, bf16[2,128,512]{2,1,0:T(8,128)(2,1)}) custom-call(bf16[32,16,512]{2,1,0:T(8,128)(2,1)} %q_ref.1, bf16[32,16,512]{2,1,0:T(8,128)(2,1)} %g_ref.1, bf16[32,16,512]{2,1,0:T(8,128)(2,1)} %k_ref.3, bf16[32,16,512]{2,1,0:T(8,128)(2,1)} %v_ref.3), custom_call_target="tpu_custom_call" | custom-call | bytes 3145728 | tf_op jit(solution)/shard_map/pack_queries/pallas_call | solution.py:102
  3.3 1.5 %collective-permute-start.2 = (bf16[2,128,512]{2,1,0:T(8,128)(2,1)}, bf16[2,128,512]{2,1,0:T(8,128)(2,1)S(1)}, u32[]{:S(2)}, u32[]{:S(2)}) collective-permute-start(bf16[2,128,512]{2,1,0:T(8,128)(2,1)} %get-tuple-element.48), channel_id=1, source_target_pairs={{0,32},{32,0},{64,96},{96,64},{1,33},{33,1},{65,97},{97,65},{2,34}... | collective-permute-start | bytes 786440 | tf_op jit(solution)/shard_map/ppermute | solution.py:534
  4.8 3.2 %collective-permute-start.3 = (bf16[2,128,512]{2,1,0:T(8,128)(2,1)}, bf16[2,128,512]{2,1,0:T(8,128)(2,1)S(1)}, u32[]{:S(2)}, u32[]{:S(2)}) collective-permute-start(bf16[2,128,512]{2,1,0:T(8,128)(2,1)} %get-tuple-element.49), channel_id=1, source_target_pairs={{32,64},{64,32},{33,65},{65,33},{34,66},{66,34},{35,67},{67,35},{3... | collective-permute-start | bytes 786440 | tf_op jit(solution)/shard_map/ppermute | solution.py:542
  8.0 8.4 %collective-permute-start.1 = (bf16[2,256,512]{2,1,0:T(8,128)(2,1)}, bf16[2,256,512]{2,1,0:T(8,128)(2,1)S(1)}, u32[]{:S(2)}, u32[]{:S(2)}) collective-permute-start(bf16[2,256,512]{2,1,0:T(8,128)(2,1)} %get-tuple-element.45.side_1.refs_1_), channel_id=1, source_target_pairs={{1,2},{2,1},{3,4},{4,3},{5,6},{6,5},{7,8},{8,7},{9,10},{10,9},{11,... | collective-permute-start | bytes 1572872 | tf_op jit(solution)/shard_map/ppermute | solution.py:542
  16.4 1.0 %copy-done.4 = bf16[32,16,512]{2,1,0:T(8,128)(2,1)S(1)} copy-done((bf16[32,16,512]{2,1,0:T(8,128)(2,1)S(1)}, bf16[32,16,512]{2,1,0:T(8,128)(2,1)}, u32[]{:S(2)}) %copy-start.4) | copy-done | bytes 524312
  17.4 1.0 %copy-done.5 = bf16[32,16,512]{2,1,0:T(8,128)(2,1)S(1)} copy-done((bf16[32,16,512]{2,1,0:T(8,128)(2,1)S(1)}, bf16[32,16,512]{2,1,0:T(8,128)(2,1)}, u32[]{:S(2)}) %copy-start.5) | copy-done | bytes 524312
  18.5 1.6 %pack_keys.1 = (bf16[512,512]{1,0:T(8,128)(2,1)S(1)}, bf16[512,512]{1,0:T(8,128)(2,1)S(1)}) custom-call(bf16[32,16,512]{2,1,0:T(8,128)(2,1)S(1)} %copy-done.4, bf16[32,16,512]{2,1,0:T(8,128)(2,1)S(1)} %copy-done.5), custom_call_target="tpu_custom_call" | custom-call | bytes 3145728 | tf_op jit(solution)/shard_map/pack_keys/pallas_call | solution.py:128
  20.1 0.0 copy-start
  20.1 1.0 %copy-done = bf16[2,256,512]{2,1,0:T(8,128)(2,1)S(1)} copy-done((bf16[2,256,512]{2,1,0:T(8,128)(2,1)S(1)}, bf16[2,256,512]{2,1,0:T(8,128)(2,1)}, u32[]{:S(2)}) %copy-start) | copy-done | bytes 524312
  21.1 1.0 %copy-done.2 = bf16[2,256,512]{2,1,0:T(8,128)(2,1)S(1)} copy-done((bf16[2,256,512]{2,1,0:T(8,128)(2,1)S(1)}, bf16[2,256,512]{2,1,0:T(8,128)(2,1)}, u32[]{:S(2)}) %copy-start.2) | copy-done | bytes 524312
  22.2 2.4 %mid_scores.1 = (f32[4,8,128]{2,1,0:T(8,128)S(1)}, f32[4,2,384,256]{3,2,1,0:T(8,128)S(1)}, f32[4,2,384,256]{3,2,1,0:T(8,128)S(1)}, bf16[512,512]{1,0:T(8,128)(2,1)S(1)}) custom-call(bf16[2,256,512]{2,1,0:T(8,128)(2,1)S(1)} %copy-done, bf16[2,256,512]{2,1,0:T(8,128)(2,1)S(1)} %copy-done.2, bf16[512,512]{1,0:T(8,128)(2,1)S(1)} %get-tuple-element.46.kd, ...), custom_call_target="tpu_custom_call" | custom-call | flops 2000000000 | bytes 1024 | tf_op jit(solution)/shard_map/mid_scores/pallas_call | solution.py:288
  24.6 0.0 copy-start.1
  24.6 0.0 copy-start.3
  24.6 0.0 collective-permute-done.2.edge_a
  24.6 1.2 %collective-permute-done.3.edge_b = bf16[2,128,512]{2,1,0:T(8,128)(2,1)S(1)} collective-permute-done((bf16[2,128,512]{2,1,0:T(8,128)(2,1)}, bf16[2,128,512]{2,1,0:T(8,128)(2,1)S(1)}, u32[]{:S(2)}, u32[]{:S(2)}) %collective-permute-start.3) | collective-permute-done | bytes 262176 | tf_op jit(solution)/shard_map/ppermute | solution.py:542
  25.7 0.5 turn_edges.1.edges_turned.refs_15_
  26.3 2.5 %edge_scores.1 = (f32[4,8,128]{2,1,0:T(8,128)S(1)}, f32[4,2,384,256]{3,2,1,0:T(8,128)S(1)}, f32[4,2,384,256]{3,2,1,0:T(8,128)S(1)}) custom-call(bf16[2,256,512]{2,1,0:T(8,128)(2,1)S(1)} %copy-done.1, bf16[2,256,512]{2,1,0:T(8,128)(2,1)S(1)} %copy-done.3, bf16[512,512]{1,0:T(8,128)(2,1)S(1)} %get-tuple-element.46.kd, ...), custom_call_target="tpu_custom_call" | custom-call | flops 2000000000 | bytes 1024 | tf_op jit(solution)/shard_map/edge_scores/pallas_call | solution.py:301
  28.7 0.0 collective-permute-done.1.q_in.refs_3_
  28.7 1.4 %halo_scores_b.1 = (f32[4,16,128]{2,1,0:T(8,128)S(1)}, f32[2,2,192,256]{3,2,1,0:T(8,128)S(1)}, f32[2,2,192,256]{3,2,1,0:T(8,128)S(1)}, f32[2,2,192,256]{3,2,1,0:T(8,128)S(1)}, f32[2,2,192,256]{3,2,1,0:T(8,128)S(1)}) custom-call(bf16[2,256,512]{2,1,0:T(8,128)(2,1)S(1)} %collective-permute-done.1.q_in.refs_3_, bf16[512,512]{1,0:T(8,128)(2,1)S(1)} %get-tuple-element.46.kd, ...), custom_call_target="tpu_custom_call" | custom-call | flops 2000000000 | bytes 1024 | tf_op jit(solution)/shard_map/halo_scores_b/pallas_call | solution.py:354
  30.1 10.0 %collective-permute-start.5 = (f32[4,16,128]{2,1,0:T(8,128)S(1)}, f32[4,16,128]{2,1,0:T(8,128)S(1)}, u32[]{:S(2)}, u32[]{:S(2)}) collective-permute-start(f32[4,16,128]{2,1,0:T(8,128)S(1)} %get-tuple-element.53.send.refs_5_), channel_id=1, source_target_pairs={{1,2},{2,1},{3,4},{4,3},{5,6},{6,5},{7,8},{8,7},{9,10},{10,9},{11,... | collective-permute-start | bytes 98312 | tf_op jit(solution)/shard_map/ppermute | solution.py:542
  40.1 1.4 %halo_scores_a.1 = (f32[4,16,128]{2,1,0:T(8,128)S(1)}, f32[2,2,192,256]{3,2,1,0:T(8,128)S(1)}, f32[2,2,192,256]{3,2,1,0:T(8,128)S(1)}, f32[2,2,192,256]{3,2,1,0:T(8,128)S(1)}, f32[2,2,192,256]{3,2,1,0:T(8,128)S(1)}) custom-call(bf16[2,256,512]{2,1,0:T(8,128)(2,1)S(1)} %collective-permute-done.q_in.refs_2_, bf16[512,512]{1,0:T(8,128)(2,1)S(1)} %get-tuple-element.46.kd, ...), custom_call_target="tpu_custom_call" | custom-call | flops 2000000000 | bytes 1024 | tf_op jit(solution)/shard_map/halo_scores_a/pallas_call | solution.py:354
  41.5 0.1 collective-permute-start.4
  41.6 1.1 %halo_queries_b.1 = (bf16[256,512]{1,0:T(8,128)(2,1)S(1)}, bf16[2,2,192,256]{3,2,1,0:T(8,128)(2,1)S(1)}, bf16[2,2,192,256]{3,2,1,0:T(8,128)(2,1)S(1)}, bf16[2,2,...) custom-call(f32[4,16,128]{2,1,0:T(8,128)S(1)} %get-tuple-element.53.send.refs_5_, ...), custom_call_target="tpu_custom_call" | custom-call | flops 2000000000 | bytes 1024 | tf_op jit(solution)/shard_map/halo_queries_b/pallas_call | solution.py:391
  42.7 7.1 %collective-permute-start.7 = (bf16[256,512]{1,0:T(8,128)(2,1)S(1)}, bf16[256,512]{1,0:T(8,128)(2,1)S(1)}, u32[]{:S(2)}, u32[]{:S(2)}) collective-permute-start(bf16[256,512]{1,0:T(8,128)(2,1)S(1)} %get-tuple-element.70.refs_17_), channel_id=1, source_target_pairs={{1,2},{2,1},{3,4},{4,3},{5,6},{6,5},{7,8},{8,7},{9,10},{10,9},{11,... | collective-permute-start | bytes 786440 | tf_op jit(solution)/shard_map/ppermute | solution.py:542
  49.8 1.1 %halo_queries_a.1 = (bf16[256,512]{1,0:T(8,128)(2,1)S(1)}, bf16[2,2,192,256]{3,2,1,0:T(8,128)(2,1)S(1)}, bf16[2,2,192,256]{3,2,1,0:T(8,128)(2,1)S(1)}, bf16[2,2,...) custom-call(f32[4,16,128]{2,1,0:T(8,128)S(1)} %get-tuple-element.52.send.refs_4_, ...), custom_call_target="tpu_custom_call" | custom-call | flops 2000000000 | bytes 1024 | tf_op jit(solution)/shard_map/halo_queries_a/pallas_call | solution.py:391
  50.8 0.1 collective-permute-start.6
  50.9 2.4 %edge_gradients.1 = (f32[2,128,512]{2,1,0:T(8,128)S(1)}, f32[512,512]{1,0:T(8,128)S(1)}, f32[512,512]{1,0:T(8,128)S(1)}, bf16[2,128,512]{2,1,0:T(8,128)(2,1)S(1)}, bf16[2,128,512]{2,1,0:T(8,128)(2,1)S(1)}) custom-call(bf16[2,256,512]{2,1,0:T(8,128)(2,1)S(1)} %copy-done.1, bf16[2,256,512]{2,1,0:T(8,128)(2,1)S(1)} %copy-done.3, ...), custom_call_target="tpu_custom_call" | custom-call | flops 3000000000 | bytes 1024 | tf_op jit(solution)/shard_map/edge_gradients/pallas_call | solution.py:465
  53.4 0.1 collective-permute-start.8
  53.5 2.7 %collective-permute-start.9 = (bf16[2,128,512]{2,1,0:T(8,128)(2,1)S(1)}, bf16[2,128,512]{2,1,0:T(8,128)(2,1)S(1)}, u32[]{:S(2)}, u32[]{:S(2)}) collective-permute-start(bf16[2,128,512]{2,1,0:T(8,128)(2,1)S(1)} %get-tuple-element.84), channel_id=1, source_target_pairs={{32,64},{64,32},{33,65},{65,33},{34,66},{66,34},{35,67},{67,35},{3... | collective-permute-start | bytes 786440 | tf_op jit(solution)/shard_map/ppermute | solution.py:542
  56.2 2.5 %mid_gradients.1 = (f32[2,128,512]{2,1,0:T(8,128)S(1)}, f32[512,512]{1,0:T(8,128)S(1)}, f32[512,512]{1,0:T(8,128)S(1)}) custom-call(bf16[2,256,512]{2,1,0:T(8,128)(2,1)S(1)} %copy-done.1, bf16[2,256,512]{2,1,0:T(8,128)(2,1)S(1)} %copy-done.3, bf16[2,256,512]{2,1,0:T(8,128)(2,1)S(1)} %collective-permute-done.q_in.refs_2_, ...), custom_call_target="tpu_custom_call" | custom-call | flops 3000000000 | bytes 1024 | tf_op jit(solution)/shard_map/mid_gradients/pallas_call | solution.py:478
  58.7 2.4 %collective-permute-done.9.from_b = bf16[2,128,512]{2,1,0:T(8,128)(2,1)S(1)} collective-permute-done((bf16[2,128,512]{2,1,0:T(8,128)(2,1)S(1)}, bf16[2,128,512]{2,1,0:T(8,128)(2,1)S(1)}, u32[]{:S(2)}, u32[]{:S(2)}) %collective-permute-start.9) | collective-permute-done | bytes 262176 | tf_op jit(solution)/shard_map/ppermute | solution.py:542
  61.2 1.3 %finish.1 = (bf16[32,16,512]{2,1,0:T(8,128)(2,1)}, bf16[32,16,512]{2,1,0:T(8,128)(2,1)}, bf16[32,16,512]{2,1,0:T(8,128)(2,1)}) custom-call(f32[2,128,512]{2,1,0:T(8,128)S(1)} %get-tuple-element.71.dq_edge, f32[2,128,512]{2,1,0:T(8,128)S(1)} %get-tuple-element.80.dq_mid, f32[512,512]{1,0:T(8,128)S(1)} %get-tuple-element.81.dk, ...), custom_call_target="tpu_custom_call" | custom-call | bytes 1024 | tf_op jit(solution)/shard_map/finish/pallas_call | solution.py:522
  (12 shorter events, 0.0 us)
Async XLA Ops:
  3.3 21.3 %collective-permute-start.2 = (bf16[2,128,512]{2,1,0:T(8,128)(2,1)}, bf16[2,128,512]{2,1,0:T(8,128)(2,1)S(1)}, u32[]{:S(2)}, u32[]{:S(2)}) collective-permute-start(bf16[2,128,512]{2,1,0:T(8,128)(2,1)} %get-tuple-element.48), channel_id=1, source_target_pairs={{0,32},{32,0},{64,96},{96,64},{1,33},{33,1},{65,97},{97,65},{2,34}... | collective-permute-start | bytes 786440 | tf_op jit(solution)/shard_map/ppermute | solution.py:534
  4.8 20.9 %collective-permute-start.3 = (bf16[2,128,512]{2,1,0:T(8,128)(2,1)}, bf16[2,128,512]{2,1,0:T(8,128)(2,1)S(1)}, u32[]{:S(2)}, u32[]{:S(2)}) collective-permute-start(bf16[2,128,512]{2,1,0:T(8,128)(2,1)} %get-tuple-element.49), channel_id=1, source_target_pairs={{32,64},{64,32},{33,65},{65,33},{34,66},{66,34},{35,67},{67,35},{3... | collective-permute-start | bytes 786440 | tf_op jit(solution)/shard_map/ppermute | solution.py:542
  8.0 20.7 %collective-permute-start.1 = (bf16[2,256,512]{2,1,0:T(8,128)(2,1)}, bf16[2,256,512]{2,1,0:T(8,128)(2,1)S(1)}, u32[]{:S(2)}, u32[]{:S(2)}) collective-permute-start(bf16[2,256,512]{2,1,0:T(8,128)(2,1)} %get-tuple-element.45.side_1.refs_1_), channel_id=1, source_target_pairs={{1,2},{2,1},{3,4},{4,3},{5,6},{6,5},{7,8},{8,7},{9,10},{10,9},{11,... | collective-permute-start | bytes 1572872 | tf_op jit(solution)/shard_map/ppermute | solution.py:542
  16.4 23.7 %collective-permute-start = (bf16[2,256,512]{2,1,0:T(8,128)(2,1)}, bf16[2,256,512]{2,1,0:T(8,128)(2,1)S(1)}, u32[]{:S(2)}, u32[]{:S(2)}) collective-permute-start(bf16[2,256,512]{2,1,0:T(8,128)(2,1)} %get-tuple-element.44.side_0.refs_0_), channel_id=1, source_target_pairs={{0,1},{1,0},{2,3},{3,2},{4,5},{5,4},{6,7},{7,6},{8,9},{9,8},{10,11... | collective-permute-start | bytes 1572872 | tf_op jit(solution)/shard_map/ppermute | solution.py:534
  16.4 1.0 %copy-start.4 = (bf16[32,16,512]{2,1,0:T(8,128)(2,1)S(1)}, bf16[32,16,512]{2,1,0:T(8,128)(2,1)}, u32[]{:S(2)}) copy-start(bf16[32,16,512]{2,1,0:T(8,128)(2,1)} %k_ref.3) | copy-start | bytes 1572868
  17.4 1.0 %copy-start.5 = (bf16[32,16,512]{2,1,0:T(8,128)(2,1)S(1)}, bf16[32,16,512]{2,1,0:T(8,128)(2,1)}, u32[]{:S(2)}) copy-start(bf16[32,16,512]{2,1,0:T(8,128)(2,1)} %v_ref.3) | copy-start | bytes 1572868
  20.1 1.0 %copy-start = (bf16[2,256,512]{2,1,0:T(8,128)(2,1)S(1)}, bf16[2,256,512]{2,1,0:T(8,128)(2,1)}, u32[]{:S(2)}) copy-start(bf16[2,256,512]{2,1,0:T(8,128)(2,1)} %get-tuple-element.44.side_0.refs_0_) | copy-start | bytes 1572868
  21.1 1.0 %copy-start.2 = (bf16[2,256,512]{2,1,0:T(8,128)(2,1)S(1)}, bf16[2,256,512]{2,1,0:T(8,128)(2,1)}, u32[]{:S(2)}) copy-start(bf16[2,256,512]{2,1,0:T(8,128)(2,1)} %get-tuple-element.45.side_1.refs_1_) | copy-start | bytes 1572868
  24.6 1.7 %copy-start.1 = (bf16[2,256,512]{2,1,0:T(8,128)(2,1)S(1)}, bf16[2,256,512]{2,1,0:T(8,128)(2,1)}, u32[]{:S(2)}) copy-start(bf16[2,256,512]{2,1,0:T(8,128)(2,1)} %get-tuple-element.44.side_0.refs_0_) | copy-start | bytes 1572868
  24.6 1.7 %copy-start.3 = (bf16[2,256,512]{2,1,0:T(8,128)(2,1)S(1)}, bf16[2,256,512]{2,1,0:T(8,128)(2,1)}, u32[]{:S(2)}) copy-start(bf16[2,256,512]{2,1,0:T(8,128)(2,1)} %get-tuple-element.45.side_1.refs_1_) | copy-start | bytes 1572868
  30.1 11.5 %collective-permute-start.5 = (f32[4,16,128]{2,1,0:T(8,128)S(1)}, f32[4,16,128]{2,1,0:T(8,128)S(1)}, u32[]{:S(2)}, u32[]{:S(2)}) collective-permute-start(f32[4,16,128]{2,1,0:T(8,128)S(1)} %get-tuple-element.53.send.refs_5_), channel_id=1, source_target_pairs={{1,2},{2,1},{3,4},{4,3},{5,6},{6,5},{7,8},{8,7},{9,10},{10,9},{11,... | collective-permute-start | bytes 98312 | tf_op jit(solution)/shard_map/ppermute | solution.py:542
  41.5 8.3 %collective-permute-start.4 = (f32[4,16,128]{2,1,0:T(8,128)S(1)}, f32[4,16,128]{2,1,0:T(8,128)S(1)}, u32[]{:S(2)}, u32[]{:S(2)}) collective-permute-start(f32[4,16,128]{2,1,0:T(8,128)S(1)} %get-tuple-element.52.send.refs_4_), channel_id=1, source_target_pairs={{0,1},{1,0},{2,3},{3,2},{4,5},{5,4},{6,7},{7,6},{8,9},{9,8},{10,11... | collective-permute-start | bytes 98312 | tf_op jit(solution)/shard_map/ppermute | solution.py:534
  42.7 18.5 %collective-permute-start.7 = (bf16[256,512]{1,0:T(8,128)(2,1)S(1)}, bf16[256,512]{1,0:T(8,128)(2,1)S(1)}, u32[]{:S(2)}, u32[]{:S(2)}) collective-permute-start(bf16[256,512]{1,0:T(8,128)(2,1)S(1)} %get-tuple-element.70.refs_17_), channel_id=1, source_target_pairs={{1,2},{2,1},{3,4},{4,3},{5,6},{6,5},{7,8},{8,7},{9,10},{10,9},{11,... | collective-permute-start | bytes 786440 | tf_op jit(solution)/shard_map/ppermute | solution.py:542
  50.8 10.3 %collective-permute-start.6 = (bf16[256,512]{1,0:T(8,128)(2,1)S(1)}, bf16[256,512]{1,0:T(8,128)(2,1)S(1)}, u32[]{:S(2)}, u32[]{:S(2)}) collective-permute-start(bf16[256,512]{1,0:T(8,128)(2,1)S(1)} %get-tuple-element.69.refs_16_), channel_id=1, source_target_pairs={{0,1},{1,0},{2,3},{3,2},{4,5},{5,4},{6,7},{7,6},{8,9},{9,8},{10,11... | collective-permute-start | bytes 786440 | tf_op jit(solution)/shard_map/ppermute | solution.py:534
  53.4 5.4 %collective-permute-start.8 = (bf16[2,128,512]{2,1,0:T(8,128)(2,1)S(1)}, bf16[2,128,512]{2,1,0:T(8,128)(2,1)S(1)}, u32[]{:S(2)}, u32[]{:S(2)}) collective-permute-start(bf16[2,128,512]{2,1,0:T(8,128)(2,1)S(1)} %get-tuple-element.83), channel_id=1, source_target_pairs={{0,32},{32,0},{64,96},{96,64},{1,33},{33,1},{65,97},{97,65},{2,34}... | collective-permute-start | bytes 786440 | tf_op jit(solution)/shard_map/ppermute | solution.py:534
  53.5 7.7 %collective-permute-start.9 = (bf16[2,128,512]{2,1,0:T(8,128)(2,1)S(1)}, bf16[2,128,512]{2,1,0:T(8,128)(2,1)S(1)}, u32[]{:S(2)}, u32[]{:S(2)}) collective-permute-start(bf16[2,128,512]{2,1,0:T(8,128)(2,1)S(1)} %get-tuple-element.84), channel_id=1, source_target_pairs={{32,64},{64,32},{33,65},{65,33},{34,66},{66,34},{35,67},{67,35},{3... | collective-permute-start | bytes 786440 | tf_op jit(solution)/shard_map/ppermute | solution.py:542

commit v8 on v7

--- a/solution.py
+++ b/solution.py
@@ -292,7 +292,7 @@
         out_specs=[part_spec] + [held_spec] * 2 + [pl.BlockSpec((PAIR, ROWS * PAIR), lambda p: (p, 0))],
         out_shape=[part_shape] + [held_shape] * 2 + [struct((FEAT, ROWS * PAIR), BF16)],
         compiler_params=params(),
-        cost_estimate=cost(2e9, 1 << 10),
+        cost_estimate=cost(6e9, 1 << 10),
         name="mid_scores",
     )(*operands)
 
@@ -328,7 +328,8 @@
     )(*operands)
 
 
-def halo_scores_kernel(c, q_in, kd, vd, edge_a, edge_b, edge_part, mid_part, send, s_edge, d_edge, s_mid, d_mid):
+def halo_scores_kernel(c, q_in, kd, vd, edge_a, edge_b, edge_part, mid_part, *refs):
+    send, s_edge, d_edge, s_mid, d_mid = refs[-5:]
     masks = head_masks(WIDE)
     groups = ((EDGE_ROWS, edge_part, s_edge, d_edge), (MID_ROWS, mid_part, s_mid, d_mid))
     for group, (rows, part, s_out, d_out) in enumerate(groups):
@@ -354,11 +355,11 @@
     return pl.pallas_call(
         functools.partial(halo_scores_kernel, c),
         grid=(GROUPS,),
-        in_specs=[all_tokens] + [keys_wide] * 2 + [edge_wide] * 2 + [part] * 2,
+        in_specs=[all_tokens] + [keys_wide] * 2 + [edge_wide] * 2 + [part] * 2 + [any_spec] * (len(operands) - 7),
         out_specs=[all_stats] + [halo_wide] * 4,
         out_shape=[stats_shape] + [halo_shape] * 4,
         compiler_params=params(),
-        cost_estimate=cost(2e9, 1 << 10),
+        cost_estimate=cost(1e9, 1 << 10),
         name="halo_scores_" + "ab"[c],
     )(*operands)
 
@@ -555,16 +556,14 @@
     mid_part, *mid_own, turned = mid_scores(*sides, kd, vd)
     edge_part, *edge_own = edge_scores(*sides, kd, vd, *edges)
     edges_turned = turn_edges(*edges)
-    sends, recvs, halo_dq, dq_parts, weights = [], [], [], [], []
-    for c in range(2):
-        send, *held = halo_scores(c, halos[c], kd, vd, *edges, edge_part, mid_part)
-        recv = swap_lon(c, send)
-        grad, *weight = halo_queries(c, send, recv, *held, turned, edges_turned)
-        sends.append(send)
-        recvs.append(recv)
-        halo_dq.append(grad)
-        dq_parts.append(swap_lon(c, grad))
-        weights.append(weight)
+    sends, recvs, halo_dq, dq_parts, weights = [{} for _ in range(5)]
+    for c in (1, 0):
+        before = halo_dq.values()
+        sends[c], *held = halo_scores(c, halos[c], kd, vd, *edges, edge_part, mid_part, *before)
+        recvs[c] = swap_lon(c, sends[c])
+        halo_dq[c], *weights[c] = halo_queries(c, sends[c], recvs[c], *held, turned, edges_turned)
+        dq_parts[c] = swap_lon(c, halo_dq[c])
+    sends, recvs, halo_dq, dq_parts = [[one[0], one[1]] for one in (sends, recvs, halo_dq, dq_parts)]
     shared = (*sides, *halos, *sends, *recvs)
     dq_edge, dk, dv, out_a, out_b = edge_gradients(*shared, *edge_own, *weights[0][:2], *weights[1][:2], turned, edges_turned,
                                                    *halo_dq)

time: 62.8 us -> 66.9 us (1.065)
  waiting for transfers between devices: 3.6 us -> 8.36 us
  starting transfers between devices: 33.1 us -> 32.4 us
    ppermute x5, waiting for transfers between devices: 0.01 us -> 3.03 us  [swap_a(): lax.ppermute(x, axis, [(i, i ^ 1) for i in range(lax.axis_size(axis))])]
    ppermute x5, waiting for transfers between devices: 3.59 us -> 5.33 us  [swap_b(): return lax.ppermute(x, axis, pairs)]
  transfers between devices with their start and end apart: 10 -> 10, of which waited for: 2 -> 4; matrix products, arithmetic and copies ran while one was open for 0% -> 0% of each run, Pallas kernels for 27% -> 23%
where the time goes in v8:
time: 66.9 us; the launch traced here: 66.5 us
  starting transfers between devices  32.4 us (48%)
  Pallas kernels  20.7 us (31%)
  waiting for transfers between devices  8.36 us (12%)
  local copies, waits for them, and re-layouts  4.17 us (6%)
  between operations  0.83 us (1%)
    ppermute x5, starting transfers between devices, swap_b(): return lax.ppermute(x, axis, pairs)  30.7 us
    ppermute x5, waiting for transfers between devices, swap_b(): return lax.ppermute(x, axis, pairs)  5.33 us
    unnamed x12, local copies, waits for them, and re-layouts  4.17 us
    ppermute x5, waiting for transfers between devices, swap_a(): lax.ppermute(x, axis, [(i, i ^ 1) for i in range(lax.axis_size(axis))])  3.03 us
    pallas_call x2, Pallas kernels, halo_scores(): pl.pallas_call(functools.partial(halo_scores_kernel, c), grid=(GROUPS,),...  2.77 us
    pallas_call x1, Pallas kernels, pack_queries(): pl.pallas_call(pack_queries_kernel, in_specs=[any_spec] * 4, out_specs=[a...  2.67 us
    pallas_call x1, Pallas kernels, mid_gradients(): pl.pallas_call(mid_kernel, grid=(GROUPS,), in_specs=row_specs(MID) + [key...  2.52 us
    pallas_call x1, Pallas kernels, edge_gradients(): pl.pallas_call(edge_kernel, grid=(GROUPS,), in_specs=row_specs(EDGE) + [e...  2.44 us
  transfers between devices with their start and end apart: 10, of which 4 were waited for; matrix products, arithmetic and copies ran while one was open for 0% of the time, Pallas kernels for 23%

profile of v8, /device:TPU:1, one launch (start us, length us, event | category | flops | bytes accessed | tf_op | source)
XLA Modules:
  0.0 66.5 jit_solution(17025202333313995223)
XLA Ops:
  0.6 2.7 %pack_queries.1 = (bf16[2,256,512]{2,1,0:T(8,128)(2,1)}, bf16[2,256,512]{2,1,0:T(8,128)(2,1)}, bf16[2,128,512]{2,1,0:T(8,128)(2,1)}, bf16[2,128,512]{2,1,0:T(8,128)(2,1)}) custom-call(bf16[32,16,512]{2,1,0:T(8,128)(2,1)} %q_ref.1, bf16[32,16,512]{2,1,0:T(8,128)(2,1)} %g_ref.1, bf16[32,16,512]{2,1,0:T(8,128)(2,1)} %k_ref.3, bf16[32,16,512]{2,1,0:T(8,128)(2,1)} %v_ref.3), custom_call_target="tpu_custom_call" | custom-call | bytes 3145728 | tf_op jit(solution)/shard_map/pack_queries/pallas_call | solution.py:102
  3.3 1.5 %collective-permute-start.2 = (bf16[2,128,512]{2,1,0:T(8,128)(2,1)}, bf16[2,128,512]{2,1,0:T(8,128)(2,1)S(1)}, u32[]{:S(2)}, u32[]{:S(2)}) collective-permute-start(bf16[2,128,512]{2,1,0:T(8,128)(2,1)} %get-tuple-element.48), channel_id=1, source_target_pairs={{0,32},{32,0},{64,96},{96,64},{1,33},{33,1},{65,97},{97,65},{2,34}... | collective-permute-start | bytes 786440 | tf_op jit(solution)/shard_map/ppermute | solution.py:535
  4.8 3.2 %collective-permute-start.3 = (bf16[2,128,512]{2,1,0:T(8,128)(2,1)}, bf16[2,128,512]{2,1,0:T(8,128)(2,1)S(1)}, u32[]{:S(2)}, u32[]{:S(2)}) collective-permute-start(bf16[2,128,512]{2,1,0:T(8,128)(2,1)} %get-tuple-element.49), channel_id=1, source_target_pairs={{32,64},{64,32},{33,65},{65,33},{34,66},{66,34},{35,67},{67,35},{3... | collective-permute-start | bytes 786440 | tf_op jit(solution)/shard_map/ppermute | solution.py:543
  8.0 8.4 %collective-permute-start.1 = (bf16[2,256,512]{2,1,0:T(8,128)(2,1)}, bf16[2,256,512]{2,1,0:T(8,128)(2,1)S(1)}, u32[]{:S(2)}, u32[]{:S(2)}) collective-permute-start(bf16[2,256,512]{2,1,0:T(8,128)(2,1)} %get-tuple-element.45.side_1.refs_1_), channel_id=1, source_target_pairs={{1,2},{2,1},{3,4},{4,3},{5,6},{6,5},{7,8},{8,7},{9,10},{10,9},{11,... | collective-permute-start | bytes 1572872 | tf_op jit(solution)/shard_map/ppermute | solution.py:543
  16.4 0.0 collective-permute-start
  16.4 1.0 %copy-done.4 = bf16[32,16,512]{2,1,0:T(8,128)(2,1)S(1)} copy-done((bf16[32,16,512]{2,1,0:T(8,128)(2,1)S(1)}, bf16[32,16,512]{2,1,0:T(8,128)(2,1)}, u32[]{:S(2)}) %copy-start.4) | copy-done | bytes 524312
  17.4 1.0 %copy-done.5 = bf16[32,16,512]{2,1,0:T(8,128)(2,1)S(1)} copy-done((bf16[32,16,512]{2,1,0:T(8,128)(2,1)S(1)}, bf16[32,16,512]{2,1,0:T(8,128)(2,1)}, u32[]{:S(2)}) %copy-start.5) | copy-done | bytes 524312
  18.5 1.6 %pack_keys.1 = (bf16[512,512]{1,0:T(8,128)(2,1)S(1)}, bf16[512,512]{1,0:T(8,128)(2,1)S(1)}) custom-call(bf16[32,16,512]{2,1,0:T(8,128)(2,1)S(1)} %copy-done.4, bf16[32,16,512]{2,1,0:T(8,128)(2,1)S(1)} %copy-done.5), custom_call_target="tpu_custom_call" | custom-call | bytes 3145728 | tf_op jit(solution)/shard_map/pack_keys/pallas_call | solution.py:128
  20.1 0.0 copy-start
  20.1 1.0 %copy-done = bf16[2,256,512]{2,1,0:T(8,128)(2,1)S(1)} copy-done((bf16[2,256,512]{2,1,0:T(8,128)(2,1)S(1)}, bf16[2,256,512]{2,1,0:T(8,128)(2,1)}, u32[]{:S(2)}) %copy-start) | copy-done | bytes 524312
  21.1 1.0 %copy-done.2 = bf16[2,256,512]{2,1,0:T(8,128)(2,1)S(1)} copy-done((bf16[2,256,512]{2,1,0:T(8,128)(2,1)S(1)}, bf16[2,256,512]{2,1,0:T(8,128)(2,1)}, u32[]{:S(2)}) %copy-start.2) | copy-done | bytes 524312
  22.2 2.4 %mid_scores.1 = (f32[4,8,128]{2,1,0:T(8,128)S(1)}, f32[4,2,384,256]{3,2,1,0:T(8,128)S(1)}, f32[4,2,384,256]{3,2,1,0:T(8,128)S(1)}, bf16[512,512]{1,0:T(8,128)(2,1)S(1)}) custom-call(bf16[2,256,512]{2,1,0:T(8,128)(2,1)S(1)} %copy-done, bf16[2,256,512]{2,1,0:T(8,128)(2,1)S(1)} %copy-done.2, bf16[512,512]{1,0:T(8,128)(2,1)S(1)} %get-tuple-element.46.kd, ...), custom_call_target="tpu_custom_call" | custom-call | flops 6000000000 | bytes 1024 | tf_op jit(solution)/shard_map/mid_scores/pallas_call | solution.py:288
  24.6 1.2 %collective-permute-done.3.edge_b = bf16[2,128,512]{2,1,0:T(8,128)(2,1)S(1)} collective-permute-done((bf16[2,128,512]{2,1,0:T(8,128)(2,1)}, bf16[2,128,512]{2,1,0:T(8,128)(2,1)S(1)}, u32[]{:S(2)}, u32[]{:S(2)}) %collective-permute-start.3) | collective-permute-done | bytes 262176 | tf_op jit(solution)/shard_map/ppermute | solution.py:543
  25.7 2.4 %edge_scores.1 = (f32[4,8,128]{2,1,0:T(8,128)S(1)}, f32[4,2,384,256]{3,2,1,0:T(8,128)S(1)}, f32[4,2,384,256]{3,2,1,0:T(8,128)S(1)}) custom-call(bf16[2,256,512]{2,1,0:T(8,128)(2,1)S(1)} %copy-done, bf16[2,256,512]{2,1,0:T(8,128)(2,1)S(1)} %copy-done.2, bf16[512,512]{1,0:T(8,128)(2,1)S(1)} %get-tuple-element.46.kd, ...), custom_call_target="tpu_custom_call" | custom-call | flops 2000000000 | bytes 1024 | tf_op jit(solution)/shard_map/edge_scores/pallas_call | solution.py:301
  28.2 0.0 collective-permute-done.1.q_in.refs_3_
  28.2 1.4 %halo_scores_b.1 = (f32[4,16,128]{2,1,0:T(8,128)S(1)}, f32[2,2,192,256]{3,2,1,0:T(8,128)S(1)}, f32[2,2,192,256]{3,2,1,0:T(8,128)S(1)}, f32[2,2,192,256]{3,2,1,0:T(8,128)S(1)}, f32[2,2,192,256]{3,2,1,0:T(8,128)S(1)}) custom-call(bf16[2,256,512]{2,1,0:T(8,128)(2,1)S(1)} %collective-permute-done.1.q_in.refs_3_, bf16[512,512]{1,0:T(8,128)(2,1)S(1)} %get-tuple-element.46.kd, ...), custom_call_target="tpu_custom_call" | custom-call | flops 1000000000 | bytes 1024 | tf_op jit(solution)/shard_map/halo_scores_b/pallas_call | solution.py:355
  29.6 10.0 %collective-permute-start.4 = (f32[4,16,128]{2,1,0:T(8,128)S(1)}, f32[4,16,128]{2,1,0:T(8,128)S(1)}, u32[]{:S(2)}, u32[]{:S(2)}) collective-permute-start(f32[4,16,128]{2,1,0:T(8,128)S(1)} %get-tuple-element.52.send.refs_5_), channel_id=1, source_target_pairs={{1,2},{2,1},{3,4},{4,3},{5,6},{6,5},{7,8},{8,7},{9,10},{10,9},{11,... | collective-permute-start | bytes 98312 | tf_op jit(solution)/shard_map/ppermute | solution.py:543
  39.6 0.5 turn_edges.1.edges_turned.refs_15_
  40.1 0.9 %collective-permute-done.4.recv.refs_7_ = f32[4,16,128]{2,1,0:T(8,128)S(1)} collective-permute-done((f32[4,16,128]{2,1,0:T(8,128)S(1)}, f32[4,16,128]{2,1,0:T(8,128)S(1)}, u32[]{:S(2)}, u32[]{:S(2)}) %collective-permute-start.4) | collective-permute-done | bytes 32800 | tf_op jit(solution)/shard_map/ppermute | solution.py:543
  41.0 1.1 %halo_queries_b.1 = (bf16[256,512]{1,0:T(8,128)(2,1)S(1)}, bf16[2,2,192,256]{3,2,1,0:T(8,128)(2,1)S(1)}, bf16[2,2,192,256]{3,2,1,0:T(8,128)(2,1)S(1)}, bf16[2,2,...) custom-call(f32[4,16,128]{2,1,0:T(8,128)S(1)} %get-tuple-element.52.send.refs_5_, ...), custom_call_target="tpu_custom_call" | custom-call | flops 2000000000 | bytes 1024 | tf_op jit(solution)/shard_map/halo_queries_b/pallas_call | solution.py:392
  42.1 1.4 %halo_scores_a.1 = (f32[4,16,128]{2,1,0:T(8,128)S(1)}, f32[2,2,192,256]{3,2,1,0:T(8,128)S(1)}, f32[2,2,192,256]{3,2,1,0:T(8,128)S(1)}, f32[2,2,192,256]{3,2,1,0:T(8,128)S(1)}, f32[2,2,192,256]{3,2,1,0:T(8,128)S(1)}) custom-call(bf16[2,256,512]{2,1,0:T(8,128)(2,1)S(1)} %collective-permute-done.q_in.refs_2_, bf16[512,512]{1,0:T(8,128)(2,1)S(1)} %get-tuple-element.46.kd, ...), custom_call_target="tpu_custom_call" | custom-call | flops 1000000000 | bytes 1024 | tf_op jit(solution)/shard_map/halo_scores_a/pallas_call | solution.py:355
  43.5 0.1 collective-permute-start.5
  43.6 7.2 %collective-permute-start.7 = (bf16[256,512]{1,0:T(8,128)(2,1)S(1)}, bf16[256,512]{1,0:T(8,128)(2,1)S(1)}, u32[]{:S(2)}, u32[]{:S(2)}) collective-permute-start(bf16[256,512]{1,0:T(8,128)(2,1)S(1)} %get-tuple-element.58.refs_0_.refs_17_), channel_id=1, source_target_pairs={{1,2},{2,1},{3,4},{4,3},{5,6},{6,5},{7,8},{8,7},{9,10},{10,9},{11,... | collective-permute-start | bytes 786440 | tf_op jit(solution)/shard_map/ppermute | solution.py:543
  50.8 3.0 %collective-permute-done.5.recv.refs_6_ = f32[4,16,128]{2,1,0:T(8,128)S(1)} collective-permute-done((f32[4,16,128]{2,1,0:T(8,128)S(1)}, f32[4,16,128]{2,1,0:T(8,128)S(1)}, u32[]{:S(2)}, u32[]{:S(2)}) %collective-permute-start.5) | collective-permute-done | bytes 32800 | tf_op jit(solution)/shard_map/ppermute | solution.py:535
  53.8 1.1 %halo_queries_a.1 = (bf16[256,512]{1,0:T(8,128)(2,1)S(1)}, bf16[2,2,192,256]{3,2,1,0:T(8,128)(2,1)S(1)}, bf16[2,2,192,256]{3,2,1,0:T(8,128)(2,1)S(1)}, bf16[2,2,...) custom-call(f32[4,16,128]{2,1,0:T(8,128)S(1)} %get-tuple-element.59.send.refs_4_, ...), custom_call_target="tpu_custom_call" | custom-call | flops 2000000000 | bytes 1024 | tf_op jit(solution)/shard_map/halo_queries_a/pallas_call | solution.py:392
  54.9 0.1 collective-permute-start.6
  55.0 2.4 %edge_gradients.1 = (f32[2,128,512]{2,1,0:T(8,128)S(1)}, f32[512,512]{1,0:T(8,128)S(1)}, f32[512,512]{1,0:T(8,128)S(1)}, bf16[2,128,512]{2,1,0:T(8,128)(2,1)S(1)}, bf16[2,128,512]{2,1,0:T(8,128)(2,1)S(1)}) custom-call(bf16[2,256,512]{2,1,0:T(8,128)(2,1)S(1)} %copy-done.1, bf16[2,256,512]{2,1,0:T(8,128)(2,1)S(1)} %copy-done.3, ...), custom_call_target="tpu_custom_call" | custom-call | flops 3000000000 | bytes 1024 | tf_op jit(solution)/shard_map/edge_gradients/pallas_call | solution.py:466
  57.4 0.1 collective-permute-start.8
  57.5 1.9 %collective-permute-start.9 = (bf16[2,128,512]{2,1,0:T(8,128)(2,1)S(1)}, bf16[2,128,512]{2,1,0:T(8,128)(2,1)S(1)}, u32[]{:S(2)}, u32[]{:S(2)}) collective-permute-start(bf16[2,128,512]{2,1,0:T(8,128)(2,1)S(1)} %get-tuple-element.84), channel_id=1, source_target_pairs={{32,64},{64,32},{33,65},{65,33},{34,66},{66,34},{35,67},{67,35},{3... | collective-permute-start | bytes 786440 | tf_op jit(solution)/shard_map/ppermute | solution.py:543
  59.5 2.5 %mid_gradients.1 = (f32[2,128,512]{2,1,0:T(8,128)S(1)}, f32[512,512]{1,0:T(8,128)S(1)}, f32[512,512]{1,0:T(8,128)S(1)}) custom-call(bf16[2,256,512]{2,1,0:T(8,128)(2,1)S(1)} %copy-done.1, bf16[2,256,512]{2,1,0:T(8,128)(2,1)S(1)} %copy-done.3, bf16[2,256,512]{2,1,0:T(8,128)(2,1)S(1)} %collective-permute-done.q_in.refs_2_, ...), custom_call_target="tpu_custom_call" | custom-call | flops 3000000000 | bytes 1024 | tf_op jit(solution)/shard_map/mid_gradients/pallas_call | solution.py:479
  62.0 3.2 %collective-permute-done.9.from_b = bf16[2,128,512]{2,1,0:T(8,128)(2,1)S(1)} collective-permute-done((bf16[2,128,512]{2,1,0:T(8,128)(2,1)S(1)}, bf16[2,128,512]{2,1,0:T(8,128)(2,1)S(1)}, u32[]{:S(2)}, u32[]{:S(2)}) %collective-permute-start.9) | collective-permute-done | bytes 262176 | tf_op jit(solution)/shard_map/ppermute | solution.py:543
  65.2 1.3 %finish.1 = (bf16[32,16,512]{2,1,0:T(8,128)(2,1)}, bf16[32,16,512]{2,1,0:T(8,128)(2,1)}, bf16[32,16,512]{2,1,0:T(8,128)(2,1)}) custom-call(f32[2,128,512]{2,1,0:T(8,128)S(1)} %get-tuple-element.71.dq_edge, f32[2,128,512]{2,1,0:T(8,128)S(1)} %get-tuple-element.80.dq_mid, f32[512,512]{1,0:T(8,128)S(1)} %get-tuple-element.81.dk, ...), custom_call_target="tpu_custom_call" | custom-call | bytes 1024 | tf_op jit(solution)/shard_map/finish/pallas_call | solution.py:523
  (12 shorter events, 0.0 us)
Async XLA Ops:
  3.3 21.2 %collective-permute-start.2 = (bf16[2,128,512]{2,1,0:T(8,128)(2,1)}, bf16[2,128,512]{2,1,0:T(8,128)(2,1)S(1)}, u32[]{:S(2)}, u32[]{:S(2)}) collective-permute-start(bf16[2,128,512]{2,1,0:T(8,128)(2,1)} %get-tuple-element.48), channel_id=1, source_target_pairs={{0,32},{32,0},{64,96},{96,64},{1,33},{33,1},{65,97},{97,65},{2,34}... | collective-permute-start | bytes 786440 | tf_op jit(solution)/shard_map/ppermute | solution.py:535
  4.8 20.9 %collective-permute-start.3 = (bf16[2,128,512]{2,1,0:T(8,128)(2,1)}, bf16[2,128,512]{2,1,0:T(8,128)(2,1)S(1)}, u32[]{:S(2)}, u32[]{:S(2)}) collective-permute-start(bf16[2,128,512]{2,1,0:T(8,128)(2,1)} %get-tuple-element.49), channel_id=1, source_target_pairs={{32,64},{64,32},{33,65},{65,33},{34,66},{66,34},{35,67},{67,35},{3... | collective-permute-start | bytes 786440 | tf_op jit(solution)/shard_map/ppermute | solution.py:543
  8.0 20.2 %collective-permute-start.1 = (bf16[2,256,512]{2,1,0:T(8,128)(2,1)}, bf16[2,256,512]{2,1,0:T(8,128)(2,1)S(1)}, u32[]{:S(2)}, u32[]{:S(2)}) collective-permute-start(bf16[2,256,512]{2,1,0:T(8,128)(2,1)} %get-tuple-element.45.side_1.refs_1_), channel_id=1, source_target_pairs={{1,2},{2,1},{3,4},{4,3},{5,6},{6,5},{7,8},{8,7},{9,10},{10,9},{11,... | collective-permute-start | bytes 1572872 | tf_op jit(solution)/shard_map/ppermute | solution.py:543
  16.4 25.7 %collective-permute-start = (bf16[2,256,512]{2,1,0:T(8,128)(2,1)}, bf16[2,256,512]{2,1,0:T(8,128)(2,1)S(1)}, u32[]{:S(2)}, u32[]{:S(2)}) collective-permute-start(bf16[2,256,512]{2,1,0:T(8,128)(2,1)} %get-tuple-element.44.side_0.refs_0_), channel_id=1, source_target_pairs={{0,1},{1,0},{2,3},{3,2},{4,5},{5,4},{6,7},{7,6},{8,9},{9,8},{10,11... | collective-permute-start | bytes 1572872 | tf_op jit(solution)/shard_map/ppermute | solution.py:535
  16.4 1.0 %copy-start.4 = (bf16[32,16,512]{2,1,0:T(8,128)(2,1)S(1)}, bf16[32,16,512]{2,1,0:T(8,128)(2,1)}, u32[]{:S(2)}) copy-start(bf16[32,16,512]{2,1,0:T(8,128)(2,1)} %k_ref.3) | copy-start | bytes 1572868
  17.4 1.0 %copy-start.5 = (bf16[32,16,512]{2,1,0:T(8,128)(2,1)S(1)}, bf16[32,16,512]{2,1,0:T(8,128)(2,1)}, u32[]{:S(2)}) copy-start(bf16[32,16,512]{2,1,0:T(8,128)(2,1)} %v_ref.3) | copy-start | bytes 1572868
  20.1 1.0 %copy-start = (bf16[2,256,512]{2,1,0:T(8,128)(2,1)S(1)}, bf16[2,256,512]{2,1,0:T(8,128)(2,1)}, u32[]{:S(2)}) copy-start(bf16[2,256,512]{2,1,0:T(8,128)(2,1)} %get-tuple-element.44.side_0.refs_0_) | copy-start | bytes 1572868
  21.1 1.0 %copy-start.2 = (bf16[2,256,512]{2,1,0:T(8,128)(2,1)S(1)}, bf16[2,256,512]{2,1,0:T(8,128)(2,1)}, u32[]{:S(2)}) copy-start(bf16[2,256,512]{2,1,0:T(8,128)(2,1)} %get-tuple-element.45.side_1.refs_1_) | copy-start | bytes 1572868
  29.6 11.4 %collective-permute-start.4 = (f32[4,16,128]{2,1,0:T(8,128)S(1)}, f32[4,16,128]{2,1,0:T(8,128)S(1)}, u32[]{:S(2)}, u32[]{:S(2)}) collective-permute-start(f32[4,16,128]{2,1,0:T(8,128)S(1)} %get-tuple-element.52.send.refs_5_), channel_id=1, source_target_pairs={{1,2},{2,1},{3,4},{4,3},{5,6},{6,5},{7,8},{8,7},{9,10},{10,9},{11,... | collective-permute-start | bytes 98312 | tf_op jit(solution)/shard_map/ppermute | solution.py:543
  43.5 10.3 %collective-permute-start.5 = (f32[4,16,128]{2,1,0:T(8,128)S(1)}, f32[4,16,128]{2,1,0:T(8,128)S(1)}, u32[]{:S(2)}, u32[]{:S(2)}) collective-permute-start(f32[4,16,128]{2,1,0:T(8,128)S(1)} %get-tuple-element.59.send.refs_4_), channel_id=1, source_target_pairs={{0,1},{1,0},{2,3},{3,2},{4,5},{5,4},{6,7},{7,6},{8,9},{9,8},{10,11... | collective-permute-start | bytes 98312 | tf_op jit(solution)/shard_map/ppermute | solution.py:535
  43.6 18.4 %collective-permute-start.7 = (bf16[256,512]{1,0:T(8,128)(2,1)S(1)}, bf16[256,512]{1,0:T(8,128)(2,1)S(1)}, u32[]{:S(2)}, u32[]{:S(2)}) collective-permute-start(bf16[256,512]{1,0:T(8,128)(2,1)S(1)} %get-tuple-element.58.refs_0_.refs_17_), channel_id=1, source_target_pairs={{1,2},{2,1},{3,4},{4,3},{5,6},{6,5},{7,8},{8,7},{9,10},{10,9},{11,... | collective-permute-start | bytes 786440 | tf_op jit(solution)/shard_map/ppermute | solution.py:543
  53.8 1.2 %copy-start.1 = (bf16[2,256,512]{2,1,0:T(8,128)(2,1)S(1)}, bf16[2,256,512]{2,1,0:T(8,128)(2,1)}, u32[]{:S(2)}) copy-start(bf16[2,256,512]{2,1,0:T(8,128)(2,1)} %get-tuple-element.44.side_0.refs_0_) | copy-start | bytes 1572868
  53.8 1.2 %copy-start.3 = (bf16[2,256,512]{2,1,0:T(8,128)(2,1)S(1)}, bf16[2,256,512]{2,1,0:T(8,128)(2,1)}, u32[]{:S(2)}) copy-start(bf16[2,256,512]{2,1,0:T(8,128)(2,1)} %get-tuple-element.45.side_1.refs_1_) | copy-start | bytes 1572868
  54.9 10.3 %collective-permute-start.6 = (bf16[256,512]{1,0:T(8,128)(2,1)S(1)}, bf16[256,512]{1,0:T(8,128)(2,1)S(1)}, u32[]{:S(2)}, u32[]{:S(2)}) collective-permute-start(bf16[256,512]{1,0:T(8,128)(2,1)S(1)} %get-tuple-element.70.refs_16_), channel_id=1, source_target_pairs={{0,1},{1,0},{2,3},{3,2},{4,5},{5,4},{6,7},{7,6},{8,9},{9,8},{10,11... | collective-permute-start | bytes 786440 | tf_op jit(solution)/shard_map/ppermute | solution.py:535
  57.4 4.6 %collective-permute-start.8 = (bf16[2,128,512]{2,1,0:T(8,128)(2,1)S(1)}, bf16[2,128,512]{2,1,0:T(8,128)(2,1)S(1)}, u32[]{:S(2)}, u32[]{:S(2)}) collective-permute-start(bf16[2,128,512]{2,1,0:T(8,128)(2,1)S(1)} %get-tuple-element.83), channel_id=1, source_target_pairs={{0,32},{32,0},{64,96},{96,64},{1,33},{33,1},{65,97},{97,65},{2,34}... | collective-permute-start | bytes 786440 | tf_op jit(solution)/shard_map/ppermute | solution.py:535
  57.5 7.7 %collective-permute-start.9 = (bf16[2,128,512]{2,1,0:T(8,128)(2,1)S(1)}, bf16[2,128,512]{2,1,0:T(8,128)(2,1)S(1)}, u32[]{:S(2)}, u32[]{:S(2)}) collective-permute-start(bf16[2,128,512]{2,1,0:T(8,128)(2,1)S(1)} %get-tuple-element.84), channel_id=1, source_target_pairs={{32,64},{64,32},{33,65},{65,33},{34,66},{66,34},{35,67},{67,35},{3... | collective-permute-start | bytes 786440 | tf_op jit(solution)/shard_map/ppermute | solution.py:543

commit v9 on v7

--- a/solution.py
+++ b/solution.py
@@ -395,7 +395,7 @@
         out_specs=[all_parts] + [halo_wide] * 4,
         out_shape=[struct((2 * CHUNK, FEAT), BF16)] + [weight_shape] * 4,
         compiler_params=params(),
-        cost_estimate=cost(2e9, 1 << 10),
+        cost_estimate=cost(0, 1 << 10),
         name="halo_queries_" + "ab"[c],
     )(*operands)
 

time: 62.8 us -> 61.9 us (0.986); the launches traced: 62.4 us -> 60.8 us
  starting transfers between devices: 33.1 us -> 30.4 us
  waiting for transfers between devices: 3.6 us -> 4.61 us
    ppermute x5, starting transfers between devices: 31.3 us -> 29.1 us  [swap_b(): return lax.ppermute(x, axis, pairs)]
    ppermute x5, waiting for transfers between devices: 3.59 us -> 4.59 us  [swap_b(): return lax.ppermute(x, axis, pairs)]
  transfers between devices with their start and end apart: 10 -> 10, of which waited for: 2 -> 2; matrix products, arithmetic and copies ran while one was open for 0% -> 0% of each run, Pallas kernels for 27% -> 28%
where the time goes in v9:
time: 61.9 us; the launch traced here: 60.8 us
  starting transfers between devices  30.4 us (49%)
  Pallas kernels  20.7 us (33%)
  waiting for transfers between devices  4.61 us (7%)
  local copies, waits for them, and re-layouts  4.17 us (7%)
  between operations  0.85 us (1%)
    ppermute x5, starting transfers between devices, swap_b(): return lax.ppermute(x, axis, pairs)  29.1 us
    ppermute x5, waiting for transfers between devices, swap_b(): return lax.ppermute(x, axis, pairs)  4.59 us
    unnamed x12, local copies, waits for them, and re-layouts  4.17 us
    pallas_call x2, Pallas kernels, halo_scores(): pl.pallas_call(functools.partial(halo_scores_kernel, c), grid=(GROUPS,),...  2.76 us
    pallas_call x1, Pallas kernels, pack_queries(): pl.pallas_call(pack_queries_kernel, in_specs=[any_spec] * 4, out_specs=[a...  2.67 us
    pallas_call x1, Pallas kernels, mid_gradients(): pl.pallas_call(mid_kernel, grid=(GROUPS,), in_specs=row_specs(MID) + [key...  2.52 us
    pallas_call x1, Pallas kernels, edge_gradients(): pl.pallas_call(edge_kernel, grid=(GROUPS,), in_specs=row_specs(EDGE) + [e...  2.44 us
    pallas_call x1, Pallas kernels, edge_scores(): pl.pallas_call(edge_scores_kernel, grid=(PAIRS,), in_specs=[tokens_spec(E...  2.43 us
  transfers between devices with their start and end apart: 10, of which 2 were waited for; matrix products, arithmetic and copies ran while one was open for 0% of the time, Pallas kernels for 28%

profile of v9, /device:TPU:1, one launch (start us, length us, event | category | flops | bytes accessed | tf_op | source)
XLA Modules:
  0.0 60.8 jit_solution(6924207004810761100)
XLA Ops:
  0.6 2.7 %pack_queries.1 = (bf16[2,256,512]{2,1,0:T(8,128)(2,1)}, bf16[2,256,512]{2,1,0:T(8,128)(2,1)}, bf16[2,128,512]{2,1,0:T(8,128)(2,1)}, bf16[2,128,512]{2,1,0:T(8,128)(2,1)}) custom-call(bf16[32,16,512]{2,1,0:T(8,128)(2,1)} %q_ref.1, bf16[32,16,512]{2,1,0:T(8,128)(2,1)} %g_ref.1, bf16[32,16,512]{2,1,0:T(8,128)(2,1)} %k_ref.3, bf16[32,16,512]{2,1,0:T(8,128)(2,1)} %v_ref.3), custom_call_target="tpu_custom_call" | custom-call | bytes 3145728 | tf_op jit(solution)/shard_map/pack_queries/pallas_call | solution.py:102
  3.3 9.5 %collective-permute-start.1 = (bf16[2,256,512]{2,1,0:T(8,128)(2,1)}, bf16[2,256,512]{2,1,0:T(8,128)(2,1)S(1)}, u32[]{:S(2)}, u32[]{:S(2)}) collective-permute-start(bf16[2,256,512]{2,1,0:T(8,128)(2,1)} %get-tuple-element.45.side_1.refs_1_), channel_id=1, source_target_pairs={{1,2},{2,1},{3,4},{4,3},{5,6},{6,5},{7,8},{8,7},{9,10},{10,9},{11,... | collective-permute-start | bytes 1572872 | tf_op jit(solution)/shard_map/ppermute | solution.py:542
  12.8 1.0 %collective-permute-start.2 = (bf16[2,128,512]{2,1,0:T(8,128)(2,1)}, bf16[2,128,512]{2,1,0:T(8,128)(2,1)S(1)}, u32[]{:S(2)}, u32[]{:S(2)}) collective-permute-start(bf16[2,128,512]{2,1,0:T(8,128)(2,1)} %get-tuple-element.48), channel_id=1, source_target_pairs={{0,32},{32,0},{64,96},{96,64},{1,33},{33,1},{65,97},{97,65},{2,34}... | collective-permute-start | bytes 786440 | tf_op jit(solution)/shard_map/ppermute | solution.py:534
  13.8 2.2 %collective-permute-start.3 = (bf16[2,128,512]{2,1,0:T(8,128)(2,1)}, bf16[2,128,512]{2,1,0:T(8,128)(2,1)S(1)}, u32[]{:S(2)}, u32[]{:S(2)}) collective-permute-start(bf16[2,128,512]{2,1,0:T(8,128)(2,1)} %get-tuple-element.49), channel_id=1, source_target_pairs={{32,64},{64,32},{33,65},{65,33},{34,66},{66,34},{35,67},{67,35},{3... | collective-permute-start | bytes 786440 | tf_op jit(solution)/shard_map/ppermute | solution.py:542
  15.9 0.1 collective-permute-start
  16.0 0.0 copy-start.4
  16.1 1.0 %copy-done.4 = bf16[32,16,512]{2,1,0:T(8,128)(2,1)S(1)} copy-done((bf16[32,16,512]{2,1,0:T(8,128)(2,1)S(1)}, bf16[32,16,512]{2,1,0:T(8,128)(2,1)}, u32[]{:S(2)}) %copy-start.4) | copy-done | bytes 524312
  17.1 1.0 %copy-done.5 = bf16[32,16,512]{2,1,0:T(8,128)(2,1)S(1)} copy-done((bf16[32,16,512]{2,1,0:T(8,128)(2,1)S(1)}, bf16[32,16,512]{2,1,0:T(8,128)(2,1)}, u32[]{:S(2)}) %copy-start.5) | copy-done | bytes 524312
  18.1 1.6 %pack_keys.1 = (bf16[512,512]{1,0:T(8,128)(2,1)S(1)}, bf16[512,512]{1,0:T(8,128)(2,1)S(1)}) custom-call(bf16[32,16,512]{2,1,0:T(8,128)(2,1)S(1)} %copy-done.4, bf16[32,16,512]{2,1,0:T(8,128)(2,1)S(1)} %copy-done.5), custom_call_target="tpu_custom_call" | custom-call | bytes 3145728 | tf_op jit(solution)/shard_map/pack_keys/pallas_call | solution.py:128
  19.8 0.0 copy-start
  19.8 1.0 %copy-done = bf16[2,256,512]{2,1,0:T(8,128)(2,1)S(1)} copy-done((bf16[2,256,512]{2,1,0:T(8,128)(2,1)S(1)}, bf16[2,256,512]{2,1,0:T(8,128)(2,1)}, u32[]{:S(2)}) %copy-start) | copy-done | bytes 524312
  20.8 1.0 %copy-done.2 = bf16[2,256,512]{2,1,0:T(8,128)(2,1)S(1)} copy-done((bf16[2,256,512]{2,1,0:T(8,128)(2,1)S(1)}, bf16[2,256,512]{2,1,0:T(8,128)(2,1)}, u32[]{:S(2)}) %copy-start.2) | copy-done | bytes 524312
  21.8 2.4 %mid_scores.1 = (f32[4,8,128]{2,1,0:T(8,128)S(1)}, f32[4,2,384,256]{3,2,1,0:T(8,128)S(1)}, f32[4,2,384,256]{3,2,1,0:T(8,128)S(1)}, bf16[512,512]{1,0:T(8,128)(2,1)S(1)}) custom-call(bf16[2,256,512]{2,1,0:T(8,128)(2,1)S(1)} %copy-done, bf16[2,256,512]{2,1,0:T(8,128)(2,1)S(1)} %copy-done.2, bf16[512,512]{1,0:T(8,128)(2,1)S(1)} %get-tuple-element.46.kd, ...), custom_call_target="tpu_custom_call" | custom-call | flops 2000000000 | bytes 1024 | tf_op jit(solution)/shard_map/mid_scores/pallas_call | solution.py:288
  24.2 2.6 %collective-permute-done.3.edge_b = bf16[2,128,512]{2,1,0:T(8,128)(2,1)S(1)} collective-permute-done((bf16[2,128,512]{2,1,0:T(8,128)(2,1)}, bf16[2,128,512]{2,1,0:T(8,128)(2,1)S(1)}, u32[]{:S(2)}, u32[]{:S(2)}) %collective-permute-start.3) | collective-permute-done | bytes 262176 | tf_op jit(solution)/shard_map/ppermute | solution.py:542
  26.8 2.4 %edge_scores.1 = (f32[4,8,128]{2,1,0:T(8,128)S(1)}, f32[4,2,384,256]{3,2,1,0:T(8,128)S(1)}, f32[4,2,384,256]{3,2,1,0:T(8,128)S(1)}) custom-call(bf16[2,256,512]{2,1,0:T(8,128)(2,1)S(1)} %copy-done, bf16[2,256,512]{2,1,0:T(8,128)(2,1)S(1)} %copy-done.2, bf16[512,512]{1,0:T(8,128)(2,1)S(1)} %get-tuple-element.46.kd, ...), custom_call_target="tpu_custom_call" | custom-call | flops 2000000000 | bytes 1024 | tf_op jit(solution)/shard_map/edge_scores/pallas_call | solution.py:301
  29.3 1.4 %halo_scores_b.1 = (f32[4,16,128]{2,1,0:T(8,128)S(1)}, f32[2,2,192,256]{3,2,1,0:T(8,128)S(1)}, f32[2,2,192,256]{3,2,1,0:T(8,128)S(1)}, f32[2,2,192,256]{3,2,1,0:T(8,128)S(1)}, f32[2,2,192,256]{3,2,1,0:T(8,128)S(1)}) custom-call(bf16[2,256,512]{2,1,0:T(8,128)(2,1)S(1)} %collective-permute-done.1.q_in.refs_3_, bf16[512,512]{1,0:T(8,128)(2,1)S(1)} %get-tuple-element.46.kd, ...), custom_call_target="tpu_custom_call" | custom-call | flops 2000000000 | bytes 1024 | tf_op jit(solution)/shard_map/halo_scores_b/pallas_call | solution.py:354
  30.7 7.1 %collective-permute-start.5 = (f32[4,16,128]{2,1,0:T(8,128)S(1)}, f32[4,16,128]{2,1,0:T(8,128)S(1)}, u32[]{:S(2)}, u32[]{:S(2)}) collective-permute-start(f32[4,16,128]{2,1,0:T(8,128)S(1)} %get-tuple-element.53.send.refs_5_), channel_id=1, source_target_pairs={{1,2},{2,1},{3,4},{4,3},{5,6},{6,5},{7,8},{8,7},{9,10},{10,9},{11,... | collective-permute-start | bytes 98312 | tf_op jit(solution)/shard_map/ppermute | solution.py:542
  37.8 1.4 %halo_scores_a.1 = (f32[4,16,128]{2,1,0:T(8,128)S(1)}, f32[2,2,192,256]{3,2,1,0:T(8,128)S(1)}, f32[2,2,192,256]{3,2,1,0:T(8,128)S(1)}, f32[2,2,192,256]{3,2,1,0:T(8,128)S(1)}, f32[2,2,192,256]{3,2,1,0:T(8,128)S(1)}) custom-call(bf16[2,256,512]{2,1,0:T(8,128)(2,1)S(1)} %collective-permute-done.q_in.refs_2_, bf16[512,512]{1,0:T(8,128)(2,1)S(1)} %get-tuple-element.46.kd, ...), custom_call_target="tpu_custom_call" | custom-call | flops 2000000000 | bytes 1024 | tf_op jit(solution)/shard_map/halo_scores_a/pallas_call | solution.py:354
  39.2 0.1 collective-permute-start.4
  39.3 0.5 turn_edges.1.edges_turned.refs_15_
  39.8 0.0 copy-start.1
  39.8 0.0 copy-start.3
  39.8 1.1 %halo_queries_b.1 = (bf16[256,512]{1,0:T(8,128)(2,1)S(1)}, bf16[2,2,192,256]{3,2,1,0:T(8,128)(2,1)S(1)}, bf16[2,2,192,256]{3,2,1,0:T(8,128)(2,1)S(1)}, bf16[2,2,...) custom-call(f32[4,16,128]{2,1,0:T(8,128)S(1)} %get-tuple-element.53.send.refs_5_, ...), custom_call_target="tpu_custom_call" | custom-call | bytes 1024 | tf_op jit(solution)/shard_map/halo_queries_b/pallas_call | solution.py:391
  40.9 7.1 %collective-permute-start.7 = (bf16[256,512]{1,0:T(8,128)(2,1)S(1)}, bf16[256,512]{1,0:T(8,128)(2,1)S(1)}, u32[]{:S(2)}, u32[]{:S(2)}) collective-permute-start(bf16[256,512]{1,0:T(8,128)(2,1)S(1)} %get-tuple-element.70.refs_17_), channel_id=1, source_target_pairs={{1,2},{2,1},{3,4},{4,3},{5,6},{6,5},{7,8},{8,7},{9,10},{10,9},{11,... | collective-permute-start | bytes 786440 | tf_op jit(solution)/shard_map/ppermute | solution.py:542
  48.0 1.1 %halo_queries_a.1 = (bf16[256,512]{1,0:T(8,128)(2,1)S(1)}, bf16[2,2,192,256]{3,2,1,0:T(8,128)(2,1)S(1)}, bf16[2,2,192,256]{3,2,1,0:T(8,128)(2,1)S(1)}, bf16[2,2,...) custom-call(f32[4,16,128]{2,1,0:T(8,128)S(1)} %get-tuple-element.52.send.refs_4_, ...), custom_call_target="tpu_custom_call" | custom-call | bytes 1024 | tf_op jit(solution)/shard_map/halo_queries_a/pallas_call | solution.py:391
  49.1 0.1 collective-permute-start.6
  49.3 2.4 %edge_gradients.1 = (f32[2,128,512]{2,1,0:T(8,128)S(1)}, f32[512,512]{1,0:T(8,128)S(1)}, f32[512,512]{1,0:T(8,128)S(1)}, bf16[2,128,512]{2,1,0:T(8,128)(2,1)S(1)}, bf16[2,128,512]{2,1,0:T(8,128)(2,1)S(1)}) custom-call(bf16[2,256,512]{2,1,0:T(8,128)(2,1)S(1)} %copy-done.1, bf16[2,256,512]{2,1,0:T(8,128)(2,1)S(1)} %copy-done.3, ...), custom_call_target="tpu_custom_call" | custom-call | flops 3000000000 | bytes 1024 | tf_op jit(solution)/shard_map/edge_gradients/pallas_call | solution.py:465
  51.7 0.1 collective-permute-start.8
  51.8 3.2 %collective-permute-start.9 = (bf16[2,128,512]{2,1,0:T(8,128)(2,1)S(1)}, bf16[2,128,512]{2,1,0:T(8,128)(2,1)S(1)}, u32[]{:S(2)}, u32[]{:S(2)}) collective-permute-start(bf16[2,128,512]{2,1,0:T(8,128)(2,1)S(1)} %get-tuple-element.84), channel_id=1, source_target_pairs={{32,64},{64,32},{33,65},{65,33},{34,66},{66,34},{35,67},{67,35},{3... | collective-permute-start | bytes 786440 | tf_op jit(solution)/shard_map/ppermute | solution.py:542
  55.0 2.5 %mid_gradients.1 = (f32[2,128,512]{2,1,0:T(8,128)S(1)}, f32[512,512]{1,0:T(8,128)S(1)}, f32[512,512]{1,0:T(8,128)S(1)}) custom-call(bf16[2,256,512]{2,1,0:T(8,128)(2,1)S(1)} %copy-done.1, bf16[2,256,512]{2,1,0:T(8,128)(2,1)S(1)} %copy-done.3, bf16[2,256,512]{2,1,0:T(8,128)(2,1)S(1)} %collective-permute-done.q_in.refs_2_, ...), custom_call_target="tpu_custom_call" | custom-call | flops 3000000000 | bytes 1024 | tf_op jit(solution)/shard_map/mid_gradients/pallas_call | solution.py:478
  57.5 2.0 %collective-permute-done.9.from_b = bf16[2,128,512]{2,1,0:T(8,128)(2,1)S(1)} collective-permute-done((bf16[2,128,512]{2,1,0:T(8,128)(2,1)S(1)}, bf16[2,128,512]{2,1,0:T(8,128)(2,1)S(1)}, u32[]{:S(2)}, u32[]{:S(2)}) %collective-permute-start.9) | collective-permute-done | bytes 262176 | tf_op jit(solution)/shard_map/ppermute | solution.py:542
  59.5 1.3 %finish.1 = (bf16[32,16,512]{2,1,0:T(8,128)(2,1)}, bf16[32,16,512]{2,1,0:T(8,128)(2,1)}, bf16[32,16,512]{2,1,0:T(8,128)(2,1)}) custom-call(f32[2,128,512]{2,1,0:T(8,128)S(1)} %get-tuple-element.71.dq_edge, f32[2,128,512]{2,1,0:T(8,128)S(1)} %get-tuple-element.80.dq_mid, f32[512,512]{1,0:T(8,128)S(1)} %get-tuple-element.81.dk, ...), custom_call_target="tpu_custom_call" | custom-call | bytes 1024 | tf_op jit(solution)/shard_map/finish/pallas_call | solution.py:522
  (12 shorter events, 0.0 us)
Async XLA Ops:
  3.3 26.0 %collective-permute-start.1 = (bf16[2,256,512]{2,1,0:T(8,128)(2,1)}, bf16[2,256,512]{2,1,0:T(8,128)(2,1)S(1)}, u32[]{:S(2)}, u32[]{:S(2)}) collective-permute-start(bf16[2,256,512]{2,1,0:T(8,128)(2,1)} %get-tuple-element.45.side_1.refs_1_), channel_id=1, source_target_pairs={{1,2},{2,1},{3,4},{4,3},{5,6},{6,5},{7,8},{8,7},{9,10},{10,9},{11,... | collective-permute-start | bytes 1572872 | tf_op jit(solution)/shard_map/ppermute | solution.py:542
  12.8 11.4 %collective-permute-start.2 = (bf16[2,128,512]{2,1,0:T(8,128)(2,1)}, bf16[2,128,512]{2,1,0:T(8,128)(2,1)S(1)}, u32[]{:S(2)}, u32[]{:S(2)}) collective-permute-start(bf16[2,128,512]{2,1,0:T(8,128)(2,1)} %get-tuple-element.48), channel_id=1, source_target_pairs={{0,32},{32,0},{64,96},{96,64},{1,33},{33,1},{65,97},{97,65},{2,34}... | collective-permute-start | bytes 786440 | tf_op jit(solution)/shard_map/ppermute | solution.py:534
  13.8 13.1 %collective-permute-start.3 = (bf16[2,128,512]{2,1,0:T(8,128)(2,1)}, bf16[2,128,512]{2,1,0:T(8,128)(2,1)S(1)}, u32[]{:S(2)}, u32[]{:S(2)}) collective-permute-start(bf16[2,128,512]{2,1,0:T(8,128)(2,1)} %get-tuple-element.49), channel_id=1, source_target_pairs={{32,64},{64,32},{33,65},{65,33},{34,66},{66,34},{35,67},{67,35},{3... | collective-permute-start | bytes 786440 | tf_op jit(solution)/shard_map/ppermute | solution.py:542
  15.9 21.9 %collective-permute-start = (bf16[2,256,512]{2,1,0:T(8,128)(2,1)}, bf16[2,256,512]{2,1,0:T(8,128)(2,1)S(1)}, u32[]{:S(2)}, u32[]{:S(2)}) collective-permute-start(bf16[2,256,512]{2,1,0:T(8,128)(2,1)} %get-tuple-element.44.side_0.refs_0_), channel_id=1, source_target_pairs={{0,1},{1,0},{2,3},{3,2},{4,5},{5,4},{6,7},{7,6},{8,9},{9,8},{10,11... | collective-permute-start | bytes 1572872 | tf_op jit(solution)/shard_map/ppermute | solution.py:534
  16.0 1.0 %copy-start.4 = (bf16[32,16,512]{2,1,0:T(8,128)(2,1)S(1)}, bf16[32,16,512]{2,1,0:T(8,128)(2,1)}, u32[]{:S(2)}) copy-start(bf16[32,16,512]{2,1,0:T(8,128)(2,1)} %k_ref.3) | copy-start | bytes 1572868
  17.1 1.0 %copy-start.5 = (bf16[32,16,512]{2,1,0:T(8,128)(2,1)S(1)}, bf16[32,16,512]{2,1,0:T(8,128)(2,1)}, u32[]{:S(2)}) copy-start(bf16[32,16,512]{2,1,0:T(8,128)(2,1)} %v_ref.3) | copy-start | bytes 1572868
  19.8 1.0 %copy-start = (bf16[2,256,512]{2,1,0:T(8,128)(2,1)S(1)}, bf16[2,256,512]{2,1,0:T(8,128)(2,1)}, u32[]{:S(2)}) copy-start(bf16[2,256,512]{2,1,0:T(8,128)(2,1)} %get-tuple-element.44.side_0.refs_0_) | copy-start | bytes 1572868
  20.8 1.0 %copy-start.2 = (bf16[2,256,512]{2,1,0:T(8,128)(2,1)S(1)}, bf16[2,256,512]{2,1,0:T(8,128)(2,1)}, u32[]{:S(2)}) copy-start(bf16[2,256,512]{2,1,0:T(8,128)(2,1)} %get-tuple-element.45.side_1.refs_1_) | copy-start | bytes 1572868
  30.7 9.1 %collective-permute-start.5 = (f32[4,16,128]{2,1,0:T(8,128)S(1)}, f32[4,16,128]{2,1,0:T(8,128)S(1)}, u32[]{:S(2)}, u32[]{:S(2)}) collective-permute-start(f32[4,16,128]{2,1,0:T(8,128)S(1)} %get-tuple-element.53.send.refs_5_), channel_id=1, source_target_pairs={{1,2},{2,1},{3,4},{4,3},{5,6},{6,5},{7,8},{8,7},{9,10},{10,9},{11,... | collective-permute-start | bytes 98312 | tf_op jit(solution)/shard_map/ppermute | solution.py:542
  39.2 8.9 %collective-permute-start.4 = (f32[4,16,128]{2,1,0:T(8,128)S(1)}, f32[4,16,128]{2,1,0:T(8,128)S(1)}, u32[]{:S(2)}, u32[]{:S(2)}) collective-permute-start(f32[4,16,128]{2,1,0:T(8,128)S(1)} %get-tuple-element.52.send.refs_4_), channel_id=1, source_target_pairs={{0,1},{1,0},{2,3},{3,2},{4,5},{5,4},{6,7},{7,6},{8,9},{9,8},{10,11... | collective-permute-start | bytes 98312 | tf_op jit(solution)/shard_map/ppermute | solution.py:534
  39.8 9.4 %copy-start.1 = (bf16[2,256,512]{2,1,0:T(8,128)(2,1)S(1)}, bf16[2,256,512]{2,1,0:T(8,128)(2,1)}, u32[]{:S(2)}) copy-start(bf16[2,256,512]{2,1,0:T(8,128)(2,1)} %get-tuple-element.44.side_0.refs_0_) | copy-start | bytes 1572868
  39.8 9.4 %copy-start.3 = (bf16[2,256,512]{2,1,0:T(8,128)(2,1)S(1)}, bf16[2,256,512]{2,1,0:T(8,128)(2,1)}, u32[]{:S(2)}) copy-start(bf16[2,256,512]{2,1,0:T(8,128)(2,1)} %get-tuple-element.45.side_1.refs_1_) | copy-start | bytes 1572868
  40.9 18.6 %collective-permute-start.7 = (bf16[256,512]{1,0:T(8,128)(2,1)S(1)}, bf16[256,512]{1,0:T(8,128)(2,1)S(1)}, u32[]{:S(2)}, u32[]{:S(2)}) collective-permute-start(bf16[256,512]{1,0:T(8,128)(2,1)S(1)} %get-tuple-element.70.refs_17_), channel_id=1, source_target_pairs={{1,2},{2,1},{3,4},{4,3},{5,6},{6,5},{7,8},{8,7},{9,10},{10,9},{11,... | collective-permute-start | bytes 786440 | tf_op jit(solution)/shard_map/ppermute | solution.py:542
  49.1 10.3 %collective-permute-start.6 = (bf16[256,512]{1,0:T(8,128)(2,1)S(1)}, bf16[256,512]{1,0:T(8,128)(2,1)S(1)}, u32[]{:S(2)}, u32[]{:S(2)}) collective-permute-start(bf16[256,512]{1,0:T(8,128)(2,1)S(1)} %get-tuple-element.69.refs_16_), channel_id=1, source_target_pairs={{0,1},{1,0},{2,3},{3,2},{4,5},{5,4},{6,7},{7,6},{8,9},{9,8},{10,11... | collective-permute-start | bytes 786440 | tf_op jit(solution)/shard_map/ppermute | solution.py:534
  51.7 5.8 %collective-permute-start.8 = (bf16[2,128,512]{2,1,0:T(8,128)(2,1)S(1)}, bf16[2,128,512]{2,1,0:T(8,128)(2,1)S(1)}, u32[]{:S(2)}, u32[]{:S(2)}) collective-permute-start(bf16[2,128,512]{2,1,0:T(8,128)(2,1)S(1)} %get-tuple-element.83), channel_id=1, source_target_pairs={{0,32},{32,0},{64,96},{96,64},{1,33},{33,1},{65,97},{97,65},{2,34}... | collective-permute-start | bytes 786440 | tf_op jit(solution)/shard_map/ppermute | solution.py:534
  51.8 7.7 %collective-permute-start.9 = (bf16[2,128,512]{2,1,0:T(8,128)(2,1)S(1)}, bf16[2,128,512]{2,1,0:T(8,128)(2,1)S(1)}, u32[]{:S(2)}, u32[]{:S(2)}) collective-permute-start(bf16[2,128,512]{2,1,0:T(8,128)(2,1)S(1)} %get-tuple-element.84), channel_id=1, source_target_pairs={{32,64},{64,32},{33,65},{65,33},{34,66},{66,34},{35,67},{67,35},{3... | collective-permute-start | bytes 786440 | tf_op jit(solution)/shard_map/ppermute | solution.py:542

commit v10 on v9

--- a/solution.py
+++ b/solution.py
@@ -492,23 +492,22 @@
     return jnp.concatenate([part.reshape(8, 8, FEAT) for part in parts], axis=1).astype(BF16)
 
 
-def finish_kernel(dq_edge, dq_mid, dk, dv, dq_0, dq_1, from_a, from_b,
-                  q_ref, k_ref, v_ref, buffers, sems):
+def sender(refs, buffers, sems):
     copies = []
 
     def send(i, t, value):
         buffers[i, t] = value
-        out = (q_ref, k_ref, v_ref)[i]
-        copies.append(pltpu.make_async_copy(buffers.at[i, t], out.at[pl.ds(8 * grid_row(t), 8)], sems.at[i, t]))
+        copies.append(pltpu.make_async_copy(buffers.at[i, t], refs[i].at[pl.ds(8 * grid_row(t), 8)], sems.at[i, t]))
         copies[-1].start()
 
-    for t in range(ROWS):
+    return copies, send
+
+
+def inner_kernel(dq_edge, dq_mid, dk, dv, dq_0, dq_1, q_ref, k_ref, v_ref, buffers, sems):
+    copies, send = sender((q_ref, k_ref, v_ref), buffers, sems)
+    for t in MID_ROWS:
         for which, own in enumerate((dk, dv)):
             full = own[t * PAIR:(t + 1) * PAIR]
-            if t == 0:
-                full = full + from_a[which].astype(F32)
-            if t == ROWS - 1:
-                full = full + from_b[which].astype(F32)
             send(1 + which, t, join_columns(full[:CELLS], full[CELLS:]))
     for place, t in enumerate(ORDER):
         dq = (dq_edge, dq_mid)[place // 2]
@@ -518,16 +517,40 @@
         copy.wait()
 
 
-def finish(*operands):
-    return pl.pallas_call(
-        finish_kernel,
+def outer_kernel(dk, dv, from_a, from_b, _k, _v, k_ref, v_ref, buffers, sems):
+    copies, send = sender((k_ref, v_ref), buffers, sems)
+    for t, part in zip(EDGE_ROWS, (from_a, from_b)):
+        for which, own in enumerate((dk, dv)):
+            full = own[t * PAIR:(t + 1) * PAIR] + part[which].astype(F32)
+            send(which, t, join_columns(full[:CELLS], full[CELLS:]))
+    for copy in copies:
+        copy.wait()
+
+
+def finish(dq_edge, dq_mid, dk, dv, dq_0, dq_1, from_a, from_b):
+    out = struct((8 * ROWS, 16, FEAT), BF16)
+    q_out, k_inner, v_inner = pl.pallas_call(
+        inner_kernel,
         out_specs=[any_spec] * 3,
-        out_shape=[struct((8 * ROWS, 16, FEAT), BF16)] * 3,
+        out_shape=[out] * 3,
         scratch_shapes=[pltpu.VMEM((3, ROWS, 8, 16, FEAT), BF16), pltpu.SemaphoreType.DMA((3, ROWS))],
         compiler_params=params(),
         cost_estimate=cost(0, 1 << 10),
-        name="finish",
-    )(*operands)
+        name="finish_inner",
+    )(dq_edge, dq_mid, dk, dv, dq_0, dq_1)
+    whole = pl.BlockSpec(memory_space=pltpu.VMEM)
+    k_out, v_out = pl.pallas_call(
+        outer_kernel,
+        in_specs=[whole] * 4 + [any_spec] * 2,
+        out_specs=[any_spec] * 2,
+        out_shape=[out] * 2,
+        input_output_aliases={4: 0, 5: 1},
+        scratch_shapes=[pltpu.VMEM((2, ROWS, 8, 16, FEAT), BF16), pltpu.SemaphoreType.DMA((2, ROWS))],
+        compiler_params=params(),
+        cost_estimate=cost(0, 1 << 10),
+        name="finish_outer",
+    )(dk, dv, from_a, from_b, k_inner, v_inner)
+    return q_out, k_out, v_out
 
 
 def swap_a(x, axis):

time: 61.9 us -> 61.5 us (level)
  waiting for transfers between devices: 4.61 us -> 3.5 us
  Pallas kernels: 20.7 us -> 21.4 us
    ppermute x5, waiting for transfers between devices: 4.59 us -> 2.91 us  [swap_b(): return lax.ppermute(x, axis, pairs)]
    pallas_call x1 -> x2, Pallas kernels: 1.27 us -> 1.97 us  [the longest x1 1.08 us: finish(): pl.pallas_call(inner_kernel, out_specs=[any_spec] * 3, out_shape=[out] *...]
  transfers between devices with their start and end apart: 10 -> 10, of which waited for: 2 -> 3; matrix products, arithmetic and copies ran while one was open for 0% -> 0% of each run, Pallas kernels for 28% -> 30%
where the time goes in v10:
time: 61.5 us; the launch traced here: 60.4 us
  starting transfers between devices  30.4 us (49%)
  Pallas kernels  21.4 us (35%)
  local copies, waits for them, and re-layouts  4.17 us (7%)
  waiting for transfers between devices  3.5 us (6%)
  between operations  0.87 us (1%)
    ppermute x5, starting transfers between devices, swap_b(): return lax.ppermute(x, axis, pairs)  29.1 us
    unnamed x12, local copies, waits for them, and re-layouts  4.17 us
    ppermute x5, waiting for transfers between devices, swap_b(): return lax.ppermute(x, axis, pairs)  2.91 us
    pallas_call x2, Pallas kernels, halo_scores(): pl.pallas_call(functools.partial(halo_scores_kernel, c), grid=(GROUPS,),...  2.76 us
    pallas_call x1, Pallas kernels, pack_queries(): pl.pallas_call(pack_queries_kernel, in_specs=[any_spec] * 4, out_specs=[a...  2.67 us
    pallas_call x1, Pallas kernels, mid_gradients(): pl.pallas_call(mid_kernel, grid=(GROUPS,), in_specs=row_specs(MID) + [key...  2.52 us
    pallas_call x1, Pallas kernels, edge_gradients(): pl.pallas_call(edge_kernel, grid=(GROUPS,), in_specs=row_specs(EDGE) + [e...  2.44 us
    pallas_call x1, Pallas kernels, edge_scores(): pl.pallas_call(edge_scores_kernel, grid=(PAIRS,), in_specs=[tokens_spec(E...  2.43 us
  transfers between devices with their start and end apart: 10, of which 3 were waited for; matrix products, arithmetic and copies ran while one was open for 0% of the time, Pallas kernels for 30%

profile of v10, /device:TPU:1, one launch (start us, length us, event | category | flops | bytes accessed | tf_op | source)
XLA Modules:
  0.0 60.4 jit_solution(9887004568413669847)
XLA Ops:
  0.6 2.7 %pack_queries.1 = (bf16[2,256,512]{2,1,0:T(8,128)(2,1)}, bf16[2,256,512]{2,1,0:T(8,128)(2,1)}, bf16[2,128,512]{2,1,0:T(8,128)(2,1)}, bf16[2,128,512]{2,1,0:T(8,128)(2,1)}) custom-call(bf16[32,16,512]{2,1,0:T(8,128)(2,1)} %q_ref.1, bf16[32,16,512]{2,1,0:T(8,128)(2,1)} %g_ref.1, bf16[32,16,512]{2,1,0:T(8,128)(2,1)} %k_ref.3, bf16[32,16,512]{2,1,0:T(8,128)(2,1)} %v_ref.3), custom_call_target="tpu_custom_call" | custom-call | bytes 3145728 | tf_op jit(solution)/shard_map/pack_queries/pallas_call | solution.py:102
  3.3 9.5 %collective-permute-start.1 = (bf16[2,256,512]{2,1,0:T(8,128)(2,1)}, bf16[2,256,512]{2,1,0:T(8,128)(2,1)S(1)}, u32[]{:S(2)}, u32[]{:S(2)}) collective-permute-start(bf16[2,256,512]{2,1,0:T(8,128)(2,1)} %get-tuple-element.50.side_1.refs_1_), channel_id=1, source_target_pairs={{1,2},{2,1},{3,4},{4,3},{5,6},{6,5},{7,8},{8,7},{9,10},{10,9},{11,... | collective-permute-start | bytes 1572872 | tf_op jit(solution)/shard_map/ppermute | solution.py:565
  12.8 1.0 %collective-permute-start.2 = (bf16[2,128,512]{2,1,0:T(8,128)(2,1)}, bf16[2,128,512]{2,1,0:T(8,128)(2,1)S(1)}, u32[]{:S(2)}, u32[]{:S(2)}) collective-permute-start(bf16[2,128,512]{2,1,0:T(8,128)(2,1)} %get-tuple-element.53), channel_id=1, source_target_pairs={{0,32},{32,0},{64,96},{96,64},{1,33},{33,1},{65,97},{97,65},{2,34}... | collective-permute-start | bytes 786440 | tf_op jit(solution)/shard_map/ppermute | solution.py:557
  13.8 2.2 %collective-permute-start.3 = (bf16[2,128,512]{2,1,0:T(8,128)(2,1)}, bf16[2,128,512]{2,1,0:T(8,128)(2,1)S(1)}, u32[]{:S(2)}, u32[]{:S(2)}) collective-permute-start(bf16[2,128,512]{2,1,0:T(8,128)(2,1)} %get-tuple-element.54), channel_id=1, source_target_pairs={{32,64},{64,32},{33,65},{65,33},{34,66},{66,34},{35,67},{67,35},{3... | collective-permute-start | bytes 786440 | tf_op jit(solution)/shard_map/ppermute | solution.py:565
  15.9 0.1 collective-permute-start
  16.0 0.0 copy-start.4
  16.1 1.0 %copy-done.4 = bf16[32,16,512]{2,1,0:T(8,128)(2,1)S(1)} copy-done((bf16[32,16,512]{2,1,0:T(8,128)(2,1)S(1)}, bf16[32,16,512]{2,1,0:T(8,128)(2,1)}, u32[]{:S(2)}) %copy-start.4) | copy-done | bytes 524312
  17.1 1.0 %copy-done.5 = bf16[32,16,512]{2,1,0:T(8,128)(2,1)S(1)} copy-done((bf16[32,16,512]{2,1,0:T(8,128)(2,1)S(1)}, bf16[32,16,512]{2,1,0:T(8,128)(2,1)}, u32[]{:S(2)}) %copy-start.5) | copy-done | bytes 524312
  18.1 1.6 %pack_keys.1 = (bf16[512,512]{1,0:T(8,128)(2,1)S(1)}, bf16[512,512]{1,0:T(8,128)(2,1)S(1)}) custom-call(bf16[32,16,512]{2,1,0:T(8,128)(2,1)S(1)} %copy-done.4, bf16[32,16,512]{2,1,0:T(8,128)(2,1)S(1)} %copy-done.5), custom_call_target="tpu_custom_call" | custom-call | bytes 3145728 | tf_op jit(solution)/shard_map/pack_keys/pallas_call | solution.py:128
  19.8 0.0 copy-start
  19.8 1.0 %copy-done = bf16[2,256,512]{2,1,0:T(8,128)(2,1)S(1)} copy-done((bf16[2,256,512]{2,1,0:T(8,128)(2,1)S(1)}, bf16[2,256,512]{2,1,0:T(8,128)(2,1)}, u32[]{:S(2)}) %copy-start) | copy-done | bytes 524312
  20.8 1.0 %copy-done.2 = bf16[2,256,512]{2,1,0:T(8,128)(2,1)S(1)} copy-done((bf16[2,256,512]{2,1,0:T(8,128)(2,1)S(1)}, bf16[2,256,512]{2,1,0:T(8,128)(2,1)}, u32[]{:S(2)}) %copy-start.2) | copy-done | bytes 524312
  21.8 2.4 %mid_scores.1 = (f32[4,8,128]{2,1,0:T(8,128)S(1)}, f32[4,2,384,256]{3,2,1,0:T(8,128)S(1)}, f32[4,2,384,256]{3,2,1,0:T(8,128)S(1)}, bf16[512,512]{1,0:T(8,128)(2,1)S(1)}) custom-call(bf16[2,256,512]{2,1,0:T(8,128)(2,1)S(1)} %copy-done, bf16[2,256,512]{2,1,0:T(8,128)(2,1)S(1)} %copy-done.2, bf16[512,512]{1,0:T(8,128)(2,1)S(1)} %get-tuple-element.51.kd, ...), custom_call_target="tpu_custom_call" | custom-call | flops 2000000000 | bytes 1024 | tf_op jit(solution)/shard_map/mid_scores/pallas_call | solution.py:288
  24.2 2.6 %collective-permute-done.3.edge_b = bf16[2,128,512]{2,1,0:T(8,128)(2,1)S(1)} collective-permute-done((bf16[2,128,512]{2,1,0:T(8,128)(2,1)}, bf16[2,128,512]{2,1,0:T(8,128)(2,1)S(1)}, u32[]{:S(2)}, u32[]{:S(2)}) %collective-permute-start.3) | collective-permute-done | bytes 262176 | tf_op jit(solution)/shard_map/ppermute | solution.py:565
  26.8 2.4 %edge_scores.1 = (f32[4,8,128]{2,1,0:T(8,128)S(1)}, f32[4,2,384,256]{3,2,1,0:T(8,128)S(1)}, f32[4,2,384,256]{3,2,1,0:T(8,128)S(1)}) custom-call(bf16[2,256,512]{2,1,0:T(8,128)(2,1)S(1)} %copy-done, bf16[2,256,512]{2,1,0:T(8,128)(2,1)S(1)} %copy-done.2, bf16[512,512]{1,0:T(8,128)(2,1)S(1)} %get-tuple-element.51.kd, ...), custom_call_target="tpu_custom_call" | custom-call | flops 2000000000 | bytes 1024 | tf_op jit(solution)/shard_map/edge_scores/pallas_call | solution.py:301
  29.3 1.4 %halo_scores_b.1 = (f32[4,16,128]{2,1,0:T(8,128)S(1)}, f32[2,2,192,256]{3,2,1,0:T(8,128)S(1)}, f32[2,2,192,256]{3,2,1,0:T(8,128)S(1)}, f32[2,2,192,256]{3,2,1,0:T(8,128)S(1)}, f32[2,2,192,256]{3,2,1,0:T(8,128)S(1)}) custom-call(bf16[2,256,512]{2,1,0:T(8,128)(2,1)S(1)} %collective-permute-done.1.q_in.refs_3_, bf16[512,512]{1,0:T(8,128)(2,1)S(1)} %get-tuple-element.51.kd, ...), custom_call_target="tpu_custom_call" | custom-call | flops 2000000000 | bytes 1024 | tf_op jit(solution)/shard_map/halo_scores_b/pallas_call | solution.py:354
  30.7 7.1 %collective-permute-start.5 = (f32[4,16,128]{2,1,0:T(8,128)S(1)}, f32[4,16,128]{2,1,0:T(8,128)S(1)}, u32[]{:S(2)}, u32[]{:S(2)}) collective-permute-start(f32[4,16,128]{2,1,0:T(8,128)S(1)} %get-tuple-element.58.send.refs_5_), channel_id=1, source_target_pairs={{1,2},{2,1},{3,4},{4,3},{5,6},{6,5},{7,8},{8,7},{9,10},{10,9},{11,... | collective-permute-start | bytes 98312 | tf_op jit(solution)/shard_map/ppermute | solution.py:565
  37.8 1.4 %halo_scores_a.1 = (f32[4,16,128]{2,1,0:T(8,128)S(1)}, f32[2,2,192,256]{3,2,1,0:T(8,128)S(1)}, f32[2,2,192,256]{3,2,1,0:T(8,128)S(1)}, f32[2,2,192,256]{3,2,1,0:T(8,128)S(1)}, f32[2,2,192,256]{3,2,1,0:T(8,128)S(1)}) custom-call(bf16[2,256,512]{2,1,0:T(8,128)(2,1)S(1)} %collective-permute-done.q_in.refs_2_, bf16[512,512]{1,0:T(8,128)(2,1)S(1)} %get-tuple-element.51.kd, ...), custom_call_target="tpu_custom_call" | custom-call | flops 2000000000 | bytes 1024 | tf_op jit(solution)/shard_map/halo_scores_a/pallas_call | solution.py:354
  39.2 0.1 collective-permute-start.4
  39.3 0.5 turn_edges.1.edges_turned.refs_15_
  39.8 1.1 %halo_queries_b.1 = (bf16[256,512]{1,0:T(8,128)(2,1)S(1)}, bf16[2,2,192,256]{3,2,1,0:T(8,128)(2,1)S(1)}, bf16[2,2,192,256]{3,2,1,0:T(8,128)(2,1)S(1)}, bf16[2,2,...) custom-call(f32[4,16,128]{2,1,0:T(8,128)S(1)} %get-tuple-element.58.send.refs_5_, ...), custom_call_target="tpu_custom_call" | custom-call | bytes 1024 | tf_op jit(solution)/shard_map/halo_queries_b/pallas_call | solution.py:391
  40.9 7.1 %collective-permute-start.7 = (bf16[256,512]{1,0:T(8,128)(2,1)S(1)}, bf16[256,512]{1,0:T(8,128)(2,1)S(1)}, u32[]{:S(2)}, u32[]{:S(2)}) collective-permute-start(bf16[256,512]{1,0:T(8,128)(2,1)S(1)} %get-tuple-element.75.refs_17_), channel_id=1, source_target_pairs={{1,2},{2,1},{3,4},{4,3},{5,6},{6,5},{7,8},{8,7},{9,10},{10,9},{11,... | collective-permute-start | bytes 786440 | tf_op jit(solution)/shard_map/ppermute | solution.py:565
  48.0 1.1 %halo_queries_a.1 = (bf16[256,512]{1,0:T(8,128)(2,1)S(1)}, bf16[2,2,192,256]{3,2,1,0:T(8,128)(2,1)S(1)}, bf16[2,2,192,256]{3,2,1,0:T(8,128)(2,1)S(1)}, bf16[2,2,...) custom-call(f32[4,16,128]{2,1,0:T(8,128)S(1)} %get-tuple-element.57.send.refs_4_, ...), custom_call_target="tpu_custom_call" | custom-call | bytes 1024 | tf_op jit(solution)/shard_map/halo_queries_a/pallas_call | solution.py:391
  49.1 0.1 collective-permute-start.6
  49.3 2.4 %edge_gradients.1 = (f32[2,128,512]{2,1,0:T(8,128)S(1)}, f32[512,512]{1,0:T(8,128)S(1)}, f32[512,512]{1,0:T(8,128)S(1)}, bf16[2,128,512]{2,1,0:T(8,128)(2,1)S(1)}, bf16[2,128,512]{2,1,0:T(8,128)(2,1)S(1)}) custom-call(bf16[2,256,512]{2,1,0:T(8,128)(2,1)S(1)} %copy-done.1, bf16[2,256,512]{2,1,0:T(8,128)(2,1)S(1)} %copy-done.3, ...), custom_call_target="tpu_custom_call" | custom-call | flops 3000000000 | bytes 1024 | tf_op jit(solution)/shard_map/edge_gradients/pallas_call | solution.py:465
  51.7 0.1 collective-permute-start.8
  51.8 3.2 %collective-permute-start.9 = (bf16[2,128,512]{2,1,0:T(8,128)(2,1)S(1)}, bf16[2,128,512]{2,1,0:T(8,128)(2,1)S(1)}, u32[]{:S(2)}, u32[]{:S(2)}) collective-permute-start(bf16[2,128,512]{2,1,0:T(8,128)(2,1)S(1)} %get-tuple-element.90), channel_id=1, source_target_pairs={{32,64},{64,32},{33,65},{65,33},{34,66},{66,34},{35,67},{67,35},{3... | collective-permute-start | bytes 786440 | tf_op jit(solution)/shard_map/ppermute | solution.py:565
  55.0 2.5 %mid_gradients.1 = (f32[2,128,512]{2,1,0:T(8,128)S(1)}, f32[512,512]{1,0:T(8,128)S(1)}, f32[512,512]{1,0:T(8,128)S(1)}) custom-call(bf16[2,256,512]{2,1,0:T(8,128)(2,1)S(1)} %copy-done.1, bf16[2,256,512]{2,1,0:T(8,128)(2,1)S(1)} %copy-done.3, bf16[2,256,512]{2,1,0:T(8,128)(2,1)S(1)} %collective-permute-done.q_in.refs_2_, ...), custom_call_target="tpu_custom_call" | custom-call | flops 3000000000 | bytes 1024 | tf_op jit(solution)/shard_map/mid_gradients/pallas_call | solution.py:478
  57.5 0.6 collective-permute-done.6.dq_0
  58.1 1.1 %finish_inner.1 = (bf16[32,16,512]{2,1,0:T(8,128)(2,1)}, bf16[32,16,512]{2,1,0:T(8,128)(2,1)}, bf16[32,16,512]{2,1,0:T(8,128)(2,1)}) custom-call(f32[2,128,512]{2,1,0:T(8,128)S(1)} %get-tuple-element.76.dq_edge, f32[2,128,512]{2,1,0:T(8,128)S(1)} %get-tuple-element.85.dq_mid, f32[512,512]{1,0:T(8,128)S(1)} %get-tuple-element.86.dk, ...), custom_call_target="tpu_custom_call" | custom-call | bytes 1024 | tf_op jit(solution)/shard_map/finish_inner/pallas_call | solution.py:532
  59.2 0.3 collective-permute-done.9.from_b
  59.5 0.9 %finish_outer.1 = (bf16[32,16,512]{2,1,0:T(8,128)(2,1)}, bf16[32,16,512]{2,1,0:T(8,128)(2,1)}) custom-call(f32[512,512]{1,0:T(8,128)S(1)} %get-tuple-element.86.dk, f32[512,512]{1,0:T(8,128)S(1)} %get-tuple-element.87.dv, bf16[2,128,512]{2,1,0:T(8,128)(2,1)S(1)} %collective-permute-done.8.from_a, ...), custom_call_target="tpu_custom_call", output_to_operand_aliasing={{0}: (4, {}), {1}: (5, {})} | custom-call | bytes 1024 | tf_op jit(solution)/shard_map/finish_outer/pallas_call | solution.py:542
  (13 shorter events, 0.0 us)
Async XLA Ops:
  3.3 26.0 %collective-permute-start.1 = (bf16[2,256,512]{2,1,0:T(8,128)(2,1)}, bf16[2,256,512]{2,1,0:T(8,128)(2,1)S(1)}, u32[]{:S(2)}, u32[]{:S(2)}) collective-permute-start(bf16[2,256,512]{2,1,0:T(8,128)(2,1)} %get-tuple-element.50.side_1.refs_1_), channel_id=1, source_target_pairs={{1,2},{2,1},{3,4},{4,3},{5,6},{6,5},{7,8},{8,7},{9,10},{10,9},{11,... | collective-permute-start | bytes 1572872 | tf_op jit(solution)/shard_map/ppermute | solution.py:565
  12.8 11.4 %collective-permute-start.2 = (bf16[2,128,512]{2,1,0:T(8,128)(2,1)}, bf16[2,128,512]{2,1,0:T(8,128)(2,1)S(1)}, u32[]{:S(2)}, u32[]{:S(2)}) collective-permute-start(bf16[2,128,512]{2,1,0:T(8,128)(2,1)} %get-tuple-element.53), channel_id=1, source_target_pairs={{0,32},{32,0},{64,96},{96,64},{1,33},{33,1},{65,97},{97,65},{2,34}... | collective-permute-start | bytes 786440 | tf_op jit(solution)/shard_map/ppermute | solution.py:557
  13.8 13.1 %collective-permute-start.3 = (bf16[2,128,512]{2,1,0:T(8,128)(2,1)}, bf16[2,128,512]{2,1,0:T(8,128)(2,1)S(1)}, u32[]{:S(2)}, u32[]{:S(2)}) collective-permute-start(bf16[2,128,512]{2,1,0:T(8,128)(2,1)} %get-tuple-element.54), channel_id=1, source_target_pairs={{32,64},{64,32},{33,65},{65,33},{34,66},{66,34},{35,67},{67,35},{3... | collective-permute-start | bytes 786440 | tf_op jit(solution)/shard_map/ppermute | solution.py:565
  15.9 21.9 %collective-permute-start = (bf16[2,256,512]{2,1,0:T(8,128)(2,1)}, bf16[2,256,512]{2,1,0:T(8,128)(2,1)S(1)}, u32[]{:S(2)}, u32[]{:S(2)}) collective-permute-start(bf16[2,256,512]{2,1,0:T(8,128)(2,1)} %get-tuple-element.49.side_0.refs_0_), channel_id=1, source_target_pairs={{0,1},{1,0},{2,3},{3,2},{4,5},{5,4},{6,7},{7,6},{8,9},{9,8},{10,11... | collective-permute-start | bytes 1572872 | tf_op jit(solution)/shard_map/ppermute | solution.py:557
  16.0 1.0 %copy-start.4 = (bf16[32,16,512]{2,1,0:T(8,128)(2,1)S(1)}, bf16[32,16,512]{2,1,0:T(8,128)(2,1)}, u32[]{:S(2)}) copy-start(bf16[32,16,512]{2,1,0:T(8,128)(2,1)} %k_ref.3) | copy-start | bytes 1572868
  17.1 1.0 %copy-start.5 = (bf16[32,16,512]{2,1,0:T(8,128)(2,1)S(1)}, bf16[32,16,512]{2,1,0:T(8,128)(2,1)}, u32[]{:S(2)}) copy-start(bf16[32,16,512]{2,1,0:T(8,128)(2,1)} %v_ref.3) | copy-start | bytes 1572868
  19.8 1.0 %copy-start = (bf16[2,256,512]{2,1,0:T(8,128)(2,1)S(1)}, bf16[2,256,512]{2,1,0:T(8,128)(2,1)}, u32[]{:S(2)}) copy-start(bf16[2,256,512]{2,1,0:T(8,128)(2,1)} %get-tuple-element.49.side_0.refs_0_) | copy-start | bytes 1572868
  20.8 1.0 %copy-start.2 = (bf16[2,256,512]{2,1,0:T(8,128)(2,1)S(1)}, bf16[2,256,512]{2,1,0:T(8,128)(2,1)}, u32[]{:S(2)}) copy-start(bf16[2,256,512]{2,1,0:T(8,128)(2,1)} %get-tuple-element.50.side_1.refs_1_) | copy-start | bytes 1572868
  30.7 9.1 %collective-permute-start.5 = (f32[4,16,128]{2,1,0:T(8,128)S(1)}, f32[4,16,128]{2,1,0:T(8,128)S(1)}, u32[]{:S(2)}, u32[]{:S(2)}) collective-permute-start(f32[4,16,128]{2,1,0:T(8,128)S(1)} %get-tuple-element.58.send.refs_5_), channel_id=1, source_target_pairs={{1,2},{2,1},{3,4},{4,3},{5,6},{6,5},{7,8},{8,7},{9,10},{10,9},{11,... | collective-permute-start | bytes 98312 | tf_op jit(solution)/shard_map/ppermute | solution.py:565
  39.2 8.9 %collective-permute-start.4 = (f32[4,16,128]{2,1,0:T(8,128)S(1)}, f32[4,16,128]{2,1,0:T(8,128)S(1)}, u32[]{:S(2)}, u32[]{:S(2)}) collective-permute-start(f32[4,16,128]{2,1,0:T(8,128)S(1)} %get-tuple-element.57.send.refs_4_), channel_id=1, source_target_pairs={{0,1},{1,0},{2,3},{3,2},{4,5},{5,4},{6,7},{7,6},{8,9},{9,8},{10,11... | collective-permute-start | bytes 98312 | tf_op jit(solution)/shard_map/ppermute | solution.py:557
  39.8 9.4 %copy-start.1 = (bf16[2,256,512]{2,1,0:T(8,128)(2,1)S(1)}, bf16[2,256,512]{2,1,0:T(8,128)(2,1)}, u32[]{:S(2)}) copy-start(bf16[2,256,512]{2,1,0:T(8,128)(2,1)} %get-tuple-element.49.side_0.refs_0_) | copy-start | bytes 1572868
  39.8 9.4 %copy-start.3 = (bf16[2,256,512]{2,1,0:T(8,128)(2,1)S(1)}, bf16[2,256,512]{2,1,0:T(8,128)(2,1)}, u32[]{:S(2)}) copy-start(bf16[2,256,512]{2,1,0:T(8,128)(2,1)} %get-tuple-element.50.side_1.refs_1_) | copy-start | bytes 1572868
  40.9 16.6 %collective-permute-start.7 = (bf16[256,512]{1,0:T(8,128)(2,1)S(1)}, bf16[256,512]{1,0:T(8,128)(2,1)S(1)}, u32[]{:S(2)}, u32[]{:S(2)}) collective-permute-start(bf16[256,512]{1,0:T(8,128)(2,1)S(1)} %get-tuple-element.75.refs_17_), channel_id=1, source_target_pairs={{1,2},{2,1},{3,4},{4,3},{5,6},{6,5},{7,8},{8,7},{9,10},{10,9},{11,... | collective-permute-start | bytes 786440 | tf_op jit(solution)/shard_map/ppermute | solution.py:565
  49.1 8.9 %collective-permute-start.6 = (bf16[256,512]{1,0:T(8,128)(2,1)S(1)}, bf16[256,512]{1,0:T(8,128)(2,1)S(1)}, u32[]{:S(2)}, u32[]{:S(2)}) collective-permute-start(bf16[256,512]{1,0:T(8,128)(2,1)S(1)} %get-tuple-element.74.refs_16_), channel_id=1, source_target_pairs={{0,1},{1,0},{2,3},{3,2},{4,5},{5,4},{6,7},{7,6},{8,9},{9,8},{10,11... | collective-permute-start | bytes 786440 | tf_op jit(solution)/shard_map/ppermute | solution.py:557
  51.7 7.5 %collective-permute-start.8 = (bf16[2,128,512]{2,1,0:T(8,128)(2,1)S(1)}, bf16[2,128,512]{2,1,0:T(8,128)(2,1)S(1)}, u32[]{:S(2)}, u32[]{:S(2)}) collective-permute-start(bf16[2,128,512]{2,1,0:T(8,128)(2,1)S(1)} %get-tuple-element.89), channel_id=1, source_target_pairs={{0,32},{32,0},{64,96},{96,64},{1,33},{33,1},{65,97},{97,65},{2,34}... | collective-permute-start | bytes 786440 | tf_op jit(solution)/shard_map/ppermute | solution.py:557
  51.8 7.7 %collective-permute-start.9 = (bf16[2,128,512]{2,1,0:T(8,128)(2,1)S(1)}, bf16[2,128,512]{2,1,0:T(8,128)(2,1)S(1)}, u32[]{:S(2)}, u32[]{:S(2)}) collective-permute-start(bf16[2,128,512]{2,1,0:T(8,128)(2,1)S(1)} %get-tuple-element.90), channel_id=1, source_target_pairs={{32,64},{64,32},{33,65},{65,33},{34,66},{66,34},{35,67},{67,35},{3... | collective-permute-start | bytes 786440 | tf_op jit(solution)/shard_map/ppermute | solution.py:565

commit v11 on v9

--- a/solution.py
+++ b/solution.py
@@ -434,7 +434,7 @@
 
 
 def edge_kernel(*refs):
-    operands, (_, _, dq_ref, dk_ref, dv_ref, out_a, out_b) = refs[:16], refs[16:]
+    operands, (_, dq_ref, dk_ref, dv_ref, out_a, out_b) = refs[:16], refs[16:]
     upper, lower = row_gradients(EDGE_ROWS, *operands, dq_ref)
     for which, (out, scale) in enumerate(((dk_ref, SCALE), (dv_ref, 1.0))):
         top, bottom = upper[which] * scale, lower[which] * scale
@@ -465,7 +465,7 @@
     return pl.pallas_call(
         edge_kernel,
         grid=(GROUPS,),
-        in_specs=row_specs(EDGE) + [edge_turned_wide, any_spec, any_spec],
+        in_specs=row_specs(EDGE) + [edge_turned_wide, any_spec],
         out_specs=GRAD_SPECS + [edge_wide] * 2,
         out_shape=GRAD_SHAPES + [struct((2, PAIR, FEAT), BF16)] * 2,
         compiler_params=params(),
@@ -492,24 +492,31 @@
     return jnp.concatenate([part.reshape(8, 8, FEAT) for part in parts], axis=1).astype(BF16)
 
 
-def finish_kernel(dq_edge, dq_mid, dk, dv, dq_0, dq_1, from_a, from_b,
-                  q_ref, k_ref, v_ref, buffers, sems):
+def sender(refs, buffers, sems):
     copies = []
 
     def send(i, t, value):
         buffers[i, t] = value
-        out = (q_ref, k_ref, v_ref)[i]
-        copies.append(pltpu.make_async_copy(buffers.at[i, t], out.at[pl.ds(8 * grid_row(t), 8)], sems.at[i, t]))
+        copies.append(pltpu.make_async_copy(buffers.at[i, t], refs[i].at[pl.ds(8 * grid_row(t), 8)], sems.at[i, t]))
         copies[-1].start()
 
-    for t in range(ROWS):
+    return copies, send
+
+
+def keys_kernel(dk, dv, from_a, from_b, k_ref, v_ref, buffers, sems):
+    copies, send = sender((k_ref, v_ref), buffers, sems)
+    for t in MID_ROWS + EDGE_ROWS:
         for which, own in enumerate((dk, dv)):
             full = own[t * PAIR:(t + 1) * PAIR]
-            if t == 0:
-                full = full + from_a[which].astype(F32)
-            if t == ROWS - 1:
-                full = full + from_b[which].astype(F32)
-            send(1 + which, t, join_columns(full[:CELLS], full[CELLS:]))
+            if t in EDGE_ROWS:
+                full = full + (from_b if t else from_a)[which].astype(F32)
+            send(which, t, join_columns(full[:CELLS], full[CELLS:]))
+    for copy in copies:
+        copy.wait()
+
+
+def queries_kernel(dq_edge, dq_mid, dq_0, dq_1, q_ref, buffers, sems):
+    copies, send = sender((q_ref,), buffers, sems)
     for place, t in enumerate(ORDER):
         dq = (dq_edge, dq_mid)[place // 2]
         at, there = at_tokens(place % 2), at_tokens(place)
@@ -518,15 +525,15 @@
         copy.wait()
 
 
-def finish(*operands):
-    return pl.pallas_call(
-        finish_kernel,
-        out_specs=[any_spec] * 3,
-        out_shape=[struct((8 * ROWS, 16, FEAT), BF16)] * 3,
-        scratch_shapes=[pltpu.VMEM((3, ROWS, 8, 16, FEAT), BF16), pltpu.SemaphoreType.DMA((3, ROWS))],
+def finish(kernel, count, operands, name):
+    return pl.pallas_call(
+        kernel,
+        out_specs=[any_spec] * count,
+        out_shape=[struct((8 * ROWS, 16, FEAT), BF16)] * count,
+        scratch_shapes=[pltpu.VMEM((count, ROWS, 8, 16, FEAT), BF16), pltpu.SemaphoreType.DMA((count, ROWS))],
         compiler_params=params(),
         cost_estimate=cost(0, 1 << 10),
-        name="finish",
+        name=name,
     )(*operands)
 
 
@@ -567,10 +574,12 @@
         weights.append(weight)
     shared = (*sides, *halos, *sends, *recvs)
     dq_edge, dk, dv, out_a, out_b = edge_gradients(*shared, *edge_own, *weights[0][:2], *weights[1][:2], turned, edges_turned,
-                                                   *halo_dq)
+                                                   halo_dq[1])
     key_parts = (swap_a(out_a, "lat"), swap_b(out_b, "lat", False))
     dq_mid, dk, dv = mid_gradients(*shared, *mid_own, *weights[0][2:], *weights[1][2:], turned, dk, dv)
-    return tuple(finish(dq_edge, dq_mid, dk, dv, *dq_parts, *key_parts))
+    k_out, v_out = finish(keys_kernel, 2, (dk, dv, *key_parts), "finish_keys")
+    q_out, = finish(queries_kernel, 1, (dq_edge, dq_mid, *dq_parts), "finish_queries")
+    return q_out, k_out, v_out
 
 
 def solution(mesh):

time: 61.9 us -> 64.1 us (1.036); the launches traced: 60.8 us -> 63.8 us
  waiting for transfers between devices: 4.61 us -> 7.01 us
  Pallas kernels: 20.7 us -> 21.4 us
    ppermute x5, waiting for transfers between devices: 0.01 us -> 1.22 us  [swap_a(): lax.ppermute(x, axis, [(i, i ^ 1) for i in range(lax.axis_size(axis))])]
    ppermute x5, waiting for transfers between devices: 4.59 us -> 5.79 us  [swap_b(): return lax.ppermute(x, axis, pairs)]
    pallas_call x1 -> x2, Pallas kernels: 1.27 us -> 1.9 us  [finish(): pl.pallas_call(kernel, out_specs=[any_spec] * count, out_shape=[struct((8...]
  transfers between devices with their start and end apart: 10 -> 10, of which waited for: 2 -> 3; matrix products, arithmetic and copies ran while one was open for 0% -> 0% of each run, Pallas kernels for 28% -> 28%
where the time goes in v11:
time: 64.1 us; the launch traced here: 63.8 us
  starting transfers between devices  30.4 us (47%)
  Pallas kernels  21.4 us (33%)
  waiting for transfers between devices  7.01 us (11%)
  local copies, waits for them, and re-layouts  4.17 us (7%)
  between operations  0.87 us (1%)
    ppermute x5, starting transfers between devices, swap_b(): return lax.ppermute(x, axis, pairs)  29.1 us
    ppermute x5, waiting for transfers between devices, swap_b(): return lax.ppermute(x, axis, pairs)  5.79 us
    unnamed x12, local copies, waits for them, and re-layouts  4.17 us
    pallas_call x2, Pallas kernels, halo_scores(): pl.pallas_call(functools.partial(halo_scores_kernel, c), grid=(GROUPS,),...  2.76 us
    pallas_call x1, Pallas kernels, pack_queries(): pl.pallas_call(pack_queries_kernel, in_specs=[any_spec] * 4, out_specs=[a...  2.67 us
    pallas_call x1, Pallas kernels, mid_gradients(): pl.pallas_call(mid_kernel, grid=(GROUPS,), in_specs=row_specs(MID) + [key...  2.52 us
    pallas_call x1, Pallas kernels, edge_gradients(): pl.pallas_call(edge_kernel, grid=(GROUPS,), in_specs=row_specs(EDGE) + [e...  2.43 us
    pallas_call x1, Pallas kernels, edge_scores(): pl.pallas_call(edge_scores_kernel, grid=(PAIRS,), in_specs=[tokens_spec(E...  2.43 us
  transfers between devices with their start and end apart: 10, of which 3 were waited for; matrix products, arithmetic and copies ran while one was open for 0% of the time, Pallas kernels for 28%

profile of v11, /device:TPU:1, one launch (start us, length us, event | category | flops | bytes accessed | tf_op | source)
XLA Modules:
  0.0 63.8 jit_solution(11282961117023300615)
XLA Ops:
  0.6 2.7 %pack_queries.1 = (bf16[2,256,512]{2,1,0:T(8,128)(2,1)}, bf16[2,256,512]{2,1,0:T(8,128)(2,1)}, bf16[2,128,512]{2,1,0:T(8,128)(2,1)}, bf16[2,128,512]{2,1,0:T(8,128)(2,1)}) custom-call(bf16[32,16,512]{2,1,0:T(8,128)(2,1)} %q_ref.1, bf16[32,16,512]{2,1,0:T(8,128)(2,1)} %g_ref.1, bf16[32,16,512]{2,1,0:T(8,128)(2,1)} %k_ref.3, bf16[32,16,512]{2,1,0:T(8,128)(2,1)} %v_ref.3), custom_call_target="tpu_custom_call" | custom-call | bytes 3145728 | tf_op jit(solution)/shard_map/pack_queries/pallas_call | solution.py:102
  3.3 9.5 %collective-permute-start.1 = (bf16[2,256,512]{2,1,0:T(8,128)(2,1)}, bf16[2,256,512]{2,1,0:T(8,128)(2,1)S(1)}, u32[]{:S(2)}, u32[]{:S(2)}) collective-permute-start(bf16[2,256,512]{2,1,0:T(8,128)(2,1)} %get-tuple-element.47.side_1.refs_1_), channel_id=1, source_target_pairs={{1,2},{2,1},{3,4},{4,3},{5,6},{6,5},{7,8},{8,7},{9,10},{10,9},{11,... | collective-permute-start | bytes 1572872 | tf_op jit(solution)/shard_map/ppermute | solution.py:549
  12.8 1.0 %collective-permute-start.2 = (bf16[2,128,512]{2,1,0:T(8,128)(2,1)}, bf16[2,128,512]{2,1,0:T(8,128)(2,1)S(1)}, u32[]{:S(2)}, u32[]{:S(2)}) collective-permute-start(bf16[2,128,512]{2,1,0:T(8,128)(2,1)} %get-tuple-element.50), channel_id=1, source_target_pairs={{0,32},{32,0},{64,96},{96,64},{1,33},{33,1},{65,97},{97,65},{2,34}... | collective-permute-start | bytes 786440 | tf_op jit(solution)/shard_map/ppermute | solution.py:541
  13.8 2.2 %collective-permute-start.3 = (bf16[2,128,512]{2,1,0:T(8,128)(2,1)}, bf16[2,128,512]{2,1,0:T(8,128)(2,1)S(1)}, u32[]{:S(2)}, u32[]{:S(2)}) collective-permute-start(bf16[2,128,512]{2,1,0:T(8,128)(2,1)} %get-tuple-element.51), channel_id=1, source_target_pairs={{32,64},{64,32},{33,65},{65,33},{34,66},{66,34},{35,67},{67,35},{3... | collective-permute-start | bytes 786440 | tf_op jit(solution)/shard_map/ppermute | solution.py:549
  15.9 0.1 collective-permute-start
  16.0 0.0 copy-start.4
  16.1 1.0 %copy-done.4 = bf16[32,16,512]{2,1,0:T(8,128)(2,1)S(1)} copy-done((bf16[32,16,512]{2,1,0:T(8,128)(2,1)S(1)}, bf16[32,16,512]{2,1,0:T(8,128)(2,1)}, u32[]{:S(2)}) %copy-start.4) | copy-done | bytes 524312
  17.1 1.0 %copy-done.5 = bf16[32,16,512]{2,1,0:T(8,128)(2,1)S(1)} copy-done((bf16[32,16,512]{2,1,0:T(8,128)(2,1)S(1)}, bf16[32,16,512]{2,1,0:T(8,128)(2,1)}, u32[]{:S(2)}) %copy-start.5) | copy-done | bytes 524312
  18.1 1.6 %pack_keys.1 = (bf16[512,512]{1,0:T(8,128)(2,1)S(1)}, bf16[512,512]{1,0:T(8,128)(2,1)S(1)}) custom-call(bf16[32,16,512]{2,1,0:T(8,128)(2,1)S(1)} %copy-done.4, bf16[32,16,512]{2,1,0:T(8,128)(2,1)S(1)} %copy-done.5), custom_call_target="tpu_custom_call" | custom-call | bytes 3145728 | tf_op jit(solution)/shard_map/pack_keys/pallas_call | solution.py:128
  19.8 1.0 %copy-done = bf16[2,256,512]{2,1,0:T(8,128)(2,1)S(1)} copy-done((bf16[2,256,512]{2,1,0:T(8,128)(2,1)S(1)}, bf16[2,256,512]{2,1,0:T(8,128)(2,1)}, u32[]{:S(2)}) %copy-start) | copy-done | bytes 524312
  20.8 1.0 %copy-done.2 = bf16[2,256,512]{2,1,0:T(8,128)(2,1)S(1)} copy-done((bf16[2,256,512]{2,1,0:T(8,128)(2,1)S(1)}, bf16[2,256,512]{2,1,0:T(8,128)(2,1)}, u32[]{:S(2)}) %copy-start.2) | copy-done | bytes 524312
  21.8 2.4 %mid_scores.1 = (f32[4,8,128]{2,1,0:T(8,128)S(1)}, f32[4,2,384,256]{3,2,1,0:T(8,128)S(1)}, f32[4,2,384,256]{3,2,1,0:T(8,128)S(1)}, bf16[512,512]{1,0:T(8,128)(2,1)S(1)}) custom-call(bf16[2,256,512]{2,1,0:T(8,128)(2,1)S(1)} %copy-done, bf16[2,256,512]{2,1,0:T(8,128)(2,1)S(1)} %copy-done.2, bf16[512,512]{1,0:T(8,128)(2,1)S(1)} %get-tuple-element.48.kd, ...), custom_call_target="tpu_custom_call" | custom-call | flops 2000000000 | bytes 1024 | tf_op jit(solution)/shard_map/mid_scores/pallas_call | solution.py:288
  24.2 2.6 %collective-permute-done.3.edge_b = bf16[2,128,512]{2,1,0:T(8,128)(2,1)S(1)} collective-permute-done((bf16[2,128,512]{2,1,0:T(8,128)(2,1)}, bf16[2,128,512]{2,1,0:T(8,128)(2,1)S(1)}, u32[]{:S(2)}, u32[]{:S(2)}) %collective-permute-start.3) | collective-permute-done | bytes 262176 | tf_op jit(solution)/shard_map/ppermute | solution.py:549
  26.8 2.4 %edge_scores.1 = (f32[4,8,128]{2,1,0:T(8,128)S(1)}, f32[4,2,384,256]{3,2,1,0:T(8,128)S(1)}, f32[4,2,384,256]{3,2,1,0:T(8,128)S(1)}) custom-call(bf16[2,256,512]{2,1,0:T(8,128)(2,1)S(1)} %copy-done, bf16[2,256,512]{2,1,0:T(8,128)(2,1)S(1)} %copy-done.2, bf16[512,512]{1,0:T(8,128)(2,1)S(1)} %get-tuple-element.48.kd, ...), custom_call_target="tpu_custom_call" | custom-call | flops 2000000000 | bytes 1024 | tf_op jit(solution)/shard_map/edge_scores/pallas_call | solution.py:301
  29.3 1.4 %halo_scores_b.1 = (f32[4,16,128]{2,1,0:T(8,128)S(1)}, f32[2,2,192,256]{3,2,1,0:T(8,128)S(1)}, f32[2,2,192,256]{3,2,1,0:T(8,128)S(1)}, f32[2,2,192,256]{3,2,1,0:T(8,128)S(1)}, f32[2,2,192,256]{3,2,1,0:T(8,128)S(1)}) custom-call(bf16[2,256,512]{2,1,0:T(8,128)(2,1)S(1)} %collective-permute-done.1.q_in.refs_3_, bf16[512,512]{1,0:T(8,128)(2,1)S(1)} %get-tuple-element.48.kd, ...), custom_call_target="tpu_custom_call" | custom-call | flops 2000000000 | bytes 1024 | tf_op jit(solution)/shard_map/halo_scores_b/pallas_call | solution.py:354
  30.7 7.1 %collective-permute-start.5 = (f32[4,16,128]{2,1,0:T(8,128)S(1)}, f32[4,16,128]{2,1,0:T(8,128)S(1)}, u32[]{:S(2)}, u32[]{:S(2)}) collective-permute-start(f32[4,16,128]{2,1,0:T(8,128)S(1)} %get-tuple-element.55.send.refs_5_), channel_id=1, source_target_pairs={{1,2},{2,1},{3,4},{4,3},{5,6},{6,5},{7,8},{8,7},{9,10},{10,9},{11,... | collective-permute-start | bytes 98312 | tf_op jit(solution)/shard_map/ppermute | solution.py:549
  37.8 1.4 %halo_scores_a.1 = (f32[4,16,128]{2,1,0:T(8,128)S(1)}, f32[2,2,192,256]{3,2,1,0:T(8,128)S(1)}, f32[2,2,192,256]{3,2,1,0:T(8,128)S(1)}, f32[2,2,192,256]{3,2,1,0:T(8,128)S(1)}, f32[2,2,192,256]{3,2,1,0:T(8,128)S(1)}) custom-call(bf16[2,256,512]{2,1,0:T(8,128)(2,1)S(1)} %collective-permute-done.q_in.refs_2_, bf16[512,512]{1,0:T(8,128)(2,1)S(1)} %get-tuple-element.48.kd, ...), custom_call_target="tpu_custom_call" | custom-call | flops 2000000000 | bytes 1024 | tf_op jit(solution)/shard_map/halo_scores_a/pallas_call | solution.py:354
  39.2 0.1 collective-permute-start.4
  39.3 0.5 turn_edges.1.edges_turned.refs_15_
  39.8 0.0 copy-start.1
  39.8 1.1 %halo_queries_b.1 = (bf16[256,512]{1,0:T(8,128)(2,1)S(1)}, bf16[2,2,192,256]{3,2,1,0:T(8,128)(2,1)S(1)}, bf16[2,2,192,256]{3,2,1,0:T(8,128)(2,1)S(1)}, bf16[2,2,...) custom-call(f32[4,16,128]{2,1,0:T(8,128)S(1)} %get-tuple-element.55.send.refs_5_, ...), custom_call_target="tpu_custom_call" | custom-call | bytes 1024 | tf_op jit(solution)/shard_map/halo_queries_b/pallas_call | solution.py:391
  40.9 7.1 %collective-permute-start.7 = (bf16[256,512]{1,0:T(8,128)(2,1)S(1)}, bf16[256,512]{1,0:T(8,128)(2,1)S(1)}, u32[]{:S(2)}, u32[]{:S(2)}) collective-permute-start(bf16[256,512]{1,0:T(8,128)(2,1)S(1)} %get-tuple-element.71.refs_16_), channel_id=1, source_target_pairs={{1,2},{2,1},{3,4},{4,3},{5,6},{6,5},{7,8},{8,7},{9,10},{10,9},{11,... | collective-permute-start | bytes 786440 | tf_op jit(solution)/shard_map/ppermute | solution.py:549
  48.0 1.1 %halo_queries_a.1 = (bf16[256,512]{1,0:T(8,128)(2,1)S(1)}, bf16[2,2,192,256]{3,2,1,0:T(8,128)(2,1)S(1)}, bf16[2,2,192,256]{3,2,1,0:T(8,128)(2,1)S(1)}, bf16[2,2,...) custom-call(f32[4,16,128]{2,1,0:T(8,128)S(1)} %get-tuple-element.54.send.refs_4_, ...), custom_call_target="tpu_custom_call" | custom-call | bytes 1024 | tf_op jit(solution)/shard_map/halo_queries_a/pallas_call | solution.py:391
  49.2 2.4 %edge_gradients.1 = (f32[2,128,512]{2,1,0:T(8,128)S(1)}, f32[512,512]{1,0:T(8,128)S(1)}, f32[512,512]{1,0:T(8,128)S(1)}, bf16[2,128,512]{2,1,0:T(8,128)(2,1)S(1)}, bf16[2,128,512]{2,1,0:T(8,128)(2,1)S(1)}) custom-call(bf16[2,256,512]{2,1,0:T(8,128)(2,1)S(1)} %copy-done.1, bf16[2,256,512]{2,1,0:T(8,128)(2,1)S(1)} %copy-done.3, ...), custom_call_target="tpu_custom_call" | custom-call | flops 3000000000 | bytes 1024 | tf_op jit(solution)/shard_map/edge_gradients/pallas_call | solution.py:465
  51.6 0.1 collective-permute-start.8
  51.7 3.2 %collective-permute-start.9 = (bf16[2,128,512]{2,1,0:T(8,128)(2,1)S(1)}, bf16[2,128,512]{2,1,0:T(8,128)(2,1)S(1)}, u32[]{:S(2)}, u32[]{:S(2)}) collective-permute-start(bf16[2,128,512]{2,1,0:T(8,128)(2,1)S(1)} %get-tuple-element.86), channel_id=1, source_target_pairs={{32,64},{64,32},{33,65},{65,33},{34,66},{66,34},{35,67},{67,35},{3... | collective-permute-start | bytes 786440 | tf_op jit(solution)/shard_map/ppermute | solution.py:549
  54.9 0.1 collective-permute-start.6
  55.0 2.5 %mid_gradients.1 = (f32[2,128,512]{2,1,0:T(8,128)S(1)}, f32[512,512]{1,0:T(8,128)S(1)}, f32[512,512]{1,0:T(8,128)S(1)}) custom-call(bf16[2,256,512]{2,1,0:T(8,128)(2,1)S(1)} %copy-done.1, bf16[2,256,512]{2,1,0:T(8,128)(2,1)S(1)} %copy-done.3, bf16[2,256,512]{2,1,0:T(8,128)(2,1)S(1)} %collective-permute-done.q_in.refs_2_, ...), custom_call_target="tpu_custom_call" | custom-call | flops 3000000000 | bytes 1024 | tf_op jit(solution)/shard_map/mid_gradients/pallas_call | solution.py:478
  57.5 3.2 %collective-permute-done.9.from_b = bf16[2,128,512]{2,1,0:T(8,128)(2,1)S(1)} collective-permute-done((bf16[2,128,512]{2,1,0:T(8,128)(2,1)S(1)}, bf16[2,128,512]{2,1,0:T(8,128)(2,1)S(1)}, u32[]{:S(2)}, u32[]{:S(2)}) %collective-permute-start.9) | collective-permute-done | bytes 262176 | tf_op jit(solution)/shard_map/ppermute | solution.py:549
  60.7 1.0 %finish_keys.1 = (bf16[32,16,512]{2,1,0:T(8,128)(2,1)}, bf16[32,16,512]{2,1,0:T(8,128)(2,1)}) custom-call(f32[512,512]{1,0:T(8,128)S(1)} %get-tuple-element.83.dk, f32[512,512]{1,0:T(8,128)S(1)} %get-tuple-element.84.dv, bf16[2,128,512]{2,1,0:T(8,128)(2,1)S(1)} %collective-permute-done.8.from_a, bf16[2,128,512]{2,1,0:T(8,128)(2,1)S(1)} %collective-permute-done.9.from_b), custom_call_target="tpu_custom_call" | custom-call | bytes 1024 | tf_op jit(solution)/shard_map/finish_keys/pallas_call | solution.py:529
  61.7 1.2 %collective-permute-done.6.dq_0 = bf16[256,512]{1,0:T(8,128)(2,1)S(1)} collective-permute-done((bf16[256,512]{1,0:T(8,128)(2,1)S(1)}, bf16[256,512]{1,0:T(8,128)(2,1)S(1)}, u32[]{:S(2)}, u32[]{:S(2)}) %collective-permute-start.6) | collective-permute-done | bytes 262176 | tf_op jit(solution)/shard_map/ppermute | solution.py:541
  62.9 0.9 %finish_queries.1 = bf16[32,16,512]{2,1,0:T(8,128)(2,1)} custom-call(f32[2,128,512]{2,1,0:T(8,128)S(1)} %get-tuple-element.72.dq_edge, f32[2,128,512]{2,1,0:T(8,128)S(1)} %get-tuple-element.81.dq_mid, bf16[256,512]{1,0:T(8,128)(2,1)S(1)} %collective-permute-done.6.dq_0, bf16[256,512]{1,0:T(8,128)(2,1)S(1)} %collective-permute-done.7.dq_1), custom_call_target="tpu_custom_call" | custom-call | bytes 1024 | tf_op jit(solution)/shard_map/finish_queries/pallas_call | solution.py:529
  (13 shorter events, 0.0 us)
Async XLA Ops:
  3.3 26.0 %collective-permute-start.1 = (bf16[2,256,512]{2,1,0:T(8,128)(2,1)}, bf16[2,256,512]{2,1,0:T(8,128)(2,1)S(1)}, u32[]{:S(2)}, u32[]{:S(2)}) collective-permute-start(bf16[2,256,512]{2,1,0:T(8,128)(2,1)} %get-tuple-element.47.side_1.refs_1_), channel_id=1, source_target_pairs={{1,2},{2,1},{3,4},{4,3},{5,6},{6,5},{7,8},{8,7},{9,10},{10,9},{11,... | collective-permute-start | bytes 1572872 | tf_op jit(solution)/shard_map/ppermute | solution.py:549
  12.8 11.4 %collective-permute-start.2 = (bf16[2,128,512]{2,1,0:T(8,128)(2,1)}, bf16[2,128,512]{2,1,0:T(8,128)(2,1)S(1)}, u32[]{:S(2)}, u32[]{:S(2)}) collective-permute-start(bf16[2,128,512]{2,1,0:T(8,128)(2,1)} %get-tuple-element.50), channel_id=1, source_target_pairs={{0,32},{32,0},{64,96},{96,64},{1,33},{33,1},{65,97},{97,65},{2,34}... | collective-permute-start | bytes 786440 | tf_op jit(solution)/shard_map/ppermute | solution.py:541
  13.8 13.1 %collective-permute-start.3 = (bf16[2,128,512]{2,1,0:T(8,128)(2,1)}, bf16[2,128,512]{2,1,0:T(8,128)(2,1)S(1)}, u32[]{:S(2)}, u32[]{:S(2)}) collective-permute-start(bf16[2,128,512]{2,1,0:T(8,128)(2,1)} %get-tuple-element.51), channel_id=1, source_target_pairs={{32,64},{64,32},{33,65},{65,33},{34,66},{66,34},{35,67},{67,35},{3... | collective-permute-start | bytes 786440 | tf_op jit(solution)/shard_map/ppermute | solution.py:549
  15.9 21.9 %collective-permute-start = (bf16[2,256,512]{2,1,0:T(8,128)(2,1)}, bf16[2,256,512]{2,1,0:T(8,128)(2,1)S(1)}, u32[]{:S(2)}, u32[]{:S(2)}) collective-permute-start(bf16[2,256,512]{2,1,0:T(8,128)(2,1)} %get-tuple-element.46.side_0.refs_0_), channel_id=1, source_target_pairs={{0,1},{1,0},{2,3},{3,2},{4,5},{5,4},{6,7},{7,6},{8,9},{9,8},{10,11... | collective-permute-start | bytes 1572872 | tf_op jit(solution)/shard_map/ppermute | solution.py:541
  16.0 1.0 %copy-start.4 = (bf16[32,16,512]{2,1,0:T(8,128)(2,1)S(1)}, bf16[32,16,512]{2,1,0:T(8,128)(2,1)}, u32[]{:S(2)}) copy-start(bf16[32,16,512]{2,1,0:T(8,128)(2,1)} %k_ref.3) | copy-start | bytes 1572868
  17.1 1.0 %copy-start.5 = (bf16[32,16,512]{2,1,0:T(8,128)(2,1)S(1)}, bf16[32,16,512]{2,1,0:T(8,128)(2,1)}, u32[]{:S(2)}) copy-start(bf16[32,16,512]{2,1,0:T(8,128)(2,1)} %v_ref.3) | copy-start | bytes 1572868
  19.8 1.0 %copy-start = (bf16[2,256,512]{2,1,0:T(8,128)(2,1)S(1)}, bf16[2,256,512]{2,1,0:T(8,128)(2,1)}, u32[]{:S(2)}) copy-start(bf16[2,256,512]{2,1,0:T(8,128)(2,1)} %get-tuple-element.46.side_0.refs_0_) | copy-start | bytes 1572868
  20.8 1.0 %copy-start.2 = (bf16[2,256,512]{2,1,0:T(8,128)(2,1)S(1)}, bf16[2,256,512]{2,1,0:T(8,128)(2,1)}, u32[]{:S(2)}) copy-start(bf16[2,256,512]{2,1,0:T(8,128)(2,1)} %get-tuple-element.47.side_1.refs_1_) | copy-start | bytes 1572868
  30.7 9.1 %collective-permute-start.5 = (f32[4,16,128]{2,1,0:T(8,128)S(1)}, f32[4,16,128]{2,1,0:T(8,128)S(1)}, u32[]{:S(2)}, u32[]{:S(2)}) collective-permute-start(f32[4,16,128]{2,1,0:T(8,128)S(1)} %get-tuple-element.55.send.refs_5_), channel_id=1, source_target_pairs={{1,2},{2,1},{3,4},{4,3},{5,6},{6,5},{7,8},{8,7},{9,10},{10,9},{11,... | collective-permute-start | bytes 98312 | tf_op jit(solution)/shard_map/ppermute | solution.py:549
  39.2 8.9 %collective-permute-start.4 = (f32[4,16,128]{2,1,0:T(8,128)S(1)}, f32[4,16,128]{2,1,0:T(8,128)S(1)}, u32[]{:S(2)}, u32[]{:S(2)}) collective-permute-start(f32[4,16,128]{2,1,0:T(8,128)S(1)} %get-tuple-element.54.send.refs_4_), channel_id=1, source_target_pairs={{0,1},{1,0},{2,3},{3,2},{4,5},{5,4},{6,7},{7,6},{8,9},{9,8},{10,11... | collective-permute-start | bytes 98312 | tf_op jit(solution)/shard_map/ppermute | solution.py:541
  39.8 9.4 %copy-start.1 = (bf16[2,256,512]{2,1,0:T(8,128)(2,1)S(1)}, bf16[2,256,512]{2,1,0:T(8,128)(2,1)}, u32[]{:S(2)}) copy-start(bf16[2,256,512]{2,1,0:T(8,128)(2,1)} %get-tuple-element.46.side_0.refs_0_) | copy-start | bytes 1572868
  39.8 9.4 %copy-start.3 = (bf16[2,256,512]{2,1,0:T(8,128)(2,1)S(1)}, bf16[2,256,512]{2,1,0:T(8,128)(2,1)}, u32[]{:S(2)}) copy-start(bf16[2,256,512]{2,1,0:T(8,128)(2,1)} %get-tuple-element.47.side_1.refs_1_) | copy-start | bytes 1572868
  40.9 20.8 %collective-permute-start.7 = (bf16[256,512]{1,0:T(8,128)(2,1)S(1)}, bf16[256,512]{1,0:T(8,128)(2,1)S(1)}, u32[]{:S(2)}, u32[]{:S(2)}) collective-permute-start(bf16[256,512]{1,0:T(8,128)(2,1)S(1)} %get-tuple-element.71.refs_16_), channel_id=1, source_target_pairs={{1,2},{2,1},{3,4},{4,3},{5,6},{6,5},{7,8},{8,7},{9,10},{10,9},{11,... | collective-permute-start | bytes 786440 | tf_op jit(solution)/shard_map/ppermute | solution.py:549
  51.6 5.9 %collective-permute-start.8 = (bf16[2,128,512]{2,1,0:T(8,128)(2,1)S(1)}, bf16[2,128,512]{2,1,0:T(8,128)(2,1)S(1)}, u32[]{:S(2)}, u32[]{:S(2)}) collective-permute-start(bf16[2,128,512]{2,1,0:T(8,128)(2,1)S(1)} %get-tuple-element.85), channel_id=1, source_target_pairs={{0,32},{32,0},{64,96},{96,64},{1,33},{33,1},{65,97},{97,65},{2,34}... | collective-permute-start | bytes 786440 | tf_op jit(solution)/shard_map/ppermute | solution.py:541
  51.7 9.0 %collective-permute-start.9 = (bf16[2,128,512]{2,1,0:T(8,128)(2,1)S(1)}, bf16[2,128,512]{2,1,0:T(8,128)(2,1)S(1)}, u32[]{:S(2)}, u32[]{:S(2)}) collective-permute-start(bf16[2,128,512]{2,1,0:T(8,128)(2,1)S(1)} %get-tuple-element.86), channel_id=1, source_target_pairs={{32,64},{64,32},{33,65},{65,33},{34,66},{66,34},{35,67},{67,35},{3... | collective-permute-start | bytes 786440 | tf_op jit(solution)/shard_map/ppermute | solution.py:549
  54.9 8.1 %collective-permute-start.6 = (bf16[256,512]{1,0:T(8,128)(2,1)S(1)}, bf16[256,512]{1,0:T(8,128)(2,1)S(1)}, u32[]{:S(2)}, u32[]{:S(2)}) collective-permute-start(bf16[256,512]{1,0:T(8,128)(2,1)S(1)} %get-tuple-element.82), channel_id=1, source_target_pairs={{0,1},{1,0},{2,3},{3,2},{4,5},{5,4},{6,7},{7,6},{8,9},{9,8},{10,11... | collective-permute-start | bytes 786440 | tf_op jit(solution)/shard_map/ppermute | solution.py:541

commit v12 on v10

--- a/solution.py
+++ b/solution.py
@@ -400,7 +400,7 @@
     )(*operands)
 
 
-def row_gradients(rows, side_0, side_1, q_0, q_1, send_0, send_1, recv_0, recv_1, s_own, d_own, p_0, ds_0, p_1, ds_1,
+def row_gradients(places, side_0, side_1, q_0, q_1, send_0, send_1, recv_0, recv_1, s_own, d_own, p_0, ds_0, p_1, ds_1,
                   own_turned, edges_turned, dq_ref):
     masks, wide_masks = head_masks(PAIR), head_masks(WIDE)
     lane = lax.broadcasted_iota(jnp.int32, (1, PAIR), 1)
@@ -409,7 +409,7 @@
         both = [both_parts(send_0, recv_0, j, 0), both_parts(send_1, recv_1, j, 0)]
         merged_rows.append([jnp.concatenate([one[w] for one in both], axis=1) for w in range(2)])
     results = []
-    for place, t in enumerate(rows):
+    for index, (place, t) in enumerate(places):
         at, row = at_tokens(place), slice(place, place + 1)
         sums = [[], []]
         for j in range(2):
@@ -420,7 +420,7 @@
             probs = jnp.exp2(s_own[j, place] - log_total[row])
             dscores = (probs * (d_own[j, place] - delta[row])).astype(BF16)
             for c, part in enumerate(query_parts(turned_window(own_turned, edges_turned, t, j), dscores, lane)):
-                dq_ref[c, at, lanes] = part
+                dq_ref[c, at_tokens(index), lanes] = part
             sums[0].append(matmul(dscores, queries, (1, 0)))
             sums[1].append(matmul(probs.astype(BF16), grads, (1, 0)))
         sums = [jnp.concatenate(parts, axis=1) for parts in sums]
@@ -433,24 +433,24 @@
     return results
 
 
-def edge_kernel(*refs):
-    operands, (_, _, dq_ref, dk_ref, dv_ref, out_a, out_b) = refs[:16], refs[16:]
-    upper, lower = row_gradients(EDGE_ROWS, *operands, dq_ref)
-    for which, (out, scale) in enumerate(((dk_ref, SCALE), (dv_ref, 1.0))):
-        top, bottom = upper[which] * scale, lower[which] * scale
-        out_a[which] = top[:PAIR].astype(BF16)
-        out[0:2 * PAIR] = top[PAIR:]
-        out_b[which] = bottom[2 * PAIR:].astype(BF16)
-        out[2 * PAIR:] = bottom[:2 * PAIR]
+def edge_kernel(place, *refs):
+    operands, (_, _, dq_ref, dk_ref, dv_ref, out) = refs[:16], refs[16:]
+    parts, = row_gradients(((place, EDGE_ROWS[place]),), *operands, dq_ref)
+    for which, (sums, scale) in enumerate(((dk_ref, SCALE), (dv_ref, 1.0))):
+        part = parts[which] * scale
+        out[which] = (part[2 * PAIR:] if place else part[:PAIR]).astype(BF16)
+        sums[...] = part[:2 * PAIR] if place else part[PAIR:]
 
 
 def mid_kernel(*refs):
-    operands, (dk_in, dv_in, dq_ref, dk_ref, dv_ref) = refs[:15], refs[15:]
-    upper, lower = row_gradients(MID_ROWS, *operands, None, dq_ref)
-    for which, (sums, out, scale) in enumerate(((dk_in, dk_ref, SCALE), (dv_in, dv_ref, 1.0))):
-        out[0:PAIR] = sums[0:PAIR] + upper[which][:PAIR] * scale
-        out[PAIR:3 * PAIR] = sums[PAIR:3 * PAIR] + (upper[which][PAIR:] + lower[which][:2 * PAIR]) * scale
-        out[3 * PAIR:] = sums[3 * PAIR:] + lower[which][2 * PAIR:] * scale
+    operands, (dk_a, dv_a, dk_b, dv_b, dq_ref, dk_ref, dv_ref) = refs[:15], refs[15:]
+    upper, lower = row_gradients(tuple(enumerate(MID_ROWS)), *operands, None, dq_ref)
+    for which, (top, bottom, out, scale) in enumerate(((dk_a, dk_b, dk_ref, SCALE), (dv_a, dv_b, dv_ref, 1.0))):
+        both = upper[which][PAIR:] + lower[which][:2 * PAIR]
+        out[0:PAIR] = top[:PAIR] + upper[which][:PAIR] * scale
+        out[PAIR:2 * PAIR] = top[PAIR:] + both[:PAIR] * scale
+        out[2 * PAIR:3 * PAIR] = bottom[:PAIR] + both[PAIR:] * scale
+        out[3 * PAIR:] = bottom[PAIR:] + lower[which][2 * PAIR:] * scale
 
 
 def row_specs(group):
@@ -461,24 +461,26 @@
 GRAD_SHAPES = [struct((2, CHUNK, FEAT), F32)] + [struct((ROWS * PAIR, FEAT), F32)] * 2
 
 
-def edge_gradients(*operands):
-    return pl.pallas_call(
-        edge_kernel,
+def edge_gradients(place, *operands):
+    half = pl.BlockSpec((2 * PAIR, WIDE), lambda g: (0, g))
+    return pl.pallas_call(
+        functools.partial(edge_kernel, place),
         grid=(GROUPS,),
         in_specs=row_specs(EDGE) + [edge_turned_wide, any_spec, any_spec],
-        out_specs=GRAD_SPECS + [edge_wide] * 2,
-        out_shape=GRAD_SHAPES + [struct((2, PAIR, FEAT), BF16)] * 2,
-        compiler_params=params(),
-        cost_estimate=cost(3e9, 1 << 10),
-        name="edge_gradients",
+        out_specs=[pl.BlockSpec((2, CELLS, WIDE), lambda g: (0, 0, g))] + [half] * 2 + [edge_wide],
+        out_shape=[struct((2, CELLS, FEAT), F32)] + [struct((2 * PAIR, FEAT), F32)] * 2 + [struct((2, PAIR, FEAT), BF16)],
+        compiler_params=params(),
+        cost_estimate=cost(2e9, 1 << 10),
+        name="edge_gradients_" + "ab"[place],
     )(*operands)
 
 
 def mid_gradients(*operands):
+    half = pl.BlockSpec((2 * PAIR, WIDE), lambda g: (0, g))
     return pl.pallas_call(
         mid_kernel,
         grid=(GROUPS,),
-        in_specs=row_specs(MID) + [keys_wide] * 2,
+        in_specs=row_specs(MID) + [half] * 4,
         out_specs=GRAD_SPECS,
         out_shape=GRAD_SHAPES,
         compiler_params=params(),
@@ -503,15 +505,15 @@
     return copies, send
 
 
-def inner_kernel(dq_edge, dq_mid, dk, dv, dq_0, dq_1, q_ref, k_ref, v_ref, buffers, sems):
+def inner_kernel(dq_a, dq_b, dq_mid, dk, dv, dq_0, dq_1, q_ref, k_ref, v_ref, buffers, sems):
     copies, send = sender((q_ref, k_ref, v_ref), buffers, sems)
     for t in MID_ROWS:
         for which, own in enumerate((dk, dv)):
             full = own[t * PAIR:(t + 1) * PAIR]
             send(1 + which, t, join_columns(full[:CELLS], full[CELLS:]))
     for place, t in enumerate(ORDER):
-        dq = (dq_edge, dq_mid)[place // 2]
-        at, there = at_tokens(place % 2), at_tokens(place)
+        dq = (dq_a, dq_b, dq_mid, dq_mid)[place]
+        at, there = at_tokens(max(place - 2, 0)), at_tokens(place)
         send(0, t, join_columns(dq[0, at] + dq_0[there].astype(F32), dq[1, at] + dq_1[there].astype(F32)))
     for copy in copies:
         copy.wait()
@@ -527,7 +529,7 @@
         copy.wait()
 
 
-def finish(dq_edge, dq_mid, dk, dv, dq_0, dq_1, from_a, from_b):
+def finish(dq_a, dq_b, dq_mid, dk, dv, dq_0, dq_1, from_a, from_b):
     out = struct((8 * ROWS, 16, FEAT), BF16)
     q_out, k_inner, v_inner = pl.pallas_call(
         inner_kernel,
@@ -537,7 +539,7 @@
         compiler_params=params(),
         cost_estimate=cost(0, 1 << 10),
         name="finish_inner",
-    )(dq_edge, dq_mid, dk, dv, dq_0, dq_1)
+    )(dq_a, dq_b, dq_mid, dk, dv, dq_0, dq_1)
     whole = pl.BlockSpec(memory_space=pltpu.VMEM)
     k_out, v_out = pl.pallas_call(
         outer_kernel,
@@ -589,11 +591,13 @@
         dq_parts.append(swap_lon(c, grad))
         weights.append(weight)
     shared = (*sides, *halos, *sends, *recvs)
-    dq_edge, dk, dv, out_a, out_b = edge_gradients(*shared, *edge_own, *weights[0][:2], *weights[1][:2], turned, edges_turned,
-                                                   *halo_dq)
-    key_parts = (swap_a(out_a, "lat"), swap_b(out_b, "lat", False))
-    dq_mid, dk, dv = mid_gradients(*shared, *mid_own, *weights[0][2:], *weights[1][2:], turned, dk, dv)
-    return tuple(finish(dq_edge, dq_mid, dk, dv, *dq_parts, *key_parts))
+    edge_operands = (*shared, *edge_own, *weights[0][:2], *weights[1][:2], turned, edges_turned)
+    dq_b, dk_b, dv_b, out_b = edge_gradients(1, *edge_operands, *halo_dq)
+    from_b = swap_b(out_b, "lat", False)
+    dq_a, dk_a, dv_a, out_a = edge_gradients(0, *edge_operands, out_b, halo_dq[1])
+    from_a = swap_a(out_a, "lat")
+    dq_mid, dk, dv = mid_gradients(*shared, *mid_own, *weights[0][2:], *weights[1][2:], turned, dk_a, dv_a, dk_b, dv_b)
+    return tuple(finish(dq_a, dq_b, dq_mid, dk, dv, *dq_parts, from_a, from_b))
 
 
 def solution(mesh):

time: 61.5 us -> 61.5 us (level)
  the two profiles are of different devices: /device:TPU:1 before, /device:TPU:14 now
where the time goes in v12:
time: 61.5 us; the launch traced here: 61.2 us
  Pallas kernels  22 us (36%)
  waiting for transfers between devices  17.5 us (28%)
  starting transfers between devices  16.6 us (27%)
  local copies, waits for them, and re-layouts  4.17 us (7%)
  between operations  0.85 us (1%)
    ppermute x5, waiting for transfers between devices, swap_b(): return lax.ppermute(x, axis, pairs)  13.5 us
    ppermute x5, starting transfers between devices, swap_a(): lax.ppermute(x, axis, [(i, i ^ 1) for i in range(lax.axis_size(axis))])  8.53 us
    ppermute x5, starting transfers between devices, swap_b(): return lax.ppermute(x, axis, pairs)  8.09 us
    unnamed x12, local copies, waits for them, and re-layouts  4.17 us
    ppermute x5, waiting for transfers between devices, swap_a(): lax.ppermute(x, axis, [(i, i ^ 1) for i in range(lax.axis_size(axis))])  3.99 us
    pallas_call x2, Pallas kernels, edge_gradients(): pl.pallas_call(functools.partial(edge_kernel, place), grid=(GROUPS,), in_...  3.01 us
    pallas_call x2, Pallas kernels, halo_scores(): pl.pallas_call(functools.partial(halo_scores_kernel, c), grid=(GROUPS,),...  2.75 us
    pallas_call x1, Pallas kernels, pack_queries(): pl.pallas_call(pack_queries_kernel, in_specs=[any_spec] * 4, out_specs=[a...  2.67 us
  transfers between devices with their start and end apart: 10, of which 4 were waited for; matrix products, arithmetic and copies ran while one was open for 0% of the time, Pallas kernels for 30%

profile of v12, /device:TPU:14, one launch (start us, length us, event | category | flops | bytes accessed | tf_op | source)
XLA Modules:
  0.0 61.2 jit_solution(15285161142013101395)
XLA Ops:
  0.6 2.7 %pack_queries.1 = (bf16[2,256,512]{2,1,0:T(8,128)(2,1)}, bf16[2,256,512]{2,1,0:T(8,128)(2,1)}, bf16[2,128,512]{2,1,0:T(8,128)(2,1)}, bf16[2,128,512]{2,1,0:T(8,128)(2,1)}) custom-call(bf16[32,16,512]{2,1,0:T(8,128)(2,1)} %q_ref.1, bf16[32,16,512]{2,1,0:T(8,128)(2,1)} %g_ref.1, bf16[32,16,512]{2,1,0:T(8,128)(2,1)} %k_ref.3, bf16[32,16,512]{2,1,0:T(8,128)(2,1)} %v_ref.3), custom_call_target="tpu_custom_call" | custom-call | bytes 3145728 | tf_op jit(solution)/shard_map/pack_queries/pallas_call | solution.py:102
  3.3 2.6 %collective-permute-start.1 = (bf16[2,256,512]{2,1,0:T(8,128)(2,1)}, bf16[2,256,512]{2,1,0:T(8,128)(2,1)S(1)}, u32[]{:S(2)}, u32[]{:S(2)}) collective-permute-start(bf16[2,256,512]{2,1,0:T(8,128)(2,1)} %get-tuple-element.53.side_1.refs_1_), channel_id=1, source_target_pairs={{1,2},{2,1},{3,4},{4,3},{5,6},{6,5},{7,8},{8,7},{9,10},{10,9},{11,... | collective-permute-start | bytes 1572872 | tf_op jit(solution)/shard_map/ppermute | solution.py:567
  6.0 3.4 %collective-permute-start.3 = (bf16[2,128,512]{2,1,0:T(8,128)(2,1)}, bf16[2,128,512]{2,1,0:T(8,128)(2,1)S(1)}, u32[]{:S(2)}, u32[]{:S(2)}) collective-permute-start(bf16[2,128,512]{2,1,0:T(8,128)(2,1)} %get-tuple-element.57), channel_id=1, source_target_pairs={{32,64},{64,32},{33,65},{65,33},{34,66},{66,34},{35,67},{67,35},{3... | collective-permute-start | bytes 786440 | tf_op jit(solution)/shard_map/ppermute | solution.py:567
  9.3 0.9 %collective-permute-start = (bf16[2,256,512]{2,1,0:T(8,128)(2,1)}, bf16[2,256,512]{2,1,0:T(8,128)(2,1)S(1)}, u32[]{:S(2)}, u32[]{:S(2)}) collective-permute-start(bf16[2,256,512]{2,1,0:T(8,128)(2,1)} %get-tuple-element.52.side_0.refs_0_), channel_id=1, source_target_pairs={{0,1},{1,0},{2,3},{3,2},{4,5},{5,4},{6,7},{7,6},{8,9},{9,8},{10,11... | collective-permute-start | bytes 1572872 | tf_op jit(solution)/shard_map/ppermute | solution.py:559
  10.2 1.0 %copy-done.4 = bf16[32,16,512]{2,1,0:T(8,128)(2,1)S(1)} copy-done((bf16[32,16,512]{2,1,0:T(8,128)(2,1)S(1)}, bf16[32,16,512]{2,1,0:T(8,128)(2,1)}, u32[]{:S(2)}) %copy-start.4) | copy-done | bytes 524312
  11.2 1.0 %copy-done.5 = bf16[32,16,512]{2,1,0:T(8,128)(2,1)S(1)} copy-done((bf16[32,16,512]{2,1,0:T(8,128)(2,1)S(1)}, bf16[32,16,512]{2,1,0:T(8,128)(2,1)}, u32[]{:S(2)}) %copy-start.5) | copy-done | bytes 524312
  12.3 1.6 %pack_keys.1 = (bf16[512,512]{1,0:T(8,128)(2,1)S(1)}, bf16[512,512]{1,0:T(8,128)(2,1)S(1)}) custom-call(bf16[32,16,512]{2,1,0:T(8,128)(2,1)S(1)} %copy-done.4, bf16[32,16,512]{2,1,0:T(8,128)(2,1)S(1)} %copy-done.5), custom_call_target="tpu_custom_call" | custom-call | bytes 3145728 | tf_op jit(solution)/shard_map/pack_keys/pallas_call | solution.py:128
  13.9 0.0 copy-start
  13.9 1.0 %copy-done = bf16[2,256,512]{2,1,0:T(8,128)(2,1)S(1)} copy-done((bf16[2,256,512]{2,1,0:T(8,128)(2,1)S(1)}, bf16[2,256,512]{2,1,0:T(8,128)(2,1)}, u32[]{:S(2)}) %copy-start) | copy-done | bytes 524312
  14.9 1.0 %copy-done.2 = bf16[2,256,512]{2,1,0:T(8,128)(2,1)S(1)} copy-done((bf16[2,256,512]{2,1,0:T(8,128)(2,1)S(1)}, bf16[2,256,512]{2,1,0:T(8,128)(2,1)}, u32[]{:S(2)}) %copy-start.2) | copy-done | bytes 524312
  16.0 2.4 %mid_scores.1 = (f32[4,8,128]{2,1,0:T(8,128)S(1)}, f32[4,2,384,256]{3,2,1,0:T(8,128)S(1)}, f32[4,2,384,256]{3,2,1,0:T(8,128)S(1)}, bf16[512,512]{1,0:T(8,128)(2,1)S(1)}) custom-call(bf16[2,256,512]{2,1,0:T(8,128)(2,1)S(1)} %copy-done, bf16[2,256,512]{2,1,0:T(8,128)(2,1)S(1)} %copy-done.2, bf16[512,512]{1,0:T(8,128)(2,1)S(1)} %get-tuple-element.54.kd, ...), custom_call_target="tpu_custom_call" | custom-call | flops 2000000000 | bytes 1024 | tf_op jit(solution)/shard_map/mid_scores/pallas_call | solution.py:288
  18.4 9.4 %collective-permute-done.3.edge_b = bf16[2,128,512]{2,1,0:T(8,128)(2,1)S(1)} collective-permute-done((bf16[2,128,512]{2,1,0:T(8,128)(2,1)}, bf16[2,128,512]{2,1,0:T(8,128)(2,1)S(1)}, u32[]{:S(2)}, u32[]{:S(2)}) %collective-permute-start.3) | collective-permute-done | bytes 262176 | tf_op jit(solution)/shard_map/ppermute | solution.py:567
  27.8 2.4 %edge_scores.1 = (f32[4,8,128]{2,1,0:T(8,128)S(1)}, f32[4,2,384,256]{3,2,1,0:T(8,128)S(1)}, f32[4,2,384,256]{3,2,1,0:T(8,128)S(1)}) custom-call(bf16[2,256,512]{2,1,0:T(8,128)(2,1)S(1)} %copy-done, bf16[2,256,512]{2,1,0:T(8,128)(2,1)S(1)} %copy-done.2, bf16[512,512]{1,0:T(8,128)(2,1)S(1)} %get-tuple-element.54.kd, ...), custom_call_target="tpu_custom_call" | custom-call | flops 2000000000 | bytes 1024 | tf_op jit(solution)/shard_map/edge_scores/pallas_call | solution.py:301
  30.2 1.4 %halo_scores_b.1 = (f32[4,16,128]{2,1,0:T(8,128)S(1)}, f32[2,2,192,256]{3,2,1,0:T(8,128)S(1)}, f32[2,2,192,256]{3,2,1,0:T(8,128)S(1)}, f32[2,2,192,256]{3,2,1,0:T(8,128)S(1)}, f32[2,2,192,256]{3,2,1,0:T(8,128)S(1)}) custom-call(bf16[2,256,512]{2,1,0:T(8,128)(2,1)S(1)} %collective-permute-done.1.q_in.refs_3_, bf16[512,512]{1,0:T(8,128)(2,1)S(1)} %get-tuple-element.54.kd, ...), custom_call_target="tpu_custom_call" | custom-call | flops 2000000000 | bytes 1024 | tf_op jit(solution)/shard_map/halo_scores_b/pallas_call | solution.py:354
  31.6 0.1 collective-permute-start.5
  31.7 3.8 %collective-permute-done.q_in.refs_2_ = bf16[2,256,512]{2,1,0:T(8,128)(2,1)S(1)} collective-permute-done((bf16[2,256,512]{2,1,0:T(8,128)(2,1)}, bf16[2,256,512]{2,1,0:T(8,128)(2,1)S(1)}, u32[]{:S(2)}, u32[]{:S(2)}) %collective-permute-start) | collective-permute-done | bytes 524320 | tf_op jit(solution)/shard_map/ppermute | solution.py:559
  35.5 1.4 %halo_scores_a.1 = (f32[4,16,128]{2,1,0:T(8,128)S(1)}, f32[2,2,192,256]{3,2,1,0:T(8,128)S(1)}, f32[2,2,192,256]{3,2,1,0:T(8,128)S(1)}, f32[2,2,192,256]{3,2,1,0:T(8,128)S(1)}, f32[2,2,192,256]{3,2,1,0:T(8,128)S(1)}) custom-call(bf16[2,256,512]{2,1,0:T(8,128)(2,1)S(1)} %collective-permute-done.q_in.refs_2_, bf16[512,512]{1,0:T(8,128)(2,1)S(1)} %get-tuple-element.54.kd, ...), custom_call_target="tpu_custom_call" | custom-call | flops 2000000000 | bytes 1024 | tf_op jit(solution)/shard_map/halo_scores_a/pallas_call | solution.py:354
  36.9 4.0 %collective-permute-start.4 = (f32[4,16,128]{2,1,0:T(8,128)S(1)}, f32[4,16,128]{2,1,0:T(8,128)S(1)}, u32[]{:S(2)}, u32[]{:S(2)}) collective-permute-start(f32[4,16,128]{2,1,0:T(8,128)S(1)} %get-tuple-element.60.send.refs_4_), channel_id=1, source_target_pairs={{0,1},{1,0},{2,3},{3,2},{4,5},{5,4},{6,7},{7,6},{8,9},{9,8},{10,11... | collective-permute-start | bytes 98312 | tf_op jit(solution)/shard_map/ppermute | solution.py:559
  40.9 0.5 turn_edges.1.edges_turned.refs_15_
  41.4 1.1 %halo_queries_b.1 = (bf16[256,512]{1,0:T(8,128)(2,1)S(1)}, bf16[2,2,192,256]{3,2,1,0:T(8,128)(2,1)S(1)}, bf16[2,2,192,256]{3,2,1,0:T(8,128)(2,1)S(1)}, bf16[2,2,...) custom-call(f32[4,16,128]{2,1,0:T(8,128)S(1)} %get-tuple-element.61.send.refs_5_, ...), custom_call_target="tpu_custom_call" | custom-call | bytes 1024 | tf_op jit(solution)/shard_map/halo_queries_b/pallas_call | solution.py:391
  42.5 0.1 collective-permute-start.7
  42.6 0.2 collective-permute-done.4.recv.refs_6_
  42.7 1.1 %halo_queries_a.1 = (bf16[256,512]{1,0:T(8,128)(2,1)S(1)}, bf16[2,2,192,256]{3,2,1,0:T(8,128)(2,1)S(1)}, bf16[2,2,192,256]{3,2,1,0:T(8,128)(2,1)S(1)}, bf16[2,2,...) custom-call(f32[4,16,128]{2,1,0:T(8,128)S(1)} %get-tuple-element.60.send.refs_4_, ...), custom_call_target="tpu_custom_call" | custom-call | bytes 1024 | tf_op jit(solution)/shard_map/halo_queries_a/pallas_call | solution.py:391
  43.8 3.6 %collective-permute-start.6 = (bf16[256,512]{1,0:T(8,128)(2,1)S(1)}, bf16[256,512]{1,0:T(8,128)(2,1)S(1)}, u32[]{:S(2)}, u32[]{:S(2)}) collective-permute-start(bf16[256,512]{1,0:T(8,128)(2,1)S(1)} %get-tuple-element.77.refs_16_), channel_id=1, source_target_pairs={{0,1},{1,0},{2,3},{3,2},{4,5},{5,4},{6,7},{7,6},{8,9},{9,8},{10,11... | collective-permute-start | bytes 786440 | tf_op jit(solution)/shard_map/ppermute | solution.py:559
  47.5 1.5 %edge_gradients_b.1 = (f32[2,64,512]{2,1,0:T(8,128)S(1)}, f32[256,512]{1,0:T(8,128)S(1)}, f32[256,512]{1,0:T(8,128)S(1)}, bf16[2,128,512]{2,1,0:T(8,128)(2,1)S(1)}) custom-call(bf16[2,256,512]{2,1,0:T(8,128)(2,1)S(1)} %copy-done.1, bf16[2,256,512]{2,1,0:T(8,128)(2,1)S(1)} %copy-done.3, bf16[2,256,512]{2,1,0:T(8,128)(2,1)S(1)} %collective-permute-done.q_in.refs_2_, ...), custom_call_target="tpu_custom_call" | custom-call | flops 2000000000 | bytes 1024 | tf_op jit(solution)/shard_map/edge_gradients_b/pallas_call | solution.py:466
  49.0 1.9 %collective-permute-start.9 = (bf16[2,128,512]{2,1,0:T(8,128)(2,1)S(1)}, bf16[2,128,512]{2,1,0:T(8,128)(2,1)S(1)}, u32[]{:S(2)}, u32[]{:S(2)}) collective-permute-start(bf16[2,128,512]{2,1,0:T(8,128)(2,1)S(1)} %get-tuple-element.79.refs_16_), channel_id=1, source_target_pairs={{32,64},{64,32},{33,65},{65,33},{34,66},{66,34},{35,67},{67,35},{3... | collective-permute-start | bytes 786440 | tf_op jit(solution)/shard_map/ppermute | solution.py:567
  50.9 1.5 %edge_gradients_a.1 = (f32[2,64,512]{2,1,0:T(8,128)S(1)}, f32[256,512]{1,0:T(8,128)S(1)}, f32[256,512]{1,0:T(8,128)S(1)}, bf16[2,128,512]{2,1,0:T(8,128)(2,1)S(1)}) custom-call(bf16[2,256,512]{2,1,0:T(8,128)(2,1)S(1)} %copy-done.1, bf16[2,256,512]{2,1,0:T(8,128)(2,1)S(1)} %copy-done.3, bf16[2,256,512]{2,1,0:T(8,128)(2,1)S(1)} %collective-permute-done.q_in.refs_2_, ...), custom_call_target="tpu_custom_call" | custom-call | flops 2000000000 | bytes 1024 | tf_op jit(solution)/shard_map/edge_gradients_a/pallas_call | solution.py:466
  52.4 0.1 collective-permute-start.8
  52.5 2.5 %mid_gradients.1 = (f32[2,128,512]{2,1,0:T(8,128)S(1)}, f32[512,512]{1,0:T(8,128)S(1)}, f32[512,512]{1,0:T(8,128)S(1)}) custom-call(bf16[2,256,512]{2,1,0:T(8,128)(2,1)S(1)} %copy-done.1, bf16[2,256,512]{2,1,0:T(8,128)(2,1)S(1)} %copy-done.3, bf16[2,256,512]{2,1,0:T(8,128)(2,1)S(1)} %collective-permute-done.q_in.refs_2_, ...), custom_call_target="tpu_custom_call" | custom-call | flops 3000000000 | bytes 1024 | tf_op jit(solution)/shard_map/mid_gradients/pallas_call | solution.py:480
  55.1 1.1 %finish_inner.1 = (bf16[32,16,512]{2,1,0:T(8,128)(2,1)}, bf16[32,16,512]{2,1,0:T(8,128)(2,1)}, bf16[32,16,512]{2,1,0:T(8,128)(2,1)}) custom-call(f32[2,64,512]{2,1,0:T(8,128)S(1)} %get-tuple-element.80.dq_a, f32[2,64,512]{2,1,0:T(8,128)S(1)} %get-tuple-element.81.dq_b, f32[2,128,512]{2,1,0:T(8,128)S(1)} %get-tuple-element.92.dq_mid, ...), custom_call_target="tpu_custom_call" | custom-call | bytes 1024 | tf_op jit(solution)/shard_map/finish_inner/pallas_call | solution.py:534
  56.2 4.1 %collective-permute-done.9.from_b = bf16[2,128,512]{2,1,0:T(8,128)(2,1)S(1)} collective-permute-done((bf16[2,128,512]{2,1,0:T(8,128)(2,1)S(1)}, bf16[2,128,512]{2,1,0:T(8,128)(2,1)S(1)}, u32[]{:S(2)}, u32[]{:S(2)}) %collective-permute-start.9) | collective-permute-done | bytes 262176 | tf_op jit(solution)/shard_map/ppermute | solution.py:567
  60.3 0.9 %finish_outer.1 = (bf16[32,16,512]{2,1,0:T(8,128)(2,1)}, bf16[32,16,512]{2,1,0:T(8,128)(2,1)}) custom-call(f32[512,512]{1,0:T(8,128)S(1)} %get-tuple-element.93.dk, f32[512,512]{1,0:T(8,128)S(1)} %get-tuple-element.94.dv, bf16[2,128,512]{2,1,0:T(8,128)(2,1)S(1)} %collective-permute-done.8.from_a, ...), custom_call_target="tpu_custom_call", output_to_operand_aliasing={{0}: (4, {}), {1}: (5, {})} | custom-call | bytes 1024 | tf_op jit(solution)/shard_map/finish_outer/pallas_call | solution.py:544
  (14 shorter events, 0.0 us)
Async XLA Ops:
  3.3 26.9 %collective-permute-start.1 = (bf16[2,256,512]{2,1,0:T(8,128)(2,1)}, bf16[2,256,512]{2,1,0:T(8,128)(2,1)S(1)}, u32[]{:S(2)}, u32[]{:S(2)}) collective-permute-start(bf16[2,256,512]{2,1,0:T(8,128)(2,1)} %get-tuple-element.53.side_1.refs_1_), channel_id=1, source_target_pairs={{1,2},{2,1},{3,4},{4,3},{5,6},{6,5},{7,8},{8,7},{9,10},{10,9},{11,... | collective-permute-start | bytes 1572872 | tf_op jit(solution)/shard_map/ppermute | solution.py:567
  6.0 12.4 %collective-permute-start.2 = (bf16[2,128,512]{2,1,0:T(8,128)(2,1)}, bf16[2,128,512]{2,1,0:T(8,128)(2,1)S(1)}, u32[]{:S(2)}, u32[]{:S(2)}) collective-permute-start(bf16[2,128,512]{2,1,0:T(8,128)(2,1)} %get-tuple-element.56), channel_id=1, source_target_pairs={{0,32},{32,0},{64,96},{96,64},{1,33},{33,1},{65,97},{97,65},{2,34}... | collective-permute-start | bytes 786440 | tf_op jit(solution)/shard_map/ppermute | solution.py:559
  6.0 21.8 %collective-permute-start.3 = (bf16[2,128,512]{2,1,0:T(8,128)(2,1)}, bf16[2,128,512]{2,1,0:T(8,128)(2,1)S(1)}, u32[]{:S(2)}, u32[]{:S(2)}) collective-permute-start(bf16[2,128,512]{2,1,0:T(8,128)(2,1)} %get-tuple-element.57), channel_id=1, source_target_pairs={{32,64},{64,32},{33,65},{65,33},{34,66},{66,34},{35,67},{67,35},{3... | collective-permute-start | bytes 786440 | tf_op jit(solution)/shard_map/ppermute | solution.py:567
  9.3 26.2 %collective-permute-start = (bf16[2,256,512]{2,1,0:T(8,128)(2,1)}, bf16[2,256,512]{2,1,0:T(8,128)(2,1)S(1)}, u32[]{:S(2)}, u32[]{:S(2)}) collective-permute-start(bf16[2,256,512]{2,1,0:T(8,128)(2,1)} %get-tuple-element.52.side_0.refs_0_), channel_id=1, source_target_pairs={{0,1},{1,0},{2,3},{3,2},{4,5},{5,4},{6,7},{7,6},{8,9},{9,8},{10,11... | collective-permute-start | bytes 1572872 | tf_op jit(solution)/shard_map/ppermute | solution.py:559
  10.2 1.0 %copy-start.4 = (bf16[32,16,512]{2,1,0:T(8,128)(2,1)S(1)}, bf16[32,16,512]{2,1,0:T(8,128)(2,1)}, u32[]{:S(2)}) copy-start(bf16[32,16,512]{2,1,0:T(8,128)(2,1)} %k_ref.3) | copy-start | bytes 1572868
  11.2 1.0 %copy-start.5 = (bf16[32,16,512]{2,1,0:T(8,128)(2,1)S(1)}, bf16[32,16,512]{2,1,0:T(8,128)(2,1)}, u32[]{:S(2)}) copy-start(bf16[32,16,512]{2,1,0:T(8,128)(2,1)} %v_ref.3) | copy-start | bytes 1572868
  13.9 1.0 %copy-start = (bf16[2,256,512]{2,1,0:T(8,128)(2,1)S(1)}, bf16[2,256,512]{2,1,0:T(8,128)(2,1)}, u32[]{:S(2)}) copy-start(bf16[2,256,512]{2,1,0:T(8,128)(2,1)} %get-tuple-element.52.side_0.refs_0_) | copy-start | bytes 1572868
  14.9 1.0 %copy-start.2 = (bf16[2,256,512]{2,1,0:T(8,128)(2,1)S(1)}, bf16[2,256,512]{2,1,0:T(8,128)(2,1)}, u32[]{:S(2)}) copy-start(bf16[2,256,512]{2,1,0:T(8,128)(2,1)} %get-tuple-element.53.side_1.refs_1_) | copy-start | bytes 1572868
  31.6 9.7 %collective-permute-start.5 = (f32[4,16,128]{2,1,0:T(8,128)S(1)}, f32[4,16,128]{2,1,0:T(8,128)S(1)}, u32[]{:S(2)}, u32[]{:S(2)}) collective-permute-start(f32[4,16,128]{2,1,0:T(8,128)S(1)} %get-tuple-element.61.send.refs_5_), channel_id=1, source_target_pairs={{1,2},{2,1},{3,4},{4,3},{5,6},{6,5},{7,8},{8,7},{9,10},{10,9},{11,... | collective-permute-start | bytes 98312 | tf_op jit(solution)/shard_map/ppermute | solution.py:567
  36.9 5.9 %collective-permute-start.4 = (f32[4,16,128]{2,1,0:T(8,128)S(1)}, f32[4,16,128]{2,1,0:T(8,128)S(1)}, u32[]{:S(2)}, u32[]{:S(2)}) collective-permute-start(f32[4,16,128]{2,1,0:T(8,128)S(1)} %get-tuple-element.60.send.refs_4_), channel_id=1, source_target_pairs={{0,1},{1,0},{2,3},{3,2},{4,5},{5,4},{6,7},{7,6},{8,9},{9,8},{10,11... | collective-permute-start | bytes 98312 | tf_op jit(solution)/shard_map/ppermute | solution.py:559
  41.4 6.1 %copy-start.1 = (bf16[2,256,512]{2,1,0:T(8,128)(2,1)S(1)}, bf16[2,256,512]{2,1,0:T(8,128)(2,1)}, u32[]{:S(2)}) copy-start(bf16[2,256,512]{2,1,0:T(8,128)(2,1)} %get-tuple-element.52.side_0.refs_0_) | copy-start | bytes 1572868
  41.4 6.1 %copy-start.3 = (bf16[2,256,512]{2,1,0:T(8,128)(2,1)S(1)}, bf16[2,256,512]{2,1,0:T(8,128)(2,1)}, u32[]{:S(2)}) copy-start(bf16[2,256,512]{2,1,0:T(8,128)(2,1)} %get-tuple-element.53.side_1.refs_1_) | copy-start | bytes 1572868
  42.5 12.6 %collective-permute-start.7 = (bf16[256,512]{1,0:T(8,128)(2,1)S(1)}, bf16[256,512]{1,0:T(8,128)(2,1)S(1)}, u32[]{:S(2)}, u32[]{:S(2)}) collective-permute-start(bf16[256,512]{1,0:T(8,128)(2,1)S(1)} %get-tuple-element.78.refs_17_), channel_id=1, source_target_pairs={{1,2},{2,1},{3,4},{4,3},{5,6},{6,5},{7,8},{8,7},{9,10},{10,9},{11,... | collective-permute-start | bytes 786440 | tf_op jit(solution)/shard_map/ppermute | solution.py:567
  43.8 11.2 %collective-permute-start.6 = (bf16[256,512]{1,0:T(8,128)(2,1)S(1)}, bf16[256,512]{1,0:T(8,128)(2,1)S(1)}, u32[]{:S(2)}, u32[]{:S(2)}) collective-permute-start(bf16[256,512]{1,0:T(8,128)(2,1)S(1)} %get-tuple-element.77.refs_16_), channel_id=1, source_target_pairs={{0,1},{1,0},{2,3},{3,2},{4,5},{5,4},{6,7},{7,6},{8,9},{9,8},{10,11... | collective-permute-start | bytes 786440 | tf_op jit(solution)/shard_map/ppermute | solution.py:559
  49.0 11.3 %collective-permute-start.9 = (bf16[2,128,512]{2,1,0:T(8,128)(2,1)S(1)}, bf16[2,128,512]{2,1,0:T(8,128)(2,1)S(1)}, u32[]{:S(2)}, u32[]{:S(2)}) collective-permute-start(bf16[2,128,512]{2,1,0:T(8,128)(2,1)S(1)} %get-tuple-element.79.refs_16_), channel_id=1, source_target_pairs={{32,64},{64,32},{33,65},{65,33},{34,66},{66,34},{35,67},{67,35},{3... | collective-permute-start | bytes 786440 | tf_op jit(solution)/shard_map/ppermute | solution.py:567
  52.4 3.8 %collective-permute-start.8 = (bf16[2,128,512]{2,1,0:T(8,128)(2,1)S(1)}, bf16[2,128,512]{2,1,0:T(8,128)(2,1)S(1)}, u32[]{:S(2)}, u32[]{:S(2)}) collective-permute-start(bf16[2,128,512]{2,1,0:T(8,128)(2,1)S(1)} %get-tuple-element.96), channel_id=1, source_target_pairs={{0,32},{32,0},{64,96},{96,64},{1,33},{33,1},{65,97},{97,65},{2,34}... | collective-permute-start | bytes 786440 | tf_op jit(solution)/shard_map/ppermute | solution.py:559

commit v13 on v10

--- a/solution.py
+++ b/solution.py
@@ -310,7 +310,7 @@
     )(*operands)
 
 
-def turn_edges_kernel(edge_a, edge_b, turned):
+def turn_edges_kernel(edge_a, edge_b, _, turned):
     turned[0] = edge_a[0].T
     turned[1] = edge_b[0].T
 
@@ -319,7 +319,7 @@
     return pl.pallas_call(
         turn_edges_kernel,
         grid=(PAIRS,),
-        in_specs=[edge_spec] * 2,
+        in_specs=[edge_spec] * 2 + [any_spec],
         out_specs=pl.BlockSpec((2, PAIR, PAIR), lambda p: (0, p, 0)),
         out_shape=struct((2, FEAT, PAIR), BF16),
         compiler_params=params(),
@@ -328,7 +328,8 @@
     )(*operands)
 
 
-def halo_scores_kernel(c, q_in, kd, vd, edge_a, edge_b, edge_part, mid_part, send, s_edge, d_edge, s_mid, d_mid):
+def halo_scores_kernel(c, q_in, kd, vd, edge_a, edge_b, edge_part, mid_part, *refs):
+    send, s_edge, d_edge, s_mid, d_mid = refs[-5:]
     masks = head_masks(WIDE)
     groups = ((EDGE_ROWS, edge_part, s_edge, d_edge), (MID_ROWS, mid_part, s_mid, d_mid))
     for group, (rows, part, s_out, d_out) in enumerate(groups):
@@ -354,7 +355,7 @@
     return pl.pallas_call(
         functools.partial(halo_scores_kernel, c),
         grid=(GROUPS,),
-        in_specs=[all_tokens] + [keys_wide] * 2 + [edge_wide] * 2 + [part] * 2,
+        in_specs=[all_tokens] + [keys_wide] * 2 + [edge_wide] * 2 + [part] * 2 + [any_spec] * (len(operands) - 7),
         out_specs=[all_stats] + [halo_wide] * 4,
         out_shape=[stats_shape] + [halo_shape] * 4,
         compiler_params=params(),
@@ -577,17 +578,16 @@
     edges = (swap_a(own_edge_a, "lat"), edge_b)
     mid_part, *mid_own, turned = mid_scores(*sides, kd, vd)
     edge_part, *edge_own = edge_scores(*sides, kd, vd, *edges)
-    edges_turned = turn_edges(*edges)
-    sends, recvs, halo_dq, dq_parts, weights = [], [], [], [], []
-    for c in range(2):
-        send, *held = halo_scores(c, halos[c], kd, vd, *edges, edge_part, mid_part)
-        recv = swap_lon(c, send)
-        grad, *weight = halo_queries(c, send, recv, *held, turned, edges_turned)
-        sends.append(send)
-        recvs.append(recv)
-        halo_dq.append(grad)
-        dq_parts.append(swap_lon(c, grad))
-        weights.append(weight)
+    sends, recvs, halo_dq, dq_parts, weights = [{} for _ in range(5)]
+    for c in (1, 0):
+        before = () if c else (edges_turned,)
+        sends[c], *held = halo_scores(c, halos[c], kd, vd, *edges, edge_part, mid_part, *before)
+        if c:
+            edges_turned = turn_edges(*edges, sends[c])
+        recvs[c] = swap_lon(c, sends[c])
+        halo_dq[c], *weights[c] = halo_queries(c, sends[c], recvs[c], *held, turned, edges_turned)
+        dq_parts[c] = swap_lon(c, halo_dq[c])
+    sends, recvs, halo_dq, dq_parts = [[one[0], one[1]] for one in (sends, recvs, halo_dq, dq_parts)]
     shared = (*sides, *halos, *sends, *recvs)
     dq_edge, dk, dv, out_a, out_b = edge_gradients(*shared, *edge_own, *weights[0][:2], *weights[1][:2], turned, edges_turned,
                                                    *halo_dq)

time: 61.5 us -> 61.5 us (level)
  the two profiles are of different devices: /device:TPU:1 before, /device:TPU:14 now
where the time goes in v13:
time: 61.5 us; the launch traced here: 61.2 us
  Pallas kernels  21.4 us (35%)
  waiting for transfers between devices  18.1 us (29%)
  starting transfers between devices  16.6 us (27%)
  local copies, waits for them, and re-layouts  4.17 us (7%)
  between operations  0.82 us (1%)
    ppermute x5, waiting for transfers between devices, swap_b(): return lax.ppermute(x, axis, pairs)  14.1 us
    ppermute x5, starting transfers between devices, swap_a(): lax.ppermute(x, axis, [(i, i ^ 1) for i in range(lax.axis_size(axis))])  8.53 us
    ppermute x5, starting transfers between devices, swap_b(): return lax.ppermute(x, axis, pairs)  8.09 us
    unnamed x12, local copies, waits for them, and re-layouts  4.17 us
    ppermute x5, waiting for transfers between devices, swap_a(): lax.ppermute(x, axis, [(i, i ^ 1) for i in range(lax.axis_size(axis))])  4.01 us
    pallas_call x2, Pallas kernels, halo_scores(): pl.pallas_call(functools.partial(halo_scores_kernel, c), grid=(GROUPS,),...  2.75 us
    pallas_call x1, Pallas kernels, pack_queries(): pl.pallas_call(pack_queries_kernel, in_specs=[any_spec] * 4, out_specs=[a...  2.67 us
    pallas_call x1, Pallas kernels, mid_gradients(): pl.pallas_call(mid_kernel, grid=(GROUPS,), in_specs=row_specs(MID) + [key...  2.52 us
  transfers between devices with their start and end apart: 10, of which 4 were waited for; matrix products, arithmetic and copies ran while one was open for 0% of the time, Pallas kernels for 29%

profile of v13, /device:TPU:14, one launch (start us, length us, event | category | flops | bytes accessed | tf_op | source)
XLA Modules:
  0.0 61.2 jit_solution(16343805718485315811)
XLA Ops:
  0.6 2.7 %pack_queries.1 = (bf16[2,256,512]{2,1,0:T(8,128)(2,1)}, bf16[2,256,512]{2,1,0:T(8,128)(2,1)}, bf16[2,128,512]{2,1,0:T(8,128)(2,1)}, bf16[2,128,512]{2,1,0:T(8,128)(2,1)}) custom-call(bf16[32,16,512]{2,1,0:T(8,128)(2,1)} %q_ref.1, bf16[32,16,512]{2,1,0:T(8,128)(2,1)} %g_ref.1, bf16[32,16,512]{2,1,0:T(8,128)(2,1)} %k_ref.3, bf16[32,16,512]{2,1,0:T(8,128)(2,1)} %v_ref.3), custom_call_target="tpu_custom_call" | custom-call | bytes 3145728 | tf_op jit(solution)/shard_map/pack_queries/pallas_call | solution.py:102
  3.3 2.6 %collective-permute-start.1 = (bf16[2,256,512]{2,1,0:T(8,128)(2,1)}, bf16[2,256,512]{2,1,0:T(8,128)(2,1)S(1)}, u32[]{:S(2)}, u32[]{:S(2)}) collective-permute-start(bf16[2,256,512]{2,1,0:T(8,128)(2,1)} %get-tuple-element.50.side_1.refs_1_), channel_id=1, source_target_pairs={{1,2},{2,1},{3,4},{4,3},{5,6},{6,5},{7,8},{8,7},{9,10},{10,9},{11,... | collective-permute-start | bytes 1572872 | tf_op jit(solution)/shard_map/ppermute | solution.py:566
  6.0 0.0 collective-permute-start.2
  6.0 3.4 %collective-permute-start.3 = (bf16[2,128,512]{2,1,0:T(8,128)(2,1)}, bf16[2,128,512]{2,1,0:T(8,128)(2,1)S(1)}, u32[]{:S(2)}, u32[]{:S(2)}) collective-permute-start(bf16[2,128,512]{2,1,0:T(8,128)(2,1)} %get-tuple-element.54), channel_id=1, source_target_pairs={{32,64},{64,32},{33,65},{65,33},{34,66},{66,34},{35,67},{67,35},{3... | collective-permute-start | bytes 786440 | tf_op jit(solution)/shard_map/ppermute | solution.py:566
  9.3 0.9 %collective-permute-start = (bf16[2,256,512]{2,1,0:T(8,128)(2,1)}, bf16[2,256,512]{2,1,0:T(8,128)(2,1)S(1)}, u32[]{:S(2)}, u32[]{:S(2)}) collective-permute-start(bf16[2,256,512]{2,1,0:T(8,128)(2,1)} %get-tuple-element.49.side_0.refs_0_), channel_id=1, source_target_pairs={{0,1},{1,0},{2,3},{3,2},{4,5},{5,4},{6,7},{7,6},{8,9},{9,8},{10,11... | collective-permute-start | bytes 1572872 | tf_op jit(solution)/shard_map/ppermute | solution.py:558
  10.2 1.0 %copy-done.4 = bf16[32,16,512]{2,1,0:T(8,128)(2,1)S(1)} copy-done((bf16[32,16,512]{2,1,0:T(8,128)(2,1)S(1)}, bf16[32,16,512]{2,1,0:T(8,128)(2,1)}, u32[]{:S(2)}) %copy-start.4) | copy-done | bytes 524312
  11.2 1.0 %copy-done.5 = bf16[32,16,512]{2,1,0:T(8,128)(2,1)S(1)} copy-done((bf16[32,16,512]{2,1,0:T(8,128)(2,1)S(1)}, bf16[32,16,512]{2,1,0:T(8,128)(2,1)}, u32[]{:S(2)}) %copy-start.5) | copy-done | bytes 524312
  12.3 1.6 %pack_keys.1 = (bf16[512,512]{1,0:T(8,128)(2,1)S(1)}, bf16[512,512]{1,0:T(8,128)(2,1)S(1)}) custom-call(bf16[32,16,512]{2,1,0:T(8,128)(2,1)S(1)} %copy-done.4, bf16[32,16,512]{2,1,0:T(8,128)(2,1)S(1)} %copy-done.5), custom_call_target="tpu_custom_call" | custom-call | bytes 3145728 | tf_op jit(solution)/shard_map/pack_keys/pallas_call | solution.py:128
  13.9 0.0 copy-start
  13.9 1.0 %copy-done = bf16[2,256,512]{2,1,0:T(8,128)(2,1)S(1)} copy-done((bf16[2,256,512]{2,1,0:T(8,128)(2,1)S(1)}, bf16[2,256,512]{2,1,0:T(8,128)(2,1)}, u32[]{:S(2)}) %copy-start) | copy-done | bytes 524312
  14.9 1.0 %copy-done.2 = bf16[2,256,512]{2,1,0:T(8,128)(2,1)S(1)} copy-done((bf16[2,256,512]{2,1,0:T(8,128)(2,1)S(1)}, bf16[2,256,512]{2,1,0:T(8,128)(2,1)}, u32[]{:S(2)}) %copy-start.2) | copy-done | bytes 524312
  16.0 2.4 %mid_scores.1 = (f32[4,8,128]{2,1,0:T(8,128)S(1)}, f32[4,2,384,256]{3,2,1,0:T(8,128)S(1)}, f32[4,2,384,256]{3,2,1,0:T(8,128)S(1)}, bf16[512,512]{1,0:T(8,128)(2,1)S(1)}) custom-call(bf16[2,256,512]{2,1,0:T(8,128)(2,1)S(1)} %copy-done, bf16[2,256,512]{2,1,0:T(8,128)(2,1)S(1)} %copy-done.2, bf16[512,512]{1,0:T(8,128)(2,1)S(1)} %get-tuple-element.51.kd, ...), custom_call_target="tpu_custom_call" | custom-call | flops 2000000000 | bytes 1024 | tf_op jit(solution)/shard_map/mid_scores/pallas_call | solution.py:288
  18.4 9.4 %collective-permute-done.3.edge_b = bf16[2,128,512]{2,1,0:T(8,128)(2,1)S(1)} collective-permute-done((bf16[2,128,512]{2,1,0:T(8,128)(2,1)}, bf16[2,128,512]{2,1,0:T(8,128)(2,1)S(1)}, u32[]{:S(2)}, u32[]{:S(2)}) %collective-permute-start.3) | collective-permute-done | bytes 262176 | tf_op jit(solution)/shard_map/ppermute | solution.py:566
  27.8 2.4 %edge_scores.1 = (f32[4,8,128]{2,1,0:T(8,128)S(1)}, f32[4,2,384,256]{3,2,1,0:T(8,128)S(1)}, f32[4,2,384,256]{3,2,1,0:T(8,128)S(1)}) custom-call(bf16[2,256,512]{2,1,0:T(8,128)(2,1)S(1)} %copy-done, bf16[2,256,512]{2,1,0:T(8,128)(2,1)S(1)} %copy-done.2, bf16[512,512]{1,0:T(8,128)(2,1)S(1)} %get-tuple-element.51.kd, ...), custom_call_target="tpu_custom_call" | custom-call | flops 2000000000 | bytes 1024 | tf_op jit(solution)/shard_map/edge_scores/pallas_call | solution.py:301
  30.2 1.4 %halo_scores_b.1 = (f32[4,16,128]{2,1,0:T(8,128)S(1)}, f32[2,2,192,256]{3,2,1,0:T(8,128)S(1)}, f32[2,2,192,256]{3,2,1,0:T(8,128)S(1)}, f32[2,2,192,256]{3,2,1,0:T(8,128)S(1)}, f32[2,2,192,256]{3,2,1,0:T(8,128)S(1)}) custom-call(bf16[2,256,512]{2,1,0:T(8,128)(2,1)S(1)} %collective-permute-done.1.q_in.refs_3_, bf16[512,512]{1,0:T(8,128)(2,1)S(1)} %get-tuple-element.51.kd, ...), custom_call_target="tpu_custom_call" | custom-call | flops 2000000000 | bytes 1024 | tf_op jit(solution)/shard_map/halo_scores_b/pallas_call | solution.py:355
  31.6 0.1 collective-permute-start.5
  31.7 0.5 turn_edges.1.refs_0_.edges_turned.refs_15_
  32.2 3.3 %collective-permute-done.q_in.refs_2_ = bf16[2,256,512]{2,1,0:T(8,128)(2,1)S(1)} collective-permute-done((bf16[2,256,512]{2,1,0:T(8,128)(2,1)}, bf16[2,256,512]{2,1,0:T(8,128)(2,1)S(1)}, u32[]{:S(2)}, u32[]{:S(2)}) %collective-permute-start) | collective-permute-done | bytes 524320 | tf_op jit(solution)/shard_map/ppermute | solution.py:558
  35.5 1.4 %halo_scores_a.1 = (f32[4,16,128]{2,1,0:T(8,128)S(1)}, f32[2,2,192,256]{3,2,1,0:T(8,128)S(1)}, f32[2,2,192,256]{3,2,1,0:T(8,128)S(1)}, f32[2,2,192,256]{3,2,1,0:T(8,128)S(1)}, f32[2,2,192,256]{3,2,1,0:T(8,128)S(1)}) custom-call(bf16[2,256,512]{2,1,0:T(8,128)(2,1)S(1)} %collective-permute-done.q_in.refs_2_, bf16[512,512]{1,0:T(8,128)(2,1)S(1)} %get-tuple-element.51.kd, ...), custom_call_target="tpu_custom_call" | custom-call | flops 2000000000 | bytes 1024 | tf_op jit(solution)/shard_map/halo_scores_a/pallas_call | solution.py:355
  36.9 4.0 %collective-permute-start.4 = (f32[4,16,128]{2,1,0:T(8,128)S(1)}, f32[4,16,128]{2,1,0:T(8,128)S(1)}, u32[]{:S(2)}, u32[]{:S(2)}) collective-permute-start(f32[4,16,128]{2,1,0:T(8,128)S(1)} %get-tuple-element.58.send.refs_4_), channel_id=1, source_target_pairs={{0,1},{1,0},{2,3},{3,2},{4,5},{5,4},{6,7},{7,6},{8,9},{9,8},{10,11... | collective-permute-start | bytes 98312 | tf_op jit(solution)/shard_map/ppermute | solution.py:558
  40.9 1.1 %halo_queries_b.1 = (bf16[256,512]{1,0:T(8,128)(2,1)S(1)}, bf16[2,2,192,256]{3,2,1,0:T(8,128)(2,1)S(1)}, bf16[2,2,192,256]{3,2,1,0:T(8,128)(2,1)S(1)}, bf16[2,2,...) custom-call(f32[4,16,128]{2,1,0:T(8,128)S(1)} %get-tuple-element.57._.send.refs_5_, ...), custom_call_target="tpu_custom_call" | custom-call | bytes 1024 | tf_op jit(solution)/shard_map/halo_queries_b/pallas_call | solution.py:392
  41.9 0.1 collective-permute-start.7
  42.0 0.7 %collective-permute-done.4.recv.refs_6_ = f32[4,16,128]{2,1,0:T(8,128)S(1)} collective-permute-done((f32[4,16,128]{2,1,0:T(8,128)S(1)}, f32[4,16,128]{2,1,0:T(8,128)S(1)}, u32[]{:S(2)}, u32[]{:S(2)}) %collective-permute-start.4) | collective-permute-done | bytes 32800 | tf_op jit(solution)/shard_map/ppermute | solution.py:558
  42.7 1.1 %halo_queries_a.1 = (bf16[256,512]{1,0:T(8,128)(2,1)S(1)}, bf16[2,2,192,256]{3,2,1,0:T(8,128)(2,1)S(1)}, bf16[2,2,192,256]{3,2,1,0:T(8,128)(2,1)S(1)}, bf16[2,2,...) custom-call(f32[4,16,128]{2,1,0:T(8,128)S(1)} %get-tuple-element.58.send.refs_4_, ...), custom_call_target="tpu_custom_call" | custom-call | bytes 1024 | tf_op jit(solution)/shard_map/halo_queries_a/pallas_call | solution.py:392
  43.8 3.6 %collective-permute-start.6 = (bf16[256,512]{1,0:T(8,128)(2,1)S(1)}, bf16[256,512]{1,0:T(8,128)(2,1)S(1)}, u32[]{:S(2)}, u32[]{:S(2)}) collective-permute-start(bf16[256,512]{1,0:T(8,128)(2,1)S(1)} %get-tuple-element.74.refs_16_), channel_id=1, source_target_pairs={{0,1},{1,0},{2,3},{3,2},{4,5},{5,4},{6,7},{7,6},{8,9},{9,8},{10,11... | collective-permute-start | bytes 786440 | tf_op jit(solution)/shard_map/ppermute | solution.py:558
  47.5 2.4 %edge_gradients.1 = (f32[2,128,512]{2,1,0:T(8,128)S(1)}, f32[512,512]{1,0:T(8,128)S(1)}, f32[512,512]{1,0:T(8,128)S(1)}, bf16[2,128,512]{2,1,0:T(8,128)(2,1)S(1)}, bf16[2,128,512]{2,1,0:T(8,128)(2,1)S(1)}) custom-call(bf16[2,256,512]{2,1,0:T(8,128)(2,1)S(1)} %copy-done.1, bf16[2,256,512]{2,1,0:T(8,128)(2,1)S(1)} %copy-done.3, ...), custom_call_target="tpu_custom_call" | custom-call | flops 3000000000 | bytes 1024 | tf_op jit(solution)/shard_map/edge_gradients/pallas_call | solution.py:466
  49.9 0.1 collective-permute-start.8
  50.0 1.9 %collective-permute-start.9 = (bf16[2,128,512]{2,1,0:T(8,128)(2,1)S(1)}, bf16[2,128,512]{2,1,0:T(8,128)(2,1)S(1)}, u32[]{:S(2)}, u32[]{:S(2)}) collective-permute-start(bf16[2,128,512]{2,1,0:T(8,128)(2,1)S(1)} %get-tuple-element.90), channel_id=1, source_target_pairs={{32,64},{64,32},{33,65},{65,33},{34,66},{66,34},{35,67},{67,35},{3... | collective-permute-start | bytes 786440 | tf_op jit(solution)/shard_map/ppermute | solution.py:566
  51.9 2.5 %mid_gradients.1 = (f32[2,128,512]{2,1,0:T(8,128)S(1)}, f32[512,512]{1,0:T(8,128)S(1)}, f32[512,512]{1,0:T(8,128)S(1)}) custom-call(bf16[2,256,512]{2,1,0:T(8,128)(2,1)S(1)} %copy-done.1, bf16[2,256,512]{2,1,0:T(8,128)(2,1)S(1)} %copy-done.3, bf16[2,256,512]{2,1,0:T(8,128)(2,1)S(1)} %collective-permute-done.q_in.refs_2_, ...), custom_call_target="tpu_custom_call" | custom-call | flops 3000000000 | bytes 1024 | tf_op jit(solution)/shard_map/mid_gradients/pallas_call | solution.py:479
  54.4 1.1 %finish_inner.1 = (bf16[32,16,512]{2,1,0:T(8,128)(2,1)}, bf16[32,16,512]{2,1,0:T(8,128)(2,1)}, bf16[32,16,512]{2,1,0:T(8,128)(2,1)}) custom-call(f32[2,128,512]{2,1,0:T(8,128)S(1)} %get-tuple-element.76.dq_edge, f32[2,128,512]{2,1,0:T(8,128)S(1)} %get-tuple-element.85.dq_mid, f32[512,512]{1,0:T(8,128)S(1)} %get-tuple-element.86.dk, ...), custom_call_target="tpu_custom_call" | custom-call | bytes 1024 | tf_op jit(solution)/shard_map/finish_inner/pallas_call | solution.py:533
  55.6 4.7 %collective-permute-done.9.from_b = bf16[2,128,512]{2,1,0:T(8,128)(2,1)S(1)} collective-permute-done((bf16[2,128,512]{2,1,0:T(8,128)(2,1)S(1)}, bf16[2,128,512]{2,1,0:T(8,128)(2,1)S(1)}, u32[]{:S(2)}, u32[]{:S(2)}) %collective-permute-start.9) | collective-permute-done | bytes 262176 | tf_op jit(solution)/shard_map/ppermute | solution.py:566
  60.3 0.9 %finish_outer.1 = (bf16[32,16,512]{2,1,0:T(8,128)(2,1)}, bf16[32,16,512]{2,1,0:T(8,128)(2,1)}) custom-call(f32[512,512]{1,0:T(8,128)S(1)} %get-tuple-element.86.dk, f32[512,512]{1,0:T(8,128)S(1)} %get-tuple-element.87.dv, bf16[2,128,512]{2,1,0:T(8,128)(2,1)S(1)} %collective-permute-done.8.from_a, ...), custom_call_target="tpu_custom_call", output_to_operand_aliasing={{0}: (4, {}), {1}: (5, {})} | custom-call | bytes 1024 | tf_op jit(solution)/shard_map/finish_outer/pallas_call | solution.py:543
  (13 shorter events, 0.0 us)
Async XLA Ops:
  3.3 26.9 %collective-permute-start.1 = (bf16[2,256,512]{2,1,0:T(8,128)(2,1)}, bf16[2,256,512]{2,1,0:T(8,128)(2,1)S(1)}, u32[]{:S(2)}, u32[]{:S(2)}) collective-permute-start(bf16[2,256,512]{2,1,0:T(8,128)(2,1)} %get-tuple-element.50.side_1.refs_1_), channel_id=1, source_target_pairs={{1,2},{2,1},{3,4},{4,3},{5,6},{6,5},{7,8},{8,7},{9,10},{10,9},{11,... | collective-permute-start | bytes 1572872 | tf_op jit(solution)/shard_map/ppermute | solution.py:566
  6.0 12.4 %collective-permute-start.2 = (bf16[2,128,512]{2,1,0:T(8,128)(2,1)}, bf16[2,128,512]{2,1,0:T(8,128)(2,1)S(1)}, u32[]{:S(2)}, u32[]{:S(2)}) collective-permute-start(bf16[2,128,512]{2,1,0:T(8,128)(2,1)} %get-tuple-element.53), channel_id=1, source_target_pairs={{0,32},{32,0},{64,96},{96,64},{1,33},{33,1},{65,97},{97,65},{2,34}... | collective-permute-start | bytes 786440 | tf_op jit(solution)/shard_map/ppermute | solution.py:558
  6.0 21.8 %collective-permute-start.3 = (bf16[2,128,512]{2,1,0:T(8,128)(2,1)}, bf16[2,128,512]{2,1,0:T(8,128)(2,1)S(1)}, u32[]{:S(2)}, u32[]{:S(2)}) collective-permute-start(bf16[2,128,512]{2,1,0:T(8,128)(2,1)} %get-tuple-element.54), channel_id=1, source_target_pairs={{32,64},{64,32},{33,65},{65,33},{34,66},{66,34},{35,67},{67,35},{3... | collective-permute-start | bytes 786440 | tf_op jit(solution)/shard_map/ppermute | solution.py:566
  9.3 26.2 %collective-permute-start = (bf16[2,256,512]{2,1,0:T(8,128)(2,1)}, bf16[2,256,512]{2,1,0:T(8,128)(2,1)S(1)}, u32[]{:S(2)}, u32[]{:S(2)}) collective-permute-start(bf16[2,256,512]{2,1,0:T(8,128)(2,1)} %get-tuple-element.49.side_0.refs_0_), channel_id=1, source_target_pairs={{0,1},{1,0},{2,3},{3,2},{4,5},{5,4},{6,7},{7,6},{8,9},{9,8},{10,11... | collective-permute-start | bytes 1572872 | tf_op jit(solution)/shard_map/ppermute | solution.py:558
  10.2 1.0 %copy-start.4 = (bf16[32,16,512]{2,1,0:T(8,128)(2,1)S(1)}, bf16[32,16,512]{2,1,0:T(8,128)(2,1)}, u32[]{:S(2)}) copy-start(bf16[32,16,512]{2,1,0:T(8,128)(2,1)} %k_ref.3) | copy-start | bytes 1572868
  11.2 1.0 %copy-start.5 = (bf16[32,16,512]{2,1,0:T(8,128)(2,1)S(1)}, bf16[32,16,512]{2,1,0:T(8,128)(2,1)}, u32[]{:S(2)}) copy-start(bf16[32,16,512]{2,1,0:T(8,128)(2,1)} %v_ref.3) | copy-start | bytes 1572868
  13.9 1.0 %copy-start = (bf16[2,256,512]{2,1,0:T(8,128)(2,1)S(1)}, bf16[2,256,512]{2,1,0:T(8,128)(2,1)}, u32[]{:S(2)}) copy-start(bf16[2,256,512]{2,1,0:T(8,128)(2,1)} %get-tuple-element.49.side_0.refs_0_) | copy-start | bytes 1572868
  14.9 1.0 %copy-start.2 = (bf16[2,256,512]{2,1,0:T(8,128)(2,1)S(1)}, bf16[2,256,512]{2,1,0:T(8,128)(2,1)}, u32[]{:S(2)}) copy-start(bf16[2,256,512]{2,1,0:T(8,128)(2,1)} %get-tuple-element.50.side_1.refs_1_) | copy-start | bytes 1572868
  31.6 9.2 %collective-permute-start.5 = (f32[4,16,128]{2,1,0:T(8,128)S(1)}, f32[4,16,128]{2,1,0:T(8,128)S(1)}, u32[]{:S(2)}, u32[]{:S(2)}) collective-permute-start(f32[4,16,128]{2,1,0:T(8,128)S(1)} %get-tuple-element.57._.send.refs_5_), channel_id=1, source_target_pairs={{1,2},{2,1},{3,4},{4,3},{5,6},{6,5},{7,8},{8,7},{9,10},{10,9},{11,... | collective-permute-start | bytes 98312 | tf_op jit(solution)/shard_map/ppermute | solution.py:566
  36.9 5.9 %collective-permute-start.4 = (f32[4,16,128]{2,1,0:T(8,128)S(1)}, f32[4,16,128]{2,1,0:T(8,128)S(1)}, u32[]{:S(2)}, u32[]{:S(2)}) collective-permute-start(f32[4,16,128]{2,1,0:T(8,128)S(1)} %get-tuple-element.58.send.refs_4_), channel_id=1, source_target_pairs={{0,1},{1,0},{2,3},{3,2},{4,5},{5,4},{6,7},{7,6},{8,9},{9,8},{10,11... | collective-permute-start | bytes 98312 | tf_op jit(solution)/shard_map/ppermute | solution.py:558
  40.9 6.6 %copy-start.1 = (bf16[2,256,512]{2,1,0:T(8,128)(2,1)S(1)}, bf16[2,256,512]{2,1,0:T(8,128)(2,1)}, u32[]{:S(2)}) copy-start(bf16[2,256,512]{2,1,0:T(8,128)(2,1)} %get-tuple-element.49.side_0.refs_0_) | copy-start | bytes 1572868
  40.9 6.6 %copy-start.3 = (bf16[2,256,512]{2,1,0:T(8,128)(2,1)S(1)}, bf16[2,256,512]{2,1,0:T(8,128)(2,1)}, u32[]{:S(2)}) copy-start(bf16[2,256,512]{2,1,0:T(8,128)(2,1)} %get-tuple-element.50.side_1.refs_1_) | copy-start | bytes 1572868
  41.9 12.5 %collective-permute-start.7 = (bf16[256,512]{1,0:T(8,128)(2,1)S(1)}, bf16[256,512]{1,0:T(8,128)(2,1)S(1)}, u32[]{:S(2)}, u32[]{:S(2)}) collective-permute-start(bf16[256,512]{1,0:T(8,128)(2,1)S(1)} %get-tuple-element.75.refs_17_), channel_id=1, source_target_pairs={{1,2},{2,1},{3,4},{4,3},{5,6},{6,5},{7,8},{8,7},{9,10},{10,9},{11,... | collective-permute-start | bytes 786440 | tf_op jit(solution)/shard_map/ppermute | solution.py:566
  43.8 10.6 %collective-permute-start.6 = (bf16[256,512]{1,0:T(8,128)(2,1)S(1)}, bf16[256,512]{1,0:T(8,128)(2,1)S(1)}, u32[]{:S(2)}, u32[]{:S(2)}) collective-permute-start(bf16[256,512]{1,0:T(8,128)(2,1)S(1)} %get-tuple-element.74.refs_16_), channel_id=1, source_target_pairs={{0,1},{1,0},{2,3},{3,2},{4,5},{5,4},{6,7},{7,6},{8,9},{9,8},{10,11... | collective-permute-start | bytes 786440 | tf_op jit(solution)/shard_map/ppermute | solution.py:558
  49.9 5.7 %collective-permute-start.8 = (bf16[2,128,512]{2,1,0:T(8,128)(2,1)S(1)}, bf16[2,128,512]{2,1,0:T(8,128)(2,1)S(1)}, u32[]{:S(2)}, u32[]{:S(2)}) collective-permute-start(bf16[2,128,512]{2,1,0:T(8,128)(2,1)S(1)} %get-tuple-element.89), channel_id=1, source_target_pairs={{0,32},{32,0},{64,96},{96,64},{1,33},{33,1},{65,97},{97,65},{2,34}... | collective-permute-start | bytes 786440 | tf_op jit(solution)/shard_map/ppermute | solution.py:558
  50.0 10.3 %collective-permute-start.9 = (bf16[2,128,512]{2,1,0:T(8,128)(2,1)S(1)}, bf16[2,128,512]{2,1,0:T(8,128)(2,1)S(1)}, u32[]{:S(2)}, u32[]{:S(2)}) collective-permute-start(bf16[2,128,512]{2,1,0:T(8,128)(2,1)S(1)} %get-tuple-element.90), channel_id=1, source_target_pairs={{32,64},{64,32},{33,65},{65,33},{34,66},{66,34},{35,67},{67,35},{3... | collective-permute-start | bytes 786440 | tf_op jit(solution)/shard_map/ppermute | solution.py:566
